TPU v7x, 32 devices: a whole 2x2x4 slice. The times are simulated.
32 devices in a mesh: gx: 4 (over y, x), gz: 8 (over z, core).
Axes of the slice: x: 2, y: 2, z: 4, core: 2. Of those that a mesh axis runs over, the one named last changes fastest.
Arguments:
- density: float32 [512, 64, 256], P('gx', 'gz'), may hold values from 0 to 1
- bin_rows: int32 [32], replicated, may hold values from 0 to 255
- tf_extinction: float32 [256, 16], replicated, may hold values from 0.5 to 2
- tf_color: float32 [256, 16], replicated, may hold values from 0 to 1
- extinction_scale: float32 [16], replicated, may hold values from 0.3 to 20
- ambient: float32 [16], replicated, may hold values from 0.1 to 1
- backdrop: float32 [16], replicated, may hold values from 0 to 1
Outputs:
- image: float32 [512, 16, 256], P(('gx', 'gz'))
All inputs are finite; a program needn't handle non-finite values.
Results may differ from a plain program's by a relative error of at most 0.0003.
Values sent between devices are 32-bit elements; how exact they have to be, the bound alone decides.
No kernel may reach another device: no remote copies, remote signals or barrier semaphores. Data moves between devices by JAX's collectives and lax.ppermute only.
A program may use at most 128 MiB of HBM per device.

v0:
```python
import jax
import jax.numpy as jnp
from jax import lax
from jax.sharding import PartitionSpec as P


def with_halo(x, sides, width):
    for axis, dim in sides:
        size, length = (lax.axis_size(axis), x.shape[dim])
        up = [(i, (i + 1) % size) for i in range(size - 1)]
        down = [(j, i) for i, j in up]
        last = lax.slice_in_dim(x, length - width, length, axis=dim)
        first = lax.slice_in_dim(x, 0, width, axis=dim)
        before = lax.ppermute(last, axis, up)
        after = lax.ppermute(first, axis, down)
        x = jnp.concatenate([before, x, after], axis=dim)
    return x


def entering(x, axis, combine, identity):
    length, mine = (lax.axis_size(axis), lax.axis_index(axis))
    everything = lax.all_gather(x, axis)
    start = jnp.broadcast_to(jnp.asarray(identity, x.dtype), x.shape)

    def step(k, before):
        reached = k < mine
        new = combine(before, everything[k])
        return jnp.where(reached, new, before)

    return lax.fori_loop(0, length, step, start)


def from_partner(value, axis, apart):
    mask = 2**apart
    pairs = [(source, source ^ mask) for source in range(lax.axis_size(axis))]
    return lax.ppermute(value, axis, pairs)


def blur(padded, axis):
    size = padded.shape[axis]
    low = lax.slice_in_dim(padded, 0, size - 2, axis=axis)
    mid = lax.slice_in_dim(padded, 1, size - 1, axis=axis)
    high = lax.slice_in_dim(padded, 2, size, axis=axis)
    return (low + 2.0 * mid + high) * 0.25


def plane_props(rho, table_cols, centers):
    scaled = rho * (centers.shape[0] - 1)
    weights = jnp.maximum(0.0, 1.0 - jnp.abs(scaled[None] - centers[:, None, None]))
    return jnp.einsum(
        "kb,bzy->kzy",
        table_cols,
        weights,
        precision=lax.Precision.HIGHEST,
        preferred_element_type=jnp.float32,
    )


def local(density, bin_rows, tf_extinction, tf_color, extinction_scale, ambient, backdrop):
    rows_x = density.shape[0]
    colors = tf_color.shape[1]
    bins = bin_rows.shape[0]
    count = lax.axis_size("gz")
    padded = with_halo(density, (("gx", 0), ("gz", 1)), 1)
    padded = jnp.pad(padded, ((0, 0), (0, 0), (1, 1)))
    smooth = blur(blur(blur(padded, 0), 1), 2)
    width_y = smooth.shape[2]
    both = jnp.concatenate([tf_extinction, tf_color], axis=1)
    onehot = (bin_rows[:, None] == jnp.arange(both.shape[0], dtype=jnp.int32)[None, :]).astype(
        jnp.float32
    )
    table = jnp.dot(
        onehot, both, precision=lax.Precision.HIGHEST, preferred_element_type=jnp.float32
    )
    table_cols = table.T
    centers = jnp.arange(bins, dtype=jnp.float32)
    scale_col = extinction_scale[:, None, None]
    step_x = 1.0 / (rows_x * lax.axis_size("gx"))
    step_z = 1.0 / (density.shape[1] * count)

    def combine_add(earlier, later):
        return earlier + later

    blocks = smooth.reshape(rows_x // 4, 4, smooth.shape[1], smooth.shape[2])

    def depth_advance(total, block):
        kept = []
        for plane in range(4):
            props = plane_props(block[plane], table_cols, centers)
            total = total + step_x * (props[:colors] * scale_col)
            kept.append(props)
        return (total, jnp.stack(kept))

    start = jnp.zeros((colors, smooth.shape[1], smooth.shape[2]), jnp.float32)
    total, saved = lax.scan(depth_advance, start, blocks)
    prefix = entering(total, "gx", combine_add, jnp.zeros_like(total))

    def render_advance(depth, block):
        partials = []
        throughs = []
        for plane in range(4):
            props = block[plane]
            sigma = props[:colors] * scale_col
            color = props[colors:]
            light = jnp.exp(-depth)
            shade = color * (ambient[:, None, None] + light)
            inclusive = jnp.cumsum(sigma, axis=1)
            weight = jnp.exp(-step_z * (inclusive - sigma)) * -jnp.expm1(-step_z * sigma)
            partials.append(jnp.sum(weight * shade, axis=1))
            throughs.append(jnp.exp(-step_z * inclusive[:, -1]))
            depth = depth + step_x * sigma
        return (depth, (jnp.stack(partials), jnp.stack(throughs)))

    depth_end, outputs = lax.scan(render_advance, prefix, saved)
    shape_out = (rows_x, colors, saved.shape[-1])
    partial_value = outputs[0].reshape(shape_out)
    through = outputs[1].reshape(shape_out)
    stacked = jnp.stack([partial_value, through])
    piece = stacked.reshape(2, count, rows_x // count, colors, width_y)
    piece = piece.transpose(0, 2, 1, 3, 4).reshape(2, rows_x, colors, width_y)
    position = lax.axis_index("gz")
    for bit in range(count.bit_length() - 1):
        length = piece.shape[1]
        pairs = piece.reshape(2, length // 2, 2, colors, width_y)
        side = position >> bit & 1
        keep = lax.dynamic_index_in_dim(pairs, side, 2, keepdims=False)
        give = lax.dynamic_index_in_dim(pairs, 1 - side, 2, keepdims=False)
        taken = from_partner(give, "gz", bit)
        front = jnp.where(side == 0, keep, taken)
        behind = jnp.where(side == 0, taken, keep)
        piece = jnp.stack([front[0] + front[1] * behind[0], front[1] * behind[1]])
    final_c = piece[0]
    final_a = piece[1]
    return final_c + final_a * backdrop[None, :, None]


def solution(mesh):
    in_specs = (P("gx", "gz", None), P(), P(), P(), P(), P(), P())
    out_specs = P(("gx", "gz"), None, None)
    return jax.shard_map(local, mesh=mesh, in_specs=in_specs, out_specs=out_specs, check_vma=False)
```

profile of v0, /device:TPU:0, one launch (start us, length us, event | category | flops | bytes accessed | tf_op | source)
XLA Modules:
  0.0 321.7 jit_solution(333776049377050768)
XLA Ops:
  0.8 4.9 %collective-permute-start = (f32[1,8,256]{2,0,1:T(1,128)S(1)}, f32[1,8,256]{2,0,1:T(1,128)S(1)}, u32[]{:S(2)}, u32[]{:S(2)}) collective-permute-start(f32[1,8,256]{2,0,1:T(1,128)S(1)} %copy.16), channel_id=1, source_target_pairs={{0,8},{8,16},{16,24},{1,9},{9,17},{17,25},{2,10},{10,18},{18,26},{... | collective-permute-start | bytes 24584 | tf_op jit(solution)/shard_map/ppermute | solution.py:14
  6.9 1.6 copy.18
  8.6 2.6 collective-permute-done.1
  14.1 3.5 %collective-permute-done.3 = f32[130,1,256]{2,0,1:T(8,128)S(1)} collective-permute-done((f32[130,1,256]{2,0,1:T(8,128)S(1)}, f32[130,1,256]{2,0,1:T(8,128)S(1)}, u32[]{:S(2)}, u32[]{:S(2)}) %collective-permute-start.3) | collective-permute-done | bytes 133152 | tf_op jit(solution)/shard_map/ppermute | solution.py:15
  20.3 94.9 %while.44 = (s32[]{:T(128)}, f32[16,8,256]{2,0,1:T(8,128)S(1)}, f32[32,4,32,8,256]{4,2,3,1,0:T(8,128)}, f32[32,4,8,256]{3,2,1,0:T(8,128)S(1)}, f32[32,32]{1,0:T(...) while((s32[]{:T(128)}, f32[16,8,256]{2,0,1:T(8,128)S(1)}, ...), condition=%wide.region_1.2_spmd.clone.clone, body=%wide.region_0.1_spmd.clone.clone.sunk | while | flops 102932480 | bytes 4047595 | solution.py:95
  115.2 10.9 %all-gather = f32[64,8,256]{2,0,1:T(8,128)S(1)} all-gather(f32[16,8,256]{2,0,1:T(8,128)S(1)} %get-tuple-element.169), channel_id=2, replica_groups=mesh['gx'=4,'gz'=8] {'gx'}, dimensions={0}, use_global_device_ids=true | all-gather | bytes 655360 | tf_op jit(solution)/shard_map/all_gather | solution.py:22
  126.8 124.7 %while.42 = (s32[]{:T(128)}, f32[16,8,256]{2,1,0:T(8,128)S(1)}, f32[32,4,16,256]{3,2,1,0:T(8,128)}, f32[32,4,16,256]{3,2,1,0:T(8,128)}, f32[32,4,32,8,256]{4,2,3...) while((s32[]{:T(128)}, f32[16,8,256]{2,1,0:T(8,128)S(1)}, ...), condition=%wide.region_13.14_spmd, body=%wide.region_4.13_spmd.sunk | while | flops 2785286 | bytes 7144281 | solution.py:114
  126.9 1.4 constant_dynamic-slice_fusion.11
  130.7 1.4 constant_dynamic-slice_fusion.11
  134.6 1.4 constant_dynamic-slice_fusion.11
  138.5 1.4 constant_dynamic-slice_fusion.11
  142.4 1.4 constant_dynamic-slice_fusion.11
  146.3 1.4 constant_dynamic-slice_fusion.11
  150.2 1.4 constant_dynamic-slice_fusion.11
  154.1 1.4 constant_dynamic-slice_fusion.11
  158.0 1.4 constant_dynamic-slice_fusion.11
  165.8 1.4 constant_dynamic-slice_fusion.11
  169.7 1.4 constant_dynamic-slice_fusion.11
  189.2 1.4 constant_dynamic-slice_fusion.11
  204.7 1.4 constant_dynamic-slice_fusion.11
  232.0 1.4 constant_dynamic-slice_fusion.11
  247.6 1.4 constant_dynamic-slice_fusion.11
  251.5 2.9 maximum_bitcast_fusion.3
  255.1 1.7 dynamic-slice_bitcast_fusion
  257.7 2.5 collective-permute-start.4
  260.2 4.0 %collective-permute-done.4 = f32[2,64,16,256]{3,2,1,0:T(8,128)S(1)} collective-permute-done((f32[2,64,16,256]{3,2,1,0:T(8,128)}, f32[2,64,16,256]{3,2,1,0:T(8,128)S(1)}, u32[]{:S(2)}, u32[]{:S(2)}) %collective-permute-start.4) | collective-permute-done | bytes 2097184 | tf_op jit(solution)/shard_map/ppermute | solution.py:36
  264.2 2.2 bitcast_select_fusion.1
  267.0 2.7 collective-permute-start.5
  269.7 23.6 %collective-permute-done.5 = f32[2,32,16,256]{3,2,1,0:T(8,128)} collective-permute-done((f32[2,32,16,256]{3,2,1,0:T(8,128)S(1)}, f32[2,32,16,256]{3,2,1,0:T(8,128)}, u32[]{:S(2)}, u32[]{:S(2)}) %collective-permute-start.5) | collective-permute-done | bytes 1048608 | tf_op jit(solution)/shard_map/ppermute | solution.py:36
  293.3 1.5 broadcast_select_fusion.1
  295.1 2.8 collective-permute-start.6
  297.9 22.8 %collective-permute-done.6 = f32[2,16,16,256]{3,2,1,0:T(8,128)S(1)} collective-permute-done((f32[2,16,16,256]{3,2,1,0:T(8,128)S(1)}, f32[2,16,16,256]{3,2,1,0:T(8,128)S(1)}, u32[]{:S(2)}, u32[]{:S(2)}) %collective-permute-start.6) | collective-permute-done | bytes 524320 | tf_op jit(solution)/shard_map/ppermute | solution.py:36
  (707 shorter events, 206.1 us)
Async XLA Ops:
  0.0 13.8 %copy-start.6 = (s32[32]{0:T(128)S(1)}, s32[32]{0:T(128)}, u32[]{:S(2)}) copy-start(s32[32]{0:T(128)} %param.14) | copy-start | bytes 388
  0.0 13.8 %copy-start.5 = (f32[256,16]{0,1:T(8,128)S(1)}, f32[256,16]{0,1:T(8,128)}, u32[]{:S(2)}) copy-start(f32[256,16]{0,1:T(8,128)} %param.15) | copy-start | bytes 49156
  0.0 13.8 %copy-start.4 = (f32[256,16]{0,1:T(8,128)S(1)}, f32[256,16]{0,1:T(8,128)}, u32[]{:S(2)}) copy-start(f32[256,16]{0,1:T(8,128)} %param.16) | copy-start | bytes 49156
  0.8 7.8 %collective-permute-start = (f32[1,8,256]{2,0,1:T(1,128)S(1)}, f32[1,8,256]{2,0,1:T(1,128)S(1)}, u32[]{:S(2)}, u32[]{:S(2)}) collective-permute-start(f32[1,8,256]{2,0,1:T(1,128)S(1)} %copy.16), channel_id=1, source_target_pairs={{0,8},{8,16},{16,24},{1,9},{9,17},{17,25},{2,10},{10,18},{18,26},{... | collective-permute-start | bytes 24584 | tf_op jit(solution)/shard_map/ppermute | solution.py:14
  5.6 5.5 %collective-permute-start.1 = (f32[1,8,256]{2,0,1:T(1,128)S(1)}, f32[1,8,256]{2,0,1:T(1,128)S(1)}, u32[]{:S(2)}, u32[]{:S(2)}) collective-permute-start(f32[1,8,256]{2,0,1:T(1,128)S(1)} %copy.17), channel_id=1, source_target_pairs={{8,0},{16,8},{24,16},{9,1},{17,9},{25,17},{10,2},{18,10},{26,18},{... | collective-permute-start | bytes 24584 | tf_op jit(solution)/shard_map/ppermute | solution.py:15
  11.2 2.9 collective-permute-start.2
  12.5 5.1 %collective-permute-start.3 = (f32[130,1,256]{2,0,1:T(8,128)S(1)}, f32[130,1,256]{2,0,1:T(8,128)S(1)}, u32[]{:S(2)}, u32[]{:S(2)}) collective-permute-start(f32[130,1,256]{2,0,1:T(8,128)S(1)} %get-tuple-element.341), channel_id=1, source_target_pairs={{1,0},{2,1},{3,2},{4,3},{5,4},{6,5},{7,6},{9,8},{10,9},{11,10},{12... | collective-permute-start | bytes 399368 | tf_op jit(solution)/shard_map/ppermute | solution.py:15
  19.6 0.7 copy-start.1
  115.2 11.6 %copy-start.2 = (f32[16]{0:T(128)S(1)}, f32[16]{0:T(128)}, u32[]{:S(2)}) copy-start(f32[16]{0:T(128)} %param.18) | copy-start | bytes 196
  255.1 2.6 copy-start
  257.7 6.5 %collective-permute-start.4 = (f32[2,64,16,256]{3,2,1,0:T(8,128)}, f32[2,64,16,256]{3,2,1,0:T(8,128)S(1)}, u32[]{:S(2)}, u32[]{:S(2)}) collective-permute-start(f32[2,64,16,256]{3,2,1,0:T(8,128)} %dynamic-slice_bitcast_fusion), channel_id=1, source_target_pairs={{0,1},{1,0},{2,3},{3,2},{4,5},{5,4},{6,7},{7,6},{8,9},{9,8},{10,11... | collective-permute-start | bytes 6291464 | tf_op jit(solution)/shard_map/ppermute | solution.py:36
  267.0 26.3 %collective-permute-start.5 = (f32[2,32,16,256]{3,2,1,0:T(8,128)S(1)}, f32[2,32,16,256]{3,2,1,0:T(8,128)}, u32[]{:S(2)}, u32[]{:S(2)}) collective-permute-start(f32[2,32,16,256]{3,2,1,0:T(8,128)S(1)} %fusion.90), channel_id=1, source_target_pairs={{0,2},{1,3},{2,0},{3,1},{4,6},{5,7},{6,4},{7,5},{8,10},{9,11},{10,... | collective-permute-start | bytes 3145736 | tf_op jit(solution)/shard_map/ppermute | solution.py:36
  295.0 25.9 %copy-start.3 = (f32[16]{0:T(128)S(1)}, f32[16]{0:T(128)}, u32[]{:S(2)}) copy-start(f32[16]{0:T(128)} %param.19) | copy-start | bytes 196
  295.1 25.7 %collective-permute-start.6 = (f32[2,16,16,256]{3,2,1,0:T(8,128)S(1)}, f32[2,16,16,256]{3,2,1,0:T(8,128)S(1)}, u32[]{:S(2)}, u32[]{:S(2)}) collective-permute-start(f32[2,16,16,256]{3,2,1,0:T(8,128)S(1)} %fusion.97), channel_id=1, source_target_pairs={{0,4},{1,5},{2,6},{3,7},{4,0},{5,1},{6,2},{7,3},{8,12},{9,13},{10,... | collective-permute-start | bytes 1572872 | tf_op jit(solution)/shard_map/ppermute | solution.py:36
where the time goes:
time: 323 us; the launch traced here: 322 us
  other arithmetic  128 us (40%)
  waiting for transfers between devices  56.5 us (17%)
  matrix products  53.3 us (17%)
  local copies, waits for them, and re-layouts  51.2 us (16%)
  starting transfers between devices  16.8 us (5%)
  blocking collectives  10.9 us (3%)
  loops' own time  4.63 us (1%)
    dot_general x128, matrix products, plane_props(): jnp.einsum('kb,bzy->kzy', table_cols, weights, precision=lax.Precision.HI...  53.1 us
    ppermute x3, waiting for transfers between devices, from_partner(): return lax.ppermute(value, axis, pairs)  50.4 us
    slice x32, local copies, waits for them, and re-layouts, render_advance(): color = props[colors:]  44.9 us
    dynamic_update_slice x32, other arithmetic, local(): total, saved = lax.scan(depth_advance, start, blocks)  35.5 us
    reduce_sum x32, other arithmetic, render_advance(): partials.append(jnp.sum(weight * shade, axis=1))  22.8 us
    dynamic_update_slice x32, other arithmetic, local(): depth_end, outputs = lax.scan(render_advance, prefix, saved)  21.3 us
    another operation x128, other arithmetic, render_advance(): inclusive = jnp.cumsum(sigma, axis=1)  15.9 us
    all_gather x1, blocking collectives, entering(): everything = lax.all_gather(x, axis)  10.9 us
  transfers between devices with their start and end apart: 7, of which 5 were waited for; matrix products, arithmetic and copies ran while one was open for 1% of the time, Pallas kernels for 0%

commit v1 on v0

v1 whole, which is shorter than its diff:
```python
import functools

import jax
import jax.numpy as jnp
from jax import lax
from jax.experimental import pallas as pl
from jax.experimental.pallas import tpu as pltpu
from jax.sharding import PartitionSpec as P

LANES = 128
LOG2E = 1.4426950408889634
MIB = 1 << 20


def group_ids(shape, width):
    return lax.broadcasted_iota(jnp.int32, shape, len(shape) - 1) // width


def swap_groups(tiles, groups, width):
    tiles = list(tiles)
    lane = group_ids(tiles[0].shape, width)
    bit = 1
    while bit < groups:
        upper = (lane & bit) != 0
        shift = bit * width
        for first in range(groups):
            if first & bit:
                continue
            a, b = tiles[first], tiles[first | bit]
            axis = a.ndim - 1
            tiles[first] = jnp.where(upper, pltpu.roll(b, shift, axis), a)
            tiles[first | bit] = jnp.where(upper, b, pltpu.roll(a, LANES - shift, axis))
        bit *= 2
    return tiles


def pack_kernel(groups, width, x_ref, out_ref):
    tile_count = x_ref.shape[3] // LANES
    steps, depth = x_ref.shape[1], x_ref.shape[2]
    lane = lax.broadcasted_iota(jnp.int32, (depth, LANES), 1)

    def body(step, carry):
        wide = []
        for part in range(groups):
            tiles = [x_ref[part, step, :, t * LANES:(t + 1) * LANES] for t in range(tile_count)]
            up = [pltpu.roll(tile, 1, 1) for tile in tiles]
            down = [pltpu.roll(tile, LANES - 1, 1) for tile in tiles]
            row = []
            for t in range(tile_count):
                before = up[t - 1] if t > 0 else jnp.zeros_like(up[0])
                after = down[t + 1] if t + 1 < tile_count else jnp.zeros_like(up[0])
                low = jnp.where(lane == 0, before, up[t])
                high = jnp.where(lane == LANES - 1, after, down[t])
                row.append(low + 2.0 * tiles[t] + high)
            wide.append(row)
        for t in range(tile_count):
            swapped = swap_groups([wide[part][t] for part in range(groups)], groups, width)
            for part in range(groups):
                out_ref[t * groups + part, step] = swapped[part]
        return carry

    lax.fori_loop(0, steps, body, 0)


def pack(x, groups, width):
    steps = x.shape[0] // groups
    blocks = x.shape[2] // width
    return pl.pallas_call(
        functools.partial(pack_kernel, groups, width),
        out_shape=jax.ShapeDtypeStruct((blocks, steps, x.shape[1], LANES), jnp.float32),
        in_specs=[pl.BlockSpec(memory_space=pltpu.VMEM)],
        out_specs=pl.BlockSpec(memory_space=pltpu.VMEM),
        compiler_params=pltpu.CompilerParams(vmem_limit_bytes=32 * MIB),
        name="pack",
    )(x.reshape(groups, steps, x.shape[1], x.shape[2]))


def depth_kernel(groups, width, bins, scale, *refs):
    count = len(refs) - 9
    pieces = refs[:count]
    halo_ref, table_ref, s_ref, start_ref, total_ref, raw, sums, halves, sem = refs[count:]
    steps, depth = pieces[0].shape[-3], pieces[0].shape[-2]
    layers = depth * count
    colors = table_ref.shape[0]
    me = lax.axis_index("gz")
    copies = []
    for apart in range(count):
        source = me ^ apart
        place = pl.multiple_of(8 + source * depth, 8)
        origin = pieces[apart].at[me] if apart == 0 else pieces[apart]
        copies.append(pltpu.make_async_copy(
            origin, raw.at[pl.ds(1, steps), pl.ds(place, depth), :], sem.at[apart]))
    for copy in copies:
        copy.start()
    zeros = jnp.zeros((steps + 2, 8, LANES), jnp.float32)
    raw[:, 0:8, :] = zeros
    raw[:, 8 + layers:16 + layers, :] = zeros
    for copy in copies:
        copy.wait()
    lane = group_ids((layers, LANES), width)
    halo = halo_ref[...].reshape(layers, LANES)
    low = pltpu.roll(raw[steps, 8:8 + layers, :], width, 1)
    high = pltpu.roll(raw[1, 8:8 + layers, :], LANES - width, 1)
    raw[0, 8:8 + layers, :] = jnp.where(lane == 0, halo, low)
    raw[steps + 1, 8:8 + layers, :] = jnp.where(lane == groups - 1, halo, high)

    def smooth(step, carry):
        v = raw[step] + 2.0 * raw[step + 1] + raw[step + 2]
        size = v.shape[0]
        before = pltpu.roll(v, 1, 0)
        after = pltpu.roll(v, size - 1, 0)
        total = before + 2.0 * v + after
        s_ref[step] = total[8:8 + layers] * (scale / 64.0)
        return carry

    lax.fori_loop(0, steps, smooth, 0)
    edge = lax.broadcasted_iota(jnp.int32, (bins, LANES), 0).astype(jnp.float32) - 1.0
    rows = steps // 2

    def count_layer(z, carry):
        for half in range(2):
            acc = jnp.zeros((bins, LANES), jnp.float32)
            for step in range(rows):
                row = jnp.broadcast_to(s_ref[half * rows + step, pl.ds(z, 1), :], (bins, LANES))
                acc = acc + jnp.minimum(jnp.maximum(row, edge), edge + 1.0)
            sums[half, z] = acc - edge * rows
        return carry

    lax.fori_loop(0, layers, count_layer, 0)
    table = table_ref[...]
    at_once = 4

    def products(chunk, carry):
        for half in range(2):
            wide = jnp.concatenate(
                [sums[half, chunk * at_once + k] for k in range(at_once)], axis=1)
            out = jnp.dot(table, wide, precision=lax.Precision.HIGHEST,
                          preferred_element_type=jnp.float32)
            for k in range(at_once):
                halves[half, chunk * at_once + k] = out[:, k * LANES:(k + 1) * LANES]
        return carry

    lax.fori_loop(0, layers // at_once, products, 0)
    group = group_ids((colors, LANES), width)

    def scan_groups(chunk, carry):
        packed = jnp.zeros((colors, LANES), jnp.float32)
        for k in range(groups):
            z = chunk * groups + k
            first = halves[0, z]
            both = first + halves[1, z]
            inclusive = both
            everything = both
            shift = 1
            while shift < groups:
                moved = pltpu.roll(inclusive, shift * width, 1)
                inclusive = inclusive + jnp.where(group >= shift, moved, 0.0)
                everything = everything + pltpu.roll(everything, shift * width, 1)
                shift *= 2
            begin = inclusive - both
            start_ref[0, z] = begin
            start_ref[1, z] = begin + first
            packed = jnp.where(group == k, everything, packed)
        total_ref[chunk] = packed
        return carry

    lax.fori_loop(0, layers // groups, scan_groups, 0)


def depths(own, received, halo, table, groups, width, bins):
    count, steps, depth, _ = own.shape
    layers = count * depth
    colors = table.shape[0]
    return pl.pallas_call(
        functools.partial(depth_kernel, groups, width, bins, float(bins - 1)),
        out_shape=(
            jax.ShapeDtypeStruct((steps, layers, LANES), jnp.float32),
            jax.ShapeDtypeStruct((2, layers, colors, LANES), jnp.float32),
            jax.ShapeDtypeStruct((layers // groups, colors, LANES), jnp.float32),
        ),
        in_specs=[pl.BlockSpec(memory_space=pl.ANY)] * count
        + [pl.BlockSpec(memory_space=pltpu.VMEM)] * 2,
        out_specs=[pl.BlockSpec(memory_space=pltpu.VMEM)] * 3,
        scratch_shapes=[
            pltpu.VMEM((steps + 2, layers + 16, LANES), jnp.float32),
            pltpu.VMEM((2, layers, bins, LANES), jnp.float32),
            pltpu.VMEM((2, layers, colors, LANES), jnp.float32),
            pltpu.SemaphoreType.DMA((count,)),
        ],
        compiler_params=pltpu.CompilerParams(vmem_limit_bytes=48 * MIB),
        name="depths",
    )(own, *received, halo, table)


def render_kernel(groups, width, bins, ratio, turn, s_ref, start_ref, table_ref, ambient_ref,
                  backdrop_ref, *refs):
    *before_refs, image_ref, depth = refs
    steps, layers, _ = s_ref.shape
    rows = steps // 2
    colors = ambient_ref.shape[0]
    half = (lax.axis_index("gz") + turn) % 2
    group = group_ids((colors, LANES), width)

    def begin(chunk, carry):
        packed = before_refs[0][chunk]
        for ref in before_refs[1:]:
            packed = packed + ref[chunk]
        for k in range(groups):
            z = chunk * groups + k
            value = jnp.where(group == k, packed, 0.0)
            shift = 1
            while shift < groups:
                value = value + pltpu.roll(value, shift * width, 1)
                shift *= 2
            depth[z] = start_ref[half, z] + value
        return carry

    lax.fori_loop(0, layers // groups, begin, 0)
    ambient = ambient_ref[...]
    table = table_ref[...]
    edge = (lax.broadcasted_iota(jnp.int32, (bins, LANES), 0).astype(jnp.float32) - 1.0).astype(
        jnp.bfloat16)
    zero = jnp.zeros((bins, LANES), jnp.bfloat16)
    one = jnp.ones((bins, LANES), jnp.bfloat16)
    block = 8

    def advance(step, carry):
        row = half * rows + step

        def layer_block(chunk, state):
            through, partial = state
            place = pl.multiple_of(chunk * block, block)
            s = s_ref[row, pl.ds(place, block), :]
            lower = jnp.floor(s)
            frac = s - lower
            coarse = frac.astype(jnp.bfloat16).astype(jnp.float32)
            fine = frac - coarse

            def wide(value, r):
                return jnp.broadcast_to(value[r:r + 1], (bins, LANES)).astype(jnp.bfloat16)

            columns = []
            for r in range(block):
                away = wide(lower, r) - edge
                main = jnp.minimum(jnp.maximum(away + wide(coarse, r), zero), one)
                rest = jnp.where(away == zero, wide(fine, r), zero)
                columns.append(jnp.concatenate([main, main, rest], axis=0))
            weights = jnp.concatenate(columns, axis=1)
            props = jnp.dot(table, weights, preferred_element_type=jnp.float32)
            for r in range(block):
                part = props[:, r * LANES:(r + 1) * LANES]
                sigma, color = part[:colors], part[colors:]
                later = through * jnp.exp2(sigma)
                z = place + r
                above = depth[z]
                shade = color * (ambient + jnp.exp2(above))
                partial = partial + (through - later) * shade
                depth[z] = above + sigma * ratio
                through = later
            return through, partial

        state = (jnp.ones((colors, LANES), jnp.float32), jnp.zeros((colors, LANES), jnp.float32))
        through, partial = lax.fori_loop(0, layers // block, layer_block, state, unroll=True)
        image_ref[step] = partial + through * backdrop_ref[...]
        return carry

    lax.fori_loop(0, rows, advance, 0)


def pack_image_kernel(groups, width, x_ref, out_ref):
    for chunk in range(x_ref.shape[0] // groups):
        tiles = swap_groups([x_ref[chunk * groups + k] for k in range(groups)], groups, width)
        for part in range(groups):
            out_ref[part, chunk] = tiles[part]


def pack_image(image, groups, width):
    rows, colors, _ = image.shape
    return pl.pallas_call(
        functools.partial(pack_image_kernel, groups, width),
        out_shape=jax.ShapeDtypeStruct((groups, rows // groups, colors, LANES), jnp.float32),
        in_specs=[pl.BlockSpec(memory_space=pltpu.VMEM)],
        out_specs=pl.BlockSpec(memory_space=pltpu.VMEM),
        name="pack_image",
    )(image)


def render(s, start, table, ambient, backdrop, before, groups, width, bins, ratio, turn):
    steps, layers, _ = s.shape
    colors = ambient.shape[0]
    return pl.pallas_call(
        functools.partial(render_kernel, groups, width, bins, ratio, turn),
        out_shape=jax.ShapeDtypeStruct((steps // 2, colors, LANES), jnp.float32),
        in_specs=[pl.BlockSpec(memory_space=pltpu.VMEM)] * (5 + len(before)),
        out_specs=pl.BlockSpec(memory_space=pltpu.VMEM),
        scratch_shapes=[pltpu.VMEM((layers, colors, LANES), jnp.float32)],
        compiler_params=pltpu.CompilerParams(vmem_limit_bytes=48 * MIB),
        name="render",
    )(s, start, table, ambient, backdrop, *before)


def unpack_kernel(groups, width, *refs):
    *pieces, out_ref = refs
    count = len(pieces)
    me = lax.axis_index("gz")
    chunks, colors, _ = pieces[0].shape
    for tile in range(count // groups):
        for chunk in range(chunks):
            values = []
            for part in range(groups):
                values.append(pieces[tile * groups + part][chunk])
            tiles = swap_groups(values, groups, width)
            for part in range(groups):
                out_ref[chunk * groups + part, :, tile * LANES:(tile + 1) * LANES] = tiles[part]


def unpack(pieces, groups, width):
    count, chunks, colors, _ = pieces.shape
    return pl.pallas_call(
        lambda x_ref, out_ref: unpack_kernel(
            groups, width, *[x_ref.at[k] for k in range(count)], out_ref),
        out_shape=jax.ShapeDtypeStruct((chunks * groups, colors, count * width), jnp.float32),
        in_specs=[pl.BlockSpec(memory_space=pltpu.VMEM)],
        out_specs=pl.BlockSpec(memory_space=pltpu.VMEM),
        name="unpack",
    )(pieces)


def exchange(value, axis, apart):
    pairs = [(source, source ^ apart) for source in range(lax.axis_size(axis))]
    return lax.ppermute(value, axis, pairs)


def local(density, bin_rows, tf_extinction, tf_color, extinction_scale, ambient, backdrop):
    rows_x, depth, width_y = density.shape
    colors = tf_color.shape[1]
    bins = bin_rows.shape[0]
    count = lax.axis_size("gz")
    size_x = lax.axis_size("gx")
    me = lax.axis_index("gz")
    width = width_y // count
    groups = LANES // width
    steps = rows_x // groups
    step_x = 1.0 / (rows_x * size_x)
    step_z = 1.0 / (depth * count)

    up = [(i, i + 1) for i in range(size_x - 1)]
    down = [(j, i) for i, j in up]
    before = lax.ppermute(density[rows_x - 1:], "gx", up)
    after = lax.ppermute(density[:1], "gx", down)

    packed = pack(density, groups, width)
    received = []
    for apart in range(count - 1, 0, -1):
        give = lax.dynamic_index_in_dim(packed, me ^ apart, 0, keepdims=False)
        received.insert(0, exchange(give, "gz", apart))
    middle = jnp.zeros((groups - 2,) + density.shape[1:], jnp.float32)
    halo = pack(jnp.concatenate([before, middle, after], axis=0), groups, width)
    halo = lax.all_to_all(halo[:, 0], "gz", 0, 0)

    both = jnp.concatenate([tf_extinction, tf_color], axis=1)
    onehot = (bin_rows[:, None] == jnp.arange(both.shape[0], dtype=jnp.int32)[None, :]).astype(
        jnp.float32)
    table = jnp.dot(onehot, both, precision=lax.Precision.HIGHEST,
                    preferred_element_type=jnp.float32)
    rises = jnp.concatenate([table[:1], table[1:] - table[:-1]], axis=0).T
    rise_sigma = rises[:colors] * extinction_scale[:, None]
    rise_all = jnp.concatenate([rise_sigma * (-step_z * LOG2E), rises[colors:]], axis=0)
    coarse = lax.reduce_precision(rise_all, 8, 7)
    fine = rise_all - coarse
    split = jnp.concatenate([coarse, fine, coarse], axis=1).astype(jnp.bfloat16)

    s, start, total = depths(
        packed, received, halo, rise_sigma * (-step_x * LOG2E), groups, width, bins)
    sums = []
    for hop in range(1, size_x):
        sums.append(lax.ppermute(total, "gx", [(i, i + hop) for i in range(size_x - hop)]))

    ambient = jnp.broadcast_to(ambient[:, None], (colors, LANES))
    backdrop = jnp.broadcast_to(backdrop[:, None], (colors, LANES))
    halves = [
        render(s, start, split, ambient, backdrop, sums, groups, width, bins, step_x / step_z, turn)
        for turn in range(2)
    ]
    share = steps // 2
    if share % groups == 0:
        parts = [pack_image(half, groups, width) for half in halves]
        got = []
        for apart in range(count):
            give = lax.dynamic_index_in_dim(
                parts[apart % 2], (me ^ apart) // 2, 0, keepdims=False)
            got.append(exchange(give, "gz", apart) if apart else give)
        pieces = jnp.stack(got)[jnp.arange(count) ^ me]
        return unpack(pieces, groups, width)
    even = me % 2 == 0
    image = jnp.stack([jnp.where(even, halves[0], halves[1]),
                       jnp.where(even, halves[1], halves[0])])
    image = image.reshape(2, share, colors, groups, width).transpose(3, 0, 1, 2, 4)
    image = lax.all_to_all(image.reshape(count, share, colors, width), "gz", 0, 0)
    return image.transpose(1, 2, 0, 3).reshape(share, colors, width_y)


def solution(mesh):
    in_specs = (P("gx", "gz", None), P(), P(), P(), P(), P(), P())
    out_specs = P(("gx", "gz"), None, None)
    return jax.shard_map(local, mesh=mesh, in_specs=in_specs, out_specs=out_specs, check_vma=False)
```

time: 323 us -> 119 us (0.37)
  other arithmetic: 128 us -> 0.4 us
  matrix products: 53.3 us -> 0.21 us
  Pallas kernels: 0 us -> 42.1 us
  local copies, waits for them, and re-layouts: 51.2 us -> 16.1 us
  waiting for transfers between devices: 56.5 us -> 22.6 us
  starting transfers between devices: 16.8 us -> 36.6 us
  blocking collectives: 10.9 us -> 0 us
  loops' own time: 4.63 us -> 0 us
    dynamic_update_slice x64 -> x0, other arithmetic: 56.8 us -> none  [the longest x32 35.5 us: local(): total, saved = lax.scan(depth_advance, start, blocks)]
    dot_general x128 -> x0, matrix products: 53.1 us -> none  [plane_props(): jnp.einsum('kb,bzy->kzy', table_cols, weights, precision=lax.Precision.HI...]
    ppermute x7 -> x19, waiting for transfers between devices: 56.5 us -> 9.06 us  [the longest x14 4.9 us: exchange(): return lax.ppermute(value, axis, pairs)]
    slice x35 -> x1, local copies, waits for them, and re-layouts: 45.7 us -> 0.72 us  [local(): before = lax.ppermute(density[rows_x - 1:], 'gx', up)]
    pallas_call x0 -> x8, Pallas kernels: none -> 42.1 us  [the longest x2 17 us: render(): pl.pallas_call(functools.partial(render_kernel, groups, width, bins, rati...]
    reduce_sum x32 -> x0, other arithmetic: 22.8 us -> none  [render_advance(): partials.append(jnp.sum(weight * shade, axis=1))]
    ppermute x7 -> x19, starting transfers between devices: 16.8 us -> 33.2 us  [the longest x14 19.9 us: exchange(): return lax.ppermute(value, axis, pairs)]
    another operation x130 -> x1, other arithmetic: 15.9 us -> 0.01 us  [the longest x128 15.9 us: render_advance(): inclusive = jnp.cumsum(sigma, axis=1)]
  transfers between devices with their start and end apart: 7 -> 20, of which waited for: 5 -> 7; matrix products, arithmetic and copies ran while one was open for 1% -> 2% of each run, Pallas kernels for 0% -> 9%
where the time goes in v1:
time: 119 us; the launch traced here: 118 us
  Pallas kernels  42.1 us (35%)
  starting transfers between devices  36.6 us (31%)
  waiting for transfers between devices  22.6 us (19%)
  local copies, waits for them, and re-layouts  16.1 us (14%)
    ppermute x14, starting transfers between devices, exchange(): return lax.ppermute(value, axis, pairs)  19.9 us
    pallas_call x2, Pallas kernels, render(): pl.pallas_call(functools.partial(render_kernel, groups, width, bins, rati...  17 us
    all_to_all x1, waiting for transfers between devices, local(): halo = lax.all_to_all(halo[:, 0], 'gz', 0, 0)  13.6 us
    unnamed x44, local copies, waits for them, and re-layouts  12.2 us
    pallas_call x1, Pallas kernels, depths(): pl.pallas_call(functools.partial(depth_kernel, groups, width, bins, float...  11.6 us
    ppermute x3, starting transfers between devices, local(): lax.ppermute(total, 'gx', [(i, i + hop) for i in range(size_x - hop)])  8.37 us
    pallas_call x2, Pallas kernels, pack(): pl.pallas_call(functools.partial(pack_kernel, groups, width), out_shape=j...  8.13 us
    ppermute x14, waiting for transfers between devices, exchange(): return lax.ppermute(value, axis, pairs)  4.9 us
  transfers between devices with their start and end apart: 20, of which 7 were waited for; matrix products, arithmetic and copies ran while one was open for 2% of the time, Pallas kernels for 9%

profile of v1, /device:TPU:0, one launch (start us, length us, event | category | flops | bytes accessed | tf_op | source)
XLA Modules:
  0.0 118.4 jit_solution(1797402822480436351)
XLA Ops:
  0.0 1.2 %copy-done = f32[128,8,256]{2,1,0:T(8,128)S(1)} copy-done((f32[128,8,256]{2,1,0:T(8,128)S(1)}, f32[128,8,256]{2,1,0:T(8,128)}, u32[]{:S(2)}) %copy-start) | copy-done | bytes 1048600
  1.2 7.3 %pack.2.refs_0_ = f32[8,32,8,128]{3,2,1,0:T(8,128)S(1)} custom-call(f32[4,32,8,256]{3,2,1,0:T(8,128)S(1)} %bitcast.51), custom_call_target="tpu_custom_call" | custom-call | tf_op jit(solution)/shard_map/pack/pallas_call | solution.py:68
  9.1 2.6 %collective-permute-start.1 = (f32[32,8,128]{2,1,0:T(8,128)S(1)}, f32[32,8,128]{2,1,0:T(8,128)S(1)}, u32[]{:S(2)}, u32[]{:S(2)}) collective-permute-start(f32[32,8,128]{2,1,0:T(8,128)S(1)} %get-tuple-element.18), channel_id=1, source_target_pairs={{0,2},{1,3},{2,0},{3,1},{4,6},{5,7},{6,4},{7,5},{8,10},{9,11},{10,... | collective-permute-start | bytes 393224 | tf_op jit(solution)/shard_map/ppermute | solution.py:331
  12.6 3.7 %collective-permute-start.7 = (f32[1,8,256]{2,1,0:T(8,128)S(1)}, f32[1,8,256]{2,1,0:T(8,128)S(1)}, u32[]{:S(2)}, u32[]{:S(2)}) collective-permute-start(f32[1,8,256]{2,1,0:T(8,128)S(1)} %get-tuple-element.11), channel_id=1, source_target_pairs={{0,8},{8,16},{16,24},{1,9},{9,17},{17,25},{2,10},{10,18},{18,26},{... | collective-permute-start | bytes 24584 | tf_op jit(solution)/shard_map/ppermute | solution.py:349
  16.2 1.3 %collective-permute-start.8 = (f32[1,8,256]{2,1,0:T(8,128)S(1)}, f32[1,8,256]{2,1,0:T(8,128)S(1)}, u32[]{:S(2)}, u32[]{:S(2)}) collective-permute-start(f32[1,8,256]{2,1,0:T(8,128)S(1)} %get-tuple-element.12), channel_id=1, source_target_pairs={{8,0},{16,8},{24,16},{9,1},{17,9},{25,17},{10,2},{18,10},{26,18},{... | collective-permute-start | bytes 24584 | tf_op jit(solution)/shard_map/ppermute | solution.py:350
  18.7 2.6 %collective-permute-start.3 = (f32[32,8,128]{2,1,0:T(8,128)S(1)}, f32[32,8,128]{2,1,0:T(8,128)S(1)}, u32[]{:S(2)}, u32[]{:S(2)}) collective-permute-start(f32[32,8,128]{2,1,0:T(8,128)S(1)} %get-tuple-element.16), channel_id=1, source_target_pairs={{0,4},{1,5},{2,6},{3,7},{4,0},{5,1},{6,2},{7,3},{8,12},{9,13},{10,... | collective-permute-start | bytes 393224 | tf_op jit(solution)/shard_map/ppermute | solution.py:331
  21.8 1.1 collective-permute-start.4
  22.9 2.5 %collective-permute-start.5 = (f32[32,8,128]{2,1,0:T(8,128)S(1)}, f32[32,8,128]{2,1,0:T(8,128)S(1)}, u32[]{:S(2)}, u32[]{:S(2)}) collective-permute-start(f32[32,8,128]{2,1,0:T(8,128)S(1)} %get-tuple-element.14), channel_id=1, source_target_pairs={{0,6},{1,7},{2,4},{3,5},{4,2},{5,3},{6,0},{7,1},{8,14},{9,15},{10,... | collective-permute-start | bytes 393224 | tf_op jit(solution)/shard_map/ppermute | solution.py:331
  25.4 2.2 %collective-permute-start.6 = (f32[32,8,128]{2,1,0:T(8,128)S(1)}, f32[32,8,128]{2,1,0:T(8,128)S(1)}, u32[]{:S(2)}, u32[]{:S(2)}) collective-permute-start(f32[32,8,128]{2,1,0:T(8,128)S(1)} %get-tuple-element.13), channel_id=1, source_target_pairs={{0,7},{1,6},{2,5},{3,4},{4,3},{5,2},{6,1},{7,0},{8,15},{9,14},{10,... | collective-permute-start | bytes 393224 | tf_op jit(solution)/shard_map/ppermute | solution.py:331
  28.6 3.3 %all-to-all-start = ((f32[8,8,128]{2,1,0:T(8,128)}), f32[8,8,128]{2,1,0:T(8,128)S(1)}, u32[]{:S(2)}, u32[]{:S(2)}) async-start(f32[8,8,128]{2,1,0:T(8,128)} %bitcast.9), calls=%async_computation | async-start | bytes 65536 | tf_op jit(solution)/shard_map/all_to_all | solution.py:359
  31.9 13.6 %all-to-all-done.refs_8_ = f32[8,8,128]{2,1,0:T(8,128)S(1)} async-done(((f32[8,8,128]{2,1,0:T(8,128)}), f32[8,8,128]{2,1,0:T(8,128)S(1)}, u32[]{:S(2)}, u32[]{:S(2)}) %all-to-all-start) | async-done | bytes 32800 | tf_op jit(solution)/shard_map/all_to_all | solution.py:359
  48.8 0.9 copy-done.4
  49.7 0.9 copy-done.6
  52.4 0.9 copy-done.12
  53.3 11.6 %depths.1 = (f32[32,64,128]{2,1,0:T(8,128)S(1)}, f32[2,64,16,128]{3,2,1,0:T(8,128)S(1)}, f32[16,16,128]{2,1,0:T(8,128)}) custom-call(f32[8,32,8,128]{3,2,1,0:T(8,128)S(1)} %pack.2.refs_0_, f32[32,8,128]{2,1,0:T(8,128)S(1)} %collective-permute-done.refs_1_, f32[32,8,128]{2,1,0:T(8,128)S(1)} %collective-permute-done.1.refs_2_, f32[32,8,128]{2,1,0:T(8,128)S(1)} %copy-done.4, ...), custom_call_target="tpu_custom_call" | custom-call | tf_op jit(solution)/shard_map/depths/pallas_call | solution.py:174
  64.9 5.2 %collective-permute-start.10 = (f32[16,16,128]{2,1,0:T(8,128)}, f32[16,16,128]{2,1,0:T(8,128)S(1)}, u32[]{:S(2)}, u32[]{:S(2)}) collective-permute-start(f32[16,16,128]{2,1,0:T(8,128)} %get-tuple-element.10), channel_id=1, source_target_pairs={{0,16},{8,24},{1,17},{9,25},{2,18},{10,26},{3,19},{11,27},{4,20},{... | collective-permute-start | bytes 393224 | tf_op jit(solution)/shard_map/ppermute | solution.py:377
  70.1 1.3 %collective-permute-start.11 = (f32[16,16,128]{2,1,0:T(8,128)}, f32[16,16,128]{2,1,0:T(8,128)S(1)}, u32[]{:S(2)}, u32[]{:S(2)}) collective-permute-start(f32[16,16,128]{2,1,0:T(8,128)} %get-tuple-element.10), channel_id=1, source_target_pairs={{0,24},{1,25},{2,26},{3,27},{4,28},{5,29},{6,30},{7,31}} | collective-permute-start | bytes 393224 | tf_op jit(solution)/shard_map/ppermute | solution.py:377
  71.5 1.9 %collective-permute-start.9 = (f32[16,16,128]{2,1,0:T(8,128)}, f32[16,16,128]{2,1,0:T(8,128)S(1)}, u32[]{:S(2)}, u32[]{:S(2)}) collective-permute-start(f32[16,16,128]{2,1,0:T(8,128)} %get-tuple-element.10), channel_id=1, source_target_pairs={{0,8},{8,16},{16,24},{1,9},{9,17},{17,25},{2,10},{10,18},{18,26},{... | collective-permute-start | bytes 393224 | tf_op jit(solution)/shard_map/ppermute | solution.py:377
  73.6 2.0 %collective-permute-done.11.refs_2_ = f32[16,16,128]{2,1,0:T(8,128)S(1)} collective-permute-done((f32[16,16,128]{2,1,0:T(8,128)}, f32[16,16,128]{2,1,0:T(8,128)S(1)}, u32[]{:S(2)}, u32[]{:S(2)}) %collective-permute-start.11) | collective-permute-done | bytes 131104 | tf_op jit(solution)/shard_map/ppermute | solution.py:377
  75.7 1.7 %collective-permute-done.9.refs_0_ = f32[16,16,128]{2,1,0:T(8,128)S(1)} collective-permute-done((f32[16,16,128]{2,1,0:T(8,128)}, f32[16,16,128]{2,1,0:T(8,128)S(1)}, u32[]{:S(2)}, u32[]{:S(2)}) %collective-permute-start.9) | collective-permute-done | bytes 131104 | tf_op jit(solution)/shard_map/ppermute | solution.py:377
  78.7 8.5 %render.3.x_ref = f32[16,16,128]{2,1,0:T(8,128)S(1)} custom-call(f32[32,64,128]{2,1,0:T(8,128)S(1)} %get-tuple-element.8.s_ref, f32[2,64,16,128]{3,2,1,0:T(8,128)S(1)} %get-tuple-element.9.start_ref, bf16[32,96]{1,0:T(8,128)(2,1)S(1)} %pad_maximum_fusion.1.table_ref, f32[16,128]{1,0:T(8,128)S(1)} %broadcast_in_dim.7.ambient_ref, ...), custom_call_target="tpu_custom_call" | custom-call | tf_op jit(solution)/shard_map/render/pallas_call | solution.py:291
  87.8 1.7 %pack_image.3 = f32[4,4,16,128]{3,2,1,0:T(8,128)} custom-call(f32[16,16,128]{2,1,0:T(8,128)} %copy-done.2), custom_call_target="tpu_custom_call" | custom-call | tf_op jit(solution)/shard_map/pack_image/pallas_call | solution.py:279
  90.5 8.5 %render.2.x_ref = f32[16,16,128]{2,1,0:T(8,128)S(1)} custom-call(f32[32,64,128]{2,1,0:T(8,128)S(1)} %get-tuple-element.8.s_ref, f32[2,64,16,128]{3,2,1,0:T(8,128)S(1)} %get-tuple-element.9.start_ref, bf16[32,96]{1,0:T(8,128)(2,1)S(1)} %pad_maximum_fusion.1.table_ref, f32[16,128]{1,0:T(8,128)S(1)} %broadcast_in_dim.7.ambient_ref, ...), custom_call_target="tpu_custom_call" | custom-call | tf_op jit(solution)/shard_map/render/pallas_call | solution.py:291
  99.6 1.7 %pack_image.2 = f32[4,4,16,128]{3,2,1,0:T(8,128)} custom-call(f32[16,16,128]{2,1,0:T(8,128)} %copy-done.1), custom_call_target="tpu_custom_call" | custom-call | tf_op jit(solution)/shard_map/pack_image/pallas_call | solution.py:279
  102.2 0.9 collective-permute-start.13
  103.1 1.0 collective-permute-start.14
  104.1 2.7 %collective-permute-start.15 = (f32[4,16,128]{2,1,0:T(8,128)S(1)}, f32[4,16,128]{2,1,0:T(8,128)S(1)}, u32[]{:S(2)}, u32[]{:S(2)}) collective-permute-start(f32[4,16,128]{2,1,0:T(8,128)S(1)} %get-tuple-element.25), channel_id=1, source_target_pairs={{0,4},{1,5},{2,6},{3,7},{4,0},{5,1},{6,2},{7,3},{8,12},{9,13},{10,... | collective-permute-start | bytes 98312 | tf_op jit(solution)/shard_map/ppermute | solution.py:331
  106.8 3.3 %collective-permute-start.17 = (f32[4,16,128]{2,1,0:T(8,128)S(1)}, f32[4,16,128]{2,1,0:T(8,128)S(1)}, u32[]{:S(2)}, u32[]{:S(2)}) collective-permute-start(f32[4,16,128]{2,1,0:T(8,128)S(1)} %get-tuple-element.24), channel_id=1, source_target_pairs={{0,6},{1,7},{2,4},{3,5},{4,2},{5,3},{6,0},{7,1},{8,14},{9,15},{10,... | collective-permute-start | bytes 98312 | tf_op jit(solution)/shard_map/ppermute | solution.py:331
  111.2 1.8 %collective-permute-done.17 = f32[4,16,128]{2,1,0:T(8,128)S(1)} collective-permute-done((f32[4,16,128]{2,1,0:T(8,128)S(1)}, f32[4,16,128]{2,1,0:T(8,128)S(1)}, u32[]{:S(2)}, u32[]{:S(2)}) %collective-permute-start.17) | collective-permute-done | bytes 32800 | tf_op jit(solution)/shard_map/ppermute | solution.py:331
  112.9 2.3 %collective-permute-done.18 = f32[4,16,128]{2,1,0:T(8,128)S(1)} collective-permute-done((f32[4,16,128]{2,1,0:T(8,128)S(1)}, f32[4,16,128]{2,1,0:T(8,128)S(1)}, u32[]{:S(2)}, u32[]{:S(2)}) %collective-permute-start.18) | collective-permute-done | bytes 32800 | tf_op jit(solution)/shard_map/ppermute | solution.py:331
  115.2 1.3 %gather_fusion = f32[8,4,16,128]{3,2,1,0:T(8,128)} fusion(f32[8,4,16,128]{3,2,1,0:T(8,128)S(1)} %bitcast_dynamic-update-slice_fusion, s32[1024]{0:T(1024)S(1)} %pad_clamp_fusion), kind=kCustom, calls=%fused_computation | custom fusion | bytes 524320 | tf_op jit(solution)/shard_map/gather | solution.py:393
  116.5 1.9 %unpack.1 = f32[16,16,256]{2,1,0:T(8,128)} custom-call(f32[8,4,16,128]{3,2,1,0:T(8,128)} %gather_fusion), custom_call_target="tpu_custom_call" | custom-call | tf_op jit(solution)/shard_map/unpack/pallas_call | solution.py:319
  (79 shorter events, 14.5 us)
Async XLA Ops:
  0.0 1.2 %copy-start = (f32[128,8,256]{2,1,0:T(8,128)S(1)}, f32[128,8,256]{2,1,0:T(8,128)}, u32[]{:S(2)}) copy-start(f32[128,8,256]{2,1,0:T(8,128)} %param.7) | copy-start | bytes 3145732
  8.6 14.3 %collective-permute-start = (f32[32,8,128]{2,1,0:T(8,128)S(1)}, f32[32,8,128]{2,1,0:T(8,128)S(1)}, u32[]{:S(2)}, u32[]{:S(2)}) collective-permute-start(f32[32,8,128]{2,1,0:T(8,128)S(1)} %get-tuple-element.19), channel_id=1, source_target_pairs={{0,1},{1,0},{2,3},{3,2},{4,5},{5,4},{6,7},{7,6},{8,9},{9,8},{10,11... | collective-permute-start | bytes 393224 | tf_op jit(solution)/shard_map/ppermute | solution.py:331
  9.1 16.3 %collective-permute-start.1 = (f32[32,8,128]{2,1,0:T(8,128)S(1)}, f32[32,8,128]{2,1,0:T(8,128)S(1)}, u32[]{:S(2)}, u32[]{:S(2)}) collective-permute-start(f32[32,8,128]{2,1,0:T(8,128)S(1)} %get-tuple-element.18), channel_id=1, source_target_pairs={{0,2},{1,3},{2,0},{3,1},{4,6},{5,7},{6,4},{7,5},{8,10},{9,11},{10,... | collective-permute-start | bytes 393224 | tf_op jit(solution)/shard_map/ppermute | solution.py:331
  11.8 5.8 %copy-start.16 = (f32[256,16]{0,1:T(8,128)S(1)}, f32[256,16]{0,1:T(8,128)}, u32[]{:S(2)}) copy-start(f32[256,16]{0,1:T(8,128)} %param.10) | copy-start | bytes 49156
  11.8 5.8 %copy-start.17 = (f32[256,16]{0,1:T(8,128)S(1)}, f32[256,16]{0,1:T(8,128)}, u32[]{:S(2)}) copy-start(f32[256,16]{0,1:T(8,128)} %param.9) | copy-start | bytes 49156
  11.8 33.7 %collective-permute-start.2 = (f32[32,8,128]{2,1,0:T(8,128)S(1)}, f32[32,8,128]{2,1,0:T(8,128)S(1)}, u32[]{:S(2)}, u32[]{:S(2)}) collective-permute-start(f32[32,8,128]{2,1,0:T(8,128)S(1)} %get-tuple-element.17), channel_id=1, source_target_pairs={{0,3},{1,2},{2,1},{3,0},{4,7},{5,6},{6,5},{7,4},{8,11},{9,10},{10,... | collective-permute-start | bytes 393224 | tf_op jit(solution)/shard_map/ppermute | solution.py:331
  12.6 5.0 %copy-start.18 = (s32[32]{0:T(128)S(1)}, s32[32]{0:T(128)}, u32[]{:S(2)}) copy-start(s32[32]{0:T(128)} %param.8) | copy-start | bytes 388
  12.6 6.1 %collective-permute-start.7 = (f32[1,8,256]{2,1,0:T(8,128)S(1)}, f32[1,8,256]{2,1,0:T(8,128)S(1)}, u32[]{:S(2)}, u32[]{:S(2)}) collective-permute-start(f32[1,8,256]{2,1,0:T(8,128)S(1)} %get-tuple-element.11), channel_id=1, source_target_pairs={{0,8},{8,16},{16,24},{1,9},{9,17},{17,25},{2,10},{10,18},{18,26},{... | collective-permute-start | bytes 24584 | tf_op jit(solution)/shard_map/ppermute | solution.py:349
  16.2 5.5 %collective-permute-start.8 = (f32[1,8,256]{2,1,0:T(8,128)S(1)}, f32[1,8,256]{2,1,0:T(8,128)S(1)}, u32[]{:S(2)}, u32[]{:S(2)}) collective-permute-start(f32[1,8,256]{2,1,0:T(8,128)S(1)} %get-tuple-element.12), channel_id=1, source_target_pairs={{8,0},{16,8},{24,16},{9,1},{17,9},{25,17},{10,2},{18,10},{26,18},{... | collective-permute-start | bytes 24584 | tf_op jit(solution)/shard_map/ppermute | solution.py:350
  17.9 0.7 copy-start.15
  18.7 27.4 %collective-permute-start.3 = (f32[32,8,128]{2,1,0:T(8,128)S(1)}, f32[32,8,128]{2,1,0:T(8,128)S(1)}, u32[]{:S(2)}, u32[]{:S(2)}) collective-permute-start(f32[32,8,128]{2,1,0:T(8,128)S(1)} %get-tuple-element.16), channel_id=1, source_target_pairs={{0,4},{1,5},{2,6},{3,7},{4,0},{5,1},{6,2},{7,3},{8,12},{9,13},{10,... | collective-permute-start | bytes 393224 | tf_op jit(solution)/shard_map/ppermute | solution.py:331
  21.8 25.0 %collective-permute-start.4 = (f32[32,8,128]{2,1,0:T(8,128)S(1)}, f32[32,8,128]{2,1,0:T(8,128)S(1)}, u32[]{:S(2)}, u32[]{:S(2)}) collective-permute-start(f32[32,8,128]{2,1,0:T(8,128)S(1)} %get-tuple-element.15), channel_id=1, source_target_pairs={{0,5},{1,4},{2,7},{3,6},{4,1},{5,0},{6,3},{7,2},{8,13},{9,12},{10,... | collective-permute-start | bytes 393224 | tf_op jit(solution)/shard_map/ppermute | solution.py:331
  22.9 24.6 %collective-permute-start.5 = (f32[32,8,128]{2,1,0:T(8,128)S(1)}, f32[32,8,128]{2,1,0:T(8,128)S(1)}, u32[]{:S(2)}, u32[]{:S(2)}) collective-permute-start(f32[32,8,128]{2,1,0:T(8,128)S(1)} %get-tuple-element.14), channel_id=1, source_target_pairs={{0,6},{1,7},{2,4},{3,5},{4,2},{5,3},{6,0},{7,1},{8,14},{9,15},{10,... | collective-permute-start | bytes 393224 | tf_op jit(solution)/shard_map/ppermute | solution.py:331
  25.4 22.7 %collective-permute-start.6 = (f32[32,8,128]{2,1,0:T(8,128)S(1)}, f32[32,8,128]{2,1,0:T(8,128)S(1)}, u32[]{:S(2)}, u32[]{:S(2)}) collective-permute-start(f32[32,8,128]{2,1,0:T(8,128)S(1)} %get-tuple-element.13), channel_id=1, source_target_pairs={{0,7},{1,6},{2,5},{3,4},{4,3},{5,2},{6,1},{7,0},{8,15},{9,14},{10,... | collective-permute-start | bytes 393224 | tf_op jit(solution)/shard_map/ppermute | solution.py:331
  28.6 16.9 %all-to-all-start = ((f32[8,8,128]{2,1,0:T(8,128)}), f32[8,8,128]{2,1,0:T(8,128)S(1)}, u32[]{:S(2)}, u32[]{:S(2)}) async-start(f32[8,8,128]{2,1,0:T(8,128)} %bitcast.9), calls=%async_computation | async-start | bytes 65536 | tf_op jit(solution)/shard_map/all_to_all | solution.py:359
  48.8 0.9 copy-start.4
  49.7 0.9 copy-start.6
  50.6 0.9 copy-start.8
  51.5 0.9 copy-start.10
  52.4 0.9 copy-start.12
  64.9 8.7 %collective-permute-start.10 = (f32[16,16,128]{2,1,0:T(8,128)}, f32[16,16,128]{2,1,0:T(8,128)S(1)}, u32[]{:S(2)}, u32[]{:S(2)}) collective-permute-start(f32[16,16,128]{2,1,0:T(8,128)} %get-tuple-element.10), channel_id=1, source_target_pairs={{0,16},{8,24},{1,17},{9,25},{2,18},{10,26},{3,19},{11,27},{4,20},{... | collective-permute-start | bytes 393224 | tf_op jit(solution)/shard_map/ppermute | solution.py:377
  70.1 5.5 %collective-permute-start.11 = (f32[16,16,128]{2,1,0:T(8,128)}, f32[16,16,128]{2,1,0:T(8,128)S(1)}, u32[]{:S(2)}, u32[]{:S(2)}) collective-permute-start(f32[16,16,128]{2,1,0:T(8,128)} %get-tuple-element.10), channel_id=1, source_target_pairs={{0,24},{1,25},{2,26},{3,27},{4,28},{5,29},{6,30},{7,31}} | collective-permute-start | bytes 393224 | tf_op jit(solution)/shard_map/ppermute | solution.py:377
  71.5 5.9 %collective-permute-start.9 = (f32[16,16,128]{2,1,0:T(8,128)}, f32[16,16,128]{2,1,0:T(8,128)S(1)}, u32[]{:S(2)}, u32[]{:S(2)}) collective-permute-start(f32[16,16,128]{2,1,0:T(8,128)} %get-tuple-element.10), channel_id=1, source_target_pairs={{0,8},{8,16},{16,24},{1,9},{9,17},{17,25},{2,10},{10,18},{18,26},{... | collective-permute-start | bytes 393224 | tf_op jit(solution)/shard_map/ppermute | solution.py:377
  87.2 0.7 copy-start.2
  90.4 16.4 %collective-permute-start.12 = (f32[4,16,128]{2,1,0:T(8,128)S(1)}, f32[4,16,128]{2,1,0:T(8,128)S(1)}, u32[]{:S(2)}, u32[]{:S(2)}) collective-permute-start(f32[4,16,128]{2,1,0:T(8,128)S(1)} %get-tuple-element.23), channel_id=1, source_target_pairs={{0,1},{1,0},{2,3},{3,2},{4,5},{5,4},{6,7},{7,6},{8,9},{9,8},{10,11... | collective-permute-start | bytes 98312 | tf_op jit(solution)/shard_map/ppermute | solution.py:331
  99.0 0.7 copy-start.1
  102.2 7.9 %collective-permute-start.13 = (f32[4,16,128]{2,1,0:T(8,128)S(1)}, f32[4,16,128]{2,1,0:T(8,128)S(1)}, u32[]{:S(2)}, u32[]{:S(2)}) collective-permute-start(f32[4,16,128]{2,1,0:T(8,128)S(1)} %get-tuple-element.26), channel_id=1, source_target_pairs={{0,2},{1,3},{2,0},{3,1},{4,6},{5,7},{6,4},{7,5},{8,10},{9,11},{10,... | collective-permute-start | bytes 98312 | tf_op jit(solution)/shard_map/ppermute | solution.py:331
  103.1 7.2 %collective-permute-start.14 = (f32[4,16,128]{2,1,0:T(8,128)S(1)}, f32[4,16,128]{2,1,0:T(8,128)S(1)}, u32[]{:S(2)}, u32[]{:S(2)}) collective-permute-start(f32[4,16,128]{2,1,0:T(8,128)S(1)} %get-tuple-element.22), channel_id=1, source_target_pairs={{0,3},{1,2},{2,1},{3,0},{4,7},{5,6},{6,5},{7,4},{8,11},{9,10},{10,... | collective-permute-start | bytes 98312 | tf_op jit(solution)/shard_map/ppermute | solution.py:331
  104.1 6.3 %collective-permute-start.15 = (f32[4,16,128]{2,1,0:T(8,128)S(1)}, f32[4,16,128]{2,1,0:T(8,128)S(1)}, u32[]{:S(2)}, u32[]{:S(2)}) collective-permute-start(f32[4,16,128]{2,1,0:T(8,128)S(1)} %get-tuple-element.25), channel_id=1, source_target_pairs={{0,4},{1,5},{2,6},{3,7},{4,0},{5,1},{6,2},{7,3},{8,12},{9,13},{10,... | collective-permute-start | bytes 98312 | tf_op jit(solution)/shard_map/ppermute | solution.py:331
  106.8 4.4 %collective-permute-start.16 = (f32[4,16,128]{2,1,0:T(8,128)S(1)}, f32[4,16,128]{2,1,0:T(8,128)S(1)}, u32[]{:S(2)}, u32[]{:S(2)}) collective-permute-start(f32[4,16,128]{2,1,0:T(8,128)S(1)} %get-tuple-element.21), channel_id=1, source_target_pairs={{0,5},{1,4},{2,7},{3,6},{4,1},{5,0},{6,3},{7,2},{8,13},{9,12},{10,... | collective-permute-start | bytes 98312 | tf_op jit(solution)/shard_map/ppermute | solution.py:331
  106.8 6.1 %collective-permute-start.17 = (f32[4,16,128]{2,1,0:T(8,128)S(1)}, f32[4,16,128]{2,1,0:T(8,128)S(1)}, u32[]{:S(2)}, u32[]{:S(2)}) collective-permute-start(f32[4,16,128]{2,1,0:T(8,128)S(1)} %get-tuple-element.24), channel_id=1, source_target_pairs={{0,6},{1,7},{2,4},{3,5},{4,2},{5,3},{6,0},{7,1},{8,14},{9,15},{10,... | collective-permute-start | bytes 98312 | tf_op jit(solution)/shard_map/ppermute | solution.py:331
  110.1 5.1 %collective-permute-start.18 = (f32[4,16,128]{2,1,0:T(8,128)S(1)}, f32[4,16,128]{2,1,0:T(8,128)S(1)}, u32[]{:S(2)}, u32[]{:S(2)}) collective-permute-start(f32[4,16,128]{2,1,0:T(8,128)S(1)} %get-tuple-element.20), channel_id=1, source_target_pairs={{0,7},{1,6},{2,5},{3,4},{4,3},{5,2},{6,1},{7,0},{8,15},{9,14},{10,... | collective-permute-start | bytes 98312 | tf_op jit(solution)/shard_map/ppermute | solution.py:331
  (7 other events, 4.6 us)

commit v2 on v1

v2 whole, which is shorter than its diff:
```python
import functools

import jax
import jax.numpy as jnp
from jax import lax
from jax.experimental import pallas as pl
from jax.experimental.pallas import tpu as pltpu
from jax.sharding import PartitionSpec as P

LANES = 128
LOG2E = 1.4426950408889634
MIB = 1 << 20


def group_ids(shape, width):
    return lax.broadcasted_iota(jnp.int32, shape, len(shape) - 1) // width


def swap_groups(tiles, groups, width):
    tiles = list(tiles)
    lane = group_ids(tiles[0].shape, width)
    bit = 1
    while bit < groups:
        upper = (lane & bit) != 0
        shift = bit * width
        for first in range(groups):
            if first & bit:
                continue
            a, b = tiles[first], tiles[first | bit]
            axis = a.ndim - 1
            tiles[first] = jnp.where(upper, pltpu.roll(b, shift, axis), a)
            tiles[first | bit] = jnp.where(upper, b, pltpu.roll(a, LANES - shift, axis))
        bit *= 2
    return tiles


def blur_rows(parts, lane):
    out = []
    for tiles in parts:
        axis = tiles[0].ndim - 1
        up = [pltpu.roll(tile, 1, axis) for tile in tiles]
        down = [pltpu.roll(tile, LANES - 1, axis) for tile in tiles]
        row = []
        for t in range(len(tiles)):
            before = up[t - 1] if t > 0 else jnp.zeros_like(up[0])
            after = down[t + 1] if t + 1 < len(tiles) else jnp.zeros_like(up[0])
            low = jnp.where(lane == 0, before, up[t])
            high = jnp.where(lane == LANES - 1, after, down[t])
            row.append(low + 2.0 * tiles[t] + high)
        out.append(row)
    return out


def pack_kernel(groups, width, x_ref, out_ref):
    tile_count = x_ref.shape[3] // LANES
    steps, depth = x_ref.shape[1], x_ref.shape[2]
    size = 4
    lane = lax.broadcasted_iota(jnp.int32, (size, depth, LANES), 2)

    def body(chunk, carry):
        place = pl.ds(chunk * size, size)
        wide = blur_rows(
            [[x_ref[part, place, :, t * LANES:(t + 1) * LANES] for t in range(tile_count)]
             for part in range(groups)], lane)
        for t in range(tile_count):
            swapped = swap_groups([wide[part][t] for part in range(groups)], groups, width)
            for part in range(groups):
                out_ref[t * groups + part, place] = swapped[part]
        return carry

    lax.fori_loop(0, steps // size, body, 0)


def pack(x, groups, width):
    steps = x.shape[0] // groups
    blocks = x.shape[2] // width
    return pl.pallas_call(
        functools.partial(pack_kernel, groups, width),
        out_shape=jax.ShapeDtypeStruct((blocks, steps, x.shape[1], LANES), jnp.float32),
        in_specs=[pl.BlockSpec(memory_space=pltpu.VMEM)],
        out_specs=pl.BlockSpec(memory_space=pltpu.VMEM),
        compiler_params=pltpu.CompilerParams(vmem_limit_bytes=8 * MIB),
        name="pack",
    )(x.reshape(groups, steps, x.shape[1], x.shape[2]))


def address_kernel(groups, width, packed_ref, before_ref, after_ref, *refs):
    out_refs, halo = refs[:-1], refs[-1]
    count, steps, depth, _ = packed_ref.shape
    me = lax.axis_index("gz")
    tile_count = before_ref.shape[2] // LANES
    lane = lax.broadcasted_iota(jnp.int32, (depth, LANES), 1)
    ends = blur_rows(
        [[ref[0, :, t * LANES:(t + 1) * LANES] for t in range(tile_count)]
         for ref in (before_ref, after_ref)], lane)
    for t in range(tile_count):
        tiles = [ends[0][t]] * (groups - 1) + [ends[1][t]]
        swapped = swap_groups(tiles, groups, width)
        for part in range(groups):
            halo[t * groups + part] = swapped[part]
    for apart in range(count):
        out_refs[apart][0:steps] = packed_ref[me ^ apart]
        out_refs[apart][steps] = halo[me ^ apart]


def address(packed, before, after, groups, width):
    count, steps, depth, _ = packed.shape
    shape = jax.ShapeDtypeStruct((steps + 1, depth, LANES), jnp.float32)
    return pl.pallas_call(
        functools.partial(address_kernel, groups, width),
        out_shape=[shape] * count,
        in_specs=[pl.BlockSpec(memory_space=pltpu.VMEM)] * 3,
        out_specs=[pl.BlockSpec(memory_space=pltpu.VMEM)] * count,
        scratch_shapes=[pltpu.VMEM((count, depth, LANES), jnp.float32)],
        compiler_params=pltpu.CompilerParams(vmem_limit_bytes=8 * MIB),
        name="address",
    )(packed, before, after)


def split_sum(table, wide):
    coarse = wide.astype(jnp.bfloat16)
    fine = (wide - coarse.astype(jnp.float32)).astype(jnp.bfloat16)
    weights = jnp.concatenate([coarse, coarse, fine], axis=0)
    return jnp.dot(table, weights, preferred_element_type=jnp.float32)


def depth_kernel(groups, width, bins, scale, *refs):
    count = len(refs) - 7
    pieces = refs[:count]
    table_ref, s_ref, start_ref, total_ref, raw, sums, halves = refs[count:]
    steps, depth = pieces[0].shape[-3] - 1, pieces[0].shape[-2]
    layers = depth * count
    colors = table_ref.shape[0]
    me = lax.axis_index("gz")
    zeros = jnp.zeros((steps + 2, 8, LANES), jnp.float32)
    raw[:, 0:8, :] = zeros
    raw[:, 8 + layers:16 + layers, :] = zeros
    lane = group_ids((depth, LANES), width)
    for apart in range(count):
        piece = pieces[apart]
        place = pl.ds(pl.multiple_of(8 + (me ^ apart) * depth, 8), depth)
        raw[1:steps + 1, place, :] = piece[0:steps]
        halo = piece[steps]
        low = pltpu.roll(piece[steps - 1], width, 1)
        high = pltpu.roll(piece[0], LANES - width, 1)
        raw[0, place, :] = jnp.where(lane == 0, halo, low)
        raw[steps + 1, place, :] = jnp.where(lane == groups - 1, halo, high)

    def smooth(step, carry):
        v = raw[step] + 2.0 * raw[step + 1] + raw[step + 2]
        size = v.shape[0]
        before = pltpu.roll(v, 1, 0)
        after = pltpu.roll(v, size - 1, 0)
        total = before + 2.0 * v + after
        s_ref[step] = total[8:8 + layers] * (scale / 64.0)
        return carry

    lax.fori_loop(0, steps, smooth, 0, unroll=2)
    edge = lax.broadcasted_iota(jnp.int32, (bins, LANES), 0).astype(jnp.float32) - 1.0
    rows = steps // 2

    def count_layer(z, carry):
        for half in range(2):
            acc = jnp.zeros((bins, LANES), jnp.float32)
            for step in range(rows):
                row = jnp.broadcast_to(s_ref[half * rows + step, pl.ds(z, 1), :], (bins, LANES))
                acc = acc + jnp.minimum(jnp.maximum(row, edge), edge + 1.0)
            sums[half, z] = acc - edge * rows
        return carry

    lax.fori_loop(0, layers, count_layer, 0, unroll=2)
    table = table_ref[...]
    at_once = 8

    def products(chunk, carry):
        wide = [sums[half, chunk * at_once + k] for half in range(2) for k in range(at_once)]
        out = split_sum(table, jnp.concatenate(wide, axis=1))
        for half in range(2):
            for k in range(at_once):
                place = (half * at_once + k) * LANES
                halves[half, chunk * at_once + k] = out[:, place:place + LANES]
        return carry

    lax.fori_loop(0, layers // at_once, products, 0, unroll=2)
    group = group_ids((colors, LANES), width)

    def scan_groups(chunk, carry):
        packed = jnp.zeros((colors, LANES), jnp.float32)
        for k in range(groups):
            z = chunk * groups + k
            first = halves[0, z]
            both = first + halves[1, z]
            inclusive = both
            everything = both
            shift = 1
            while shift < groups:
                moved = pltpu.roll(inclusive, shift * width, 1)
                inclusive = inclusive + jnp.where(group >= shift, moved, 0.0)
                everything = everything + pltpu.roll(everything, shift * width, 1)
                shift *= 2
            begin = inclusive - both
            start_ref[0, z] = begin
            start_ref[1, z] = begin + first
            packed = jnp.where(group == k, everything, packed)
        total_ref[chunk] = packed
        return carry

    lax.fori_loop(0, layers // groups, scan_groups, 0, unroll=4)


def depths(pieces, table, groups, width, bins):
    count = len(pieces)
    steps, depth = pieces[0].shape[0] - 1, pieces[0].shape[1]
    layers = count * depth
    colors = table.shape[0]
    return pl.pallas_call(
        functools.partial(depth_kernel, groups, width, bins, float(bins - 1)),
        out_shape=(
            jax.ShapeDtypeStruct((steps, layers, LANES), jnp.float32),
            jax.ShapeDtypeStruct((2, layers, colors, LANES), jnp.float32),
            jax.ShapeDtypeStruct((layers // groups, colors, LANES), jnp.float32),
        ),
        in_specs=[pl.BlockSpec(memory_space=pltpu.VMEM)] * (count + 1),
        out_specs=[pl.BlockSpec(memory_space=pltpu.VMEM)] * 3,
        scratch_shapes=[
            pltpu.VMEM((steps + 2, layers + 16, LANES), jnp.float32),
            pltpu.VMEM((2, layers, bins, LANES), jnp.float32),
            pltpu.VMEM((2, layers, colors, LANES), jnp.float32),
        ],
        compiler_params=pltpu.CompilerParams(
            vmem_limit_bytes=8 * MIB + layers * (LANES * 4 * 2) * (bins + 2 * colors)),
        name="depths",
    )(*pieces, table)


def render_kernel(groups, width, bins, ratio, turn, sums_count, s_ref, start_ref, table_ref,
                  columns_ref, *refs):
    before_refs = refs[:sums_count]
    out_refs, image, depth = refs[sums_count:-2], refs[-2], refs[-1]
    steps, layers, _ = s_ref.shape
    rows = steps // 2
    colors = columns_ref.shape[1]
    me = lax.axis_index("gz")
    half = (me + turn) % 2
    group = group_ids((colors, LANES), width)

    def begin(chunk, carry):
        packed = before_refs[0][chunk]
        for ref in before_refs[1:]:
            packed = packed + ref[chunk]
        for k in range(groups):
            z = chunk * groups + k
            value = jnp.where(group == k, packed, 0.0)
            shift = 1
            while shift < groups:
                value = value + pltpu.roll(value, shift * width, 1)
                shift *= 2
            depth[z] = start_ref[half, z] + value
        return carry

    lax.fori_loop(0, layers // groups, begin, 0, unroll=4)
    ambient = columns_ref[1]
    table = table_ref[...]
    edge = (lax.broadcasted_iota(jnp.int32, (bins, LANES), 0).astype(jnp.float32) - 1.0).astype(
        jnp.bfloat16)
    zero = jnp.zeros((bins, LANES), jnp.bfloat16)
    one = jnp.ones((bins, LANES), jnp.bfloat16)
    block = 8

    def advance(step, carry):
        row = half * rows + step

        def layer_block(chunk, state):
            through, partial = state
            place = pl.multiple_of(chunk * block, block)
            s = s_ref[row, pl.ds(place, block), :]
            lower = jnp.floor(s)
            frac = s - lower
            coarse = frac.astype(jnp.bfloat16).astype(jnp.float32)
            fine = frac - coarse

            def wide(value, r):
                return jnp.broadcast_to(value[r:r + 1], (bins, LANES)).astype(jnp.bfloat16)

            columns = []
            for r in range(block):
                away = wide(lower, r) - edge
                main = jnp.minimum(jnp.maximum(away + wide(coarse, r), zero), one)
                rest = jnp.where(away == zero, wide(fine, r), zero)
                columns.append(jnp.concatenate([main, main, rest], axis=0))
            weights = jnp.concatenate(columns, axis=1)
            props = jnp.dot(table, weights, preferred_element_type=jnp.float32)
            for r in range(block):
                part = props[:, r * LANES:(r + 1) * LANES]
                sigma, color = part[:colors], part[colors:]
                later = through * jnp.exp2(sigma)
                z = place + r
                above = depth[z]
                shade = color * (ambient + jnp.exp2(above))
                partial = partial + (through - later) * shade
                depth[z] = above + sigma * ratio
                through = later
            return through, partial

        state = (jnp.ones((colors, LANES), jnp.float32), jnp.zeros((colors, LANES), jnp.float32))
        through, partial = lax.fori_loop(0, layers // block, layer_block, state, unroll=True)
        image[step] = partial + through * columns_ref[2]
        return carry

    lax.fori_loop(0, rows, advance, 0)
    if len(out_refs) == 1:
        out_refs[0][...] = image[...]
        return
    for chunk in range(rows // groups):
        place = pl.ds(chunk * groups, groups)
        tiles = swap_groups([image[chunk * groups + k] for k in range(groups)], groups, width)
        for part in range(groups):
            image[chunk * groups + part] = tiles[part]
    for slot in range(groups):
        part = slot ^ (me // 2)
        for chunk in range(rows // groups):
            out_refs[slot][chunk] = image[chunk * groups + part]


def render(s, start, table, columns, before, groups, width, bins, ratio, turn):
    steps, layers, _ = s.shape
    colors = columns.shape[1]
    share = steps // 2
    if share % groups == 0:
        shapes = [jax.ShapeDtypeStruct((share // groups, colors, LANES), jnp.float32)] * groups
    else:
        shapes = [jax.ShapeDtypeStruct((share, colors, LANES), jnp.float32)]
    return pl.pallas_call(
        functools.partial(render_kernel, groups, width, bins, ratio, turn, len(before)),
        out_shape=shapes,
        in_specs=[pl.BlockSpec(memory_space=pltpu.VMEM)] * (4 + len(before)),
        out_specs=[pl.BlockSpec(memory_space=pltpu.VMEM)] * len(shapes),
        scratch_shapes=[
            pltpu.VMEM((share, colors, LANES), jnp.float32),
            pltpu.VMEM((layers, colors, LANES), jnp.float32),
        ],
        compiler_params=pltpu.CompilerParams(vmem_limit_bytes=8 * MIB + layers * colors * 512 * 4),
        name="render",
    )(s, start, table, columns, *before)


def unpack_kernel(groups, width, *refs):
    arrived, out_ref, pieces = refs[:-2], refs[-2], refs[-1]
    count = len(arrived)
    me = lax.axis_index("gz")
    for apart in range(count):
        pieces[me ^ apart] = arrived[apart][...]
    for tile in range(count // groups):
        for chunk in range(arrived[0].shape[0]):
            tiles = swap_groups(
                [pieces[tile * groups + part, chunk] for part in range(groups)], groups, width)
            for part in range(groups):
                out_ref[chunk * groups + part, :, tile * LANES:(tile + 1) * LANES] = tiles[part]


def unpack(arrived, groups, width):
    count = len(arrived)
    chunks, colors, _ = arrived[0].shape
    return pl.pallas_call(
        functools.partial(unpack_kernel, groups, width),
        out_shape=jax.ShapeDtypeStruct((chunks * groups, colors, count * width), jnp.float32),
        in_specs=[pl.BlockSpec(memory_space=pltpu.VMEM)] * count,
        out_specs=pl.BlockSpec(memory_space=pltpu.VMEM),
        scratch_shapes=[pltpu.VMEM((count, chunks, colors, LANES), jnp.float32)],
        compiler_params=pltpu.CompilerParams(vmem_limit_bytes=8 * MIB),
        name="unpack",
    )(*arrived)


def table_kernel(step_x, step_z, bins_ref, extinction_ref, color_ref, columns_ref, sum_ref,
                 split_ref):
    rows, bins = extinction_ref.shape[1], bins_ref.shape[1]
    colors = extinction_ref.shape[0]
    row = lax.broadcasted_iota(jnp.int32, (rows, bins), 0)
    bin_id = lax.broadcasted_iota(jnp.int32, (rows, bins), 1)
    here = (row == bins_ref[0:1, :]).astype(jnp.float32)
    below = ((row == bins_ref[1:2, :]) & (bin_id > 0)).astype(jnp.float32)

    def rise(ref):
        now = jnp.dot(ref[...], here, precision=lax.Precision.HIGHEST,
                      preferred_element_type=jnp.float32)
        then = jnp.dot(ref[...], below, precision=lax.Precision.HIGHEST,
                       preferred_element_type=jnp.float32)
        return now - then

    def split(value):
        coarse = value.astype(jnp.bfloat16)
        fine = (value - coarse.astype(jnp.float32)).astype(jnp.bfloat16)
        return jnp.concatenate([coarse, fine, coarse], axis=1)

    sigma = rise(extinction_ref) * columns_ref[0, :, 0:bins]
    sum_ref[...] = split(sigma * (-step_x * LOG2E))
    split_ref[0:colors] = split(sigma * (-step_z * LOG2E))
    split_ref[colors:2 * colors] = split(rise(color_ref))


def tables(bin_rows, tf_extinction, tf_color, columns, step_x, step_z):
    bins = bin_rows.shape[0]
    colors = tf_color.shape[1]
    shifted = jnp.stack([bin_rows, jnp.roll(bin_rows, 1)])
    return pl.pallas_call(
        functools.partial(table_kernel, step_x, step_z),
        out_shape=(
            jax.ShapeDtypeStruct((colors, 3 * bins), jnp.bfloat16),
            jax.ShapeDtypeStruct((2 * colors, 3 * bins), jnp.bfloat16),
        ),
        in_specs=[pl.BlockSpec(memory_space=pltpu.VMEM)] * 4,
        out_specs=[pl.BlockSpec(memory_space=pltpu.VMEM)] * 2,
        compiler_params=pltpu.CompilerParams(vmem_limit_bytes=4 * MIB),
        name="tables",
    )(shifted, tf_extinction.T, tf_color.T, columns)


def exchange(value, axis, apart):
    pairs = [(source, source ^ apart) for source in range(lax.axis_size(axis))]
    return lax.ppermute(value, axis, pairs)


def local(density, bin_rows, tf_extinction, tf_color, extinction_scale, ambient, backdrop):
    rows_x, depth, width_y = density.shape
    colors = tf_color.shape[1]
    bins = bin_rows.shape[0]
    count = lax.axis_size("gz")
    size_x = lax.axis_size("gx")
    me = lax.axis_index("gz")
    width = width_y // count
    groups = LANES // width
    steps = rows_x // groups
    step_x = 1.0 / (rows_x * size_x)
    step_z = 1.0 / (depth * count)

    up = [(i, i + 1) for i in range(size_x - 1)]
    down = [(j, i) for i, j in up]
    before = lax.ppermute(density[rows_x - 1:], "gx", up)
    after = lax.ppermute(density[:1], "gx", down)

    packed = pack(density, groups, width)
    pieces = list(address(packed, before, after, groups, width))
    for apart in range(count - 1, 0, -1):
        pieces[apart] = exchange(pieces[apart], "gz", apart)
    columns = jnp.broadcast_to(
        jnp.stack([extinction_scale, ambient, backdrop])[:, :, None], (3, colors, LANES))
    sum_table, table = tables(bin_rows, tf_extinction, tf_color, columns, step_x, step_z)

    s, start, total = depths(pieces, sum_table, groups, width, bins)
    sums = []
    for hop in range(1, size_x):
        sums.append(lax.ppermute(total, "gx", [(i, i + hop) for i in range(size_x - hop)]))

    halves = [
        render(s, start, table, columns, sums, groups, width, bins, step_x / step_z, turn)
        for turn in range(2)
    ]
    share = steps // 2
    if share % groups == 0:
        arrived = []
        for apart in range(count):
            give = halves[apart % 2][apart // 2]
            arrived.append(exchange(give, "gz", apart) if apart else give)
        return unpack(arrived, groups, width)
    halves = [half[0] for half in halves]
    even = me % 2 == 0
    image = jnp.stack([jnp.where(even, halves[0], halves[1]),
                       jnp.where(even, halves[1], halves[0])])
    image = image.reshape(2, share, colors, groups, width).transpose(3, 0, 1, 2, 4)
    image = lax.all_to_all(image.reshape(count, share, colors, width), "gz", 0, 0)
    return image.transpose(1, 2, 0, 3).reshape(share, colors, width_y)


def solution(mesh):
    in_specs = (P("gx", "gz", None), P(), P(), P(), P(), P(), P())
    out_specs = P(("gx", "gz"), None, None)
    return jax.shard_map(local, mesh=mesh, in_specs=in_specs, out_specs=out_specs, check_vma=False)
```

time: 119 us -> 86.4 us (0.73)
  Pallas kernels: 42.1 us -> 24 us
  local copies, waits for them, and re-layouts: 16.1 us -> 3.91 us
  waiting for transfers between devices: 22.6 us -> 21.1 us
    all_to_all x1 -> x0, waiting for transfers between devices: 13.6 us -> none  [local(): halo = lax.all_to_all(halo[:, 0], 'gz', 0, 0)]
    ppermute x14, waiting for transfers between devices: 4.9 us -> 17.2 us  [exchange(): return lax.ppermute(value, axis, pairs)]
    unnamed x44 -> x14, local copies, waits for them, and re-layouts: 12.2 us -> 2.54 us
    pallas_call x2 -> x1, Pallas kernels: 8.13 us -> 2.41 us  [pack(): pl.pallas_call(functools.partial(pack_kernel, groups, width), out_shape=j...]
    pallas_call x1, Pallas kernels: 11.6 us -> 5.98 us  [depths(): pl.pallas_call(functools.partial(depth_kernel, groups, width, bins, float...]
    pallas_call x3, Pallas kernels: 5.37 us -> 1.65 us  [the longest x1 0.99 us: unpack(): pl.pallas_call(functools.partial(unpack_kernel, groups, width), out_shape...]
    all_to_all x1 -> x0, starting transfers between devices: 3.34 us -> none  [local(): halo = lax.all_to_all(halo[:, 0], 'gz', 0, 0)]
    pallas_call x2, Pallas kernels: 17 us -> 13.9 us  [render(): pl.pallas_call(functools.partial(render_kernel, groups, width, bins, rati...]
  transfers between devices with their start and end apart: 20 -> 19, of which waited for: 7 -> 5; matrix products, arithmetic and copies ran while one was open for 2% -> 2% of each run, Pallas kernels for 9% -> 11%
where the time goes in v2:
time: 86.4 us; the launch traced here: 85.9 us
  starting transfers between devices  36.1 us (42%)
  Pallas kernels  24 us (28%)
  waiting for transfers between devices  21.1 us (24%)
  local copies, waits for them, and re-layouts  3.91 us (5%)
    ppermute x14, starting transfers between devices, exchange(): return lax.ppermute(value, axis, pairs)  22.7 us
    ppermute x14, waiting for transfers between devices, exchange(): return lax.ppermute(value, axis, pairs)  17.2 us
    pallas_call x2, Pallas kernels, render(): pl.pallas_call(functools.partial(render_kernel, groups, width, bins, rati...  13.9 us
    ppermute x3, starting transfers between devices, local(): lax.ppermute(total, 'gx', [(i, i + hop) for i in range(size_x - hop)])  6.59 us
    pallas_call x1, Pallas kernels, depths(): pl.pallas_call(functools.partial(depth_kernel, groups, width, bins, float...  5.98 us
    ppermute x1, starting transfers between devices, local(): before = lax.ppermute(density[rows_x - 1:], 'gx', up)  5.47 us
    ppermute x3, waiting for transfers between devices, local(): lax.ppermute(total, 'gx', [(i, i + hop) for i in range(size_x - hop)])  3.83 us
    unnamed x14, local copies, waits for them, and re-layouts  2.54 us
  transfers between devices with their start and end apart: 19, of which 5 were waited for; matrix products, arithmetic and copies ran while one was open for 2% of the time, Pallas kernels for 11%

profile of v2, /device:TPU:0, one launch (start us, length us, event | category | flops | bytes accessed | tf_op | source)
XLA Modules:
  0.0 85.9 jit_solution(13069530363484288832)
XLA Ops:
  0.0 0.7 fusion
  0.7 1.3 %collective-permute-start.1 = (f32[1,8,256]{2,1,0:T(8,128)S(1)}, f32[1,8,256]{2,1,0:T(8,128)S(1)}, u32[]{:S(2)}, u32[]{:S(2)}) collective-permute-start(f32[1,8,256]{2,1,0:T(8,128)S(1)} %get-tuple-element.47), channel_id=1, source_target_pairs={{8,0},{16,8},{24,16},{9,1},{17,9},{25,17},{10,2},{18,10},{26,18},{... | collective-permute-start | bytes 24584 | tf_op jit(solution)/shard_map/ppermute | solution.py:440
  2.0 5.5 %collective-permute-start = (f32[1,8,256]{2,1,0:T(8,128)S(1)}, f32[1,8,256]{2,1,0:T(8,128)S(1)}, u32[]{:S(2)}, u32[]{:S(2)}) collective-permute-start(f32[1,8,256]{2,1,0:T(8,128)S(1)} %get-tuple-element.48), channel_id=1, source_target_pairs={{0,8},{8,16},{16,24},{1,9},{9,17},{17,25},{2,10},{10,18},{18,26},{... | collective-permute-start | bytes 24584 | tf_op jit(solution)/shard_map/ppermute | solution.py:439
  7.5 1.2 %copy-done = f32[128,8,256]{2,1,0:T(8,128)S(1)} copy-done((f32[128,8,256]{2,1,0:T(8,128)S(1)}, f32[128,8,256]{2,1,0:T(8,128)}, u32[]{:S(2)}) %copy-start) | copy-done | bytes 1048600
  8.7 2.4 %pack.1.packed_ref = f32[8,32,8,128]{3,2,1,0:T(8,128)S(1)} custom-call(f32[4,32,8,256]{3,2,1,0:T(8,128)S(1)} %bitcast.10), custom_call_target="tpu_custom_call" | custom-call | tf_op jit(solution)/shard_map/pack/pallas_call | solution.py:77
  11.2 0.2 address.1
  11.5 2.2 %collective-permute-start.3 = (f32[33,8,128]{2,1,0:T(8,128)S(1)}, f32[33,8,128]{2,1,0:T(8,128)S(1)}, u32[]{:S(2)}, u32[]{:S(2)}) collective-permute-start(f32[33,8,128]{2,1,0:T(8,128)S(1)} %get-tuple-element.28), channel_id=1, source_target_pairs={{0,2},{1,3},{2,0},{3,1},{4,6},{5,7},{6,4},{7,5},{8,10},{9,11},{10,... | collective-permute-start | bytes 405512 | tf_op jit(solution)/shard_map/ppermute | solution.py:421
  13.6 0.6 slice.16
  14.2 0.7 add_bitcast_fusion
  15.0 2.8 %collective-permute-start.5 = (f32[33,8,128]{2,1,0:T(8,128)S(1)}, f32[33,8,128]{2,1,0:T(8,128)S(1)}, u32[]{:S(2)}, u32[]{:S(2)}) collective-permute-start(f32[33,8,128]{2,1,0:T(8,128)S(1)} %get-tuple-element.30), channel_id=1, source_target_pairs={{0,4},{1,5},{2,6},{3,7},{4,0},{5,1},{6,2},{7,3},{8,12},{9,13},{10,... | collective-permute-start | bytes 405512 | tf_op jit(solution)/shard_map/ppermute | solution.py:421
  17.8 3.5 %collective-permute-start.7 = (f32[33,8,128]{2,1,0:T(8,128)S(1)}, f32[33,8,128]{2,1,0:T(8,128)S(1)}, u32[]{:S(2)}, u32[]{:S(2)}) collective-permute-start(f32[33,8,128]{2,1,0:T(8,128)S(1)} %get-tuple-element.32), channel_id=1, source_target_pairs={{0,6},{1,7},{2,4},{3,5},{4,2},{5,3},{6,0},{7,1},{8,14},{9,15},{10,... | collective-permute-start | bytes 405512 | tf_op jit(solution)/shard_map/ppermute | solution.py:421
  21.5 0.6 copy-done.3
  22.3 0.6 copy-done.1
  22.9 0.4 tables.1
  23.4 1.1 %collective-permute-done.4.refs_3_ = f32[33,8,128]{2,1,0:T(8,128)S(1)} collective-permute-done((f32[33,8,128]{2,1,0:T(8,128)S(1)}, f32[33,8,128]{2,1,0:T(8,128)S(1)}, u32[]{:S(2)}, u32[]{:S(2)}) %collective-permute-start.4) | collective-permute-done | bytes 135200 | tf_op jit(solution)/shard_map/ppermute | solution.py:421
  24.4 11.8 %collective-permute-done.6.refs_5_ = f32[33,8,128]{2,1,0:T(8,128)S(1)} collective-permute-done((f32[33,8,128]{2,1,0:T(8,128)S(1)}, f32[33,8,128]{2,1,0:T(8,128)S(1)}, u32[]{:S(2)}, u32[]{:S(2)}) %collective-permute-start.6) | collective-permute-done | bytes 135200 | tf_op jit(solution)/shard_map/ppermute | solution.py:421
  36.2 6.0 %depths.1 = (f32[32,64,128]{2,1,0:T(8,128)S(1)}, f32[2,64,16,128]{3,2,1,0:T(8,128)S(1)}, f32[16,16,128]{2,1,0:T(8,128)S(1)}) custom-call(f32[33,8,128]{2,1,0:T(8,128)S(1)} %get-tuple-element.26.refs_0_, f32[33,8,128]{2,1,0:T(8,128)S(1)} %collective-permute-done.2.refs_1_, f32[33,8,128]{2,1,0:T(8,128)S(1)} %collective-permute-done.3.refs_2_, ...), custom_call_target="tpu_custom_call" | custom-call | tf_op jit(solution)/shard_map/depths/pallas_call | solution.py:216
  42.2 2.8 %collective-permute-start.11 = (f32[16,16,128]{2,1,0:T(8,128)S(1)}, f32[16,16,128]{2,1,0:T(8,128)S(1)}, u32[]{:S(2)}, u32[]{:S(2)}) collective-permute-start(f32[16,16,128]{2,1,0:T(8,128)S(1)} %get-tuple-element.38), channel_id=1, source_target_pairs={{0,24},{1,25},{2,26},{3,27},{4,28},{5,29},{6,30},{7,31}} | collective-permute-start | bytes 393224 | tf_op jit(solution)/shard_map/ppermute | solution.py:453
  45.0 1.5 %collective-permute-start.10 = (f32[16,16,128]{2,1,0:T(8,128)S(1)}, f32[16,16,128]{2,1,0:T(8,128)S(1)}, u32[]{:S(2)}, u32[]{:S(2)}) collective-permute-start(f32[16,16,128]{2,1,0:T(8,128)S(1)} %get-tuple-element.38), channel_id=1, source_target_pairs={{0,16},{8,24},{1,17},{9,25},{2,18},{10,26},{3,19},{11,27},{4,20},{... | collective-permute-start | bytes 393224 | tf_op jit(solution)/shard_map/ppermute | solution.py:453
  46.6 2.2 %collective-permute-start.9 = (f32[16,16,128]{2,1,0:T(8,128)S(1)}, f32[16,16,128]{2,1,0:T(8,128)S(1)}, u32[]{:S(2)}, u32[]{:S(2)}) collective-permute-start(f32[16,16,128]{2,1,0:T(8,128)S(1)} %get-tuple-element.38), channel_id=1, source_target_pairs={{0,8},{8,16},{16,24},{1,9},{9,17},{17,25},{2,10},{10,18},{18,26},{... | collective-permute-start | bytes 393224 | tf_op jit(solution)/shard_map/ppermute | solution.py:453
  48.8 3.8 %collective-permute-done.10.refs_1_ = f32[16,16,128]{2,1,0:T(8,128)S(1)} collective-permute-done((f32[16,16,128]{2,1,0:T(8,128)S(1)}, f32[16,16,128]{2,1,0:T(8,128)S(1)}, u32[]{:S(2)}, u32[]{:S(2)}) %collective-permute-start.10) | collective-permute-done | bytes 131104 | tf_op jit(solution)/shard_map/ppermute | solution.py:453
  52.7 7.0 %render.3 = (f32[4,16,128]{2,1,0:T(8,128)S(1)}, f32[4,16,128]{2,1,0:T(8,128)S(1)}, f32[4,16,128]{2,1,0:T(8,128)S(1)}, f32[4,16,128]{2,1,0:T(8,128)S(1)}) custom-call(f32[32,64,128]{2,1,0:T(8,128)S(1)} %get-tuple-element.35.s_ref, f32[2,64,16,128]{3,2,1,0:T(8,128)S(1)} %get-tuple-element.36.start_ref, bf16[32,96]{1,0:T(8,128)(2,1)S(1)} %get-tuple-element.37.table_ref, ...), custom_call_target="tpu_custom_call" | custom-call | tf_op jit(solution)/shard_map/render/pallas_call | solution.py:333
  59.7 6.2 %collective-permute-start.14 = (f32[4,16,128]{2,1,0:T(8,128)S(1)}, f32[4,16,128]{2,1,0:T(8,128)S(1)}, u32[]{:S(2)}, u32[]{:S(2)}) collective-permute-start(f32[4,16,128]{2,1,0:T(8,128)S(1)} %get-tuple-element.42), channel_id=1, source_target_pairs={{0,3},{1,2},{2,1},{3,0},{4,7},{5,6},{6,5},{7,4},{8,11},{9,10},{10,... | collective-permute-start | bytes 98312 | tf_op jit(solution)/shard_map/ppermute | solution.py:421
  66.0 2.0 %collective-permute-start.16 = (f32[4,16,128]{2,1,0:T(8,128)S(1)}, f32[4,16,128]{2,1,0:T(8,128)S(1)}, u32[]{:S(2)}, u32[]{:S(2)}) collective-permute-start(f32[4,16,128]{2,1,0:T(8,128)S(1)} %get-tuple-element.44), channel_id=1, source_target_pairs={{0,5},{1,4},{2,7},{3,6},{4,1},{5,0},{6,3},{7,2},{8,13},{9,12},{10,... | collective-permute-start | bytes 98312 | tf_op jit(solution)/shard_map/ppermute | solution.py:421
  68.0 1.1 %collective-permute-start.18 = (f32[4,16,128]{2,1,0:T(8,128)S(1)}, f32[4,16,128]{2,1,0:T(8,128)S(1)}, u32[]{:S(2)}, u32[]{:S(2)}) collective-permute-start(f32[4,16,128]{2,1,0:T(8,128)S(1)} %get-tuple-element.46), channel_id=1, source_target_pairs={{0,7},{1,6},{2,5},{3,4},{4,3},{5,2},{6,1},{7,0},{8,15},{9,14},{10,... | collective-permute-start | bytes 98312 | tf_op jit(solution)/shard_map/ppermute | solution.py:421
  69.2 7.0 %render.2 = (f32[4,16,128]{2,1,0:T(8,128)S(1)}, f32[4,16,128]{2,1,0:T(8,128)S(1)}, f32[4,16,128]{2,1,0:T(8,128)S(1)}, f32[4,16,128]{2,1,0:T(8,128)S(1)}) custom-call(f32[32,64,128]{2,1,0:T(8,128)S(1)} %get-tuple-element.35.s_ref, f32[2,64,16,128]{3,2,1,0:T(8,128)S(1)} %get-tuple-element.36.start_ref, bf16[32,96]{1,0:T(8,128)(2,1)S(1)} %get-tuple-element.37.table_ref, ...), custom_call_target="tpu_custom_call" | custom-call | tf_op jit(solution)/shard_map/render/pallas_call | solution.py:333
  76.1 0.6 collective-permute-start.13
  76.7 2.5 %collective-permute-start.15 = (f32[4,16,128]{2,1,0:T(8,128)S(1)}, f32[4,16,128]{2,1,0:T(8,128)S(1)}, u32[]{:S(2)}, u32[]{:S(2)}) collective-permute-start(f32[4,16,128]{2,1,0:T(8,128)S(1)} %get-tuple-element.43), channel_id=1, source_target_pairs={{0,4},{1,5},{2,6},{3,7},{4,0},{5,1},{6,2},{7,3},{8,12},{9,13},{10,... | collective-permute-start | bytes 98312 | tf_op jit(solution)/shard_map/ppermute | solution.py:421
  79.2 1.4 %collective-permute-start.17 = (f32[4,16,128]{2,1,0:T(8,128)S(1)}, f32[4,16,128]{2,1,0:T(8,128)S(1)}, u32[]{:S(2)}, u32[]{:S(2)}) collective-permute-start(f32[4,16,128]{2,1,0:T(8,128)S(1)} %get-tuple-element.45), channel_id=1, source_target_pairs={{0,6},{1,7},{2,4},{3,5},{4,2},{5,3},{6,0},{7,1},{8,14},{9,15},{10,... | collective-permute-start | bytes 98312 | tf_op jit(solution)/shard_map/ppermute | solution.py:421
  80.6 1.2 %collective-permute-done.15.refs_4_ = f32[4,16,128]{2,1,0:T(8,128)S(1)} collective-permute-done((f32[4,16,128]{2,1,0:T(8,128)S(1)}, f32[4,16,128]{2,1,0:T(8,128)S(1)}, u32[]{:S(2)}, u32[]{:S(2)}) %collective-permute-start.15) | collective-permute-done | bytes 32800 | tf_op jit(solution)/shard_map/ppermute | solution.py:421
  81.8 3.1 %collective-permute-done.17.refs_6_ = f32[4,16,128]{2,1,0:T(8,128)S(1)} collective-permute-done((f32[4,16,128]{2,1,0:T(8,128)S(1)}, f32[4,16,128]{2,1,0:T(8,128)S(1)}, u32[]{:S(2)}, u32[]{:S(2)}) %collective-permute-start.17) | collective-permute-done | bytes 32800 | tf_op jit(solution)/shard_map/ppermute | solution.py:421
  84.9 1.0 %unpack.1 = f32[16,16,256]{2,1,0:T(8,128)} custom-call(f32[4,16,128]{2,1,0:T(8,128)S(1)} %get-tuple-element.39.refs_0_, f32[4,16,128]{2,1,0:T(8,128)S(1)} %collective-permute-done.12.refs_1_, f32[4,16,128]{2,1,0:T(8,128)S(1)} %collective-permute-done.13.refs_2_, f32[4,16,128]{2,1,0:T(8,128)S(1)} %collective-permute-done.14.refs_3_, ...), custom_call_target="tpu_custom_call" | custom-call | tf_op jit(solution)/shard_map/unpack/pallas_call | solution.py:364
  (33 shorter events, 0.5 us)
Async XLA Ops:
  0.7 10.4 %collective-permute-start.1 = (f32[1,8,256]{2,1,0:T(8,128)S(1)}, f32[1,8,256]{2,1,0:T(8,128)S(1)}, u32[]{:S(2)}, u32[]{:S(2)}) collective-permute-start(f32[1,8,256]{2,1,0:T(8,128)S(1)} %get-tuple-element.47), channel_id=1, source_target_pairs={{8,0},{16,8},{24,16},{9,1},{17,9},{25,17},{10,2},{18,10},{26,18},{... | collective-permute-start | bytes 24584 | tf_op jit(solution)/shard_map/ppermute | solution.py:440
  2.0 9.1 %collective-permute-start = (f32[1,8,256]{2,1,0:T(8,128)S(1)}, f32[1,8,256]{2,1,0:T(8,128)S(1)}, u32[]{:S(2)}, u32[]{:S(2)}) collective-permute-start(f32[1,8,256]{2,1,0:T(8,128)S(1)} %get-tuple-element.48), channel_id=1, source_target_pairs={{0,8},{8,16},{16,24},{1,9},{9,17},{17,25},{2,10},{10,18},{18,26},{... | collective-permute-start | bytes 24584 | tf_op jit(solution)/shard_map/ppermute | solution.py:439
  7.5 1.2 %copy-start = (f32[128,8,256]{2,1,0:T(8,128)S(1)}, f32[128,8,256]{2,1,0:T(8,128)}, u32[]{:S(2)}) copy-start(f32[128,8,256]{2,1,0:T(8,128)} %param.7) | copy-start | bytes 3145732
  11.4 2.3 %copy-start.6 = (s32[32]{0:T(128)S(1)}, s32[32]{0:T(128)}, u32[]{:S(2)}) copy-start(s32[32]{0:T(128)} %param.8) | copy-start | bytes 388
  11.4 6.4 %collective-permute-start.2 = (f32[33,8,128]{2,1,0:T(8,128)S(1)}, f32[33,8,128]{2,1,0:T(8,128)S(1)}, u32[]{:S(2)}, u32[]{:S(2)}) collective-permute-start(f32[33,8,128]{2,1,0:T(8,128)S(1)} %get-tuple-element.27), channel_id=1, source_target_pairs={{0,1},{1,0},{2,3},{3,2},{4,5},{5,4},{6,7},{7,6},{8,9},{9,8},{10,11... | collective-permute-start | bytes 405512 | tf_op jit(solution)/shard_map/ppermute | solution.py:421
  11.5 9.9 %collective-permute-start.3 = (f32[33,8,128]{2,1,0:T(8,128)S(1)}, f32[33,8,128]{2,1,0:T(8,128)S(1)}, u32[]{:S(2)}, u32[]{:S(2)}) collective-permute-start(f32[33,8,128]{2,1,0:T(8,128)S(1)} %get-tuple-element.28), channel_id=1, source_target_pairs={{0,2},{1,3},{2,0},{3,1},{4,6},{5,7},{6,4},{7,5},{8,10},{9,11},{10,... | collective-permute-start | bytes 405512 | tf_op jit(solution)/shard_map/ppermute | solution.py:421
  14.9 9.5 %collective-permute-start.4 = (f32[33,8,128]{2,1,0:T(8,128)S(1)}, f32[33,8,128]{2,1,0:T(8,128)S(1)}, u32[]{:S(2)}, u32[]{:S(2)}) collective-permute-start(f32[33,8,128]{2,1,0:T(8,128)S(1)} %get-tuple-element.29), channel_id=1, source_target_pairs={{0,3},{1,2},{2,1},{3,0},{4,7},{5,6},{6,5},{7,4},{8,11},{9,10},{10,... | collective-permute-start | bytes 405512 | tf_op jit(solution)/shard_map/ppermute | solution.py:421
  15.0 9.4 %collective-permute-start.5 = (f32[33,8,128]{2,1,0:T(8,128)S(1)}, f32[33,8,128]{2,1,0:T(8,128)S(1)}, u32[]{:S(2)}, u32[]{:S(2)}) collective-permute-start(f32[33,8,128]{2,1,0:T(8,128)S(1)} %get-tuple-element.30), channel_id=1, source_target_pairs={{0,4},{1,5},{2,6},{3,7},{4,0},{5,1},{6,2},{7,3},{8,12},{9,13},{10,... | collective-permute-start | bytes 405512 | tf_op jit(solution)/shard_map/ppermute | solution.py:421
  17.8 18.4 %collective-permute-start.6 = (f32[33,8,128]{2,1,0:T(8,128)S(1)}, f32[33,8,128]{2,1,0:T(8,128)S(1)}, u32[]{:S(2)}, u32[]{:S(2)}) collective-permute-start(f32[33,8,128]{2,1,0:T(8,128)S(1)} %get-tuple-element.31), channel_id=1, source_target_pairs={{0,5},{1,4},{2,7},{3,6},{4,1},{5,0},{6,3},{7,2},{8,13},{9,12},{10,... | collective-permute-start | bytes 405512 | tf_op jit(solution)/shard_map/ppermute | solution.py:421
  17.8 18.4 %collective-permute-start.7 = (f32[33,8,128]{2,1,0:T(8,128)S(1)}, f32[33,8,128]{2,1,0:T(8,128)S(1)}, u32[]{:S(2)}, u32[]{:S(2)}) collective-permute-start(f32[33,8,128]{2,1,0:T(8,128)S(1)} %get-tuple-element.32), channel_id=1, source_target_pairs={{0,6},{1,7},{2,4},{3,5},{4,2},{5,3},{6,0},{7,1},{8,14},{9,15},{10,... | collective-permute-start | bytes 405512 | tf_op jit(solution)/shard_map/ppermute | solution.py:421
  21.4 14.9 %collective-permute-start.8 = (f32[33,8,128]{2,1,0:T(8,128)S(1)}, f32[33,8,128]{2,1,0:T(8,128)S(1)}, u32[]{:S(2)}, u32[]{:S(2)}) collective-permute-start(f32[33,8,128]{2,1,0:T(8,128)S(1)} %get-tuple-element.33), channel_id=1, source_target_pairs={{0,7},{1,6},{2,5},{3,4},{4,3},{5,2},{6,1},{7,0},{8,15},{9,14},{10,... | collective-permute-start | bytes 405512 | tf_op jit(solution)/shard_map/ppermute | solution.py:421
  21.5 0.7 copy-start.3
  21.5 0.7 copy-start.4
  21.5 0.7 copy-start.5
  22.2 0.7 copy-start.1
  22.2 0.7 copy-start.2
  42.2 6.6 %collective-permute-start.11 = (f32[16,16,128]{2,1,0:T(8,128)S(1)}, f32[16,16,128]{2,1,0:T(8,128)S(1)}, u32[]{:S(2)}, u32[]{:S(2)}) collective-permute-start(f32[16,16,128]{2,1,0:T(8,128)S(1)} %get-tuple-element.38), channel_id=1, source_target_pairs={{0,24},{1,25},{2,26},{3,27},{4,28},{5,29},{6,30},{7,31}} | collective-permute-start | bytes 393224 | tf_op jit(solution)/shard_map/ppermute | solution.py:453
  45.0 7.6 %collective-permute-start.10 = (f32[16,16,128]{2,1,0:T(8,128)S(1)}, f32[16,16,128]{2,1,0:T(8,128)S(1)}, u32[]{:S(2)}, u32[]{:S(2)}) collective-permute-start(f32[16,16,128]{2,1,0:T(8,128)S(1)} %get-tuple-element.38), channel_id=1, source_target_pairs={{0,16},{8,24},{1,17},{9,25},{2,18},{10,26},{3,19},{11,27},{4,20},{... | collective-permute-start | bytes 393224 | tf_op jit(solution)/shard_map/ppermute | solution.py:453
  46.6 6.1 %collective-permute-start.9 = (f32[16,16,128]{2,1,0:T(8,128)S(1)}, f32[16,16,128]{2,1,0:T(8,128)S(1)}, u32[]{:S(2)}, u32[]{:S(2)}) collective-permute-start(f32[16,16,128]{2,1,0:T(8,128)S(1)} %get-tuple-element.38), channel_id=1, source_target_pairs={{0,8},{8,16},{16,24},{1,9},{9,17},{17,25},{2,10},{10,18},{18,26},{... | collective-permute-start | bytes 393224 | tf_op jit(solution)/shard_map/ppermute | solution.py:453
  59.6 17.1 %collective-permute-start.12 = (f32[4,16,128]{2,1,0:T(8,128)S(1)}, f32[4,16,128]{2,1,0:T(8,128)S(1)}, u32[]{:S(2)}, u32[]{:S(2)}) collective-permute-start(f32[4,16,128]{2,1,0:T(8,128)S(1)} %get-tuple-element.40), channel_id=1, source_target_pairs={{0,1},{1,0},{2,3},{3,2},{4,5},{5,4},{6,7},{7,6},{8,9},{9,8},{10,11... | collective-permute-start | bytes 98312 | tf_op jit(solution)/shard_map/ppermute | solution.py:421
  59.7 19.5 %collective-permute-start.14 = (f32[4,16,128]{2,1,0:T(8,128)S(1)}, f32[4,16,128]{2,1,0:T(8,128)S(1)}, u32[]{:S(2)}, u32[]{:S(2)}) collective-permute-start(f32[4,16,128]{2,1,0:T(8,128)S(1)} %get-tuple-element.42), channel_id=1, source_target_pairs={{0,3},{1,2},{2,1},{3,0},{4,7},{5,6},{6,5},{7,4},{8,11},{9,10},{10,... | collective-permute-start | bytes 98312 | tf_op jit(solution)/shard_map/ppermute | solution.py:421
  66.0 14.6 %collective-permute-start.16 = (f32[4,16,128]{2,1,0:T(8,128)S(1)}, f32[4,16,128]{2,1,0:T(8,128)S(1)}, u32[]{:S(2)}, u32[]{:S(2)}) collective-permute-start(f32[4,16,128]{2,1,0:T(8,128)S(1)} %get-tuple-element.44), channel_id=1, source_target_pairs={{0,5},{1,4},{2,7},{3,6},{4,1},{5,0},{6,3},{7,2},{8,13},{9,12},{10,... | collective-permute-start | bytes 98312 | tf_op jit(solution)/shard_map/ppermute | solution.py:421
  68.0 12.6 %collective-permute-start.18 = (f32[4,16,128]{2,1,0:T(8,128)S(1)}, f32[4,16,128]{2,1,0:T(8,128)S(1)}, u32[]{:S(2)}, u32[]{:S(2)}) collective-permute-start(f32[4,16,128]{2,1,0:T(8,128)S(1)} %get-tuple-element.46), channel_id=1, source_target_pairs={{0,7},{1,6},{2,5},{3,4},{4,3},{5,2},{6,1},{7,0},{8,15},{9,14},{10,... | collective-permute-start | bytes 98312 | tf_op jit(solution)/shard_map/ppermute | solution.py:421
  76.1 4.5 %collective-permute-start.13 = (f32[4,16,128]{2,1,0:T(8,128)S(1)}, f32[4,16,128]{2,1,0:T(8,128)S(1)}, u32[]{:S(2)}, u32[]{:S(2)}) collective-permute-start(f32[4,16,128]{2,1,0:T(8,128)S(1)} %get-tuple-element.41), channel_id=1, source_target_pairs={{0,2},{1,3},{2,0},{3,1},{4,6},{5,7},{6,4},{7,5},{8,10},{9,11},{10,... | collective-permute-start | bytes 98312 | tf_op jit(solution)/shard_map/ppermute | solution.py:421
  76.7 5.1 %collective-permute-start.15 = (f32[4,16,128]{2,1,0:T(8,128)S(1)}, f32[4,16,128]{2,1,0:T(8,128)S(1)}, u32[]{:S(2)}, u32[]{:S(2)}) collective-permute-start(f32[4,16,128]{2,1,0:T(8,128)S(1)} %get-tuple-element.43), channel_id=1, source_target_pairs={{0,4},{1,5},{2,6},{3,7},{4,0},{5,1},{6,2},{7,3},{8,12},{9,13},{10,... | collective-permute-start | bytes 98312 | tf_op jit(solution)/shard_map/ppermute | solution.py:421
  79.2 5.7 %collective-permute-start.17 = (f32[4,16,128]{2,1,0:T(8,128)S(1)}, f32[4,16,128]{2,1,0:T(8,128)S(1)}, u32[]{:S(2)}, u32[]{:S(2)}) collective-permute-start(f32[4,16,128]{2,1,0:T(8,128)S(1)} %get-tuple-element.45), channel_id=1, source_target_pairs={{0,6},{1,7},{2,4},{3,5},{4,2},{5,3},{6,0},{7,1},{8,14},{9,15},{10,... | collective-permute-start | bytes 98312 | tf_op jit(solution)/shard_map/ppermute | solution.py:421

commit v3 on v2

--- a/solution.py
+++ b/solution.py
@@ -124,21 +124,21 @@
     return jnp.dot(table, weights, preferred_element_type=jnp.float32)
 
 
-def depth_kernel(groups, width, bins, scale, *refs):
-    count = len(refs) - 7
-    pieces = refs[:count]
-    table_ref, s_ref, start_ref, total_ref, raw, sums, halves = refs[count:]
+def depth_kernel(groups, width, bins, scale, far, halves_count, count, *refs):
+    pieces = refs[:-7]
+    table_ref, s_ref, start_ref, total_ref, raw, sums, products_ref = refs[-7:]
     steps, depth = pieces[0].shape[-3] - 1, pieces[0].shape[-2]
-    layers = depth * count
+    blocks = count // 2
+    layers = depth * blocks
+    slots = s_ref.shape[1]
+    used = layers + 1 if far else layers
     colors = table_ref.shape[0]
     me = lax.axis_index("gz")
-    zeros = jnp.zeros((steps + 2, 8, LANES), jnp.float32)
-    raw[:, 0:8, :] = zeros
-    raw[:, 8 + layers:16 + layers, :] = zeros
+    lower = me < blocks
     lane = group_ids((depth, LANES), width)
-    for apart in range(count):
-        piece = pieces[apart]
-        place = pl.ds(pl.multiple_of(8 + (me ^ apart) * depth, 8), depth)
+
+    def place_piece(piece, row):
+        place = pl.ds(row, depth)
         raw[1:steps + 1, place, :] = piece[0:steps]
         halo = piece[steps]
         low = pltpu.roll(piece[steps - 1], width, 1)
@@ -146,21 +146,47 @@
         raw[0, place, :] = jnp.where(lane == 0, halo, low)
         raw[steps + 1, place, :] = jnp.where(lane == groups - 1, halo, high)
 
+    zeros = jnp.zeros((steps + 2, depth, LANES), jnp.float32)
+    raw[:, 0:depth, :] = zeros
+    raw[:, depth + layers:2 * depth + layers, :] = zeros
+    for apart in range(len(pieces)):
+        block = (me ^ apart) % blocks
+        if far and apart < blocks:
+            @pl.when(block == jnp.where(lower, blocks - 1, 0))
+            def _():
+                row = jnp.where(lower, 0, depth + layers)
+                place_piece(pieces[apart], pl.multiple_of(row, 8))
+        else:
+            place_piece(pieces[apart], pl.multiple_of(depth + block * depth, 8))
+    slot = lax.broadcasted_iota(jnp.int32, (layers + depth, LANES), 0)
+    if far:
+        empty = slot > layers
+        if slots > layers + depth:
+            s_ref[:, layers + depth:slots, :] = jnp.full(
+                (steps, slots - layers - depth, LANES), -1.0, jnp.float32)
+    else:
+        empty = (slot == jnp.where(lower, layers - 1, 0))[:layers]
+
     def smooth(step, carry):
         v = raw[step] + 2.0 * raw[step + 1] + raw[step + 2]
         size = v.shape[0]
         before = pltpu.roll(v, 1, 0)
         after = pltpu.roll(v, size - 1, 0)
-        total = before + 2.0 * v + after
-        s_ref[step] = total[8:8 + layers] * (scale / 64.0)
+        total = (before + 2.0 * v + after) * (scale / 64.0)
+        if far:
+            shifted = pltpu.roll(total, size - (depth - 1), 0)[:layers + depth]
+            value = jnp.where(lower, shifted, total[depth:2 * depth + layers])
+            s_ref[step, 0:layers + depth] = jnp.where(empty, -1.0, value)
+        else:
+            s_ref[step] = jnp.where(empty, -1.0, total[depth:depth + layers])
         return carry
 
     lax.fori_loop(0, steps, smooth, 0, unroll=2)
     edge = lax.broadcasted_iota(jnp.int32, (bins, LANES), 0).astype(jnp.float32) - 1.0
-    rows = steps // 2
+    rows = steps // halves_count
 
     def count_layer(z, carry):
-        for half in range(2):
+        for half in range(halves_count):
             acc = jnp.zeros((bins, LANES), jnp.float32)
             for step in range(rows):
                 row = jnp.broadcast_to(s_ref[half * rows + step, pl.ds(z, 1), :], (bins, LANES))
@@ -169,27 +195,36 @@
         return carry
 
     lax.fori_loop(0, layers, count_layer, 0, unroll=2)
+    for z in range(layers, slots):
+        if z < used:
+            count_layer(z, 0)
+        else:
+            for half in range(halves_count):
+                sums[half, z] = jnp.zeros((bins, LANES), jnp.float32)
     table = table_ref[...]
     at_once = 8
 
     def products(chunk, carry):
-        wide = [sums[half, chunk * at_once + k] for half in range(2) for k in range(at_once)]
+        wide = [sums[half, chunk * at_once + k]
+                for half in range(halves_count) for k in range(at_once)]
         out = split_sum(table, jnp.concatenate(wide, axis=1))
-        for half in range(2):
+        for half in range(halves_count):
             for k in range(at_once):
                 place = (half * at_once + k) * LANES
-                halves[half, chunk * at_once + k] = out[:, place:place + LANES]
-        return carry
-
-    lax.fori_loop(0, layers // at_once, products, 0, unroll=2)
+                products_ref[half, chunk * at_once + k] = out[:, place:place + LANES]
+        return carry
+
+    lax.fori_loop(0, slots // at_once, products, 0, unroll=2)
     group = group_ids((colors, LANES), width)
 
     def scan_groups(chunk, carry):
         packed = jnp.zeros((colors, LANES), jnp.float32)
         for k in range(groups):
             z = chunk * groups + k
-            first = halves[0, z]
-            both = first + halves[1, z]
+            first = products_ref[0, z]
+            both = first
+            for half in range(1, halves_count):
+                both = both + products_ref[half, z]
             inclusive = both
             everything = both
             shift = 1
@@ -200,48 +235,55 @@
                 shift *= 2
             begin = inclusive - both
             start_ref[0, z] = begin
-            start_ref[1, z] = begin + first
+            if halves_count > 1:
+                start_ref[1, z] = begin + first
             packed = jnp.where(group == k, everything, packed)
         total_ref[chunk] = packed
         return carry
 
-    lax.fori_loop(0, layers // groups, scan_groups, 0, unroll=4)
-
-
-def depths(pieces, table, groups, width, bins):
-    count = len(pieces)
+    lax.fori_loop(0, slots // groups, scan_groups, 0, unroll=4)
+
+
+def depths(pieces, table, groups, width, bins, far, count):
     steps, depth = pieces[0].shape[0] - 1, pieces[0].shape[1]
-    layers = count * depth
+    layers = depth * (count // 2)
+    slots = layers + max(groups, depth) if far else layers
+    halves = 2 if far else 1
     colors = table.shape[0]
+    limit = 8 * MIB + slots * (LANES * 4 * halves) * (bins + 2 * colors)
+    work = steps * slots * LANES * bins
     return pl.pallas_call(
-        functools.partial(depth_kernel, groups, width, bins, float(bins - 1)),
+        functools.partial(depth_kernel, groups, width, bins, float(bins - 1), far, halves, count),
         out_shape=(
-            jax.ShapeDtypeStruct((steps, layers, LANES), jnp.float32),
-            jax.ShapeDtypeStruct((2, layers, colors, LANES), jnp.float32),
-            jax.ShapeDtypeStruct((layers // groups, colors, LANES), jnp.float32),
+            jax.ShapeDtypeStruct((steps, slots, LANES), jnp.float32),
+            jax.ShapeDtypeStruct((halves, slots, colors, LANES), jnp.float32),
+            jax.ShapeDtypeStruct((slots // groups, colors, LANES), jnp.float32),
         ),
-        in_specs=[pl.BlockSpec(memory_space=pltpu.VMEM)] * (count + 1),
+        in_specs=[pl.BlockSpec(memory_space=pltpu.VMEM)] * (len(pieces) + 1),
         out_specs=[pl.BlockSpec(memory_space=pltpu.VMEM)] * 3,
         scratch_shapes=[
-            pltpu.VMEM((steps + 2, layers + 16, LANES), jnp.float32),
-            pltpu.VMEM((2, layers, bins, LANES), jnp.float32),
-            pltpu.VMEM((2, layers, colors, LANES), jnp.float32),
+            pltpu.VMEM((steps + 2, layers + 2 * depth, LANES), jnp.float32),
+            pltpu.VMEM((halves, slots, bins, LANES), jnp.float32),
+            pltpu.VMEM((halves, slots, colors, LANES), jnp.float32),
         ],
-        compiler_params=pltpu.CompilerParams(
-            vmem_limit_bytes=8 * MIB + layers * (LANES * 4 * 2) * (bins + 2 * colors)),
-        name="depths",
+        compiler_params=pltpu.CompilerParams(vmem_limit_bytes=limit),
+        cost_estimate=pl.CostEstimate(
+            flops=4 * work, bytes_accessed=8 * steps * slots * LANES, transcendentals=0),
+        name="depths_far" if far else "depths_near",
     )(*pieces, table)
 
 
-def render_kernel(groups, width, bins, ratio, turn, sums_count, s_ref, start_ref, table_ref,
-                  columns_ref, *refs):
+def render_kernel(groups, width, bins, ratio, turn, near, blocks, sums_count, s_ref, start_ref,
+                  table_ref, columns_ref, *refs):
     before_refs = refs[:sums_count]
-    out_refs, image, depth = refs[sums_count:-2], refs[-2], refs[-1]
-    steps, layers, _ = s_ref.shape
-    rows = steps // 2
+    near_refs, refs = refs[sums_count:sums_count + near], refs[sums_count + near:]
+    out_refs, image, depth = refs[:-2], refs[-2], refs[-1]
+    rows, slots = image.shape[0], s_ref.shape[1]
     colors = columns_ref.shape[1]
+    block = 8
     me = lax.axis_index("gz")
-    half = (me + turn) % 2
+    lower = me < blocks
+    half = 0 if turn is None else (me + turn) % 2
     group = group_ids((colors, LANES), width)
 
     def begin(chunk, carry):
@@ -258,24 +300,23 @@
             depth[z] = start_ref[half, z] + value
         return carry
 
-    lax.fori_loop(0, layers // groups, begin, 0, unroll=4)
+    lax.fori_loop(0, slots // groups, begin, 0, unroll=4)
     ambient = columns_ref[1]
     table = table_ref[...]
     edge = (lax.broadcasted_iota(jnp.int32, (bins, LANES), 0).astype(jnp.float32) - 1.0).astype(
         jnp.bfloat16)
     zero = jnp.zeros((bins, LANES), jnp.bfloat16)
     one = jnp.ones((bins, LANES), jnp.bfloat16)
-    block = 8
+    layers = blocks * block
 
     def advance(step, carry):
         row = half * rows + step
 
-        def layer_block(chunk, state):
+        def layer_block(place, size, state):
             through, partial = state
-            place = pl.multiple_of(chunk * block, block)
             s = s_ref[row, pl.ds(place, block), :]
-            lower = jnp.floor(s)
-            frac = s - lower
+            lower_bin = jnp.floor(s)
+            frac = s - lower_bin
             coarse = frac.astype(jnp.bfloat16).astype(jnp.float32)
             fine = frac - coarse
 
@@ -283,14 +324,14 @@
                 return jnp.broadcast_to(value[r:r + 1], (bins, LANES)).astype(jnp.bfloat16)
 
             columns = []
-            for r in range(block):
-                away = wide(lower, r) - edge
+            for r in range(size):
+                away = wide(lower_bin, r) - edge
                 main = jnp.minimum(jnp.maximum(away + wide(coarse, r), zero), one)
                 rest = jnp.where(away == zero, wide(fine, r), zero)
                 columns.append(jnp.concatenate([main, main, rest], axis=0))
             weights = jnp.concatenate(columns, axis=1)
             props = jnp.dot(table, weights, preferred_element_type=jnp.float32)
-            for r in range(block):
+            for r in range(size):
                 part = props[:, r * LANES:(r + 1) * LANES]
                 sigma, color = part[:colors], part[colors:]
                 later = through * jnp.exp2(sigma)
@@ -303,16 +344,26 @@
             return through, partial
 
         state = (jnp.ones((colors, LANES), jnp.float32), jnp.zeros((colors, LANES), jnp.float32))
-        through, partial = lax.fori_loop(0, layers // block, layer_block, state, unroll=True)
-        image[step] = partial + through * columns_ref[2]
+        for chunk in range(blocks):
+            state = layer_block(chunk * block, block, state)
+        if turn is None:
+            out_refs[0][step], out_refs[1][step] = state[1], state[0]
+            return carry
+        through, partial = layer_block(layers, 1, state)
+        near_partial, near_through = near_refs[0][row], near_refs[1][row]
+        front = jnp.where(lower, near_partial, partial)
+        back = jnp.where(lower, partial, near_partial)
+        passed = jnp.where(lower, near_through, through)
+        image[step] = front + passed * back + through * near_through * columns_ref[2]
         return carry
 
     lax.fori_loop(0, rows, advance, 0)
+    if turn is None:
+        return
     if len(out_refs) == 1:
         out_refs[0][...] = image[...]
         return
     for chunk in range(rows // groups):
-        place = pl.ds(chunk * groups, groups)
         tiles = swap_groups([image[chunk * groups + k] for k in range(groups)], groups, width)
         for part in range(groups):
             image[chunk * groups + part] = tiles[part]
@@ -322,26 +373,34 @@
             out_refs[slot][chunk] = image[chunk * groups + part]
 
 
-def render(s, start, table, columns, before, groups, width, bins, ratio, turn):
-    steps, layers, _ = s.shape
+def render(s, start, table, columns, before, near, groups, width, bins, ratio, turn, blocks):
+    steps, slots, _ = s.shape
     colors = columns.shape[1]
     share = steps // 2
-    if share % groups == 0:
+    if turn is None:
+        share = steps
+        shapes = [jax.ShapeDtypeStruct((steps, colors, LANES), jnp.float32)] * 2
+    elif share % groups == 0:
         shapes = [jax.ShapeDtypeStruct((share // groups, colors, LANES), jnp.float32)] * groups
     else:
         shapes = [jax.ShapeDtypeStruct((share, colors, LANES), jnp.float32)]
+    work = share * slots * LANES
     return pl.pallas_call(
-        functools.partial(render_kernel, groups, width, bins, ratio, turn, len(before)),
+        functools.partial(render_kernel, groups, width, bins, ratio, turn, len(near), blocks,
+                          len(before)),
         out_shape=shapes,
-        in_specs=[pl.BlockSpec(memory_space=pltpu.VMEM)] * (4 + len(before)),
+        in_specs=[pl.BlockSpec(memory_space=pltpu.VMEM)] * (4 + len(before) + len(near)),
         out_specs=[pl.BlockSpec(memory_space=pltpu.VMEM)] * len(shapes),
         scratch_shapes=[
             pltpu.VMEM((share, colors, LANES), jnp.float32),
-            pltpu.VMEM((layers, colors, LANES), jnp.float32),
+            pltpu.VMEM((slots, colors, LANES), jnp.float32),
         ],
-        compiler_params=pltpu.CompilerParams(vmem_limit_bytes=8 * MIB + layers * colors * 512 * 4),
-        name="render",
-    )(s, start, table, columns, *before)
+        compiler_params=pltpu.CompilerParams(vmem_limit_bytes=8 * MIB + slots * colors * 512 * 4),
+        cost_estimate=pl.CostEstimate(
+            flops=work * bins * colors * 12, bytes_accessed=4 * work,
+            transcendentals=2 * work * colors),
+        name="render_near" if turn is None else "render_far",
+    )(s, start, table, columns, *before, *near)
 
 
 def unpack_kernel(groups, width, *refs):
@@ -441,19 +500,25 @@
 
     packed = pack(density, groups, width)
     pieces = list(address(packed, before, after, groups, width))
-    for apart in range(count - 1, 0, -1):
+    for apart in range(1, count):
         pieces[apart] = exchange(pieces[apart], "gz", apart)
     columns = jnp.broadcast_to(
         jnp.stack([extinction_scale, ambient, backdrop])[:, :, None], (3, colors, LANES))
     sum_table, table = tables(bin_rows, tf_extinction, tf_color, columns, step_x, step_z)
 
-    s, start, total = depths(pieces, sum_table, groups, width, bins)
-    sums = []
-    for hop in range(1, size_x):
-        sums.append(lax.ppermute(total, "gx", [(i, i + hop) for i in range(size_x - hop)]))
-
+    def prefixes(total):
+        return [lax.ppermute(total, "gx", [(i, i + hop) for i in range(size_x - hop)])
+                for hop in range(1, size_x)]
+
+    blocks = count // 2
+    ratio = step_x / step_z
+    s, start, total = depths(pieces[:blocks], sum_table, groups, width, bins, False, count)
+    near = render(s, start, table, columns, prefixes(total), [], groups, width, bins, ratio,
+                  None, blocks)
+    s, start, total = depths(pieces, sum_table, groups, width, bins, True, count)
+    sums = prefixes(total)
     halves = [
-        render(s, start, table, columns, sums, groups, width, bins, step_x / step_z, turn)
+        render(s, start, table, columns, sums, near, groups, width, bins, ratio, turn, blocks)
         for turn in range(2)
     ]
     share = steps // 2

time: 86.4 us -> 87.8 us (1.016)
  waiting for transfers between devices: 21.1 us -> 6.78 us
  starting transfers between devices: 36.1 us -> 43.7 us
  Pallas kernels: 24 us -> 31.2 us
    ppermute x14, waiting for transfers between devices: 17.2 us -> 6.17 us  [exchange(): return lax.ppermute(value, axis, pairs)]
    ppermute x3 -> x6, starting transfers between devices: 6.59 us -> 16.8 us  [prefixes(): lax.ppermute(total, 'gx', [(i, i + hop) for i in range(size_x - hop)])]
    pallas_call x2 -> x3, Pallas kernels: 13.9 us -> 19.7 us  [render(): pl.pallas_call(functools.partial(render_kernel, groups, width, bins, rati...]
    ppermute x3 -> x6, waiting for transfers between devices: 3.83 us -> 0.02 us  [prefixes(): lax.ppermute(total, 'gx', [(i, i + hop) for i in range(size_x - hop)])]
    ppermute x14, starting transfers between devices: 22.7 us -> 20.9 us  [exchange(): return lax.ppermute(value, axis, pairs)]
    pallas_call x1 -> x2, Pallas kernels: 5.98 us -> 7.43 us  [depths(): pl.pallas_call(functools.partial(depth_kernel, groups, width, bins, float...]
  transfers between devices with their start and end apart: 19 -> 22, of which waited for: 5 -> 5; matrix products, arithmetic and copies ran while one was open for 2% -> 2% of each run, Pallas kernels for 11% -> 28%
where the time goes in v3:
time: 87.8 us; the launch traced here: 87.2 us
  starting transfers between devices  43.7 us (50%)
  Pallas kernels  31.2 us (36%)
  waiting for transfers between devices  6.78 us (8%)
  local copies, waits for them, and re-layouts  4.57 us (5%)
    ppermute x14, starting transfers between devices, exchange(): return lax.ppermute(value, axis, pairs)  20.9 us
    pallas_call x3, Pallas kernels, render(): pl.pallas_call(functools.partial(render_kernel, groups, width, bins, rati...  19.7 us
    ppermute x6, starting transfers between devices, prefixes(): lax.ppermute(total, 'gx', [(i, i + hop) for i in range(size_x - hop)])  16.8 us
    pallas_call x2, Pallas kernels, depths(): pl.pallas_call(functools.partial(depth_kernel, groups, width, bins, float...  7.43 us
    ppermute x14, waiting for transfers between devices, exchange(): return lax.ppermute(value, axis, pairs)  6.17 us
    ppermute x1, starting transfers between devices, local(): before = lax.ppermute(density[rows_x - 1:], 'gx', up)  4.83 us
    unnamed x14, local copies, waits for them, and re-layouts  3.2 us
    pallas_call x1, Pallas kernels, pack(): pl.pallas_call(functools.partial(pack_kernel, groups, width), out_shape=j...  2.41 us
  transfers between devices with their start and end apart: 22, of which 5 were waited for; matrix products, arithmetic and copies ran while one was open for 2% of the time, Pallas kernels for 28%

profile of v3, /device:TPU:0, one launch (start us, length us, event | category | flops | bytes accessed | tf_op | source)
XLA Modules:
  0.0 87.2 jit_solution(9444357982536816298)
XLA Ops:
  0.0 0.7 fusion
  0.7 4.8 %collective-permute-start = (f32[1,8,256]{2,1,0:T(8,128)S(1)}, f32[1,8,256]{2,1,0:T(8,128)S(1)}, u32[]{:S(2)}, u32[]{:S(2)}) collective-permute-start(f32[1,8,256]{2,1,0:T(8,128)S(1)} %get-tuple-element.58), channel_id=1, source_target_pairs={{0,8},{8,16},{16,24},{1,9},{9,17},{17,25},{2,10},{10,18},{18,26},{... | collective-permute-start | bytes 24584 | tf_op jit(solution)/shard_map/ppermute | solution.py:498
  5.6 1.3 %collective-permute-start.1 = (f32[1,8,256]{2,1,0:T(8,128)S(1)}, f32[1,8,256]{2,1,0:T(8,128)S(1)}, u32[]{:S(2)}, u32[]{:S(2)}) collective-permute-start(f32[1,8,256]{2,1,0:T(8,128)S(1)} %get-tuple-element.57), channel_id=1, source_target_pairs={{8,0},{16,8},{24,16},{9,1},{17,9},{25,17},{10,2},{18,10},{26,18},{... | collective-permute-start | bytes 24584 | tf_op jit(solution)/shard_map/ppermute | solution.py:499
  6.9 1.2 %copy-done = f32[128,8,256]{2,1,0:T(8,128)S(1)} copy-done((f32[128,8,256]{2,1,0:T(8,128)S(1)}, f32[128,8,256]{2,1,0:T(8,128)}, u32[]{:S(2)}) %copy-start) | copy-done | bytes 1048600
  8.1 2.4 %pack.1.packed_ref = f32[8,32,8,128]{3,2,1,0:T(8,128)S(1)} custom-call(f32[4,32,8,256]{3,2,1,0:T(8,128)S(1)} %bitcast.10), custom_call_target="tpu_custom_call" | custom-call | tf_op jit(solution)/shard_map/pack/pallas_call | solution.py:77
  11.4 1.6 %collective-permute-start.3 = (f32[33,8,128]{2,1,0:T(8,128)S(1)}, f32[33,8,128]{2,1,0:T(8,128)S(1)}, u32[]{:S(2)}, u32[]{:S(2)}) collective-permute-start(f32[33,8,128]{2,1,0:T(8,128)S(1)} %get-tuple-element.33), channel_id=1, source_target_pairs={{0,2},{1,3},{2,0},{3,1},{4,6},{5,7},{6,4},{7,5},{8,10},{9,11},{10,... | collective-permute-start | bytes 405512 | tf_op jit(solution)/shard_map/ppermute | solution.py:480
  13.1 0.6 copy-done.3
  15.2 2.6 %collective-permute-start.5 = (f32[33,8,128]{2,1,0:T(8,128)S(1)}, f32[33,8,128]{2,1,0:T(8,128)S(1)}, u32[]{:S(2)}, u32[]{:S(2)}) collective-permute-start(f32[33,8,128]{2,1,0:T(8,128)S(1)} %get-tuple-element.35), channel_id=1, source_target_pairs={{0,4},{1,5},{2,6},{3,7},{4,0},{5,1},{6,2},{7,3},{8,12},{9,13},{10,... | collective-permute-start | bytes 405512 | tf_op jit(solution)/shard_map/ppermute | solution.py:480
  17.8 0.7 add_bitcast_fusion
  18.5 3.6 %collective-permute-start.7 = (f32[33,8,128]{2,1,0:T(8,128)S(1)}, f32[33,8,128]{2,1,0:T(8,128)S(1)}, u32[]{:S(2)}, u32[]{:S(2)}) collective-permute-start(f32[33,8,128]{2,1,0:T(8,128)S(1)} %get-tuple-element.37), channel_id=1, source_target_pairs={{0,6},{1,7},{2,4},{3,5},{4,2},{5,3},{6,0},{7,1},{8,14},{9,15},{10,... | collective-permute-start | bytes 405512 | tf_op jit(solution)/shard_map/ppermute | solution.py:480
  23.4 1.0 %collective-permute-done.4.refs_3_ = f32[33,8,128]{2,1,0:T(8,128)S(1)} collective-permute-done((f32[33,8,128]{2,1,0:T(8,128)S(1)}, f32[33,8,128]{2,1,0:T(8,128)S(1)}, u32[]{:S(2)}, u32[]{:S(2)}) %collective-permute-start.4) | collective-permute-done | bytes 135200 | tf_op jit(solution)/shard_map/ppermute | solution.py:480
  24.4 3.5 %depths_near.1 = (f32[32,32,128]{2,1,0:T(8,128)S(1)}, f32[1,32,16,128]{3,2,1,0:T(8,128)S(1)}, f32[8,16,128]{2,1,0:T(8,128)S(1)}) custom-call(f32[33,8,128]{2,1,0:T(8,128)S(1)} %get-tuple-element.31.refs_0_, f32[33,8,128]{2,1,0:T(8,128)S(1)} %collective-permute-done.2.refs_1_, f32[33,8,128]{2,1,0:T(8,128)S(1)} %collective-permute-done.3.refs_2_, ...), custom_call_target="tpu_custom_call" | custom-call | flops 16777216 | bytes 1048576 | tf_op jit(solution)/shard_map/depths_near/pallas_call | solution.py:255
  27.9 4.3 %collective-permute-start.12 = (f32[8,16,128]{2,1,0:T(8,128)S(1)}, f32[8,16,128]{2,1,0:T(8,128)S(1)}, u32[]{:S(2)}, u32[]{:S(2)}) collective-permute-start(f32[8,16,128]{2,1,0:T(8,128)S(1)} %get-tuple-element.46), channel_id=1, source_target_pairs={{0,8},{8,16},{16,24},{1,9},{9,17},{17,25},{2,10},{10,18},{18,26},{... | collective-permute-start | bytes 196616 | tf_op jit(solution)/shard_map/ppermute | solution.py:510
  32.3 3.1 %collective-permute-start.13 = (f32[8,16,128]{2,1,0:T(8,128)S(1)}, f32[8,16,128]{2,1,0:T(8,128)S(1)}, u32[]{:S(2)}, u32[]{:S(2)}) collective-permute-start(f32[8,16,128]{2,1,0:T(8,128)S(1)} %get-tuple-element.46), channel_id=1, source_target_pairs={{0,16},{8,24},{1,17},{9,25},{2,18},{10,26},{3,19},{11,27},{4,20},{... | collective-permute-start | bytes 196616 | tf_op jit(solution)/shard_map/ppermute | solution.py:510
  35.4 0.8 collective-permute-done.6.refs_5_
  36.2 4.9 %collective-permute-start.14 = (f32[8,16,128]{2,1,0:T(8,128)S(1)}, f32[8,16,128]{2,1,0:T(8,128)S(1)}, u32[]{:S(2)}, u32[]{:S(2)}) collective-permute-start(f32[8,16,128]{2,1,0:T(8,128)S(1)} %get-tuple-element.46), channel_id=1, source_target_pairs={{0,24},{1,25},{2,26},{3,27},{4,28},{5,29},{6,30},{7,31}} | collective-permute-start | bytes 196616 | tf_op jit(solution)/shard_map/ppermute | solution.py:510
  41.2 3.9 %depths_far.1 = (f32[32,40,128]{2,1,0:T(8,128)S(1)}, f32[2,40,16,128]{3,2,1,0:T(8,128)S(1)}, f32[10,16,128]{2,1,0:T(8,128)S(1)}) custom-call(f32[33,8,128]{2,1,0:T(8,128)S(1)} %get-tuple-element.31.refs_0_, f32[33,8,128]{2,1,0:T(8,128)S(1)} %collective-permute-done.2.refs_1_, f32[33,8,128]{2,1,0:T(8,128)S(1)} %collective-permute-done.3.refs_2_, ...), custom_call_target="tpu_custom_call" | custom-call | flops 20971520 | bytes 1310720 | tf_op jit(solution)/shard_map/depths_far/pallas_call | solution.py:255
  45.1 1.3 %collective-permute-start.10 = (f32[10,16,128]{2,1,0:T(8,128)S(1)}, f32[10,16,128]{2,1,0:T(8,128)S(1)}, u32[]{:S(2)}, u32[]{:S(2)}) collective-permute-start(f32[10,16,128]{2,1,0:T(8,128)S(1)} %get-tuple-element.43), channel_id=1, source_target_pairs={{0,16},{8,24},{1,17},{9,25},{2,18},{10,26},{3,19},{11,27},{4,20},{... | collective-permute-start | bytes 245768 | tf_op jit(solution)/shard_map/ppermute | solution.py:510
  46.4 1.3 %collective-permute-start.11 = (f32[10,16,128]{2,1,0:T(8,128)S(1)}, f32[10,16,128]{2,1,0:T(8,128)S(1)}, u32[]{:S(2)}, u32[]{:S(2)}) collective-permute-start(f32[10,16,128]{2,1,0:T(8,128)S(1)} %get-tuple-element.43), channel_id=1, source_target_pairs={{0,24},{1,25},{2,26},{3,27},{4,28},{5,29},{6,30},{7,31}} | collective-permute-start | bytes 245768 | tf_op jit(solution)/shard_map/ppermute | solution.py:510
  47.7 1.8 %collective-permute-start.9 = (f32[10,16,128]{2,1,0:T(8,128)S(1)}, f32[10,16,128]{2,1,0:T(8,128)S(1)}, u32[]{:S(2)}, u32[]{:S(2)}) collective-permute-start(f32[10,16,128]{2,1,0:T(8,128)S(1)} %get-tuple-element.43), channel_id=1, source_target_pairs={{0,8},{8,16},{16,24},{1,9},{9,17},{17,25},{2,10},{10,18},{18,26},{... | collective-permute-start | bytes 245768 | tf_op jit(solution)/shard_map/ppermute | solution.py:510
  49.6 9.0 %render_near.1 = (f32[32,16,128]{2,1,0:T(8,128)S(1)}, f32[32,16,128]{2,1,0:T(8,128)S(1)}) custom-call(f32[32,32,128]{2,1,0:T(8,128)S(1)} %get-tuple-element.44.s_ref, f32[1,32,16,128]{3,2,1,0:T(8,128)S(1)} %get-tuple-element.45.start_ref, bf16[32,96]{1,0:T(8,128)(2,1)S(1)} %get-tuple-element.42.table_ref, f32[3,16,128]{2,1,0:T(8,128)S(1)} %broadcast_in_dim.2.columns_ref, ...), custom_call_target="tpu_custom_call" | custom-call | flops 805306368 | bytes 524288 | tf_op jit(solution)/shard_map/render_near/pallas_call | solution.py:388
  58.6 5.4 %render_far.3 = (f32[4,16,128]{2,1,0:T(8,128)S(1)}, f32[4,16,128]{2,1,0:T(8,128)S(1)}, f32[4,16,128]{2,1,0:T(8,128)S(1)}, f32[4,16,128]{2,1,0:T(8,128)S(1)}) custom-call(f32[32,40,128]{2,1,0:T(8,128)S(1)} %get-tuple-element.40.s_ref, f32[2,40,16,128]{3,2,1,0:T(8,128)S(1)} %get-tuple-element.41.start_ref, bf16[32,96]{1,0:T(8,128)(2,1)S(1)} %get-tuple-element.42.table_ref, ...), custom_call_target="tpu_custom_call" | custom-call | flops 503316480 | bytes 327680 | tf_op jit(solution)/shard_map/render_far/pallas_call | solution.py:388
  64.1 5.5 %collective-permute-start.17 = (f32[4,16,128]{2,1,0:T(8,128)S(1)}, f32[4,16,128]{2,1,0:T(8,128)S(1)}, u32[]{:S(2)}, u32[]{:S(2)}) collective-permute-start(f32[4,16,128]{2,1,0:T(8,128)S(1)} %get-tuple-element.52), channel_id=1, source_target_pairs={{0,3},{1,2},{2,1},{3,0},{4,7},{5,6},{6,5},{7,4},{8,11},{9,10},{10,... | collective-permute-start | bytes 98312 | tf_op jit(solution)/shard_map/ppermute | solution.py:480
  69.6 1.4 %collective-permute-start.19 = (f32[4,16,128]{2,1,0:T(8,128)S(1)}, f32[4,16,128]{2,1,0:T(8,128)S(1)}, u32[]{:S(2)}, u32[]{:S(2)}) collective-permute-start(f32[4,16,128]{2,1,0:T(8,128)S(1)} %get-tuple-element.54), channel_id=1, source_target_pairs={{0,5},{1,4},{2,7},{3,6},{4,1},{5,0},{6,3},{7,2},{8,13},{9,12},{10,... | collective-permute-start | bytes 98312 | tf_op jit(solution)/shard_map/ppermute | solution.py:480
  71.0 1.1 %collective-permute-start.21 = (f32[4,16,128]{2,1,0:T(8,128)S(1)}, f32[4,16,128]{2,1,0:T(8,128)S(1)}, u32[]{:S(2)}, u32[]{:S(2)}) collective-permute-start(f32[4,16,128]{2,1,0:T(8,128)S(1)} %get-tuple-element.56), channel_id=1, source_target_pairs={{0,7},{1,6},{2,5},{3,4},{4,3},{5,2},{6,1},{7,0},{8,15},{9,14},{10,... | collective-permute-start | bytes 98312 | tf_op jit(solution)/shard_map/ppermute | solution.py:480
  72.1 5.4 %render_far.2 = (f32[4,16,128]{2,1,0:T(8,128)S(1)}, f32[4,16,128]{2,1,0:T(8,128)S(1)}, f32[4,16,128]{2,1,0:T(8,128)S(1)}, f32[4,16,128]{2,1,0:T(8,128)S(1)}) custom-call(f32[32,40,128]{2,1,0:T(8,128)S(1)} %get-tuple-element.40.s_ref, f32[2,40,16,128]{3,2,1,0:T(8,128)S(1)} %get-tuple-element.41.start_ref, bf16[32,96]{1,0:T(8,128)(2,1)S(1)} %get-tuple-element.42.table_ref, ...), custom_call_target="tpu_custom_call" | custom-call | flops 503316480 | bytes 327680 | tf_op jit(solution)/shard_map/render_far/pallas_call | solution.py:388
  77.5 0.8 collective-permute-start.16
  78.2 2.3 %collective-permute-start.18 = (f32[4,16,128]{2,1,0:T(8,128)S(1)}, f32[4,16,128]{2,1,0:T(8,128)S(1)}, u32[]{:S(2)}, u32[]{:S(2)}) collective-permute-start(f32[4,16,128]{2,1,0:T(8,128)S(1)} %get-tuple-element.53), channel_id=1, source_target_pairs={{0,4},{1,5},{2,6},{3,7},{4,0},{5,1},{6,2},{7,3},{8,12},{9,13},{10,... | collective-permute-start | bytes 98312 | tf_op jit(solution)/shard_map/ppermute | solution.py:480
  80.5 1.4 %collective-permute-start.20 = (f32[4,16,128]{2,1,0:T(8,128)S(1)}, f32[4,16,128]{2,1,0:T(8,128)S(1)}, u32[]{:S(2)}, u32[]{:S(2)}) collective-permute-start(f32[4,16,128]{2,1,0:T(8,128)S(1)} %get-tuple-element.55), channel_id=1, source_target_pairs={{0,6},{1,7},{2,4},{3,5},{4,2},{5,3},{6,0},{7,1},{8,14},{9,15},{10,... | collective-permute-start | bytes 98312 | tf_op jit(solution)/shard_map/ppermute | solution.py:480
  81.9 1.9 %collective-permute-done.18.refs_4_ = f32[4,16,128]{2,1,0:T(8,128)S(1)} collective-permute-done((f32[4,16,128]{2,1,0:T(8,128)S(1)}, f32[4,16,128]{2,1,0:T(8,128)S(1)}, u32[]{:S(2)}, u32[]{:S(2)}) %collective-permute-start.18) | collective-permute-done | bytes 32800 | tf_op jit(solution)/shard_map/ppermute | solution.py:480
  83.8 2.4 %collective-permute-done.20.refs_6_ = f32[4,16,128]{2,1,0:T(8,128)S(1)} collective-permute-done((f32[4,16,128]{2,1,0:T(8,128)S(1)}, f32[4,16,128]{2,1,0:T(8,128)S(1)}, u32[]{:S(2)}, u32[]{:S(2)}) %collective-permute-start.20) | collective-permute-done | bytes 32800 | tf_op jit(solution)/shard_map/ppermute | solution.py:480
  86.3 1.0 %unpack.1 = f32[16,16,256]{2,1,0:T(8,128)} custom-call(f32[4,16,128]{2,1,0:T(8,128)S(1)} %get-tuple-element.49.refs_0_, f32[4,16,128]{2,1,0:T(8,128)S(1)} %collective-permute-done.15.refs_1_, f32[4,16,128]{2,1,0:T(8,128)S(1)} %collective-permute-done.16.refs_2_, f32[4,16,128]{2,1,0:T(8,128)S(1)} %collective-permute-done.17.refs_3_, ...), custom_call_target="tpu_custom_call" | custom-call | tf_op jit(solution)/shard_map/unpack/pallas_call | solution.py:423
  (41 shorter events, 3.8 us)
Async XLA Ops:
  0.7 9.8 %collective-permute-start = (f32[1,8,256]{2,1,0:T(8,128)S(1)}, f32[1,8,256]{2,1,0:T(8,128)S(1)}, u32[]{:S(2)}, u32[]{:S(2)}) collective-permute-start(f32[1,8,256]{2,1,0:T(8,128)S(1)} %get-tuple-element.58), channel_id=1, source_target_pairs={{0,8},{8,16},{16,24},{1,9},{9,17},{17,25},{2,10},{10,18},{18,26},{... | collective-permute-start | bytes 24584 | tf_op jit(solution)/shard_map/ppermute | solution.py:498
  5.6 5.5 %collective-permute-start.1 = (f32[1,8,256]{2,1,0:T(8,128)S(1)}, f32[1,8,256]{2,1,0:T(8,128)S(1)}, u32[]{:S(2)}, u32[]{:S(2)}) collective-permute-start(f32[1,8,256]{2,1,0:T(8,128)S(1)} %get-tuple-element.57), channel_id=1, source_target_pairs={{8,0},{16,8},{24,16},{9,1},{17,9},{25,17},{10,2},{18,10},{26,18},{... | collective-permute-start | bytes 24584 | tf_op jit(solution)/shard_map/ppermute | solution.py:499
  6.9 1.2 %copy-start = (f32[128,8,256]{2,1,0:T(8,128)S(1)}, f32[128,8,256]{2,1,0:T(8,128)}, u32[]{:S(2)}) copy-start(f32[128,8,256]{2,1,0:T(8,128)} %param.7) | copy-start | bytes 3145732
  11.3 7.2 %collective-permute-start.2 = (f32[33,8,128]{2,1,0:T(8,128)S(1)}, f32[33,8,128]{2,1,0:T(8,128)S(1)}, u32[]{:S(2)}, u32[]{:S(2)}) collective-permute-start(f32[33,8,128]{2,1,0:T(8,128)S(1)} %get-tuple-element.32), channel_id=1, source_target_pairs={{0,1},{1,0},{2,3},{3,2},{4,5},{5,4},{6,7},{7,6},{8,9},{9,8},{10,11... | collective-permute-start | bytes 405512 | tf_op jit(solution)/shard_map/ppermute | solution.py:480
  11.4 10.7 %collective-permute-start.3 = (f32[33,8,128]{2,1,0:T(8,128)S(1)}, f32[33,8,128]{2,1,0:T(8,128)S(1)}, u32[]{:S(2)}, u32[]{:S(2)}) collective-permute-start(f32[33,8,128]{2,1,0:T(8,128)S(1)} %get-tuple-element.33), channel_id=1, source_target_pairs={{0,2},{1,3},{2,0},{3,1},{4,6},{5,7},{6,4},{7,5},{8,10},{9,11},{10,... | collective-permute-start | bytes 405512 | tf_op jit(solution)/shard_map/ppermute | solution.py:480
  13.0 0.7 copy-start.3
  13.1 0.7 copy-start.4
  13.1 0.7 copy-start.5
  13.7 0.7 copy-start.6
  15.0 9.5 %collective-permute-start.4 = (f32[33,8,128]{2,1,0:T(8,128)S(1)}, f32[33,8,128]{2,1,0:T(8,128)S(1)}, u32[]{:S(2)}, u32[]{:S(2)}) collective-permute-start(f32[33,8,128]{2,1,0:T(8,128)S(1)} %get-tuple-element.34), channel_id=1, source_target_pairs={{0,3},{1,2},{2,1},{3,0},{4,7},{5,6},{6,5},{7,4},{8,11},{9,10},{10,... | collective-permute-start | bytes 405512 | tf_op jit(solution)/shard_map/ppermute | solution.py:480
  15.2 17.1 %collective-permute-start.5 = (f32[33,8,128]{2,1,0:T(8,128)S(1)}, f32[33,8,128]{2,1,0:T(8,128)S(1)}, u32[]{:S(2)}, u32[]{:S(2)}) collective-permute-start(f32[33,8,128]{2,1,0:T(8,128)S(1)} %get-tuple-element.35), channel_id=1, source_target_pairs={{0,4},{1,5},{2,6},{3,7},{4,0},{5,1},{6,2},{7,3},{8,12},{9,13},{10,... | collective-permute-start | bytes 405512 | tf_op jit(solution)/shard_map/ppermute | solution.py:480
  17.8 18.4 %collective-permute-start.6 = (f32[33,8,128]{2,1,0:T(8,128)S(1)}, f32[33,8,128]{2,1,0:T(8,128)S(1)}, u32[]{:S(2)}, u32[]{:S(2)}) collective-permute-start(f32[33,8,128]{2,1,0:T(8,128)S(1)} %get-tuple-element.36), channel_id=1, source_target_pairs={{0,5},{1,4},{2,7},{3,6},{4,1},{5,0},{6,3},{7,2},{8,13},{9,12},{10,... | collective-permute-start | bytes 405512 | tf_op jit(solution)/shard_map/ppermute | solution.py:480
  18.5 22.6 %collective-permute-start.7 = (f32[33,8,128]{2,1,0:T(8,128)S(1)}, f32[33,8,128]{2,1,0:T(8,128)S(1)}, u32[]{:S(2)}, u32[]{:S(2)}) collective-permute-start(f32[33,8,128]{2,1,0:T(8,128)S(1)} %get-tuple-element.37), channel_id=1, source_target_pairs={{0,6},{1,7},{2,4},{3,5},{4,2},{5,3},{6,0},{7,1},{8,14},{9,15},{10,... | collective-permute-start | bytes 405512 | tf_op jit(solution)/shard_map/ppermute | solution.py:480
  22.1 19.0 %collective-permute-start.8 = (f32[33,8,128]{2,1,0:T(8,128)S(1)}, f32[33,8,128]{2,1,0:T(8,128)S(1)}, u32[]{:S(2)}, u32[]{:S(2)}) collective-permute-start(f32[33,8,128]{2,1,0:T(8,128)S(1)} %get-tuple-element.38), channel_id=1, source_target_pairs={{0,7},{1,6},{2,5},{3,4},{4,3},{5,2},{6,1},{7,0},{8,15},{9,14},{10,... | collective-permute-start | bytes 405512 | tf_op jit(solution)/shard_map/ppermute | solution.py:480
  22.3 0.7 copy-start.2
  22.3 0.7 copy-start.1
  27.9 19.8 %collective-permute-start.12 = (f32[8,16,128]{2,1,0:T(8,128)S(1)}, f32[8,16,128]{2,1,0:T(8,128)S(1)}, u32[]{:S(2)}, u32[]{:S(2)}) collective-permute-start(f32[8,16,128]{2,1,0:T(8,128)S(1)} %get-tuple-element.46), channel_id=1, source_target_pairs={{0,8},{8,16},{16,24},{1,9},{9,17},{17,25},{2,10},{10,18},{18,26},{... | collective-permute-start | bytes 196616 | tf_op jit(solution)/shard_map/ppermute | solution.py:510
  32.3 17.3 %collective-permute-start.13 = (f32[8,16,128]{2,1,0:T(8,128)S(1)}, f32[8,16,128]{2,1,0:T(8,128)S(1)}, u32[]{:S(2)}, u32[]{:S(2)}) collective-permute-start(f32[8,16,128]{2,1,0:T(8,128)S(1)} %get-tuple-element.46), channel_id=1, source_target_pairs={{0,16},{8,24},{1,17},{9,25},{2,18},{10,26},{3,19},{11,27},{4,20},{... | collective-permute-start | bytes 196616 | tf_op jit(solution)/shard_map/ppermute | solution.py:510
  36.2 13.4 %collective-permute-start.14 = (f32[8,16,128]{2,1,0:T(8,128)S(1)}, f32[8,16,128]{2,1,0:T(8,128)S(1)}, u32[]{:S(2)}, u32[]{:S(2)}) collective-permute-start(f32[8,16,128]{2,1,0:T(8,128)S(1)} %get-tuple-element.46), channel_id=1, source_target_pairs={{0,24},{1,25},{2,26},{3,27},{4,28},{5,29},{6,30},{7,31}} | collective-permute-start | bytes 196616 | tf_op jit(solution)/shard_map/ppermute | solution.py:510
  45.1 13.5 %collective-permute-start.10 = (f32[10,16,128]{2,1,0:T(8,128)S(1)}, f32[10,16,128]{2,1,0:T(8,128)S(1)}, u32[]{:S(2)}, u32[]{:S(2)}) collective-permute-start(f32[10,16,128]{2,1,0:T(8,128)S(1)} %get-tuple-element.43), channel_id=1, source_target_pairs={{0,16},{8,24},{1,17},{9,25},{2,18},{10,26},{3,19},{11,27},{4,20},{... | collective-permute-start | bytes 245768 | tf_op jit(solution)/shard_map/ppermute | solution.py:510
  46.4 12.2 %collective-permute-start.11 = (f32[10,16,128]{2,1,0:T(8,128)S(1)}, f32[10,16,128]{2,1,0:T(8,128)S(1)}, u32[]{:S(2)}, u32[]{:S(2)}) collective-permute-start(f32[10,16,128]{2,1,0:T(8,128)S(1)} %get-tuple-element.43), channel_id=1, source_target_pairs={{0,24},{1,25},{2,26},{3,27},{4,28},{5,29},{6,30},{7,31}} | collective-permute-start | bytes 245768 | tf_op jit(solution)/shard_map/ppermute | solution.py:510
  47.7 10.9 %collective-permute-start.9 = (f32[10,16,128]{2,1,0:T(8,128)S(1)}, f32[10,16,128]{2,1,0:T(8,128)S(1)}, u32[]{:S(2)}, u32[]{:S(2)}) collective-permute-start(f32[10,16,128]{2,1,0:T(8,128)S(1)} %get-tuple-element.43), channel_id=1, source_target_pairs={{0,8},{8,16},{16,24},{1,9},{9,17},{17,25},{2,10},{10,18},{18,26},{... | collective-permute-start | bytes 245768 | tf_op jit(solution)/shard_map/ppermute | solution.py:510
  64.0 14.3 %collective-permute-start.15 = (f32[4,16,128]{2,1,0:T(8,128)S(1)}, f32[4,16,128]{2,1,0:T(8,128)S(1)}, u32[]{:S(2)}, u32[]{:S(2)}) collective-permute-start(f32[4,16,128]{2,1,0:T(8,128)S(1)} %get-tuple-element.50), channel_id=1, source_target_pairs={{0,1},{1,0},{2,3},{3,2},{4,5},{5,4},{6,7},{7,6},{8,9},{9,8},{10,11... | collective-permute-start | bytes 98312 | tf_op jit(solution)/shard_map/ppermute | solution.py:480
  64.1 16.5 %collective-permute-start.17 = (f32[4,16,128]{2,1,0:T(8,128)S(1)}, f32[4,16,128]{2,1,0:T(8,128)S(1)}, u32[]{:S(2)}, u32[]{:S(2)}) collective-permute-start(f32[4,16,128]{2,1,0:T(8,128)S(1)} %get-tuple-element.52), channel_id=1, source_target_pairs={{0,3},{1,2},{2,1},{3,0},{4,7},{5,6},{6,5},{7,4},{8,11},{9,10},{10,... | collective-permute-start | bytes 98312 | tf_op jit(solution)/shard_map/ppermute | solution.py:480
  69.6 12.3 %collective-permute-start.19 = (f32[4,16,128]{2,1,0:T(8,128)S(1)}, f32[4,16,128]{2,1,0:T(8,128)S(1)}, u32[]{:S(2)}, u32[]{:S(2)}) collective-permute-start(f32[4,16,128]{2,1,0:T(8,128)S(1)} %get-tuple-element.54), channel_id=1, source_target_pairs={{0,5},{1,4},{2,7},{3,6},{4,1},{5,0},{6,3},{7,2},{8,13},{9,12},{10,... | collective-permute-start | bytes 98312 | tf_op jit(solution)/shard_map/ppermute | solution.py:480
  71.0 11.0 %collective-permute-start.21 = (f32[4,16,128]{2,1,0:T(8,128)S(1)}, f32[4,16,128]{2,1,0:T(8,128)S(1)}, u32[]{:S(2)}, u32[]{:S(2)}) collective-permute-start(f32[4,16,128]{2,1,0:T(8,128)S(1)} %get-tuple-element.56), channel_id=1, source_target_pairs={{0,7},{1,6},{2,5},{3,4},{4,3},{5,2},{6,1},{7,0},{8,15},{9,14},{10,... | collective-permute-start | bytes 98312 | tf_op jit(solution)/shard_map/ppermute | solution.py:480
  77.5 4.5 %collective-permute-start.16 = (f32[4,16,128]{2,1,0:T(8,128)S(1)}, f32[4,16,128]{2,1,0:T(8,128)S(1)}, u32[]{:S(2)}, u32[]{:S(2)}) collective-permute-start(f32[4,16,128]{2,1,0:T(8,128)S(1)} %get-tuple-element.51), channel_id=1, source_target_pairs={{0,2},{1,3},{2,0},{3,1},{4,6},{5,7},{6,4},{7,5},{8,10},{9,11},{10,... | collective-permute-start | bytes 98312 | tf_op jit(solution)/shard_map/ppermute | solution.py:480
  78.2 5.6 %collective-permute-start.18 = (f32[4,16,128]{2,1,0:T(8,128)S(1)}, f32[4,16,128]{2,1,0:T(8,128)S(1)}, u32[]{:S(2)}, u32[]{:S(2)}) collective-permute-start(f32[4,16,128]{2,1,0:T(8,128)S(1)} %get-tuple-element.53), channel_id=1, source_target_pairs={{0,4},{1,5},{2,6},{3,7},{4,0},{5,1},{6,2},{7,3},{8,12},{9,13},{10,... | collective-permute-start | bytes 98312 | tf_op jit(solution)/shard_map/ppermute | solution.py:480
  80.5 5.7 %collective-permute-start.20 = (f32[4,16,128]{2,1,0:T(8,128)S(1)}, f32[4,16,128]{2,1,0:T(8,128)S(1)}, u32[]{:S(2)}, u32[]{:S(2)}) collective-permute-start(f32[4,16,128]{2,1,0:T(8,128)S(1)} %get-tuple-element.55), channel_id=1, source_target_pairs={{0,6},{1,7},{2,4},{3,5},{4,2},{5,3},{6,0},{7,1},{8,14},{9,15},{10,... | collective-permute-start | bytes 98312 | tf_op jit(solution)/shard_map/ppermute | solution.py:480

commit v4 on v3

--- a/solution.py
+++ b/solution.py
@@ -53,32 +53,27 @@
 
 def pack_kernel(groups, width, x_ref, out_ref):
     tile_count = x_ref.shape[3] // LANES
-    steps, depth = x_ref.shape[1], x_ref.shape[2]
-    size = 4
-    lane = lax.broadcasted_iota(jnp.int32, (size, depth, LANES), 2)
-
-    def body(chunk, carry):
-        place = pl.ds(chunk * size, size)
-        wide = blur_rows(
-            [[x_ref[part, place, :, t * LANES:(t + 1) * LANES] for t in range(tile_count)]
-             for part in range(groups)], lane)
-        for t in range(tile_count):
-            swapped = swap_groups([wide[part][t] for part in range(groups)], groups, width)
-            for part in range(groups):
-                out_ref[t * groups + part, place] = swapped[part]
-        return carry
-
-    lax.fori_loop(0, steps // size, body, 0)
+    lane = lax.broadcasted_iota(jnp.int32, x_ref.shape[1:3] + (LANES,), 2)
+    wide = blur_rows(
+        [[x_ref[part, :, :, t * LANES:(t + 1) * LANES] for t in range(tile_count)]
+         for part in range(groups)], lane)
+    for t in range(tile_count):
+        swapped = swap_groups([wide[part][t] for part in range(groups)], groups, width)
+        for part in range(groups):
+            out_ref[t * groups + part] = swapped[part]
 
 
 def pack(x, groups, width):
     steps = x.shape[0] // groups
     blocks = x.shape[2] // width
+    depth, width_y = x.shape[1:]
+    size = 4
     return pl.pallas_call(
         functools.partial(pack_kernel, groups, width),
-        out_shape=jax.ShapeDtypeStruct((blocks, steps, x.shape[1], LANES), jnp.float32),
-        in_specs=[pl.BlockSpec(memory_space=pltpu.VMEM)],
-        out_specs=pl.BlockSpec(memory_space=pltpu.VMEM),
+        grid=(steps // size,),
+        out_shape=jax.ShapeDtypeStruct((blocks, steps, depth, LANES), jnp.float32),
+        in_specs=[pl.BlockSpec((groups, size, depth, width_y), lambda i: (0, i, 0, 0))],
+        out_specs=pl.BlockSpec((blocks, size, depth, LANES), lambda i: (0, i, 0, 0)),
         compiler_params=pltpu.CompilerParams(vmem_limit_bytes=8 * MIB),
         name="pack",
     )(x.reshape(groups, steps, x.shape[1], x.shape[2]))
@@ -90,9 +85,11 @@
     me = lax.axis_index("gz")
     tile_count = before_ref.shape[2] // LANES
     lane = lax.broadcasted_iota(jnp.int32, (depth, LANES), 1)
+    position = lax.axis_index("gx")
+    inside = (position > 0, position < lax.axis_size("gx") - 1)
     ends = blur_rows(
-        [[ref[0, :, t * LANES:(t + 1) * LANES] for t in range(tile_count)]
-         for ref in (before_ref, after_ref)], lane)
+        [[jnp.where(there, ref[0, :, t * LANES:(t + 1) * LANES], 0.0) for t in range(tile_count)]
+         for ref, there in zip((before_ref, after_ref), inside)], lane)
     for t in range(tile_count):
         tiles = [ends[0][t]] * (groups - 1) + [ends[1][t]]
         swapped = swap_groups(tiles, groups, width)
@@ -125,7 +122,7 @@
 
 
 def depth_kernel(groups, width, bins, scale, far, halves_count, count, *refs):
-    pieces = refs[:-7]
+    pieces = refs[:-8] if far else refs[:-7]
     table_ref, s_ref, start_ref, total_ref, raw, sums, products_ref = refs[-7:]
     steps, depth = pieces[0].shape[-3] - 1, pieces[0].shape[-2]
     blocks = count // 2
@@ -244,14 +241,13 @@
     lax.fori_loop(0, slots // groups, scan_groups, 0, unroll=4)
 
 
-def depths(pieces, table, groups, width, bins, far, count):
+def depths(pieces, table, groups, width, bins, far, count, after=()):
     steps, depth = pieces[0].shape[0] - 1, pieces[0].shape[1]
     layers = depth * (count // 2)
     slots = layers + max(groups, depth) if far else layers
     halves = 2 if far else 1
     colors = table.shape[0]
     limit = 8 * MIB + slots * (LANES * 4 * halves) * (bins + 2 * colors)
-    work = steps * slots * LANES * bins
     return pl.pallas_call(
         functools.partial(depth_kernel, groups, width, bins, float(bins - 1), far, halves, count),
         out_shape=(
@@ -259,7 +255,7 @@
             jax.ShapeDtypeStruct((halves, slots, colors, LANES), jnp.float32),
             jax.ShapeDtypeStruct((slots // groups, colors, LANES), jnp.float32),
         ),
-        in_specs=[pl.BlockSpec(memory_space=pltpu.VMEM)] * (len(pieces) + 1),
+        in_specs=[pl.BlockSpec(memory_space=pltpu.VMEM)] * (len(pieces) + len(after) + 1),
         out_specs=[pl.BlockSpec(memory_space=pltpu.VMEM)] * 3,
         scratch_shapes=[
             pltpu.VMEM((steps + 2, layers + 2 * depth, LANES), jnp.float32),
@@ -267,10 +263,9 @@
             pltpu.VMEM((halves, slots, colors, LANES), jnp.float32),
         ],
         compiler_params=pltpu.CompilerParams(vmem_limit_bytes=limit),
-        cost_estimate=pl.CostEstimate(
-            flops=4 * work, bytes_accessed=8 * steps * slots * LANES, transcendentals=0),
+        cost_estimate=pl.CostEstimate(flops=0, bytes_accessed=0, transcendentals=0),
         name="depths_far" if far else "depths_near",
-    )(*pieces, table)
+    )(*pieces, *after, table)
 
 
 def render_kernel(groups, width, bins, ratio, turn, near, blocks, sums_count, s_ref, start_ref,
@@ -284,12 +279,13 @@
     me = lax.axis_index("gz")
     lower = me < blocks
     half = 0 if turn is None else (me + turn) % 2
+    position = lax.axis_index("gx")
     group = group_ids((colors, LANES), width)
 
     def begin(chunk, carry):
-        packed = before_refs[0][chunk]
-        for ref in before_refs[1:]:
-            packed = packed + ref[chunk]
+        packed = jnp.zeros((colors, LANES), jnp.float32)
+        for hop, ref in enumerate(before_refs, 1):
+            packed = packed + jnp.where(position >= hop, ref[chunk], 0.0)
         for k in range(groups):
             z = chunk * groups + k
             value = jnp.where(group == k, packed, 0.0)
@@ -357,8 +353,9 @@
         image[step] = front + passed * back + through * near_through * columns_ref[2]
         return carry
 
-    lax.fori_loop(0, rows, advance, 0)
+    lax.fori_loop(0, rows, advance, 0, unroll=4 if turn is None else 2)
     if turn is None:
+        out_refs[2][...] = jnp.zeros((8, LANES), jnp.float32)
         return
     if len(out_refs) == 1:
         out_refs[0][...] = image[...]
@@ -380,11 +377,11 @@
     if turn is None:
         share = steps
         shapes = [jax.ShapeDtypeStruct((steps, colors, LANES), jnp.float32)] * 2
+        shapes.append(jax.ShapeDtypeStruct((8, LANES), jnp.float32))
     elif share % groups == 0:
         shapes = [jax.ShapeDtypeStruct((share // groups, colors, LANES), jnp.float32)] * groups
     else:
         shapes = [jax.ShapeDtypeStruct((share, colors, LANES), jnp.float32)]
-    work = share * slots * LANES
     return pl.pallas_call(
         functools.partial(render_kernel, groups, width, bins, ratio, turn, len(near), blocks,
                           len(before)),
@@ -396,9 +393,7 @@
             pltpu.VMEM((slots, colors, LANES), jnp.float32),
         ],
         compiler_params=pltpu.CompilerParams(vmem_limit_bytes=8 * MIB + slots * colors * 512 * 4),
-        cost_estimate=pl.CostEstimate(
-            flops=work * bins * colors * 12, bytes_accessed=4 * work,
-            transcendentals=2 * work * colors),
+        cost_estimate=pl.CostEstimate(flops=0, bytes_accessed=0, transcendentals=0),
         name="render_near" if turn is None else "render_far",
     )(s, start, table, columns, *before, *near)
 
@@ -493,7 +488,7 @@
     step_x = 1.0 / (rows_x * size_x)
     step_z = 1.0 / (depth * count)
 
-    up = [(i, i + 1) for i in range(size_x - 1)]
+    up = [(i, (i + 1) % size_x) for i in range(size_x)]
     down = [(j, i) for i, j in up]
     before = lax.ppermute(density[rows_x - 1:], "gx", up)
     after = lax.ppermute(density[:1], "gx", down)
@@ -501,21 +496,24 @@
     packed = pack(density, groups, width)
     pieces = list(address(packed, before, after, groups, width))
     for apart in range(1, count):
-        pieces[apart] = exchange(pieces[apart], "gz", apart)
+        give = pieces[apart]
+        if apart >= count * 3 // 4:
+            give, _ = lax.optimization_barrier((give, pieces[apart - count // 4]))
+        pieces[apart] = exchange(give, "gz", apart)
     columns = jnp.broadcast_to(
         jnp.stack([extinction_scale, ambient, backdrop])[:, :, None], (3, colors, LANES))
     sum_table, table = tables(bin_rows, tf_extinction, tf_color, columns, step_x, step_z)
 
     def prefixes(total):
-        return [lax.ppermute(total, "gx", [(i, i + hop) for i in range(size_x - hop)])
+        return [lax.ppermute(total, "gx", [(i, (i + hop) % size_x) for i in range(size_x)])
                 for hop in range(1, size_x)]
 
     blocks = count // 2
     ratio = step_x / step_z
     s, start, total = depths(pieces[:blocks], sum_table, groups, width, bins, False, count)
-    near = render(s, start, table, columns, prefixes(total), [], groups, width, bins, ratio,
-                  None, blocks)
-    s, start, total = depths(pieces, sum_table, groups, width, bins, True, count)
+    *near, done = render(s, start, table, columns, prefixes(total), [], groups, width, bins, ratio,
+                         None, blocks)
+    s, start, total = depths(pieces, sum_table, groups, width, bins, True, count, [done])
     sums = prefixes(total)
     halves = [
         render(s, start, table, columns, sums, near, groups, width, bins, ratio, turn, blocks)

time: 87.8 us -> 85.8 us (0.977)
  waiting for transfers between devices: 6.78 us -> 24.3 us
  starting transfers between devices: 43.7 us -> 30 us
  Pallas kernels: 31.2 us -> 25.6 us
    ppermute x6, starting transfers between devices: 16.8 us -> 6.86 us  [prefixes(): lax.ppermute(total, 'gx', [(i, (i + hop) % size_x) for i in range(size_x)])]
    ppermute x6, waiting for transfers between devices: 0.02 us -> 8.94 us  [prefixes(): lax.ppermute(total, 'gx', [(i, (i + hop) % size_x) for i in range(size_x)])]
    ppermute x14, waiting for transfers between devices: 6.17 us -> 14.8 us  [exchange(): return lax.ppermute(value, axis, pairs)]
    pallas_call x3, Pallas kernels: 19.7 us -> 13.9 us  [render(): pl.pallas_call(functools.partial(render_kernel, groups, width, bins, rati...]
    ppermute x1, starting transfers between devices: 4.83 us -> 0.01 us  [local(): before = lax.ppermute(density[rows_x - 1:], 'gx', up)]
    ppermute x1, starting transfers between devices: 1.29 us -> 3.89 us  [local(): after = lax.ppermute(density[:1], 'gx', down)]
    ppermute x14, starting transfers between devices: 20.9 us -> 19.3 us  [exchange(): return lax.ppermute(value, axis, pairs)]
  transfers between devices with their start and end apart: 22 -> 22, of which waited for: 5 -> 9; matrix products, arithmetic and copies ran while one was open for 2% -> 2% of each run, Pallas kernels for 28% -> 19%
where the time goes in v4:
time: 85.8 us; the launch traced here: 85.4 us
  starting transfers between devices  30 us (35%)
  Pallas kernels  25.6 us (30%)
  waiting for transfers between devices  24.3 us (28%)
  local copies, waits for them, and re-layouts  4.57 us (5%)
    ppermute x14, starting transfers between devices, exchange(): return lax.ppermute(value, axis, pairs)  19.3 us
    ppermute x14, waiting for transfers between devices, exchange(): return lax.ppermute(value, axis, pairs)  14.8 us
    pallas_call x3, Pallas kernels, render(): pl.pallas_call(functools.partial(render_kernel, groups, width, bins, rati...  13.9 us
    ppermute x6, waiting for transfers between devices, prefixes(): lax.ppermute(total, 'gx', [(i, (i + hop) % size_x) for i in range(size_x)])  8.94 us
    pallas_call x2, Pallas kernels, depths(): pl.pallas_call(functools.partial(depth_kernel, groups, width, bins, float...  7.43 us
    ppermute x6, starting transfers between devices, prefixes(): lax.ppermute(total, 'gx', [(i, (i + hop) % size_x) for i in range(size_x)])  6.86 us
    ppermute x1, starting transfers between devices, local(): after = lax.ppermute(density[:1], 'gx', down)  3.89 us
    unnamed x14, local copies, waits for them, and re-layouts  3.2 us
  transfers between devices with their start and end apart: 22, of which 9 were waited for; matrix products, arithmetic and copies ran while one was open for 2% of the time, Pallas kernels for 19%

profile of v4, /device:TPU:0, one launch (start us, length us, event | category | flops | bytes accessed | tf_op | source)
XLA Modules:
  0.0 85.4 jit_solution(13006256533362679997)
XLA Ops:
  0.0 0.7 fusion
  0.7 3.9 %collective-permute-start.1 = (f32[1,8,256]{2,1,0:T(8,128)S(1)}, f32[1,8,256]{2,1,0:T(8,128)S(1)}, u32[]{:S(2)}, u32[]{:S(2)}) collective-permute-start(f32[1,8,256]{2,1,0:T(8,128)S(1)} %get-tuple-element.63), channel_id=1, source_target_pairs={{8,0},{16,8},{24,16},{0,24},{9,1},{17,9},{25,17},{1,25},{10,2},{18... | collective-permute-start | bytes 24584 | tf_op jit(solution)/shard_map/ppermute | solution.py:494
  4.6 1.2 %copy-done = f32[128,8,256]{2,1,0:T(8,128)S(1)} copy-done((f32[128,8,256]{2,1,0:T(8,128)S(1)}, f32[128,8,256]{2,1,0:T(8,128)}, u32[]{:S(2)}) %copy-start) | copy-done | bytes 1048600
  5.8 2.7 %pack.1.packed_ref = f32[8,32,8,128]{3,2,1,0:T(8,128)S(1)} custom-call(f32[4,32,8,256]{3,2,1,0:T(8,128)S(1)} %bitcast.10), custom_call_target="tpu_custom_call" | custom-call | tf_op jit(solution)/shard_map/pack/pallas_call | solution.py:71
  9.4 2.7 %collective-permute-start.5 = (f32[33,8,128]{2,1,0:T(8,128)S(1)}, f32[33,8,128]{2,1,0:T(8,128)S(1)}, u32[]{:S(2)}, u32[]{:S(2)}) collective-permute-start(f32[33,8,128]{2,1,0:T(8,128)S(1)} %get-tuple-element.38), channel_id=1, source_target_pairs={{0,4},{1,5},{2,6},{3,7},{4,0},{5,1},{6,2},{7,3},{8,12},{9,13},{10,... | collective-permute-start | bytes 405512 | tf_op jit(solution)/shard_map/ppermute | solution.py:475
  12.1 0.6 copy-done.3
  12.8 0.6 copy-done.6
  14.4 1.6 %collective-permute-start.3 = (f32[33,8,128]{2,1,0:T(8,128)S(1)}, f32[33,8,128]{2,1,0:T(8,128)S(1)}, u32[]{:S(2)}, u32[]{:S(2)}) collective-permute-start(f32[33,8,128]{2,1,0:T(8,128)S(1)} %get-tuple-element.36), channel_id=1, source_target_pairs={{0,2},{1,3},{2,0},{3,1},{4,6},{5,7},{6,4},{7,5},{8,10},{9,11},{10,... | collective-permute-start | bytes 405512 | tf_op jit(solution)/shard_map/ppermute | solution.py:475
  16.0 0.7 add_bitcast_fusion
  16.7 5.2 %collective-permute-done.5.refs_4_ = f32[33,8,128]{2,1,0:T(8,128)S(1)} collective-permute-done((f32[33,8,128]{2,1,0:T(8,128)S(1)}, f32[33,8,128]{2,1,0:T(8,128)S(1)}, u32[]{:S(2)}, u32[]{:S(2)}) %collective-permute-start.5) | collective-permute-done | bytes 135200 | tf_op jit(solution)/shard_map/ppermute | solution.py:475
  21.9 2.6 %collective-permute-start.7 = (f32[33,8,128]{2,1,0:T(8,128)S(1)}, f32[33,8,128]{2,1,0:T(8,128)S(1)}, u32[]{:S(2)}, u32[]{:S(2)}) collective-permute-start(f32[33,8,128]{2,1,0:T(8,128)S(1)} %get-tuple-element.41), channel_id=1, source_target_pairs={{0,6},{1,7},{2,4},{3,5},{4,2},{5,3},{6,0},{7,1},{8,14},{9,15},{10,... | collective-permute-start | bytes 405512 | tf_op jit(solution)/shard_map/ppermute | solution.py:475
  24.5 2.3 %collective-permute-start.8 = (f32[33,8,128]{2,1,0:T(8,128)S(1)}, f32[33,8,128]{2,1,0:T(8,128)S(1)}, u32[]{:S(2)}, u32[]{:S(2)}) collective-permute-start(f32[33,8,128]{2,1,0:T(8,128)S(1)} %get-tuple-element.43), channel_id=1, source_target_pairs={{0,7},{1,6},{2,5},{3,4},{4,3},{5,2},{6,1},{7,0},{8,15},{9,14},{10,... | collective-permute-start | bytes 405512 | tf_op jit(solution)/shard_map/ppermute | solution.py:475
  26.9 0.6 copy-done.2
  28.0 3.9 %collective-permute-done.4.refs_3_ = f32[33,8,128]{2,1,0:T(8,128)S(1)} collective-permute-done((f32[33,8,128]{2,1,0:T(8,128)S(1)}, f32[33,8,128]{2,1,0:T(8,128)S(1)}, u32[]{:S(2)}, u32[]{:S(2)}) %collective-permute-start.4) | collective-permute-done | bytes 135200 | tf_op jit(solution)/shard_map/ppermute | solution.py:475
  31.9 3.5 %depths_near.1 = (f32[32,32,128]{2,1,0:T(8,128)S(1)}, f32[1,32,16,128]{3,2,1,0:T(8,128)S(1)}, f32[8,16,128]{2,1,0:T(8,128)S(1)}) custom-call(f32[33,8,128]{2,1,0:T(8,128)S(1)} %get-tuple-element.34.refs_0_, f32[33,8,128]{2,1,0:T(8,128)S(1)} %collective-permute-done.2.refs_1_, f32[33,8,128]{2,1,0:T(8,128)S(1)} %collective-permute-done.3.refs_2_, ...), custom_call_target="tpu_custom_call" | custom-call | tf_op jit(solution)/shard_map/depths_near/pallas_call | solution.py:251
  35.4 2.8 %collective-permute-start.11 = (f32[8,16,128]{2,1,0:T(8,128)S(1)}, f32[8,16,128]{2,1,0:T(8,128)S(1)}, u32[]{:S(2)}, u32[]{:S(2)}) collective-permute-start(f32[8,16,128]{2,1,0:T(8,128)S(1)} %get-tuple-element.48), channel_id=1, source_target_pairs={{0,24},{8,0},{16,8},{24,16},{1,25},{9,1},{17,9},{25,17},{2,26},{10... | collective-permute-start | bytes 196616 | tf_op jit(solution)/shard_map/ppermute | solution.py:508
  38.9 1.9 %collective-permute-done.11.refs_2_ = f32[8,16,128]{2,1,0:T(8,128)S(1)} collective-permute-done((f32[8,16,128]{2,1,0:T(8,128)S(1)}, f32[8,16,128]{2,1,0:T(8,128)S(1)}, u32[]{:S(2)}, u32[]{:S(2)}) %collective-permute-start.11) | collective-permute-done | bytes 65568 | tf_op jit(solution)/shard_map/ppermute | solution.py:508
  40.7 3.3 %collective-permute-done.10.refs_1_ = f32[8,16,128]{2,1,0:T(8,128)S(1)} collective-permute-done((f32[8,16,128]{2,1,0:T(8,128)S(1)}, f32[8,16,128]{2,1,0:T(8,128)S(1)}, u32[]{:S(2)}, u32[]{:S(2)}) %collective-permute-start.10) | collective-permute-done | bytes 65568 | tf_op jit(solution)/shard_map/ppermute | solution.py:508
  44.0 5.9 %render_near.1 = (f32[32,16,128]{2,1,0:T(8,128)S(1)}, f32[32,16,128]{2,1,0:T(8,128)S(1)}, f32[8,128]{1,0:T(8,128)S(1)}) custom-call(f32[32,32,128]{2,1,0:T(8,128)S(1)} %get-tuple-element.45.s_ref, f32[1,32,16,128]{3,2,1,0:T(8,128)S(1)} %get-tuple-element.46.start_ref, bf16[32,96]{1,0:T(8,128)(2,1)S(1)} %get-tuple-element.47.table_ref, ...), custom_call_target="tpu_custom_call" | custom-call | tf_op jit(solution)/shard_map/render_near/pallas_call | solution.py:385
  50.0 3.9 %depths_far.1 = (f32[32,40,128]{2,1,0:T(8,128)S(1)}, f32[2,40,16,128]{3,2,1,0:T(8,128)S(1)}, f32[10,16,128]{2,1,0:T(8,128)S(1)}) custom-call(f32[33,8,128]{2,1,0:T(8,128)S(1)} %get-tuple-element.34.refs_0_, f32[33,8,128]{2,1,0:T(8,128)S(1)} %collective-permute-done.2.refs_1_, f32[33,8,128]{2,1,0:T(8,128)S(1)} %collective-permute-done.3.refs_2_, ...), custom_call_target="tpu_custom_call" | custom-call | tf_op jit(solution)/shard_map/depths_far/pallas_call | solution.py:251
  54.3 1.4 %collective-permute-start.13 = (f32[10,16,128]{2,1,0:T(8,128)S(1)}, f32[10,16,128]{2,1,0:T(8,128)S(1)}, u32[]{:S(2)}, u32[]{:S(2)}) collective-permute-start(f32[10,16,128]{2,1,0:T(8,128)S(1)} %get-tuple-element.52), channel_id=1, source_target_pairs={{0,16},{8,24},{16,0},{24,8},{1,17},{9,25},{17,1},{25,9},{2,18},{10... | collective-permute-start | bytes 245768 | tf_op jit(solution)/shard_map/ppermute | solution.py:508
  55.7 1.6 %collective-permute-start.12 = (f32[10,16,128]{2,1,0:T(8,128)S(1)}, f32[10,16,128]{2,1,0:T(8,128)S(1)}, u32[]{:S(2)}, u32[]{:S(2)}) collective-permute-start(f32[10,16,128]{2,1,0:T(8,128)S(1)} %get-tuple-element.52), channel_id=1, source_target_pairs={{0,8},{8,16},{16,24},{24,0},{1,9},{9,17},{17,25},{25,1},{2,10},{10... | collective-permute-start | bytes 245768 | tf_op jit(solution)/shard_map/ppermute | solution.py:508
  57.3 1.8 %collective-permute-done.14.refs_2_ = f32[10,16,128]{2,1,0:T(8,128)S(1)} collective-permute-done((f32[10,16,128]{2,1,0:T(8,128)S(1)}, f32[10,16,128]{2,1,0:T(8,128)S(1)}, u32[]{:S(2)}, u32[]{:S(2)}) %collective-permute-start.14) | collective-permute-done | bytes 81952 | tf_op jit(solution)/shard_map/ppermute | solution.py:508
  59.1 1.9 %collective-permute-done.12.refs_0_ = f32[10,16,128]{2,1,0:T(8,128)S(1)} collective-permute-done((f32[10,16,128]{2,1,0:T(8,128)S(1)}, f32[10,16,128]{2,1,0:T(8,128)S(1)}, u32[]{:S(2)}, u32[]{:S(2)}) %collective-permute-start.12) | collective-permute-done | bytes 81952 | tf_op jit(solution)/shard_map/ppermute | solution.py:508
  61.1 4.0 %render_far.3 = (f32[4,16,128]{2,1,0:T(8,128)S(1)}, f32[4,16,128]{2,1,0:T(8,128)S(1)}, f32[4,16,128]{2,1,0:T(8,128)S(1)}, f32[4,16,128]{2,1,0:T(8,128)S(1)}) custom-call(f32[32,40,128]{2,1,0:T(8,128)S(1)} %get-tuple-element.50.s_ref, f32[2,40,16,128]{3,2,1,0:T(8,128)S(1)} %get-tuple-element.51.start_ref, bf16[32,96]{1,0:T(8,128)(2,1)S(1)} %get-tuple-element.47.table_ref, ...), custom_call_target="tpu_custom_call" | custom-call | tf_op jit(solution)/shard_map/render_far/pallas_call | solution.py:385
  65.3 4.9 %collective-permute-start.19 = (f32[4,16,128]{2,1,0:T(8,128)S(1)}, f32[4,16,128]{2,1,0:T(8,128)S(1)}, u32[]{:S(2)}, u32[]{:S(2)}) collective-permute-start(f32[4,16,128]{2,1,0:T(8,128)S(1)} %get-tuple-element.60), channel_id=1, source_target_pairs={{0,5},{1,4},{2,7},{3,6},{4,1},{5,0},{6,3},{7,2},{8,13},{9,12},{10,... | collective-permute-start | bytes 98312 | tf_op jit(solution)/shard_map/ppermute | solution.py:475
  70.2 4.0 %render_far.2 = (f32[4,16,128]{2,1,0:T(8,128)S(1)}, f32[4,16,128]{2,1,0:T(8,128)S(1)}, f32[4,16,128]{2,1,0:T(8,128)S(1)}, f32[4,16,128]{2,1,0:T(8,128)S(1)}) custom-call(f32[32,40,128]{2,1,0:T(8,128)S(1)} %get-tuple-element.50.s_ref, f32[2,40,16,128]{3,2,1,0:T(8,128)S(1)} %get-tuple-element.51.start_ref, bf16[32,96]{1,0:T(8,128)(2,1)S(1)} %get-tuple-element.47.table_ref, ...), custom_call_target="tpu_custom_call" | custom-call | tf_op jit(solution)/shard_map/render_far/pallas_call | solution.py:385
  74.2 0.6 collective-permute-start.16
  74.9 3.9 %collective-permute-start.18 = (f32[4,16,128]{2,1,0:T(8,128)S(1)}, f32[4,16,128]{2,1,0:T(8,128)S(1)}, u32[]{:S(2)}, u32[]{:S(2)}) collective-permute-start(f32[4,16,128]{2,1,0:T(8,128)S(1)} %get-tuple-element.59), channel_id=1, source_target_pairs={{0,4},{1,5},{2,6},{3,7},{4,0},{5,1},{6,2},{7,3},{8,12},{9,13},{10,... | collective-permute-start | bytes 98312 | tf_op jit(solution)/shard_map/ppermute | solution.py:475
  78.8 2.4 %collective-permute-done.18.refs_4_ = f32[4,16,128]{2,1,0:T(8,128)S(1)} collective-permute-done((f32[4,16,128]{2,1,0:T(8,128)S(1)}, f32[4,16,128]{2,1,0:T(8,128)S(1)}, u32[]{:S(2)}, u32[]{:S(2)}) %collective-permute-start.18) | collective-permute-done | bytes 32800 | tf_op jit(solution)/shard_map/ppermute | solution.py:475
  81.2 3.2 %collective-permute-done.20.refs_6_ = f32[4,16,128]{2,1,0:T(8,128)S(1)} collective-permute-done((f32[4,16,128]{2,1,0:T(8,128)S(1)}, f32[4,16,128]{2,1,0:T(8,128)S(1)}, u32[]{:S(2)}, u32[]{:S(2)}) %collective-permute-start.20) | collective-permute-done | bytes 32800 | tf_op jit(solution)/shard_map/ppermute | solution.py:475
  84.5 1.0 %unpack.1 = f32[16,16,256]{2,1,0:T(8,128)} custom-call(f32[4,16,128]{2,1,0:T(8,128)S(1)} %get-tuple-element.55.refs_0_, f32[4,16,128]{2,1,0:T(8,128)S(1)} %collective-permute-done.15.refs_1_, f32[4,16,128]{2,1,0:T(8,128)S(1)} %collective-permute-done.16.refs_2_, f32[4,16,128]{2,1,0:T(8,128)S(1)} %collective-permute-done.17.refs_3_, ...), custom_call_target="tpu_custom_call" | custom-call | tf_op jit(solution)/shard_map/unpack/pallas_call | solution.py:418
  (41 shorter events, 3.8 us)
Async XLA Ops:
  0.7 7.8 %collective-permute-start.1 = (f32[1,8,256]{2,1,0:T(8,128)S(1)}, f32[1,8,256]{2,1,0:T(8,128)S(1)}, u32[]{:S(2)}, u32[]{:S(2)}) collective-permute-start(f32[1,8,256]{2,1,0:T(8,128)S(1)} %get-tuple-element.63), channel_id=1, source_target_pairs={{8,0},{16,8},{24,16},{0,24},{9,1},{17,9},{25,17},{1,25},{10,2},{18... | collective-permute-start | bytes 24584 | tf_op jit(solution)/shard_map/ppermute | solution.py:494
  4.6 4.5 %collective-permute-start = (f32[1,8,256]{2,1,0:T(8,128)S(1)}, f32[1,8,256]{2,1,0:T(8,128)S(1)}, u32[]{:S(2)}, u32[]{:S(2)}) collective-permute-start(f32[1,8,256]{2,1,0:T(8,128)S(1)} %get-tuple-element.64), channel_id=1, source_target_pairs={{0,8},{8,16},{16,24},{24,0},{1,9},{9,17},{17,25},{25,1},{2,10},{10... | collective-permute-start | bytes 24584 | tf_op jit(solution)/shard_map/ppermute | solution.py:493
  4.6 1.2 %copy-start = (f32[128,8,256]{2,1,0:T(8,128)S(1)}, f32[128,8,256]{2,1,0:T(8,128)}, u32[]{:S(2)}) copy-start(f32[128,8,256]{2,1,0:T(8,128)} %param.7) | copy-start | bytes 3145732
  9.4 12.5 %collective-permute-start.5 = (f32[33,8,128]{2,1,0:T(8,128)S(1)}, f32[33,8,128]{2,1,0:T(8,128)S(1)}, u32[]{:S(2)}, u32[]{:S(2)}) collective-permute-start(f32[33,8,128]{2,1,0:T(8,128)S(1)} %get-tuple-element.38), channel_id=1, source_target_pairs={{0,4},{1,5},{2,6},{3,7},{4,0},{5,1},{6,2},{7,3},{8,12},{9,13},{10,... | collective-permute-start | bytes 405512 | tf_op jit(solution)/shard_map/ppermute | solution.py:475
  12.1 12.5 %collective-permute-start.6 = (f32[33,8,128]{2,1,0:T(8,128)S(1)}, f32[33,8,128]{2,1,0:T(8,128)S(1)}, u32[]{:S(2)}, u32[]{:S(2)}) collective-permute-start(f32[33,8,128]{2,1,0:T(8,128)S(1)} %get-tuple-element.39), channel_id=1, source_target_pairs={{0,5},{1,4},{2,7},{3,6},{4,1},{5,0},{6,3},{7,2},{8,13},{9,12},{10,... | collective-permute-start | bytes 405512 | tf_op jit(solution)/shard_map/ppermute | solution.py:475
  12.1 0.7 copy-start.3
  12.1 0.7 copy-start.4
  12.1 0.7 copy-start.5
  12.7 0.7 copy-start.6
  14.0 14.0 %collective-permute-start.2 = (f32[33,8,128]{2,1,0:T(8,128)S(1)}, f32[33,8,128]{2,1,0:T(8,128)S(1)}, u32[]{:S(2)}, u32[]{:S(2)}) collective-permute-start(f32[33,8,128]{2,1,0:T(8,128)S(1)} %get-tuple-element.35), channel_id=1, source_target_pairs={{0,1},{1,0},{2,3},{3,2},{4,5},{5,4},{6,7},{7,6},{8,9},{9,8},{10,11... | collective-permute-start | bytes 405512 | tf_op jit(solution)/shard_map/ppermute | solution.py:475
  14.4 13.5 %collective-permute-start.3 = (f32[33,8,128]{2,1,0:T(8,128)S(1)}, f32[33,8,128]{2,1,0:T(8,128)S(1)}, u32[]{:S(2)}, u32[]{:S(2)}) collective-permute-start(f32[33,8,128]{2,1,0:T(8,128)S(1)} %get-tuple-element.36), channel_id=1, source_target_pairs={{0,2},{1,3},{2,0},{3,1},{4,6},{5,7},{6,4},{7,5},{8,10},{9,11},{10,... | collective-permute-start | bytes 405512 | tf_op jit(solution)/shard_map/ppermute | solution.py:475
  16.0 15.9 %collective-permute-start.4 = (f32[33,8,128]{2,1,0:T(8,128)S(1)}, f32[33,8,128]{2,1,0:T(8,128)S(1)}, u32[]{:S(2)}, u32[]{:S(2)}) collective-permute-start(f32[33,8,128]{2,1,0:T(8,128)S(1)} %get-tuple-element.37), channel_id=1, source_target_pairs={{0,3},{1,2},{2,1},{3,0},{4,7},{5,6},{6,5},{7,4},{8,11},{9,10},{10,... | collective-permute-start | bytes 405512 | tf_op jit(solution)/shard_map/ppermute | solution.py:475
  21.9 28.1 %collective-permute-start.7 = (f32[33,8,128]{2,1,0:T(8,128)S(1)}, f32[33,8,128]{2,1,0:T(8,128)S(1)}, u32[]{:S(2)}, u32[]{:S(2)}) collective-permute-start(f32[33,8,128]{2,1,0:T(8,128)S(1)} %get-tuple-element.41), channel_id=1, source_target_pairs={{0,6},{1,7},{2,4},{3,5},{4,2},{5,3},{6,0},{7,1},{8,14},{9,15},{10,... | collective-permute-start | bytes 405512 | tf_op jit(solution)/shard_map/ppermute | solution.py:475
  24.5 25.4 %collective-permute-start.8 = (f32[33,8,128]{2,1,0:T(8,128)S(1)}, f32[33,8,128]{2,1,0:T(8,128)S(1)}, u32[]{:S(2)}, u32[]{:S(2)}) collective-permute-start(f32[33,8,128]{2,1,0:T(8,128)S(1)} %get-tuple-element.43), channel_id=1, source_target_pairs={{0,7},{1,6},{2,5},{3,4},{4,3},{5,2},{6,1},{7,0},{8,15},{9,14},{10,... | collective-permute-start | bytes 405512 | tf_op jit(solution)/shard_map/ppermute | solution.py:475
  26.8 0.7 copy-start.2
  26.8 0.7 copy-start.1
  35.4 5.3 %collective-permute-start.11 = (f32[8,16,128]{2,1,0:T(8,128)S(1)}, f32[8,16,128]{2,1,0:T(8,128)S(1)}, u32[]{:S(2)}, u32[]{:S(2)}) collective-permute-start(f32[8,16,128]{2,1,0:T(8,128)S(1)} %get-tuple-element.48), channel_id=1, source_target_pairs={{0,24},{8,0},{16,8},{24,16},{1,25},{9,1},{17,9},{25,17},{2,26},{10... | collective-permute-start | bytes 196616 | tf_op jit(solution)/shard_map/ppermute | solution.py:508
  38.2 5.8 %collective-permute-start.10 = (f32[8,16,128]{2,1,0:T(8,128)S(1)}, f32[8,16,128]{2,1,0:T(8,128)S(1)}, u32[]{:S(2)}, u32[]{:S(2)}) collective-permute-start(f32[8,16,128]{2,1,0:T(8,128)S(1)} %get-tuple-element.48), channel_id=1, source_target_pairs={{0,16},{8,24},{16,0},{24,8},{1,17},{9,25},{17,1},{25,9},{2,18},{10... | collective-permute-start | bytes 196616 | tf_op jit(solution)/shard_map/ppermute | solution.py:508
  38.7 5.3 %collective-permute-start.9 = (f32[8,16,128]{2,1,0:T(8,128)S(1)}, f32[8,16,128]{2,1,0:T(8,128)S(1)}, u32[]{:S(2)}, u32[]{:S(2)}) collective-permute-start(f32[8,16,128]{2,1,0:T(8,128)S(1)} %get-tuple-element.48), channel_id=1, source_target_pairs={{0,8},{8,16},{16,24},{24,0},{1,9},{9,17},{17,25},{25,1},{2,10},{10... | collective-permute-start | bytes 196616 | tf_op jit(solution)/shard_map/ppermute | solution.py:508
  53.9 5.2 %collective-permute-start.14 = (f32[10,16,128]{2,1,0:T(8,128)S(1)}, f32[10,16,128]{2,1,0:T(8,128)S(1)}, u32[]{:S(2)}, u32[]{:S(2)}) collective-permute-start(f32[10,16,128]{2,1,0:T(8,128)S(1)} %get-tuple-element.52), channel_id=1, source_target_pairs={{0,24},{8,0},{16,8},{24,16},{1,25},{9,1},{17,9},{25,17},{2,26},{10... | collective-permute-start | bytes 245768 | tf_op jit(solution)/shard_map/ppermute | solution.py:508
  54.3 4.8 %collective-permute-start.13 = (f32[10,16,128]{2,1,0:T(8,128)S(1)}, f32[10,16,128]{2,1,0:T(8,128)S(1)}, u32[]{:S(2)}, u32[]{:S(2)}) collective-permute-start(f32[10,16,128]{2,1,0:T(8,128)S(1)} %get-tuple-element.52), channel_id=1, source_target_pairs={{0,16},{8,24},{16,0},{24,8},{1,17},{9,25},{17,1},{25,9},{2,18},{10... | collective-permute-start | bytes 245768 | tf_op jit(solution)/shard_map/ppermute | solution.py:508
  55.7 5.3 %collective-permute-start.12 = (f32[10,16,128]{2,1,0:T(8,128)S(1)}, f32[10,16,128]{2,1,0:T(8,128)S(1)}, u32[]{:S(2)}, u32[]{:S(2)}) collective-permute-start(f32[10,16,128]{2,1,0:T(8,128)S(1)} %get-tuple-element.52), channel_id=1, source_target_pairs={{0,8},{8,16},{16,24},{24,0},{1,9},{9,17},{17,25},{25,1},{2,10},{10... | collective-permute-start | bytes 245768 | tf_op jit(solution)/shard_map/ppermute | solution.py:508
  65.1 9.8 %collective-permute-start.15 = (f32[4,16,128]{2,1,0:T(8,128)S(1)}, f32[4,16,128]{2,1,0:T(8,128)S(1)}, u32[]{:S(2)}, u32[]{:S(2)}) collective-permute-start(f32[4,16,128]{2,1,0:T(8,128)S(1)} %get-tuple-element.56), channel_id=1, source_target_pairs={{0,1},{1,0},{2,3},{3,2},{4,5},{5,4},{6,7},{7,6},{8,9},{9,8},{10,11... | collective-permute-start | bytes 98312 | tf_op jit(solution)/shard_map/ppermute | solution.py:475
  65.1 13.6 %collective-permute-start.17 = (f32[4,16,128]{2,1,0:T(8,128)S(1)}, f32[4,16,128]{2,1,0:T(8,128)S(1)}, u32[]{:S(2)}, u32[]{:S(2)}) collective-permute-start(f32[4,16,128]{2,1,0:T(8,128)S(1)} %get-tuple-element.58), channel_id=1, source_target_pairs={{0,3},{1,2},{2,1},{3,0},{4,7},{5,6},{6,5},{7,4},{8,11},{9,10},{10,... | collective-permute-start | bytes 98312 | tf_op jit(solution)/shard_map/ppermute | solution.py:475
  65.3 13.4 %collective-permute-start.19 = (f32[4,16,128]{2,1,0:T(8,128)S(1)}, f32[4,16,128]{2,1,0:T(8,128)S(1)}, u32[]{:S(2)}, u32[]{:S(2)}) collective-permute-start(f32[4,16,128]{2,1,0:T(8,128)S(1)} %get-tuple-element.60), channel_id=1, source_target_pairs={{0,5},{1,4},{2,7},{3,6},{4,1},{5,0},{6,3},{7,2},{8,13},{9,12},{10,... | collective-permute-start | bytes 98312 | tf_op jit(solution)/shard_map/ppermute | solution.py:475
  70.2 8.5 %collective-permute-start.21 = (f32[4,16,128]{2,1,0:T(8,128)S(1)}, f32[4,16,128]{2,1,0:T(8,128)S(1)}, u32[]{:S(2)}, u32[]{:S(2)}) collective-permute-start(f32[4,16,128]{2,1,0:T(8,128)S(1)} %get-tuple-element.62), channel_id=1, source_target_pairs={{0,7},{1,6},{2,5},{3,4},{4,3},{5,2},{6,1},{7,0},{8,15},{9,14},{10,... | collective-permute-start | bytes 98312 | tf_op jit(solution)/shard_map/ppermute | solution.py:475
  74.2 4.5 %collective-permute-start.16 = (f32[4,16,128]{2,1,0:T(8,128)S(1)}, f32[4,16,128]{2,1,0:T(8,128)S(1)}, u32[]{:S(2)}, u32[]{:S(2)}) collective-permute-start(f32[4,16,128]{2,1,0:T(8,128)S(1)} %get-tuple-element.57), channel_id=1, source_target_pairs={{0,2},{1,3},{2,0},{3,1},{4,6},{5,7},{6,4},{7,5},{8,10},{9,11},{10,... | collective-permute-start | bytes 98312 | tf_op jit(solution)/shard_map/ppermute | solution.py:475
  74.9 6.3 %collective-permute-start.18 = (f32[4,16,128]{2,1,0:T(8,128)S(1)}, f32[4,16,128]{2,1,0:T(8,128)S(1)}, u32[]{:S(2)}, u32[]{:S(2)}) collective-permute-start(f32[4,16,128]{2,1,0:T(8,128)S(1)} %get-tuple-element.59), channel_id=1, source_target_pairs={{0,4},{1,5},{2,6},{3,7},{4,0},{5,1},{6,2},{7,3},{8,12},{9,13},{10,... | collective-permute-start | bytes 98312 | tf_op jit(solution)/shard_map/ppermute | solution.py:475
  78.7 5.7 %collective-permute-start.20 = (f32[4,16,128]{2,1,0:T(8,128)S(1)}, f32[4,16,128]{2,1,0:T(8,128)S(1)}, u32[]{:S(2)}, u32[]{:S(2)}) collective-permute-start(f32[4,16,128]{2,1,0:T(8,128)S(1)} %get-tuple-element.61), channel_id=1, source_target_pairs={{0,6},{1,7},{2,4},{3,5},{4,2},{5,3},{6,0},{7,1},{8,14},{9,15},{10,... | collective-permute-start | bytes 98312 | tf_op jit(solution)/shard_map/ppermute | solution.py:475

commit v5 on v4

--- a/solution.py
+++ b/solution.py
@@ -497,8 +497,9 @@
     pieces = list(address(packed, before, after, groups, width))
     for apart in range(1, count):
         give = pieces[apart]
-        if apart >= count * 3 // 4:
-            give, _ = lax.optimization_barrier((give, pieces[apart - count // 4]))
+        if apart > count // 2:
+            ahead = apart - count // 2 + 1
+            give, _ = lax.optimization_barrier((give, pieces[ahead]))
         pieces[apart] = exchange(give, "gz", apart)
     columns = jnp.broadcast_to(
         jnp.stack([extinction_scale, ambient, backdrop])[:, :, None], (3, colors, LANES))

time: 85.8 us -> 83.6 us (0.974)
  waiting for transfers between devices: 24.3 us -> 15.8 us
  starting transfers between devices: 30 us -> 36.4 us
    ppermute x14, waiting for transfers between devices: 14.8 us -> 5.35 us  [exchange(): return lax.ppermute(value, axis, pairs)]
    ppermute x6, starting transfers between devices: 6.86 us -> 12.5 us  [prefixes(): lax.ppermute(total, 'gx', [(i, (i + hop) % size_x) for i in range(size_x)])]
  transfers between devices with their start and end apart: 22 -> 22, of which waited for: 9 -> 10; matrix products, arithmetic and copies ran while one was open for 2% -> 2% of each run, Pallas kernels for 19% -> 20%
where the time goes in v5:
time: 83.6 us; the launch traced here: 83.3 us
  starting transfers between devices  36.4 us (44%)
  Pallas kernels  25.6 us (31%)
  waiting for transfers between devices  15.8 us (19%)
  local copies, waits for them, and re-layouts  4.57 us (5%)
    ppermute x14, starting transfers between devices, exchange(): return lax.ppermute(value, axis, pairs)  20 us
    pallas_call x3, Pallas kernels, render(): pl.pallas_call(functools.partial(render_kernel, groups, width, bins, rati...  13.9 us
    ppermute x6, starting transfers between devices, prefixes(): lax.ppermute(total, 'gx', [(i, (i + hop) % size_x) for i in range(size_x)])  12.5 us
    ppermute x6, waiting for transfers between devices, prefixes(): lax.ppermute(total, 'gx', [(i, (i + hop) % size_x) for i in range(size_x)])  9.8 us
    pallas_call x2, Pallas kernels, depths(): pl.pallas_call(functools.partial(depth_kernel, groups, width, bins, float...  7.44 us
    ppermute x14, waiting for transfers between devices, exchange(): return lax.ppermute(value, axis, pairs)  5.35 us
    ppermute x1, starting transfers between devices, local(): after = lax.ppermute(density[:1], 'gx', down)  3.89 us
    unnamed x14, local copies, waits for them, and re-layouts  3.2 us
  transfers between devices with their start and end apart: 22, of which 10 were waited for; matrix products, arithmetic and copies ran while one was open for 2% of the time, Pallas kernels for 20%

profile of v5, /device:TPU:0, one launch (start us, length us, event | category | flops | bytes accessed | tf_op | source)
XLA Modules:
  0.0 83.3 jit_solution(2759090498290647991)
XLA Ops:
  0.0 0.7 fusion
  0.7 3.9 %collective-permute-start.1 = (f32[1,8,256]{2,1,0:T(8,128)S(1)}, f32[1,8,256]{2,1,0:T(8,128)S(1)}, u32[]{:S(2)}, u32[]{:S(2)}) collective-permute-start(f32[1,8,256]{2,1,0:T(8,128)S(1)} %get-tuple-element.65), channel_id=1, source_target_pairs={{8,0},{16,8},{24,16},{0,24},{9,1},{17,9},{25,17},{1,25},{10,2},{18... | collective-permute-start | bytes 24584 | tf_op jit(solution)/shard_map/ppermute | solution.py:494
  4.6 1.2 %copy-done = f32[128,8,256]{2,1,0:T(8,128)S(1)} copy-done((f32[128,8,256]{2,1,0:T(8,128)S(1)}, f32[128,8,256]{2,1,0:T(8,128)}, u32[]{:S(2)}) %copy-start) | copy-done | bytes 1048600
  5.8 2.7 %pack.1.packed_ref = f32[8,32,8,128]{3,2,1,0:T(8,128)S(1)} custom-call(f32[4,32,8,256]{3,2,1,0:T(8,128)S(1)} %bitcast.10), custom_call_target="tpu_custom_call" | custom-call | tf_op jit(solution)/shard_map/pack/pallas_call | solution.py:71
  8.5 0.6 collective-permute-done.before_ref
  9.4 1.6 %collective-permute-start.3 = (f32[33,8,128]{2,1,0:T(8,128)S(1)}, f32[33,8,128]{2,1,0:T(8,128)S(1)}, u32[]{:S(2)}, u32[]{:S(2)}) collective-permute-start(f32[33,8,128]{2,1,0:T(8,128)S(1)} %get-tuple-element.37), channel_id=1, source_target_pairs={{0,2},{1,3},{2,0},{3,1},{4,6},{5,7},{6,4},{7,5},{8,10},{9,11},{10,... | collective-permute-start | bytes 405512 | tf_op jit(solution)/shard_map/ppermute | solution.py:475
  11.0 2.6 %collective-permute-start.5 = (f32[33,8,128]{2,1,0:T(8,128)S(1)}, f32[33,8,128]{2,1,0:T(8,128)S(1)}, u32[]{:S(2)}, u32[]{:S(2)}) collective-permute-start(f32[33,8,128]{2,1,0:T(8,128)S(1)} %get-tuple-element.39), channel_id=1, source_target_pairs={{0,4},{1,5},{2,6},{3,7},{4,0},{5,1},{6,2},{7,3},{8,12},{9,13},{10,... | collective-permute-start | bytes 405512 | tf_op jit(solution)/shard_map/ppermute | solution.py:475
  13.6 0.6 copy-done.3
  14.3 0.6 copy-done.6
  15.8 0.7 add_bitcast_fusion
  16.7 3.1 %collective-permute-done.4.refs_3_ = f32[33,8,128]{2,1,0:T(8,128)S(1)} collective-permute-done((f32[33,8,128]{2,1,0:T(8,128)S(1)}, f32[33,8,128]{2,1,0:T(8,128)S(1)}, u32[]{:S(2)}, u32[]{:S(2)}) %collective-permute-start.4) | collective-permute-done | bytes 135200 | tf_op jit(solution)/shard_map/ppermute | solution.py:475
  19.8 2.0 %collective-permute-start.7 = (f32[33,8,128]{2,1,0:T(8,128)S(1)}, f32[33,8,128]{2,1,0:T(8,128)S(1)}, u32[]{:S(2)}, u32[]{:S(2)}) collective-permute-start(f32[33,8,128]{2,1,0:T(8,128)S(1)} %get-tuple-element.43), channel_id=1, source_target_pairs={{0,6},{1,7},{2,4},{3,5},{4,2},{5,3},{6,0},{7,1},{8,14},{9,15},{10,... | collective-permute-start | bytes 405512 | tf_op jit(solution)/shard_map/ppermute | solution.py:475
  21.8 4.6 %collective-permute-start.8 = (f32[33,8,128]{2,1,0:T(8,128)S(1)}, f32[33,8,128]{2,1,0:T(8,128)S(1)}, u32[]{:S(2)}, u32[]{:S(2)}) collective-permute-start(f32[33,8,128]{2,1,0:T(8,128)S(1)} %get-tuple-element.45), channel_id=1, source_target_pairs={{0,7},{1,6},{2,5},{3,4},{4,3},{5,2},{6,1},{7,0},{8,15},{9,14},{10,... | collective-permute-start | bytes 405512 | tf_op jit(solution)/shard_map/ppermute | solution.py:475
  26.5 0.6 copy-done.2
  27.6 3.5 %depths_near.1 = (f32[32,32,128]{2,1,0:T(8,128)S(1)}, f32[1,32,16,128]{3,2,1,0:T(8,128)S(1)}, f32[8,16,128]{2,1,0:T(8,128)S(1)}) custom-call(f32[33,8,128]{2,1,0:T(8,128)S(1)} %get-tuple-element.35.refs_0_, f32[33,8,128]{2,1,0:T(8,128)S(1)} %collective-permute-done.2.refs_1_, f32[33,8,128]{2,1,0:T(8,128)S(1)} %collective-permute-done.3.refs_2_, ...), custom_call_target="tpu_custom_call" | custom-call | tf_op jit(solution)/shard_map/depths_near/pallas_call | solution.py:251
  31.1 7.0 %collective-permute-start.11 = (f32[8,16,128]{2,1,0:T(8,128)S(1)}, f32[8,16,128]{2,1,0:T(8,128)S(1)}, u32[]{:S(2)}, u32[]{:S(2)}) collective-permute-start(f32[8,16,128]{2,1,0:T(8,128)S(1)} %get-tuple-element.50), channel_id=1, source_target_pairs={{0,24},{8,0},{16,8},{24,16},{1,25},{9,1},{17,9},{25,17},{2,26},{10... | collective-permute-start | bytes 196616 | tf_op jit(solution)/shard_map/ppermute | solution.py:509
  38.6 1.4 %collective-permute-done.11.refs_2_ = f32[8,16,128]{2,1,0:T(8,128)S(1)} collective-permute-done((f32[8,16,128]{2,1,0:T(8,128)S(1)}, f32[8,16,128]{2,1,0:T(8,128)S(1)}, u32[]{:S(2)}, u32[]{:S(2)}) %collective-permute-start.11) | collective-permute-done | bytes 65568 | tf_op jit(solution)/shard_map/ppermute | solution.py:509
  40.0 2.3 %collective-permute-start.9 = (f32[8,16,128]{2,1,0:T(8,128)S(1)}, f32[8,16,128]{2,1,0:T(8,128)S(1)}, u32[]{:S(2)}, u32[]{:S(2)}) collective-permute-start(f32[8,16,128]{2,1,0:T(8,128)S(1)} %get-tuple-element.50), channel_id=1, source_target_pairs={{0,8},{8,16},{16,24},{24,0},{1,9},{9,17},{17,25},{25,1},{2,10},{10... | collective-permute-start | bytes 196616 | tf_op jit(solution)/shard_map/ppermute | solution.py:509
  42.3 3.1 %collective-permute-done.9.refs_0_ = f32[8,16,128]{2,1,0:T(8,128)S(1)} collective-permute-done((f32[8,16,128]{2,1,0:T(8,128)S(1)}, f32[8,16,128]{2,1,0:T(8,128)S(1)}, u32[]{:S(2)}, u32[]{:S(2)}) %collective-permute-start.9) | collective-permute-done | bytes 65568 | tf_op jit(solution)/shard_map/ppermute | solution.py:509
  45.5 5.9 %render_near.1 = (f32[32,16,128]{2,1,0:T(8,128)S(1)}, f32[32,16,128]{2,1,0:T(8,128)S(1)}, f32[8,128]{1,0:T(8,128)S(1)}) custom-call(f32[32,32,128]{2,1,0:T(8,128)S(1)} %get-tuple-element.47.s_ref, f32[1,32,16,128]{3,2,1,0:T(8,128)S(1)} %get-tuple-element.48.start_ref, bf16[32,96]{1,0:T(8,128)(2,1)S(1)} %get-tuple-element.49.table_ref, ...), custom_call_target="tpu_custom_call" | custom-call | tf_op jit(solution)/shard_map/render_near/pallas_call | solution.py:385
  51.4 3.9 %depths_far.1 = (f32[32,40,128]{2,1,0:T(8,128)S(1)}, f32[2,40,16,128]{3,2,1,0:T(8,128)S(1)}, f32[10,16,128]{2,1,0:T(8,128)S(1)}) custom-call(f32[33,8,128]{2,1,0:T(8,128)S(1)} %get-tuple-element.35.refs_0_, f32[33,8,128]{2,1,0:T(8,128)S(1)} %collective-permute-done.2.refs_1_, f32[33,8,128]{2,1,0:T(8,128)S(1)} %collective-permute-done.3.refs_2_, ...), custom_call_target="tpu_custom_call" | custom-call | tf_op jit(solution)/shard_map/depths_far/pallas_call | solution.py:251
  55.3 2.1 %collective-permute-start.14 = (f32[10,16,128]{2,1,0:T(8,128)S(1)}, f32[10,16,128]{2,1,0:T(8,128)S(1)}, u32[]{:S(2)}, u32[]{:S(2)}) collective-permute-start(f32[10,16,128]{2,1,0:T(8,128)S(1)} %get-tuple-element.54), channel_id=1, source_target_pairs={{0,24},{8,0},{16,8},{24,16},{1,25},{9,1},{17,9},{25,17},{2,26},{10... | collective-permute-start | bytes 245768 | tf_op jit(solution)/shard_map/ppermute | solution.py:509
  58.0 1.8 %collective-permute-done.14.refs_2_ = f32[10,16,128]{2,1,0:T(8,128)S(1)} collective-permute-done((f32[10,16,128]{2,1,0:T(8,128)S(1)}, f32[10,16,128]{2,1,0:T(8,128)S(1)}, u32[]{:S(2)}, u32[]{:S(2)}) %collective-permute-start.14) | collective-permute-done | bytes 81952 | tf_op jit(solution)/shard_map/ppermute | solution.py:509
  59.8 2.0 %collective-permute-done.13.refs_1_ = f32[10,16,128]{2,1,0:T(8,128)S(1)} collective-permute-done((f32[10,16,128]{2,1,0:T(8,128)S(1)}, f32[10,16,128]{2,1,0:T(8,128)S(1)}, u32[]{:S(2)}, u32[]{:S(2)}) %collective-permute-start.13) | collective-permute-done | bytes 81952 | tf_op jit(solution)/shard_map/ppermute | solution.py:509
  61.8 1.4 %collective-permute-done.12.refs_0_ = f32[10,16,128]{2,1,0:T(8,128)S(1)} collective-permute-done((f32[10,16,128]{2,1,0:T(8,128)S(1)}, f32[10,16,128]{2,1,0:T(8,128)S(1)}, u32[]{:S(2)}, u32[]{:S(2)}) %collective-permute-start.12) | collective-permute-done | bytes 81952 | tf_op jit(solution)/shard_map/ppermute | solution.py:509
  63.2 4.0 %render_far.3 = (f32[4,16,128]{2,1,0:T(8,128)S(1)}, f32[4,16,128]{2,1,0:T(8,128)S(1)}, f32[4,16,128]{2,1,0:T(8,128)S(1)}, f32[4,16,128]{2,1,0:T(8,128)S(1)}) custom-call(f32[32,40,128]{2,1,0:T(8,128)S(1)} %get-tuple-element.52.s_ref, f32[2,40,16,128]{3,2,1,0:T(8,128)S(1)} %get-tuple-element.53.start_ref, bf16[32,96]{1,0:T(8,128)(2,1)S(1)} %get-tuple-element.49.table_ref, ...), custom_call_target="tpu_custom_call" | custom-call | tf_op jit(solution)/shard_map/render_far/pallas_call | solution.py:385
  67.5 4.1 %collective-permute-start.21 = (f32[4,16,128]{2,1,0:T(8,128)S(1)}, f32[4,16,128]{2,1,0:T(8,128)S(1)}, u32[]{:S(2)}, u32[]{:S(2)}) collective-permute-start(f32[4,16,128]{2,1,0:T(8,128)S(1)} %get-tuple-element.64), channel_id=1, source_target_pairs={{0,7},{1,6},{2,5},{3,4},{4,3},{5,2},{6,1},{7,0},{8,15},{9,14},{10,... | collective-permute-start | bytes 98312 | tf_op jit(solution)/shard_map/ppermute | solution.py:475
  71.6 4.0 %render_far.2 = (f32[4,16,128]{2,1,0:T(8,128)S(1)}, f32[4,16,128]{2,1,0:T(8,128)S(1)}, f32[4,16,128]{2,1,0:T(8,128)S(1)}, f32[4,16,128]{2,1,0:T(8,128)S(1)}) custom-call(f32[32,40,128]{2,1,0:T(8,128)S(1)} %get-tuple-element.52.s_ref, f32[2,40,16,128]{3,2,1,0:T(8,128)S(1)} %get-tuple-element.53.start_ref, bf16[32,96]{1,0:T(8,128)(2,1)S(1)} %get-tuple-element.49.table_ref, ...), custom_call_target="tpu_custom_call" | custom-call | tf_op jit(solution)/shard_map/render_far/pallas_call | solution.py:385
  76.1 3.9 %collective-permute-start.20 = (f32[4,16,128]{2,1,0:T(8,128)S(1)}, f32[4,16,128]{2,1,0:T(8,128)S(1)}, u32[]{:S(2)}, u32[]{:S(2)}) collective-permute-start(f32[4,16,128]{2,1,0:T(8,128)S(1)} %get-tuple-element.63), channel_id=1, source_target_pairs={{0,6},{1,7},{2,4},{3,5},{4,2},{5,3},{6,0},{7,1},{8,14},{9,15},{10,... | collective-permute-start | bytes 98312 | tf_op jit(solution)/shard_map/ppermute | solution.py:475
  80.0 1.2 %collective-permute-done.18.refs_4_ = f32[4,16,128]{2,1,0:T(8,128)S(1)} collective-permute-done((f32[4,16,128]{2,1,0:T(8,128)S(1)}, f32[4,16,128]{2,1,0:T(8,128)S(1)}, u32[]{:S(2)}, u32[]{:S(2)}) %collective-permute-start.18) | collective-permute-done | bytes 32800 | tf_op jit(solution)/shard_map/ppermute | solution.py:475
  81.2 1.1 %collective-permute-done.20.refs_6_ = f32[4,16,128]{2,1,0:T(8,128)S(1)} collective-permute-done((f32[4,16,128]{2,1,0:T(8,128)S(1)}, f32[4,16,128]{2,1,0:T(8,128)S(1)}, u32[]{:S(2)}, u32[]{:S(2)}) %collective-permute-start.20) | collective-permute-done | bytes 32800 | tf_op jit(solution)/shard_map/ppermute | solution.py:475
  82.3 1.0 %unpack.1 = f32[16,16,256]{2,1,0:T(8,128)} custom-call(f32[4,16,128]{2,1,0:T(8,128)S(1)} %get-tuple-element.57.refs_0_, f32[4,16,128]{2,1,0:T(8,128)S(1)} %collective-permute-done.15.refs_1_, f32[4,16,128]{2,1,0:T(8,128)S(1)} %collective-permute-done.16.refs_2_, f32[4,16,128]{2,1,0:T(8,128)S(1)} %collective-permute-done.17.refs_3_, ...), custom_call_target="tpu_custom_call" | custom-call | tf_op jit(solution)/shard_map/unpack/pallas_call | solution.py:418
  (41 shorter events, 3.9 us)
Async XLA Ops:
  0.7 7.8 %collective-permute-start.1 = (f32[1,8,256]{2,1,0:T(8,128)S(1)}, f32[1,8,256]{2,1,0:T(8,128)S(1)}, u32[]{:S(2)}, u32[]{:S(2)}) collective-permute-start(f32[1,8,256]{2,1,0:T(8,128)S(1)} %get-tuple-element.65), channel_id=1, source_target_pairs={{8,0},{16,8},{24,16},{0,24},{9,1},{17,9},{25,17},{1,25},{10,2},{18... | collective-permute-start | bytes 24584 | tf_op jit(solution)/shard_map/ppermute | solution.py:494
  4.6 4.5 %collective-permute-start = (f32[1,8,256]{2,1,0:T(8,128)S(1)}, f32[1,8,256]{2,1,0:T(8,128)S(1)}, u32[]{:S(2)}, u32[]{:S(2)}) collective-permute-start(f32[1,8,256]{2,1,0:T(8,128)S(1)} %get-tuple-element.66), channel_id=1, source_target_pairs={{0,8},{8,16},{16,24},{24,0},{1,9},{9,17},{17,25},{25,1},{2,10},{10... | collective-permute-start | bytes 24584 | tf_op jit(solution)/shard_map/ppermute | solution.py:493
  4.6 1.2 %copy-start = (f32[128,8,256]{2,1,0:T(8,128)S(1)}, f32[128,8,256]{2,1,0:T(8,128)}, u32[]{:S(2)}) copy-start(f32[128,8,256]{2,1,0:T(8,128)} %param.7) | copy-start | bytes 3145732
  9.4 7.2 %collective-permute-start.3 = (f32[33,8,128]{2,1,0:T(8,128)S(1)}, f32[33,8,128]{2,1,0:T(8,128)S(1)}, u32[]{:S(2)}, u32[]{:S(2)}) collective-permute-start(f32[33,8,128]{2,1,0:T(8,128)S(1)} %get-tuple-element.37), channel_id=1, source_target_pairs={{0,2},{1,3},{2,0},{3,1},{4,6},{5,7},{6,4},{7,5},{8,10},{9,11},{10,... | collective-permute-start | bytes 405512 | tf_op jit(solution)/shard_map/ppermute | solution.py:475
  11.0 8.8 %collective-permute-start.4 = (f32[33,8,128]{2,1,0:T(8,128)S(1)}, f32[33,8,128]{2,1,0:T(8,128)S(1)}, u32[]{:S(2)}, u32[]{:S(2)}) collective-permute-start(f32[33,8,128]{2,1,0:T(8,128)S(1)} %get-tuple-element.38), channel_id=1, source_target_pairs={{0,3},{1,2},{2,1},{3,0},{4,7},{5,6},{6,5},{7,4},{8,11},{9,10},{10,... | collective-permute-start | bytes 405512 | tf_op jit(solution)/shard_map/ppermute | solution.py:475
  11.0 10.8 %collective-permute-start.5 = (f32[33,8,128]{2,1,0:T(8,128)S(1)}, f32[33,8,128]{2,1,0:T(8,128)S(1)}, u32[]{:S(2)}, u32[]{:S(2)}) collective-permute-start(f32[33,8,128]{2,1,0:T(8,128)S(1)} %get-tuple-element.39), channel_id=1, source_target_pairs={{0,4},{1,5},{2,6},{3,7},{4,0},{5,1},{6,2},{7,3},{8,12},{9,13},{10,... | collective-permute-start | bytes 405512 | tf_op jit(solution)/shard_map/ppermute | solution.py:475
  13.6 0.7 copy-start.3
  13.6 0.7 copy-start.4
  13.6 0.7 copy-start.5
  14.3 0.7 copy-start.6
  15.6 12.0 %collective-permute-start.2 = (f32[33,8,128]{2,1,0:T(8,128)S(1)}, f32[33,8,128]{2,1,0:T(8,128)S(1)}, u32[]{:S(2)}, u32[]{:S(2)}) collective-permute-start(f32[33,8,128]{2,1,0:T(8,128)S(1)} %get-tuple-element.36), channel_id=1, source_target_pairs={{0,1},{1,0},{2,3},{3,2},{4,5},{5,4},{6,7},{7,6},{8,9},{9,8},{10,11... | collective-permute-start | bytes 405512 | tf_op jit(solution)/shard_map/ppermute | solution.py:475
  16.6 34.8 %collective-permute-start.6 = (f32[33,8,128]{2,1,0:T(8,128)S(1)}, f32[33,8,128]{2,1,0:T(8,128)S(1)}, u32[]{:S(2)}, u32[]{:S(2)}) collective-permute-start(f32[33,8,128]{2,1,0:T(8,128)S(1)} %get-tuple-element.41), channel_id=1, source_target_pairs={{0,5},{1,4},{2,7},{3,6},{4,1},{5,0},{6,3},{7,2},{8,13},{9,12},{10,... | collective-permute-start | bytes 405512 | tf_op jit(solution)/shard_map/ppermute | solution.py:475
  19.8 31.6 %collective-permute-start.7 = (f32[33,8,128]{2,1,0:T(8,128)S(1)}, f32[33,8,128]{2,1,0:T(8,128)S(1)}, u32[]{:S(2)}, u32[]{:S(2)}) collective-permute-start(f32[33,8,128]{2,1,0:T(8,128)S(1)} %get-tuple-element.43), channel_id=1, source_target_pairs={{0,6},{1,7},{2,4},{3,5},{4,2},{5,3},{6,0},{7,1},{8,14},{9,15},{10,... | collective-permute-start | bytes 405512 | tf_op jit(solution)/shard_map/ppermute | solution.py:475
  21.8 29.6 %collective-permute-start.8 = (f32[33,8,128]{2,1,0:T(8,128)S(1)}, f32[33,8,128]{2,1,0:T(8,128)S(1)}, u32[]{:S(2)}, u32[]{:S(2)}) collective-permute-start(f32[33,8,128]{2,1,0:T(8,128)S(1)} %get-tuple-element.45), channel_id=1, source_target_pairs={{0,7},{1,6},{2,5},{3,4},{4,3},{5,2},{6,1},{7,0},{8,15},{9,14},{10,... | collective-permute-start | bytes 405512 | tf_op jit(solution)/shard_map/ppermute | solution.py:475
  26.4 0.7 copy-start.2
  26.4 0.7 copy-start.1
  31.1 8.9 %collective-permute-start.11 = (f32[8,16,128]{2,1,0:T(8,128)S(1)}, f32[8,16,128]{2,1,0:T(8,128)S(1)}, u32[]{:S(2)}, u32[]{:S(2)}) collective-permute-start(f32[8,16,128]{2,1,0:T(8,128)S(1)} %get-tuple-element.50), channel_id=1, source_target_pairs={{0,24},{8,0},{16,8},{24,16},{1,25},{9,1},{17,9},{25,17},{2,26},{10... | collective-permute-start | bytes 196616 | tf_op jit(solution)/shard_map/ppermute | solution.py:509
  38.1 4.3 %collective-permute-start.10 = (f32[8,16,128]{2,1,0:T(8,128)S(1)}, f32[8,16,128]{2,1,0:T(8,128)S(1)}, u32[]{:S(2)}, u32[]{:S(2)}) collective-permute-start(f32[8,16,128]{2,1,0:T(8,128)S(1)} %get-tuple-element.50), channel_id=1, source_target_pairs={{0,16},{8,24},{16,0},{24,8},{1,17},{9,25},{17,1},{25,9},{2,18},{10... | collective-permute-start | bytes 196616 | tf_op jit(solution)/shard_map/ppermute | solution.py:509
  40.0 5.5 %collective-permute-start.9 = (f32[8,16,128]{2,1,0:T(8,128)S(1)}, f32[8,16,128]{2,1,0:T(8,128)S(1)}, u32[]{:S(2)}, u32[]{:S(2)}) collective-permute-start(f32[8,16,128]{2,1,0:T(8,128)S(1)} %get-tuple-element.50), channel_id=1, source_target_pairs={{0,8},{8,16},{16,24},{24,0},{1,9},{9,17},{17,25},{25,1},{2,10},{10... | collective-permute-start | bytes 196616 | tf_op jit(solution)/shard_map/ppermute | solution.py:509
  55.3 4.5 %collective-permute-start.14 = (f32[10,16,128]{2,1,0:T(8,128)S(1)}, f32[10,16,128]{2,1,0:T(8,128)S(1)}, u32[]{:S(2)}, u32[]{:S(2)}) collective-permute-start(f32[10,16,128]{2,1,0:T(8,128)S(1)} %get-tuple-element.54), channel_id=1, source_target_pairs={{0,24},{8,0},{16,8},{24,16},{1,25},{9,1},{17,9},{25,17},{2,26},{10... | collective-permute-start | bytes 245768 | tf_op jit(solution)/shard_map/ppermute | solution.py:509
  57.4 4.4 %collective-permute-start.13 = (f32[10,16,128]{2,1,0:T(8,128)S(1)}, f32[10,16,128]{2,1,0:T(8,128)S(1)}, u32[]{:S(2)}, u32[]{:S(2)}) collective-permute-start(f32[10,16,128]{2,1,0:T(8,128)S(1)} %get-tuple-element.54), channel_id=1, source_target_pairs={{0,16},{8,24},{16,0},{24,8},{1,17},{9,25},{17,1},{25,9},{2,18},{10... | collective-permute-start | bytes 245768 | tf_op jit(solution)/shard_map/ppermute | solution.py:509
  57.9 5.3 %collective-permute-start.12 = (f32[10,16,128]{2,1,0:T(8,128)S(1)}, f32[10,16,128]{2,1,0:T(8,128)S(1)}, u32[]{:S(2)}, u32[]{:S(2)}) collective-permute-start(f32[10,16,128]{2,1,0:T(8,128)S(1)} %get-tuple-element.54), channel_id=1, source_target_pairs={{0,8},{8,16},{16,24},{24,0},{1,9},{9,17},{17,25},{25,1},{2,10},{10... | collective-permute-start | bytes 245768 | tf_op jit(solution)/shard_map/ppermute | solution.py:509
  67.2 8.4 %collective-permute-start.15 = (f32[4,16,128]{2,1,0:T(8,128)S(1)}, f32[4,16,128]{2,1,0:T(8,128)S(1)}, u32[]{:S(2)}, u32[]{:S(2)}) collective-permute-start(f32[4,16,128]{2,1,0:T(8,128)S(1)} %get-tuple-element.58), channel_id=1, source_target_pairs={{0,1},{1,0},{2,3},{3,2},{4,5},{5,4},{6,7},{7,6},{8,9},{9,8},{10,11... | collective-permute-start | bytes 98312 | tf_op jit(solution)/shard_map/ppermute | solution.py:475
  67.3 8.8 %collective-permute-start.17 = (f32[4,16,128]{2,1,0:T(8,128)S(1)}, f32[4,16,128]{2,1,0:T(8,128)S(1)}, u32[]{:S(2)}, u32[]{:S(2)}) collective-permute-start(f32[4,16,128]{2,1,0:T(8,128)S(1)} %get-tuple-element.60), channel_id=1, source_target_pairs={{0,3},{1,2},{2,1},{3,0},{4,7},{5,6},{6,5},{7,4},{8,11},{9,10},{10,... | collective-permute-start | bytes 98312 | tf_op jit(solution)/shard_map/ppermute | solution.py:475
  67.4 12.6 %collective-permute-start.19 = (f32[4,16,128]{2,1,0:T(8,128)S(1)}, f32[4,16,128]{2,1,0:T(8,128)S(1)}, u32[]{:S(2)}, u32[]{:S(2)}) collective-permute-start(f32[4,16,128]{2,1,0:T(8,128)S(1)} %get-tuple-element.62), channel_id=1, source_target_pairs={{0,5},{1,4},{2,7},{3,6},{4,1},{5,0},{6,3},{7,2},{8,13},{9,12},{10,... | collective-permute-start | bytes 98312 | tf_op jit(solution)/shard_map/ppermute | solution.py:475
  67.5 12.5 %collective-permute-start.21 = (f32[4,16,128]{2,1,0:T(8,128)S(1)}, f32[4,16,128]{2,1,0:T(8,128)S(1)}, u32[]{:S(2)}, u32[]{:S(2)}) collective-permute-start(f32[4,16,128]{2,1,0:T(8,128)S(1)} %get-tuple-element.64), channel_id=1, source_target_pairs={{0,7},{1,6},{2,5},{3,4},{4,3},{5,2},{6,1},{7,0},{8,15},{9,14},{10,... | collective-permute-start | bytes 98312 | tf_op jit(solution)/shard_map/ppermute | solution.py:475
  75.5 4.5 %collective-permute-start.16 = (f32[4,16,128]{2,1,0:T(8,128)S(1)}, f32[4,16,128]{2,1,0:T(8,128)S(1)}, u32[]{:S(2)}, u32[]{:S(2)}) collective-permute-start(f32[4,16,128]{2,1,0:T(8,128)S(1)} %get-tuple-element.59), channel_id=1, source_target_pairs={{0,2},{1,3},{2,0},{3,1},{4,6},{5,7},{6,4},{7,5},{8,10},{9,11},{10,... | collective-permute-start | bytes 98312 | tf_op jit(solution)/shard_map/ppermute | solution.py:475
  75.6 5.6 %collective-permute-start.18 = (f32[4,16,128]{2,1,0:T(8,128)S(1)}, f32[4,16,128]{2,1,0:T(8,128)S(1)}, u32[]{:S(2)}, u32[]{:S(2)}) collective-permute-start(f32[4,16,128]{2,1,0:T(8,128)S(1)} %get-tuple-element.61), channel_id=1, source_target_pairs={{0,4},{1,5},{2,6},{3,7},{4,0},{5,1},{6,2},{7,3},{8,12},{9,13},{10,... | collective-permute-start | bytes 98312 | tf_op jit(solution)/shard_map/ppermute | solution.py:475
  76.1 6.1 %collective-permute-start.20 = (f32[4,16,128]{2,1,0:T(8,128)S(1)}, f32[4,16,128]{2,1,0:T(8,128)S(1)}, u32[]{:S(2)}, u32[]{:S(2)}) collective-permute-start(f32[4,16,128]{2,1,0:T(8,128)S(1)} %get-tuple-element.63), channel_id=1, source_target_pairs={{0,6},{1,7},{2,4},{3,5},{4,2},{5,3},{6,0},{7,1},{8,14},{9,15},{10,... | collective-permute-start | bytes 98312 | tf_op jit(solution)/shard_map/ppermute | solution.py:475

commit v6 on v5

--- a/solution.py
+++ b/solution.py
@@ -498,7 +498,7 @@
     for apart in range(1, count):
         give = pieces[apart]
         if apart > count // 2:
-            ahead = apart - count // 2 + 1
+            ahead = min(apart - count // 2 + 1, count // 2 - 1)
             give, _ = lax.optimization_barrier((give, pieces[ahead]))
         pieces[apart] = exchange(give, "gz", apart)
     columns = jnp.broadcast_to(

time: 83.6 us -> 84.3 us (level)
  waiting for transfers between devices: 15.8 us -> 21.7 us
  starting transfers between devices: 36.4 us -> 31.7 us
    ppermute x6, starting transfers between devices: 12.5 us -> 6.06 us  [prefixes(): lax.ppermute(total, 'gx', [(i, (i + hop) % size_x) for i in range(size_x)])]
    ppermute x14, waiting for transfers between devices: 5.35 us -> 9.07 us  [exchange(): return lax.ppermute(value, axis, pairs)]
    ppermute x6, waiting for transfers between devices: 9.8 us -> 12.7 us  [prefixes(): lax.ppermute(total, 'gx', [(i, (i + hop) % size_x) for i in range(size_x)])]
    ppermute x14, starting transfers between devices: 20 us -> 21.8 us  [exchange(): return lax.ppermute(value, axis, pairs)]
  transfers between devices with their start and end apart: 22 -> 22, of which waited for: 10 -> 8; matrix products, arithmetic and copies ran while one was open for 2% -> 2% of each run, Pallas kernels for 20% -> 15%
where the time goes in v6:
time: 84.3 us; the launch traced here: 83.9 us
  starting transfers between devices  31.7 us (38%)
  Pallas kernels  25.6 us (30%)
  waiting for transfers between devices  21.7 us (26%)
  local copies, waits for them, and re-layouts  3.91 us (5%)
    ppermute x14, starting transfers between devices, exchange(): return lax.ppermute(value, axis, pairs)  21.8 us
    pallas_call x3, Pallas kernels, render(): pl.pallas_call(functools.partial(render_kernel, groups, width, bins, rati...  13.9 us
    ppermute x6, waiting for transfers between devices, prefixes(): lax.ppermute(total, 'gx', [(i, (i + hop) % size_x) for i in range(size_x)])  12.7 us
    ppermute x14, waiting for transfers between devices, exchange(): return lax.ppermute(value, axis, pairs)  9.07 us
    pallas_call x2, Pallas kernels, depths(): pl.pallas_call(functools.partial(depth_kernel, groups, width, bins, float...  7.43 us
    ppermute x6, starting transfers between devices, prefixes(): lax.ppermute(total, 'gx', [(i, (i + hop) % size_x) for i in range(size_x)])  6.06 us
    ppermute x1, starting transfers between devices, local(): after = lax.ppermute(density[:1], 'gx', down)  3.89 us
    pallas_call x1, Pallas kernels, pack(): pl.pallas_call(functools.partial(pack_kernel, groups, width), grid=(steps...  2.69 us
  transfers between devices with their start and end apart: 22, of which 8 were waited for; matrix products, arithmetic and copies ran while one was open for 2% of the time, Pallas kernels for 15%

profile of v6, /device:TPU:0, one launch (start us, length us, event | category | flops | bytes accessed | tf_op | source)
XLA Modules:
  0.0 83.9 jit_solution(15591913455810893751)
XLA Ops:
  0.0 0.7 fusion
  0.7 3.9 %collective-permute-start.1 = (f32[1,8,256]{2,1,0:T(8,128)S(1)}, f32[1,8,256]{2,1,0:T(8,128)S(1)}, u32[]{:S(2)}, u32[]{:S(2)}) collective-permute-start(f32[1,8,256]{2,1,0:T(8,128)S(1)} %get-tuple-element.65), channel_id=1, source_target_pairs={{8,0},{16,8},{24,16},{0,24},{9,1},{17,9},{25,17},{1,25},{10,2},{18... | collective-permute-start | bytes 24584 | tf_op jit(solution)/shard_map/ppermute | solution.py:494
  5.2 0.7 add_bitcast_fusion
  5.9 1.2 %copy-done = f32[128,8,256]{2,1,0:T(8,128)S(1)} copy-done((f32[128,8,256]{2,1,0:T(8,128)S(1)}, f32[128,8,256]{2,1,0:T(8,128)}, u32[]{:S(2)}) %copy-start) | copy-done | bytes 1048600
  7.1 2.7 %pack.1.packed_ref = f32[8,32,8,128]{3,2,1,0:T(8,128)S(1)} custom-call(f32[4,32,8,256]{3,2,1,0:T(8,128)S(1)} %bitcast.10), custom_call_target="tpu_custom_call" | custom-call | tf_op jit(solution)/shard_map/pack/pallas_call | solution.py:71
  10.2 1.6 %collective-permute-start.3 = (f32[33,8,128]{2,1,0:T(8,128)S(1)}, f32[33,8,128]{2,1,0:T(8,128)S(1)}, u32[]{:S(2)}, u32[]{:S(2)}) collective-permute-start(f32[33,8,128]{2,1,0:T(8,128)S(1)} %get-tuple-element.37), channel_id=1, source_target_pairs={{0,2},{1,3},{2,0},{3,1},{4,6},{5,7},{6,4},{7,5},{8,10},{9,11},{10,... | collective-permute-start | bytes 405512 | tf_op jit(solution)/shard_map/ppermute | solution.py:475
  12.1 0.6 copy-done.3
  12.8 0.6 copy-done.1
  13.9 2.7 %collective-permute-done.3.refs_2_ = f32[33,8,128]{2,1,0:T(8,128)S(1)} collective-permute-done((f32[33,8,128]{2,1,0:T(8,128)S(1)}, f32[33,8,128]{2,1,0:T(8,128)S(1)}, u32[]{:S(2)}, u32[]{:S(2)}) %collective-permute-start.3) | collective-permute-done | bytes 135200 | tf_op jit(solution)/shard_map/ppermute | solution.py:475
  16.6 2.0 %collective-permute-done.4.refs_3_ = f32[33,8,128]{2,1,0:T(8,128)S(1)} collective-permute-done((f32[33,8,128]{2,1,0:T(8,128)S(1)}, f32[33,8,128]{2,1,0:T(8,128)S(1)}, u32[]{:S(2)}, u32[]{:S(2)}) %collective-permute-start.4) | collective-permute-done | bytes 135200 | tf_op jit(solution)/shard_map/ppermute | solution.py:475
  18.6 3.5 %depths_near.1 = (f32[32,32,128]{2,1,0:T(8,128)S(1)}, f32[1,32,16,128]{3,2,1,0:T(8,128)S(1)}, f32[8,16,128]{2,1,0:T(8,128)S(1)}) custom-call(f32[33,8,128]{2,1,0:T(8,128)S(1)} %get-tuple-element.35.refs_0_, f32[33,8,128]{2,1,0:T(8,128)S(1)} %collective-permute-done.2.refs_1_, f32[33,8,128]{2,1,0:T(8,128)S(1)} %collective-permute-done.3.refs_2_, ...), custom_call_target="tpu_custom_call" | custom-call | tf_op jit(solution)/shard_map/depths_near/pallas_call | solution.py:251
  22.2 3.0 %collective-permute-start.11 = (f32[8,16,128]{2,1,0:T(8,128)S(1)}, f32[8,16,128]{2,1,0:T(8,128)S(1)}, u32[]{:S(2)}, u32[]{:S(2)}) collective-permute-start(f32[8,16,128]{2,1,0:T(8,128)S(1)} %get-tuple-element.50), channel_id=1, source_target_pairs={{0,24},{8,0},{16,8},{24,16},{1,25},{9,1},{17,9},{25,17},{2,26},{10... | collective-permute-start | bytes 196616 | tf_op jit(solution)/shard_map/ppermute | solution.py:509
  25.1 2.6 %collective-permute-start.5 = (f32[33,8,128]{2,1,0:T(8,128)S(1)}, f32[33,8,128]{2,1,0:T(8,128)S(1)}, u32[]{:S(2)}, u32[]{:S(2)}) collective-permute-start(f32[33,8,128]{2,1,0:T(8,128)S(1)} %get-tuple-element.39), channel_id=1, source_target_pairs={{0,4},{1,5},{2,6},{3,7},{4,0},{5,1},{6,2},{7,3},{8,12},{9,13},{10,... | collective-permute-start | bytes 405512 | tf_op jit(solution)/shard_map/ppermute | solution.py:475
  27.7 3.3 %collective-permute-start.7 = (f32[33,8,128]{2,1,0:T(8,128)S(1)}, f32[33,8,128]{2,1,0:T(8,128)S(1)}, u32[]{:S(2)}, u32[]{:S(2)}) collective-permute-start(f32[33,8,128]{2,1,0:T(8,128)S(1)} %get-tuple-element.43), channel_id=1, source_target_pairs={{0,6},{1,7},{2,4},{3,5},{4,2},{5,3},{6,0},{7,1},{8,14},{9,15},{10,... | collective-permute-start | bytes 405512 | tf_op jit(solution)/shard_map/ppermute | solution.py:475
  31.9 3.8 %collective-permute-done.10.refs_1_ = f32[8,16,128]{2,1,0:T(8,128)S(1)} collective-permute-done((f32[8,16,128]{2,1,0:T(8,128)S(1)}, f32[8,16,128]{2,1,0:T(8,128)S(1)}, u32[]{:S(2)}, u32[]{:S(2)}) %collective-permute-start.10) | collective-permute-done | bytes 65568 | tf_op jit(solution)/shard_map/ppermute | solution.py:509
  35.7 5.2 %collective-permute-done.9.refs_0_ = f32[8,16,128]{2,1,0:T(8,128)S(1)} collective-permute-done((f32[8,16,128]{2,1,0:T(8,128)S(1)}, f32[8,16,128]{2,1,0:T(8,128)S(1)}, u32[]{:S(2)}, u32[]{:S(2)}) %collective-permute-start.9) | collective-permute-done | bytes 65568 | tf_op jit(solution)/shard_map/ppermute | solution.py:509
  40.8 5.9 %render_near.1 = (f32[32,16,128]{2,1,0:T(8,128)S(1)}, f32[32,16,128]{2,1,0:T(8,128)S(1)}, f32[8,128]{1,0:T(8,128)S(1)}) custom-call(f32[32,32,128]{2,1,0:T(8,128)S(1)} %get-tuple-element.47.s_ref, f32[1,32,16,128]{3,2,1,0:T(8,128)S(1)} %get-tuple-element.48.start_ref, bf16[32,96]{1,0:T(8,128)(2,1)S(1)} %get-tuple-element.49.table_ref, ...), custom_call_target="tpu_custom_call" | custom-call | tf_op jit(solution)/shard_map/render_near/pallas_call | solution.py:385
  46.8 3.9 %depths_far.1 = (f32[32,40,128]{2,1,0:T(8,128)S(1)}, f32[2,40,16,128]{3,2,1,0:T(8,128)S(1)}, f32[10,16,128]{2,1,0:T(8,128)S(1)}) custom-call(f32[33,8,128]{2,1,0:T(8,128)S(1)} %get-tuple-element.35.refs_0_, f32[33,8,128]{2,1,0:T(8,128)S(1)} %collective-permute-done.2.refs_1_, f32[33,8,128]{2,1,0:T(8,128)S(1)} %collective-permute-done.3.refs_2_, ...), custom_call_target="tpu_custom_call" | custom-call | tf_op jit(solution)/shard_map/depths_far/pallas_call | solution.py:251
  51.3 1.9 %collective-permute-start.12 = (f32[10,16,128]{2,1,0:T(8,128)S(1)}, f32[10,16,128]{2,1,0:T(8,128)S(1)}, u32[]{:S(2)}, u32[]{:S(2)}) collective-permute-start(f32[10,16,128]{2,1,0:T(8,128)S(1)} %get-tuple-element.54), channel_id=1, source_target_pairs={{0,8},{8,16},{16,24},{24,0},{1,9},{9,17},{17,25},{25,1},{2,10},{10... | collective-permute-start | bytes 245768 | tf_op jit(solution)/shard_map/ppermute | solution.py:509
  53.3 2.5 %collective-permute-done.14.refs_2_ = f32[10,16,128]{2,1,0:T(8,128)S(1)} collective-permute-done((f32[10,16,128]{2,1,0:T(8,128)S(1)}, f32[10,16,128]{2,1,0:T(8,128)S(1)}, u32[]{:S(2)}, u32[]{:S(2)}) %collective-permute-start.14) | collective-permute-done | bytes 81952 | tf_op jit(solution)/shard_map/ppermute | solution.py:509
  55.8 1.2 %collective-permute-done.13.refs_1_ = f32[10,16,128]{2,1,0:T(8,128)S(1)} collective-permute-done((f32[10,16,128]{2,1,0:T(8,128)S(1)}, f32[10,16,128]{2,1,0:T(8,128)S(1)}, u32[]{:S(2)}, u32[]{:S(2)}) %collective-permute-start.13) | collective-permute-done | bytes 81952 | tf_op jit(solution)/shard_map/ppermute | solution.py:509
  57.0 4.0 %render_far.3 = (f32[4,16,128]{2,1,0:T(8,128)S(1)}, f32[4,16,128]{2,1,0:T(8,128)S(1)}, f32[4,16,128]{2,1,0:T(8,128)S(1)}, f32[4,16,128]{2,1,0:T(8,128)S(1)}) custom-call(f32[32,40,128]{2,1,0:T(8,128)S(1)} %get-tuple-element.52.s_ref, f32[2,40,16,128]{3,2,1,0:T(8,128)S(1)} %get-tuple-element.53.start_ref, bf16[32,96]{1,0:T(8,128)(2,1)S(1)} %get-tuple-element.49.table_ref, ...), custom_call_target="tpu_custom_call" | custom-call | tf_op jit(solution)/shard_map/render_far/pallas_call | solution.py:385
  61.1 6.0 %collective-permute-start.17 = (f32[4,16,128]{2,1,0:T(8,128)S(1)}, f32[4,16,128]{2,1,0:T(8,128)S(1)}, u32[]{:S(2)}, u32[]{:S(2)}) collective-permute-start(f32[4,16,128]{2,1,0:T(8,128)S(1)} %get-tuple-element.60), channel_id=1, source_target_pairs={{0,3},{1,2},{2,1},{3,0},{4,7},{5,6},{6,5},{7,4},{8,11},{9,10},{10,... | collective-permute-start | bytes 98312 | tf_op jit(solution)/shard_map/ppermute | solution.py:475
  67.1 1.9 %collective-permute-start.19 = (f32[4,16,128]{2,1,0:T(8,128)S(1)}, f32[4,16,128]{2,1,0:T(8,128)S(1)}, u32[]{:S(2)}, u32[]{:S(2)}) collective-permute-start(f32[4,16,128]{2,1,0:T(8,128)S(1)} %get-tuple-element.62), channel_id=1, source_target_pairs={{0,5},{1,4},{2,7},{3,6},{4,1},{5,0},{6,3},{7,2},{8,13},{9,12},{10,... | collective-permute-start | bytes 98312 | tf_op jit(solution)/shard_map/ppermute | solution.py:475
  69.0 1.1 %collective-permute-start.21 = (f32[4,16,128]{2,1,0:T(8,128)S(1)}, f32[4,16,128]{2,1,0:T(8,128)S(1)}, u32[]{:S(2)}, u32[]{:S(2)}) collective-permute-start(f32[4,16,128]{2,1,0:T(8,128)S(1)} %get-tuple-element.64), channel_id=1, source_target_pairs={{0,7},{1,6},{2,5},{3,4},{4,3},{5,2},{6,1},{7,0},{8,15},{9,14},{10,... | collective-permute-start | bytes 98312 | tf_op jit(solution)/shard_map/ppermute | solution.py:475
  70.1 4.0 %render_far.2 = (f32[4,16,128]{2,1,0:T(8,128)S(1)}, f32[4,16,128]{2,1,0:T(8,128)S(1)}, f32[4,16,128]{2,1,0:T(8,128)S(1)}, f32[4,16,128]{2,1,0:T(8,128)S(1)}) custom-call(f32[32,40,128]{2,1,0:T(8,128)S(1)} %get-tuple-element.52.s_ref, f32[2,40,16,128]{3,2,1,0:T(8,128)S(1)} %get-tuple-element.53.start_ref, bf16[32,96]{1,0:T(8,128)(2,1)S(1)} %get-tuple-element.49.table_ref, ...), custom_call_target="tpu_custom_call" | custom-call | tf_op jit(solution)/shard_map/render_far/pallas_call | solution.py:385
  74.1 0.6 collective-permute-start.16
  74.8 2.5 %collective-permute-start.18 = (f32[4,16,128]{2,1,0:T(8,128)S(1)}, f32[4,16,128]{2,1,0:T(8,128)S(1)}, u32[]{:S(2)}, u32[]{:S(2)}) collective-permute-start(f32[4,16,128]{2,1,0:T(8,128)S(1)} %get-tuple-element.61), channel_id=1, source_target_pairs={{0,4},{1,5},{2,6},{3,7},{4,0},{5,1},{6,2},{7,3},{8,12},{9,13},{10,... | collective-permute-start | bytes 98312 | tf_op jit(solution)/shard_map/ppermute | solution.py:475
  77.2 1.4 %collective-permute-start.20 = (f32[4,16,128]{2,1,0:T(8,128)S(1)}, f32[4,16,128]{2,1,0:T(8,128)S(1)}, u32[]{:S(2)}, u32[]{:S(2)}) collective-permute-start(f32[4,16,128]{2,1,0:T(8,128)S(1)} %get-tuple-element.63), channel_id=1, source_target_pairs={{0,6},{1,7},{2,4},{3,5},{4,2},{5,3},{6,0},{7,1},{8,14},{9,15},{10,... | collective-permute-start | bytes 98312 | tf_op jit(solution)/shard_map/ppermute | solution.py:475
  78.6 1.2 %collective-permute-done.18.refs_4_ = f32[4,16,128]{2,1,0:T(8,128)S(1)} collective-permute-done((f32[4,16,128]{2,1,0:T(8,128)S(1)}, f32[4,16,128]{2,1,0:T(8,128)S(1)}, u32[]{:S(2)}, u32[]{:S(2)}) %collective-permute-start.18) | collective-permute-done | bytes 32800 | tf_op jit(solution)/shard_map/ppermute | solution.py:475
  79.8 3.1 %collective-permute-done.20.refs_6_ = f32[4,16,128]{2,1,0:T(8,128)S(1)} collective-permute-done((f32[4,16,128]{2,1,0:T(8,128)S(1)}, f32[4,16,128]{2,1,0:T(8,128)S(1)}, u32[]{:S(2)}, u32[]{:S(2)}) %collective-permute-start.20) | collective-permute-done | bytes 32800 | tf_op jit(solution)/shard_map/ppermute | solution.py:475
  82.9 1.0 %unpack.1 = f32[16,16,256]{2,1,0:T(8,128)} custom-call(f32[4,16,128]{2,1,0:T(8,128)S(1)} %get-tuple-element.57.refs_0_, f32[4,16,128]{2,1,0:T(8,128)S(1)} %collective-permute-done.15.refs_1_, f32[4,16,128]{2,1,0:T(8,128)S(1)} %collective-permute-done.16.refs_2_, f32[4,16,128]{2,1,0:T(8,128)S(1)} %collective-permute-done.17.refs_3_, ...), custom_call_target="tpu_custom_call" | custom-call | tf_op jit(solution)/shard_map/unpack/pallas_call | solution.py:418
  (41 shorter events, 3.4 us)
Async XLA Ops:
  0.7 3.9 %copy-start.6 = (s32[32]{0:T(128)S(1)}, s32[32]{0:T(128)}, u32[]{:S(2)}) copy-start(s32[32]{0:T(128)} %param.8) | copy-start | bytes 388
  0.7 9.1 %collective-permute-start.1 = (f32[1,8,256]{2,1,0:T(8,128)S(1)}, f32[1,8,256]{2,1,0:T(8,128)S(1)}, u32[]{:S(2)}, u32[]{:S(2)}) collective-permute-start(f32[1,8,256]{2,1,0:T(8,128)S(1)} %get-tuple-element.65), channel_id=1, source_target_pairs={{8,0},{16,8},{24,16},{0,24},{9,1},{17,9},{25,17},{1,25},{10,2},{18... | collective-permute-start | bytes 24584 | tf_op jit(solution)/shard_map/ppermute | solution.py:494
  4.6 5.2 %collective-permute-start = (f32[1,8,256]{2,1,0:T(8,128)S(1)}, f32[1,8,256]{2,1,0:T(8,128)S(1)}, u32[]{:S(2)}, u32[]{:S(2)}) collective-permute-start(f32[1,8,256]{2,1,0:T(8,128)S(1)} %get-tuple-element.66), channel_id=1, source_target_pairs={{0,8},{8,16},{16,24},{24,0},{1,9},{9,17},{17,25},{25,1},{2,10},{10... | collective-permute-start | bytes 24584 | tf_op jit(solution)/shard_map/ppermute | solution.py:493
  5.9 1.2 %copy-start = (f32[128,8,256]{2,1,0:T(8,128)S(1)}, f32[128,8,256]{2,1,0:T(8,128)}, u32[]{:S(2)}) copy-start(f32[128,8,256]{2,1,0:T(8,128)} %param.7) | copy-start | bytes 3145732
  10.1 3.8 %collective-permute-start.2 = (f32[33,8,128]{2,1,0:T(8,128)S(1)}, f32[33,8,128]{2,1,0:T(8,128)S(1)}, u32[]{:S(2)}, u32[]{:S(2)}) collective-permute-start(f32[33,8,128]{2,1,0:T(8,128)S(1)} %get-tuple-element.36), channel_id=1, source_target_pairs={{0,1},{1,0},{2,3},{3,2},{4,5},{5,4},{6,7},{7,6},{8,9},{9,8},{10,11... | collective-permute-start | bytes 405512 | tf_op jit(solution)/shard_map/ppermute | solution.py:475
  10.2 6.5 %collective-permute-start.3 = (f32[33,8,128]{2,1,0:T(8,128)S(1)}, f32[33,8,128]{2,1,0:T(8,128)S(1)}, u32[]{:S(2)}, u32[]{:S(2)}) collective-permute-start(f32[33,8,128]{2,1,0:T(8,128)S(1)} %get-tuple-element.37), channel_id=1, source_target_pairs={{0,2},{1,3},{2,0},{3,1},{4,6},{5,7},{6,4},{7,5},{8,10},{9,11},{10,... | collective-permute-start | bytes 405512 | tf_op jit(solution)/shard_map/ppermute | solution.py:475
  11.8 6.8 %collective-permute-start.4 = (f32[33,8,128]{2,1,0:T(8,128)S(1)}, f32[33,8,128]{2,1,0:T(8,128)S(1)}, u32[]{:S(2)}, u32[]{:S(2)}) collective-permute-start(f32[33,8,128]{2,1,0:T(8,128)S(1)} %get-tuple-element.38), channel_id=1, source_target_pairs={{0,3},{1,2},{2,1},{3,0},{4,7},{5,6},{6,5},{7,4},{8,11},{9,10},{10,... | collective-permute-start | bytes 405512 | tf_op jit(solution)/shard_map/ppermute | solution.py:475
  12.1 0.7 copy-start.3
  12.1 0.7 copy-start.4
  12.1 0.7 copy-start.5
  12.7 0.7 copy-start.1
  12.7 0.7 copy-start.2
  22.2 9.3 %collective-permute-start.11 = (f32[8,16,128]{2,1,0:T(8,128)S(1)}, f32[8,16,128]{2,1,0:T(8,128)S(1)}, u32[]{:S(2)}, u32[]{:S(2)}) collective-permute-start(f32[8,16,128]{2,1,0:T(8,128)S(1)} %get-tuple-element.50), channel_id=1, source_target_pairs={{0,24},{8,0},{16,8},{24,16},{1,25},{9,1},{17,9},{25,17},{2,26},{10... | collective-permute-start | bytes 196616 | tf_op jit(solution)/shard_map/ppermute | solution.py:509
  25.1 21.6 %collective-permute-start.5 = (f32[33,8,128]{2,1,0:T(8,128)S(1)}, f32[33,8,128]{2,1,0:T(8,128)S(1)}, u32[]{:S(2)}, u32[]{:S(2)}) collective-permute-start(f32[33,8,128]{2,1,0:T(8,128)S(1)} %get-tuple-element.39), channel_id=1, source_target_pairs={{0,4},{1,5},{2,6},{3,7},{4,0},{5,1},{6,2},{7,3},{8,12},{9,13},{10,... | collective-permute-start | bytes 405512 | tf_op jit(solution)/shard_map/ppermute | solution.py:475
  27.7 19.0 %collective-permute-start.6 = (f32[33,8,128]{2,1,0:T(8,128)S(1)}, f32[33,8,128]{2,1,0:T(8,128)S(1)}, u32[]{:S(2)}, u32[]{:S(2)}) collective-permute-start(f32[33,8,128]{2,1,0:T(8,128)S(1)} %get-tuple-element.41), channel_id=1, source_target_pairs={{0,5},{1,4},{2,7},{3,6},{4,1},{5,0},{6,3},{7,2},{8,13},{9,12},{10,... | collective-permute-start | bytes 405512 | tf_op jit(solution)/shard_map/ppermute | solution.py:475
  27.7 19.0 %collective-permute-start.7 = (f32[33,8,128]{2,1,0:T(8,128)S(1)}, f32[33,8,128]{2,1,0:T(8,128)S(1)}, u32[]{:S(2)}, u32[]{:S(2)}) collective-permute-start(f32[33,8,128]{2,1,0:T(8,128)S(1)} %get-tuple-element.43), channel_id=1, source_target_pairs={{0,6},{1,7},{2,4},{3,5},{4,2},{5,3},{6,0},{7,1},{8,14},{9,15},{10,... | collective-permute-start | bytes 405512 | tf_op jit(solution)/shard_map/ppermute | solution.py:475
  31.0 15.8 %collective-permute-start.8 = (f32[33,8,128]{2,1,0:T(8,128)S(1)}, f32[33,8,128]{2,1,0:T(8,128)S(1)}, u32[]{:S(2)}, u32[]{:S(2)}) collective-permute-start(f32[33,8,128]{2,1,0:T(8,128)S(1)} %get-tuple-element.45), channel_id=1, source_target_pairs={{0,7},{1,6},{2,5},{3,4},{4,3},{5,2},{6,1},{7,0},{8,15},{9,14},{10,... | collective-permute-start | bytes 405512 | tf_op jit(solution)/shard_map/ppermute | solution.py:475
  31.4 4.3 %collective-permute-start.10 = (f32[8,16,128]{2,1,0:T(8,128)S(1)}, f32[8,16,128]{2,1,0:T(8,128)S(1)}, u32[]{:S(2)}, u32[]{:S(2)}) collective-permute-start(f32[8,16,128]{2,1,0:T(8,128)S(1)} %get-tuple-element.50), channel_id=1, source_target_pairs={{0,16},{8,24},{16,0},{24,8},{1,17},{9,25},{17,1},{25,9},{2,18},{10... | collective-permute-start | bytes 196616 | tf_op jit(solution)/shard_map/ppermute | solution.py:509
  35.7 5.2 %collective-permute-start.9 = (f32[8,16,128]{2,1,0:T(8,128)S(1)}, f32[8,16,128]{2,1,0:T(8,128)S(1)}, u32[]{:S(2)}, u32[]{:S(2)}) collective-permute-start(f32[8,16,128]{2,1,0:T(8,128)S(1)} %get-tuple-element.50), channel_id=1, source_target_pairs={{0,8},{8,16},{16,24},{24,0},{1,9},{9,17},{17,25},{25,1},{2,10},{10... | collective-permute-start | bytes 196616 | tf_op jit(solution)/shard_map/ppermute | solution.py:509
  50.7 5.1 %collective-permute-start.14 = (f32[10,16,128]{2,1,0:T(8,128)S(1)}, f32[10,16,128]{2,1,0:T(8,128)S(1)}, u32[]{:S(2)}, u32[]{:S(2)}) collective-permute-start(f32[10,16,128]{2,1,0:T(8,128)S(1)} %get-tuple-element.54), channel_id=1, source_target_pairs={{0,24},{8,0},{16,8},{24,16},{1,25},{9,1},{17,9},{25,17},{2,26},{10... | collective-permute-start | bytes 245768 | tf_op jit(solution)/shard_map/ppermute | solution.py:509
  50.8 6.3 %collective-permute-start.13 = (f32[10,16,128]{2,1,0:T(8,128)S(1)}, f32[10,16,128]{2,1,0:T(8,128)S(1)}, u32[]{:S(2)}, u32[]{:S(2)}) collective-permute-start(f32[10,16,128]{2,1,0:T(8,128)S(1)} %get-tuple-element.54), channel_id=1, source_target_pairs={{0,16},{8,24},{16,0},{24,8},{1,17},{9,25},{17,1},{25,9},{2,18},{10... | collective-permute-start | bytes 245768 | tf_op jit(solution)/shard_map/ppermute | solution.py:509
  51.3 5.7 %collective-permute-start.12 = (f32[10,16,128]{2,1,0:T(8,128)S(1)}, f32[10,16,128]{2,1,0:T(8,128)S(1)}, u32[]{:S(2)}, u32[]{:S(2)}) collective-permute-start(f32[10,16,128]{2,1,0:T(8,128)S(1)} %get-tuple-element.54), channel_id=1, source_target_pairs={{0,8},{8,16},{16,24},{24,0},{1,9},{9,17},{17,25},{25,1},{2,10},{10... | collective-permute-start | bytes 245768 | tf_op jit(solution)/shard_map/ppermute | solution.py:509
  61.0 13.7 %collective-permute-start.15 = (f32[4,16,128]{2,1,0:T(8,128)S(1)}, f32[4,16,128]{2,1,0:T(8,128)S(1)}, u32[]{:S(2)}, u32[]{:S(2)}) collective-permute-start(f32[4,16,128]{2,1,0:T(8,128)S(1)} %get-tuple-element.58), channel_id=1, source_target_pairs={{0,1},{1,0},{2,3},{3,2},{4,5},{5,4},{6,7},{7,6},{8,9},{9,8},{10,11... | collective-permute-start | bytes 98312 | tf_op jit(solution)/shard_map/ppermute | solution.py:475
  61.1 16.1 %collective-permute-start.17 = (f32[4,16,128]{2,1,0:T(8,128)S(1)}, f32[4,16,128]{2,1,0:T(8,128)S(1)}, u32[]{:S(2)}, u32[]{:S(2)}) collective-permute-start(f32[4,16,128]{2,1,0:T(8,128)S(1)} %get-tuple-element.60), channel_id=1, source_target_pairs={{0,3},{1,2},{2,1},{3,0},{4,7},{5,6},{6,5},{7,4},{8,11},{9,10},{10,... | collective-permute-start | bytes 98312 | tf_op jit(solution)/shard_map/ppermute | solution.py:475
  67.1 11.5 %collective-permute-start.19 = (f32[4,16,128]{2,1,0:T(8,128)S(1)}, f32[4,16,128]{2,1,0:T(8,128)S(1)}, u32[]{:S(2)}, u32[]{:S(2)}) collective-permute-start(f32[4,16,128]{2,1,0:T(8,128)S(1)} %get-tuple-element.62), channel_id=1, source_target_pairs={{0,5},{1,4},{2,7},{3,6},{4,1},{5,0},{6,3},{7,2},{8,13},{9,12},{10,... | collective-permute-start | bytes 98312 | tf_op jit(solution)/shard_map/ppermute | solution.py:475
  69.0 9.6 %collective-permute-start.21 = (f32[4,16,128]{2,1,0:T(8,128)S(1)}, f32[4,16,128]{2,1,0:T(8,128)S(1)}, u32[]{:S(2)}, u32[]{:S(2)}) collective-permute-start(f32[4,16,128]{2,1,0:T(8,128)S(1)} %get-tuple-element.64), channel_id=1, source_target_pairs={{0,7},{1,6},{2,5},{3,4},{4,3},{5,2},{6,1},{7,0},{8,15},{9,14},{10,... | collective-permute-start | bytes 98312 | tf_op jit(solution)/shard_map/ppermute | solution.py:475
  74.1 4.5 %collective-permute-start.16 = (f32[4,16,128]{2,1,0:T(8,128)S(1)}, f32[4,16,128]{2,1,0:T(8,128)S(1)}, u32[]{:S(2)}, u32[]{:S(2)}) collective-permute-start(f32[4,16,128]{2,1,0:T(8,128)S(1)} %get-tuple-element.59), channel_id=1, source_target_pairs={{0,2},{1,3},{2,0},{3,1},{4,6},{5,7},{6,4},{7,5},{8,10},{9,11},{10,... | collective-permute-start | bytes 98312 | tf_op jit(solution)/shard_map/ppermute | solution.py:475
  74.8 5.1 %collective-permute-start.18 = (f32[4,16,128]{2,1,0:T(8,128)S(1)}, f32[4,16,128]{2,1,0:T(8,128)S(1)}, u32[]{:S(2)}, u32[]{:S(2)}) collective-permute-start(f32[4,16,128]{2,1,0:T(8,128)S(1)} %get-tuple-element.61), channel_id=1, source_target_pairs={{0,4},{1,5},{2,6},{3,7},{4,0},{5,1},{6,2},{7,3},{8,12},{9,13},{10,... | collective-permute-start | bytes 98312 | tf_op jit(solution)/shard_map/ppermute | solution.py:475
  77.2 5.7 %collective-permute-start.20 = (f32[4,16,128]{2,1,0:T(8,128)S(1)}, f32[4,16,128]{2,1,0:T(8,128)S(1)}, u32[]{:S(2)}, u32[]{:S(2)}) collective-permute-start(f32[4,16,128]{2,1,0:T(8,128)S(1)} %get-tuple-element.63), channel_id=1, source_target_pairs={{0,6},{1,7},{2,4},{3,5},{4,2},{5,3},{6,0},{7,1},{8,14},{9,15},{10,... | collective-permute-start | bytes 98312 | tf_op jit(solution)/shard_map/ppermute | solution.py:475

commit v7 on v6

--- a/solution.py
+++ b/solution.py
@@ -121,15 +121,11 @@
     return jnp.dot(table, weights, preferred_element_type=jnp.float32)
 
 
-def depth_kernel(groups, width, bins, scale, far, halves_count, count, *refs):
-    pieces = refs[:-8] if far else refs[:-7]
-    table_ref, s_ref, start_ref, total_ref, raw, sums, products_ref = refs[-7:]
+def smooth_layers(groups, width, scale, far, count, pieces, s_ref, raw):
     steps, depth = pieces[0].shape[-3] - 1, pieces[0].shape[-2]
     blocks = count // 2
     layers = depth * blocks
     slots = s_ref.shape[1]
-    used = layers + 1 if far else layers
-    colors = table_ref.shape[0]
     me = lax.axis_index("gz")
     lower = me < blocks
     lane = group_ids((depth, LANES), width)
@@ -179,49 +175,18 @@
         return carry
 
     lax.fori_loop(0, steps, smooth, 0, unroll=2)
-    edge = lax.broadcasted_iota(jnp.int32, (bins, LANES), 0).astype(jnp.float32) - 1.0
-    rows = steps // halves_count
-
-    def count_layer(z, carry):
-        for half in range(halves_count):
-            acc = jnp.zeros((bins, LANES), jnp.float32)
-            for step in range(rows):
-                row = jnp.broadcast_to(s_ref[half * rows + step, pl.ds(z, 1), :], (bins, LANES))
-                acc = acc + jnp.minimum(jnp.maximum(row, edge), edge + 1.0)
-            sums[half, z] = acc - edge * rows
-        return carry
-
-    lax.fori_loop(0, layers, count_layer, 0, unroll=2)
-    for z in range(layers, slots):
-        if z < used:
-            count_layer(z, 0)
-        else:
-            for half in range(halves_count):
-                sums[half, z] = jnp.zeros((bins, LANES), jnp.float32)
-    table = table_ref[...]
-    at_once = 8
-
-    def products(chunk, carry):
-        wide = [sums[half, chunk * at_once + k]
-                for half in range(halves_count) for k in range(at_once)]
-        out = split_sum(table, jnp.concatenate(wide, axis=1))
-        for half in range(halves_count):
-            for k in range(at_once):
-                place = (half * at_once + k) * LANES
-                products_ref[half, chunk * at_once + k] = out[:, place:place + LANES]
-        return carry
-
-    lax.fori_loop(0, slots // at_once, products, 0, unroll=2)
+
+
+def scan_quarters(groups, width, first_ref, second_ref, start_ref, total_ref, offset):
+    slots, colors = first_ref.shape[0], first_ref.shape[1]
     group = group_ids((colors, LANES), width)
 
     def scan_groups(chunk, carry):
         packed = jnp.zeros((colors, LANES), jnp.float32)
         for k in range(groups):
             z = chunk * groups + k
-            first = products_ref[0, z]
-            both = first
-            for half in range(1, halves_count):
-                both = both + products_ref[half, z]
+            first = first_ref[z]
+            both = first if second_ref is None else first + second_ref[z]
             inclusive = both
             everything = both
             shift = 1
@@ -232,133 +197,247 @@
                 shift *= 2
             begin = inclusive - both
             start_ref[0, z] = begin
-            if halves_count > 1:
+            if second_ref is not None:
                 start_ref[1, z] = begin + first
             packed = jnp.where(group == k, everything, packed)
-        total_ref[chunk] = packed
+        total_ref[offset + chunk] = packed
         return carry
 
     lax.fori_loop(0, slots // groups, scan_groups, 0, unroll=4)
 
 
-def depths(pieces, table, groups, width, bins, far, count, after=()):
+def bin_edges(bins):
+    return lax.broadcasted_iota(jnp.int32, (bins, LANES), 0).astype(jnp.float32) - 1.0
+
+
+def properties(s, size, table, bins):
+    edge = bin_edges(bins).astype(jnp.bfloat16)
+    zero = jnp.zeros((bins, LANES), jnp.bfloat16)
+    one = jnp.ones((bins, LANES), jnp.bfloat16)
+    lower_bin = jnp.floor(s)
+    frac = s - lower_bin
+    coarse = frac.astype(jnp.bfloat16).astype(jnp.float32)
+    fine = frac - coarse
+
+    def wide(value, r):
+        return jnp.broadcast_to(value[r:r + 1], (bins, LANES)).astype(jnp.bfloat16)
+
+    columns = []
+    for r in range(size):
+        away = wide(lower_bin, r) - edge
+        main = jnp.minimum(jnp.maximum(away + wide(coarse, r), zero), one)
+        rest = jnp.where(away == zero, wide(fine, r), zero)
+        columns.append(jnp.concatenate([main, main, rest], axis=0))
+    return jnp.dot(table, jnp.concatenate(columns, axis=1), preferred_element_type=jnp.float32)
+
+
+def near_kernel(groups, width, bins, ratio, count, *refs):
+    pieces = refs[:count // 2]
+    (table_ref, lit_ref, unlit_ref, through_ref, start_ref, total_ref, raw, s_ref,
+     depth) = refs[count // 2:]
+    steps, layers, colors, _ = lit_ref.shape
+    smooth_layers(groups, width, float(bins - 1), False, count, pieces, s_ref, raw)
+    depth[...] = jnp.zeros(depth.shape, jnp.float32)
+    table = table_ref[...]
+    block = 8
+
+    def advance(step, carry):
+        through = jnp.ones((colors, LANES), jnp.float32)
+        unlit = jnp.zeros((colors, LANES), jnp.float32)
+        for chunk in range(layers // block):
+            place = chunk * block
+            props = properties(s_ref[step, place:place + block, :], block, table, bins)
+            for r in range(block):
+                part = props[:, r * LANES:(r + 1) * LANES]
+                sigma, color = part[:colors], part[colors:]
+                later = through * jnp.exp2(sigma)
+                seen = (through - later) * color
+                above = depth[place + r]
+                unlit = unlit + seen
+                lit_ref[step, place + r] = seen * jnp.exp2(above)
+                depth[place + r] = above + sigma * ratio
+                through = later
+        unlit_ref[step], through_ref[step] = unlit, through
+        return carry
+
+    lax.fori_loop(0, steps, advance, 0, unroll=4)
+    scan_quarters(groups, width, depth, None, start_ref, total_ref, 0)
+
+
+def render_near(pieces, table, colors, groups, width, bins, ratio, count):
+    steps, depth = pieces[0].shape[0] - 1, pieces[0].shape[1]
+    layers = depth * len(pieces)
+    plane = jax.ShapeDtypeStruct((steps, colors, LANES), jnp.float32)
+    return pl.pallas_call(
+        functools.partial(near_kernel, groups, width, bins, ratio, count),
+        out_shape=(
+            jax.ShapeDtypeStruct((steps, layers, colors, LANES), jnp.float32),
+            plane,
+            plane,
+            jax.ShapeDtypeStruct((1, layers, colors, LANES), jnp.float32),
+            jax.ShapeDtypeStruct((layers // groups, colors, LANES), jnp.float32),
+        ),
+        in_specs=[pl.BlockSpec(memory_space=pltpu.VMEM)] * (len(pieces) + 1),
+        out_specs=[pl.BlockSpec(memory_space=pltpu.VMEM)] * 5,
+        scratch_shapes=[
+            pltpu.VMEM((steps + 2, layers + 2 * depth, LANES), jnp.float32),
+            pltpu.VMEM((steps, layers, LANES), jnp.float32),
+            pltpu.VMEM((layers, colors, LANES), jnp.float32),
+        ],
+        compiler_params=pltpu.CompilerParams(vmem_limit_bytes=20 * MIB),
+        cost_estimate=pl.CostEstimate(flops=0, bytes_accessed=0, transcendentals=0),
+        name="render_near",
+    )(*pieces, table)
+
+
+def depth_kernel(groups, width, bins, count, *refs):
+    pieces = refs[:count]
+    near_ref, table_ref, s_ref, start_ref, total_ref, raw, sums, products_ref = refs[count:]
+    steps, depth = pieces[0].shape[-3] - 1, pieces[0].shape[-2]
+    layers = depth * (count // 2)
+    slots = s_ref.shape[1]
+    used = layers + 1
+    smooth_layers(groups, width, float(bins - 1), True, count, pieces, s_ref, raw)
+    edge = bin_edges(bins)
+    rows = steps // 2
+
+    def count_layer(z, carry):
+        for half in range(2):
+            acc = jnp.zeros((bins, LANES), jnp.float32)
+            for step in range(rows):
+                row = jnp.broadcast_to(s_ref[half * rows + step, pl.ds(z, 1), :], (bins, LANES))
+                acc = acc + jnp.minimum(jnp.maximum(row, edge), edge + 1.0)
+            sums[half, z] = acc - edge * rows
+        return carry
+
+    lax.fori_loop(0, layers, count_layer, 0, unroll=2)
+    count_layer(layers, 0)
+    for z in range(used, slots):
+        for half in range(2):
+            sums[half, z] = jnp.zeros((bins, LANES), jnp.float32)
+    table = table_ref[...]
+    at_once = 8
+
+    def products(chunk, carry):
+        wide = [sums[half, chunk * at_once + k] for half in range(2) for k in range(at_once)]
+        out = split_sum(table, jnp.concatenate(wide, axis=1))
+        for half in range(2):
+            for k in range(at_once):
+                place = (half * at_once + k) * LANES
+                products_ref[half, chunk * at_once + k] = out[:, place:place + LANES]
+        return carry
+
+    lax.fori_loop(0, slots // at_once, products, 0, unroll=True)
+    ahead = near_ref.shape[0]
+    total_ref[0:ahead] = near_ref[...]
+    scan_quarters(groups, width, products_ref.at[0], products_ref.at[1], start_ref, total_ref,
+                  ahead)
+
+
+def far_depths(pieces, near_total, table, groups, width, bins):
+    count = len(pieces)
     steps, depth = pieces[0].shape[0] - 1, pieces[0].shape[1]
     layers = depth * (count // 2)
-    slots = layers + max(groups, depth) if far else layers
-    halves = 2 if far else 1
+    slots = layers + max(groups, depth)
     colors = table.shape[0]
-    limit = 8 * MIB + slots * (LANES * 4 * halves) * (bins + 2 * colors)
+    limit = 8 * MIB + slots * (LANES * 4 * 2) * (bins + 2 * colors)
     return pl.pallas_call(
-        functools.partial(depth_kernel, groups, width, bins, float(bins - 1), far, halves, count),
+        functools.partial(depth_kernel, groups, width, bins, count),
         out_shape=(
             jax.ShapeDtypeStruct((steps, slots, LANES), jnp.float32),
-            jax.ShapeDtypeStruct((halves, slots, colors, LANES), jnp.float32),
-            jax.ShapeDtypeStruct((slots // groups, colors, LANES), jnp.float32),
+            jax.ShapeDtypeStruct((2, slots, colors, LANES), jnp.float32),
+            jax.ShapeDtypeStruct((near_total.shape[0] + slots // groups, colors, LANES),
+                                 jnp.float32),
         ),
-        in_specs=[pl.BlockSpec(memory_space=pltpu.VMEM)] * (len(pieces) + len(after) + 1),
+        in_specs=[pl.BlockSpec(memory_space=pltpu.VMEM)] * (count + 2),
         out_specs=[pl.BlockSpec(memory_space=pltpu.VMEM)] * 3,
         scratch_shapes=[
             pltpu.VMEM((steps + 2, layers + 2 * depth, LANES), jnp.float32),
-            pltpu.VMEM((halves, slots, bins, LANES), jnp.float32),
-            pltpu.VMEM((halves, slots, colors, LANES), jnp.float32),
+            pltpu.VMEM((2, slots, bins, LANES), jnp.float32),
+            pltpu.VMEM((2, slots, colors, LANES), jnp.float32),
         ],
         compiler_params=pltpu.CompilerParams(vmem_limit_bytes=limit),
         cost_estimate=pl.CostEstimate(flops=0, bytes_accessed=0, transcendentals=0),
-        name="depths_far" if far else "depths_near",
-    )(*pieces, *after, table)
-
-
-def render_kernel(groups, width, bins, ratio, turn, near, blocks, sums_count, s_ref, start_ref,
-                  table_ref, columns_ref, *refs):
-    before_refs = refs[:sums_count]
-    near_refs, refs = refs[sums_count:sums_count + near], refs[sums_count + near:]
-    out_refs, image, depth = refs[:-2], refs[-2], refs[-1]
+        name="far_depths",
+    )(*pieces, near_total, table)
+
+
+def render_kernel(groups, width, bins, ratio, turn, blocks, hops, s_ref, start_ref, table_ref,
+                  columns_ref, lit_ref, unlit_ref, near_through_ref, near_start_ref, *refs):
+    before_refs, out_ref, image, depth, light = refs[:hops], *refs[hops:]
     rows, slots = image.shape[0], s_ref.shape[1]
     colors = columns_ref.shape[1]
     block = 8
+    layers = blocks * block
     me = lax.axis_index("gz")
     lower = me < blocks
-    half = 0 if turn is None else (me + turn) % 2
+    half = (me + turn) % 2
     position = lax.axis_index("gx")
     group = group_ids((colors, LANES), width)
-
-    def begin(chunk, carry):
+    ahead = layers // groups
+
+    def before(chunk):
         packed = jnp.zeros((colors, LANES), jnp.float32)
         for hop, ref in enumerate(before_refs, 1):
             packed = packed + jnp.where(position >= hop, ref[chunk], 0.0)
+        values = []
         for k in range(groups):
-            z = chunk * groups + k
             value = jnp.where(group == k, packed, 0.0)
             shift = 1
             while shift < groups:
                 value = value + pltpu.roll(value, shift * width, 1)
                 shift *= 2
+            values.append(value)
+        return values
+
+    def begin_near(chunk, carry):
+        for k, value in enumerate(before(chunk)):
+            z = chunk * groups + k
+            light[z] = jnp.exp2(near_start_ref[0, z] + value)
+        return carry
+
+    def begin_far(chunk, carry):
+        for k, value in enumerate(before(ahead + chunk)):
+            z = chunk * groups + k
             depth[z] = start_ref[half, z] + value
         return carry
 
-    lax.fori_loop(0, slots // groups, begin, 0, unroll=4)
+    lax.fori_loop(0, ahead, begin_near, 0, unroll=4)
+    lax.fori_loop(0, slots // groups, begin_far, 0, unroll=4)
     ambient = columns_ref[1]
     table = table_ref[...]
-    edge = (lax.broadcasted_iota(jnp.int32, (bins, LANES), 0).astype(jnp.float32) - 1.0).astype(
-        jnp.bfloat16)
-    zero = jnp.zeros((bins, LANES), jnp.bfloat16)
-    one = jnp.ones((bins, LANES), jnp.bfloat16)
-    layers = blocks * block
 
     def advance(step, carry):
         row = half * rows + step
-
-        def layer_block(place, size, state):
-            through, partial = state
-            s = s_ref[row, pl.ds(place, block), :]
-            lower_bin = jnp.floor(s)
-            frac = s - lower_bin
-            coarse = frac.astype(jnp.bfloat16).astype(jnp.float32)
-            fine = frac - coarse
-
-            def wide(value, r):
-                return jnp.broadcast_to(value[r:r + 1], (bins, LANES)).astype(jnp.bfloat16)
-
-            columns = []
-            for r in range(size):
-                away = wide(lower_bin, r) - edge
-                main = jnp.minimum(jnp.maximum(away + wide(coarse, r), zero), one)
-                rest = jnp.where(away == zero, wide(fine, r), zero)
-                columns.append(jnp.concatenate([main, main, rest], axis=0))
-            weights = jnp.concatenate(columns, axis=1)
-            props = jnp.dot(table, weights, preferred_element_type=jnp.float32)
+        through = jnp.ones((colors, LANES), jnp.float32)
+        partial = jnp.zeros((colors, LANES), jnp.float32)
+        for chunk in range(blocks + 1):
+            place = chunk * block
+            size = block if chunk < blocks else 1
+            props = properties(s_ref[row, place:place + block, :], size, table, bins)
             for r in range(size):
                 part = props[:, r * LANES:(r + 1) * LANES]
                 sigma, color = part[:colors], part[colors:]
                 later = through * jnp.exp2(sigma)
-                z = place + r
-                above = depth[z]
+                above = depth[place + r]
                 shade = color * (ambient + jnp.exp2(above))
                 partial = partial + (through - later) * shade
-                depth[z] = above + sigma * ratio
+                depth[place + r] = above + sigma * ratio
                 through = later
-            return through, partial
-
-        state = (jnp.ones((colors, LANES), jnp.float32), jnp.zeros((colors, LANES), jnp.float32))
-        for chunk in range(blocks):
-            state = layer_block(chunk * block, block, state)
-        if turn is None:
-            out_refs[0][step], out_refs[1][step] = state[1], state[0]
-            return carry
-        through, partial = layer_block(layers, 1, state)
-        near_partial, near_through = near_refs[0][row], near_refs[1][row]
+        sums = [unlit_ref[row] * ambient] + [jnp.zeros((colors, LANES), jnp.float32)] * 3
+        for z in range(layers):
+            sums[z % 4] = sums[z % 4] + lit_ref[row, z] * light[z]
+        near_partial = (sums[0] + sums[1]) + (sums[2] + sums[3])
+        near_through = near_through_ref[row]
         front = jnp.where(lower, near_partial, partial)
         back = jnp.where(lower, partial, near_partial)
         passed = jnp.where(lower, near_through, through)
         image[step] = front + passed * back + through * near_through * columns_ref[2]
         return carry
 
-    lax.fori_loop(0, rows, advance, 0, unroll=4 if turn is None else 2)
-    if turn is None:
-        out_refs[2][...] = jnp.zeros((8, LANES), jnp.float32)
-        return
-    if len(out_refs) == 1:
-        out_refs[0][...] = image[...]
+    lax.fori_loop(0, rows, advance, 0, unroll=2)
+    if len(out_ref.shape) == 3:
+        out_ref[...] = image[...]
         return
     for chunk in range(rows // groups):
         tiles = swap_groups([image[chunk * groups + k] for k in range(groups)], groups, width)
@@ -367,45 +446,42 @@
     for slot in range(groups):
         part = slot ^ (me // 2)
         for chunk in range(rows // groups):
-            out_refs[slot][chunk] = image[chunk * groups + part]
-
-
-def render(s, start, table, columns, before, near, groups, width, bins, ratio, turn, blocks):
+            out_ref[slot, chunk] = image[chunk * groups + part]
+
+
+def render(s, start, table, columns, near, before, groups, width, bins, ratio, turn, blocks):
     steps, slots, _ = s.shape
+    layers = near[0].shape[1]
     colors = columns.shape[1]
     share = steps // 2
-    if turn is None:
-        share = steps
-        shapes = [jax.ShapeDtypeStruct((steps, colors, LANES), jnp.float32)] * 2
-        shapes.append(jax.ShapeDtypeStruct((8, LANES), jnp.float32))
-    elif share % groups == 0:
-        shapes = [jax.ShapeDtypeStruct((share // groups, colors, LANES), jnp.float32)] * groups
-    else:
-        shapes = [jax.ShapeDtypeStruct((share, colors, LANES), jnp.float32)]
+    shape = (share, colors, LANES)
+    if share % groups == 0:
+        shape = (groups, share // groups, colors, LANES)
+    operands = [s, start, table, columns, *near, *before]
     return pl.pallas_call(
-        functools.partial(render_kernel, groups, width, bins, ratio, turn, len(near), blocks,
-                          len(before)),
-        out_shape=shapes,
-        in_specs=[pl.BlockSpec(memory_space=pltpu.VMEM)] * (4 + len(before) + len(near)),
-        out_specs=[pl.BlockSpec(memory_space=pltpu.VMEM)] * len(shapes),
+        functools.partial(render_kernel, groups, width, bins, ratio, turn, blocks, len(before)),
+        out_shape=jax.ShapeDtypeStruct(shape, jnp.float32),
+        in_specs=[pl.BlockSpec(memory_space=pltpu.VMEM)] * len(operands),
+        out_specs=pl.BlockSpec(memory_space=pltpu.VMEM),
         scratch_shapes=[
             pltpu.VMEM((share, colors, LANES), jnp.float32),
             pltpu.VMEM((slots, colors, LANES), jnp.float32),
+            pltpu.VMEM((layers, colors, LANES), jnp.float32),
         ],
-        compiler_params=pltpu.CompilerParams(vmem_limit_bytes=8 * MIB + slots * colors * 512 * 4),
+        compiler_params=pltpu.CompilerParams(vmem_limit_bytes=20 * MIB),
         cost_estimate=pl.CostEstimate(flops=0, bytes_accessed=0, transcendentals=0),
-        name="render_near" if turn is None else "render_far",
-    )(s, start, table, columns, *before, *near)
+        name="render",
+    )(*operands)
 
 
 def unpack_kernel(groups, width, *refs):
     arrived, out_ref, pieces = refs[:-2], refs[-2], refs[-1]
-    count = len(arrived)
+    count = 2 * len(arrived)
     me = lax.axis_index("gz")
     for apart in range(count):
-        pieces[me ^ apart] = arrived[apart][...]
+        pieces[me ^ apart] = arrived[apart // 2][apart % 2]
     for tile in range(count // groups):
-        for chunk in range(arrived[0].shape[0]):
+        for chunk in range(arrived[0].shape[1]):
             tiles = swap_groups(
                 [pieces[tile * groups + part, chunk] for part in range(groups)], groups, width)
             for part in range(groups):
@@ -413,12 +489,12 @@
 
 
 def unpack(arrived, groups, width):
-    count = len(arrived)
-    chunks, colors, _ = arrived[0].shape
+    count = 2 * len(arrived)
+    _, chunks, colors, _ = arrived[0].shape
     return pl.pallas_call(
         functools.partial(unpack_kernel, groups, width),
         out_shape=jax.ShapeDtypeStruct((chunks * groups, colors, count * width), jnp.float32),
-        in_specs=[pl.BlockSpec(memory_space=pltpu.VMEM)] * count,
+        in_specs=[pl.BlockSpec(memory_space=pltpu.VMEM)] * len(arrived),
         out_specs=pl.BlockSpec(memory_space=pltpu.VMEM),
         scratch_shapes=[pltpu.VMEM((count, chunks, colors, LANES), jnp.float32)],
         compiler_params=pltpu.CompilerParams(vmem_limit_bytes=8 * MIB),
@@ -505,29 +581,26 @@
         jnp.stack([extinction_scale, ambient, backdrop])[:, :, None], (3, colors, LANES))
     sum_table, table = tables(bin_rows, tf_extinction, tf_color, columns, step_x, step_z)
 
-    def prefixes(total):
-        return [lax.ppermute(total, "gx", [(i, (i + hop) % size_x) for i in range(size_x)])
-                for hop in range(1, size_x)]
-
     blocks = count // 2
     ratio = step_x / step_z
-    s, start, total = depths(pieces[:blocks], sum_table, groups, width, bins, False, count)
-    *near, done = render(s, start, table, columns, prefixes(total), [], groups, width, bins, ratio,
-                         None, blocks)
-    s, start, total = depths(pieces, sum_table, groups, width, bins, True, count, [done])
-    sums = prefixes(total)
-    halves = [
-        render(s, start, table, columns, sums, near, groups, width, bins, ratio, turn, blocks)
-        for turn in range(2)
-    ]
+    *near, near_total = render_near(
+        pieces[:blocks], table, colors, groups, width, bins, ratio, count)
+    s, start, total = far_depths(pieces, near_total, sum_table, groups, width, bins)
+    sums = [lax.ppermute(total, "gx", [(i, (i + hop) % size_x) for i in range(size_x)])
+            for hop in range(1, size_x)]
+
+    def half_of(turn):
+        return render(s, start, table, columns, near, sums, groups, width, bins, ratio, turn, blocks)
+
     share = steps // 2
     if share % groups == 0:
+        joined = exchange(half_of(1), "gz", 1)
+        both = jnp.stack([half_of(0), joined], axis=1)
         arrived = []
-        for apart in range(count):
-            give = halves[apart % 2][apart // 2]
-            arrived.append(exchange(give, "gz", apart) if apart else give)
+        for slot in range(count // 2):
+            arrived.append(exchange(both[slot], "gz", 2 * slot) if slot else both[0])
         return unpack(arrived, groups, width)
-    halves = [half[0] for half in halves]
+    halves = [half_of(0), half_of(1)]
     even = me % 2 == 0
     image = jnp.stack([jnp.where(even, halves[0], halves[1]),
                        jnp.where(even, halves[1], halves[0])])

time: 84.3 us -> 75.4 us (0.89)
  starting transfers between devices: 31.7 us -> 24.8 us
  Pallas kernels: 25.6 us -> 23.2 us
  waiting for transfers between devices: 21.7 us -> 19.3 us
  other arithmetic: 0.74 us -> 2.75 us
    pallas_call x3 -> x2, Pallas kernels: 13.9 us -> 8.96 us  [render(): pl.pallas_call(functools.partial(render_kernel, groups, width, bins, rati...]
    ppermute x14 -> x11, starting transfers between devices: 21.8 us -> 17.9 us  [exchange(): return lax.ppermute(value, axis, pairs)]
    ppermute x6 -> x3, waiting for transfers between devices: 12.7 us -> 8.83 us  [local(): lax.ppermute(total, 'gx', [(i, (i + hop) % size_x) for i in range(size_x)])]
    ppermute x6 -> x3, starting transfers between devices: 6.06 us -> 3.02 us  [local(): lax.ppermute(total, 'gx', [(i, (i + hop) % size_x) for i in range(size_x)])]
    pallas_call x2, Pallas kernels: 7.43 us -> 9.94 us  [the longest x1 6.29 us: render_near(): pl.pallas_call(functools.partial(near_kernel, groups, width, bins, ratio,...]
    another operation x2, other arithmetic: 0.73 us -> 2.04 us  [tables(): shifted = jnp.stack([bin_rows, jnp.roll(bin_rows, 1)])]
    ppermute x14 -> x11, waiting for transfers between devices: 9.07 us -> 9.9 us  [exchange(): return lax.ppermute(value, axis, pairs)]
    unnamed x14 -> x6, local copies, waits for them, and re-layouts: 2.54 us -> 2.66 us
  transfers between devices with their start and end apart: 22 -> 16, of which waited for: 8 -> 8; matrix products, arithmetic and copies ran while one was open for 2% -> 5% of each run, Pallas kernels for 15% -> 19%
where the time goes in v7:
time: 75.4 us; the launch traced here: 74.9 us
  starting transfers between devices  24.8 us (33%)
  Pallas kernels  23.2 us (31%)
  waiting for transfers between devices  19.3 us (26%)
  local copies, waits for them, and re-layouts  4.69 us (6%)
  other arithmetic  2.75 us (4%)
    ppermute x11, starting transfers between devices, exchange(): return lax.ppermute(value, axis, pairs)  17.9 us
    ppermute x11, waiting for transfers between devices, exchange(): return lax.ppermute(value, axis, pairs)  9.9 us
    pallas_call x2, Pallas kernels, render(): pl.pallas_call(functools.partial(render_kernel, groups, width, bins, rati...  8.96 us
    ppermute x3, waiting for transfers between devices, local(): lax.ppermute(total, 'gx', [(i, (i + hop) % size_x) for i in range(size_x)])  8.83 us
    pallas_call x1, Pallas kernels, render_near(): pl.pallas_call(functools.partial(near_kernel, groups, width, bins, ratio,...  6.29 us
    ppermute x1, starting transfers between devices, local(): after = lax.ppermute(density[:1], 'gx', down)  3.89 us
    pallas_call x1, Pallas kernels, far_depths(): pl.pallas_call(functools.partial(depth_kernel, groups, width, bins, count...  3.65 us
    ppermute x3, starting transfers between devices, local(): lax.ppermute(total, 'gx', [(i, (i + hop) % size_x) for i in range(size_x)])  3.02 us
  transfers between devices with their start and end apart: 16, of which 8 were waited for; matrix products, arithmetic and copies ran while one was open for 5% of the time, Pallas kernels for 19%

profile of v7, /device:TPU:0, one launch (start us, length us, event | category | flops | bytes accessed | tf_op | source)
XLA Modules:
  0.0 74.9 jit_solution(13033827424092922019)
XLA Ops:
  0.0 0.7 fusion.7
  0.7 3.9 %collective-permute-start.1 = (f32[1,8,256]{2,1,0:T(8,128)S(1)}, f32[1,8,256]{2,1,0:T(8,128)S(1)}, u32[]{:S(2)}, u32[]{:S(2)}) collective-permute-start(f32[1,8,256]{2,1,0:T(8,128)S(1)} %get-tuple-element.47), channel_id=1, source_target_pairs={{8,0},{16,8},{24,16},{0,24},{9,1},{17,9},{25,17},{1,25},{10,2},{18... | collective-permute-start | bytes 24584 | tf_op jit(solution)/shard_map/ppermute | solution.py:570
  4.6 1.2 %copy-done = f32[128,8,256]{2,1,0:T(8,128)S(1)} copy-done((f32[128,8,256]{2,1,0:T(8,128)S(1)}, f32[128,8,256]{2,1,0:T(8,128)}, u32[]{:S(2)}) %copy-start) | copy-done | bytes 1048600
  5.8 2.7 %pack.1.packed_ref = f32[8,32,8,128]{3,2,1,0:T(8,128)S(1)} custom-call(f32[4,32,8,256]{3,2,1,0:T(8,128)S(1)} %bitcast.20), custom_call_target="tpu_custom_call" | custom-call | tf_op jit(solution)/shard_map/pack/pallas_call | solution.py:71
  8.5 0.6 collective-permute-done.before_ref
  9.4 1.6 %collective-permute-start.3 = (f32[33,8,128]{2,1,0:T(8,128)S(1)}, f32[33,8,128]{2,1,0:T(8,128)S(1)}, u32[]{:S(2)}, u32[]{:S(2)}) collective-permute-start(f32[33,8,128]{2,1,0:T(8,128)S(1)} %get-tuple-element.28), channel_id=1, source_target_pairs={{0,2},{1,3},{2,0},{3,1},{4,6},{5,7},{6,4},{7,5},{8,10},{9,11},{10,... | collective-permute-start | bytes 405512 | tf_op jit(solution)/shard_map/ppermute | solution.py:551
  11.0 1.2 %slice.28 = s32[1]{0:T(128)} slice(s32[32]{0:T(128)} %param.8), slice={[31:32]} | slice | bytes 8 | tf_op jit(solution)/shard_map/jit(_roll_static)/slice | solution.py:535
  12.3 1.4 %add_bitcast_fusion = s32[1,32]{1,0:T(1,128)S(1)} fusion(s32[31]{0:T(128)} %bitcast.28, s32[1]{0:T(128)} %slice.28), kind=kLoop, calls=%fused_computation.16 | loop fusion | flops 32 | bytes 256 | tf_op jit(solution)/shard_map/stack | solution.py:535
  13.7 0.6 collective-permute-start.2
  14.2 2.6 %collective-permute-start.5 = (f32[33,8,128]{2,1,0:T(8,128)S(1)}, f32[33,8,128]{2,1,0:T(8,128)S(1)}, u32[]{:S(2)}, u32[]{:S(2)}) collective-permute-start(f32[33,8,128]{2,1,0:T(8,128)S(1)} %get-tuple-element.30), channel_id=1, source_target_pairs={{0,4},{1,5},{2,6},{3,7},{4,0},{5,1},{6,2},{7,3},{8,12},{9,13},{10,... | collective-permute-start | bytes 405512 | tf_op jit(solution)/shard_map/ppermute | solution.py:551
  16.9 3.2 %collective-permute-start.7 = (f32[33,8,128]{2,1,0:T(8,128)S(1)}, f32[33,8,128]{2,1,0:T(8,128)S(1)}, u32[]{:S(2)}, u32[]{:S(2)}) collective-permute-start(f32[33,8,128]{2,1,0:T(8,128)S(1)} %get-tuple-element.34), channel_id=1, source_target_pairs={{0,6},{1,7},{2,4},{3,5},{4,2},{5,3},{6,0},{7,1},{8,14},{9,15},{10,... | collective-permute-start | bytes 405512 | tf_op jit(solution)/shard_map/ppermute | solution.py:551
  20.1 0.7 collective-permute-start.8
  20.8 0.7 pad_add_fusion.bins_ref
  21.5 0.7 pad_maximum_fusion.1
  22.2 0.7 copy-done.1
  22.9 0.7 copy-done.2
  23.7 0.4 tables.1
  24.1 6.3 %render_near.1 = (f32[32,32,16,128]{3,2,1,0:T(8,128)S(1)}, f32[32,16,128]{2,1,0:T(8,128)S(1)}, f32[32,16,128]{2,1,0:T(8,128)S(1)}, f32[1,32,16,128]{3,2,1,0:T(8,128)S(1)}, f32[8,16,128]{2,1,0:T(8,128)S(1)}) custom-call(f32[33,8,128]{2,1,0:T(8,128)S(1)} %get-tuple-element.26.refs_0_, f32[33,8,128]{2,1,0:T(8,128)S(1)} %collective-permute-done.2.refs_1_, ...), custom_call_target="tpu_custom_call" | custom-call | tf_op jit(solution)/shard_map/render_near/pallas_call | solution.py:271
  30.4 2.8 %collective-permute-done.5.refs_4_ = f32[33,8,128]{2,1,0:T(8,128)S(1)} collective-permute-done((f32[33,8,128]{2,1,0:T(8,128)S(1)}, f32[33,8,128]{2,1,0:T(8,128)S(1)}, u32[]{:S(2)}, u32[]{:S(2)}) %collective-permute-start.5) | collective-permute-done | bytes 135200 | tf_op jit(solution)/shard_map/ppermute | solution.py:551
  33.2 1.0 %collective-permute-done.6.refs_5_ = f32[33,8,128]{2,1,0:T(8,128)S(1)} collective-permute-done((f32[33,8,128]{2,1,0:T(8,128)S(1)}, f32[33,8,128]{2,1,0:T(8,128)S(1)}, u32[]{:S(2)}, u32[]{:S(2)}) %collective-permute-start.6) | collective-permute-done | bytes 135200 | tf_op jit(solution)/shard_map/ppermute | solution.py:551
  34.1 3.7 %far_depths.1 = (f32[32,40,128]{2,1,0:T(8,128)S(1)}, f32[2,40,16,128]{3,2,1,0:T(8,128)S(1)}, f32[18,16,128]{2,1,0:T(8,128)S(1)}) custom-call(f32[33,8,128]{2,1,0:T(8,128)S(1)} %get-tuple-element.26.refs_0_, f32[33,8,128]{2,1,0:T(8,128)S(1)} %collective-permute-done.2.refs_1_, f32[33,8,128]{2,1,0:T(8,128)S(1)} %collective-permute-done.3.refs_2_, ...), custom_call_target="tpu_custom_call" | custom-call | tf_op jit(solution)/shard_map/far_depths/pallas_call | solution.py:344
  37.8 2.4 %collective-permute-start.11 = (f32[18,16,128]{2,1,0:T(8,128)S(1)}, f32[18,16,128]{2,1,0:T(8,128)S(1)}, u32[]{:S(2)}, u32[]{:S(2)}) collective-permute-start(f32[18,16,128]{2,1,0:T(8,128)S(1)} %get-tuple-element.46), channel_id=1, source_target_pairs={{0,24},{8,0},{16,8},{24,16},{1,25},{9,1},{17,9},{25,17},{2,26},{10... | collective-permute-start | bytes 442376 | tf_op jit(solution)/shard_map/ppermute | solution.py:589
  40.2 0.5 collective-permute-start.10
  40.8 3.0 %collective-permute-done.11.refs_2_ = f32[18,16,128]{2,1,0:T(8,128)S(1)} collective-permute-done((f32[18,16,128]{2,1,0:T(8,128)S(1)}, f32[18,16,128]{2,1,0:T(8,128)S(1)}, u32[]{:S(2)}, u32[]{:S(2)}) %collective-permute-start.11) | collective-permute-done | bytes 147488 | tf_op jit(solution)/shard_map/ppermute | solution.py:589
  43.8 5.8 %collective-permute-done.10.refs_1_ = f32[18,16,128]{2,1,0:T(8,128)S(1)} collective-permute-done((f32[18,16,128]{2,1,0:T(8,128)S(1)}, f32[18,16,128]{2,1,0:T(8,128)S(1)}, u32[]{:S(2)}, u32[]{:S(2)}) %collective-permute-start.10) | collective-permute-done | bytes 147488 | tf_op jit(solution)/shard_map/ppermute | solution.py:589
  49.6 4.5 %render.3 = f32[4,4,16,128]{3,2,1,0:T(8,128)S(1)} custom-call(f32[32,40,128]{2,1,0:T(8,128)S(1)} %get-tuple-element.40.s_ref, f32[2,40,16,128]{3,2,1,0:T(8,128)S(1)} %get-tuple-element.41.start_ref, bf16[32,96]{1,0:T(8,128)(2,1)S(1)} %get-tuple-element.37.refs_4_.table_ref, f32[3,16,128]{2,1,0:T(8,128)S(1)} %broadcast_in_dim.2.columns_ref, ...), custom_call_target="tpu_custom_call" | custom-call | tf_op jit(solution)/shard_map/render/pallas_call | solution.py:461
  54.4 4.5 %render.2 = f32[4,4,16,128]{3,2,1,0:T(8,128)S(1)} custom-call(f32[32,40,128]{2,1,0:T(8,128)S(1)} %get-tuple-element.40.s_ref, f32[2,40,16,128]{3,2,1,0:T(8,128)S(1)} %get-tuple-element.41.start_ref, bf16[32,96]{1,0:T(8,128)(2,1)S(1)} %get-tuple-element.37.refs_4_.table_ref, f32[3,16,128]{2,1,0:T(8,128)S(1)} %broadcast_in_dim.2.columns_ref, ...), custom_call_target="tpu_custom_call" | custom-call | tf_op jit(solution)/shard_map/render/pallas_call | solution.py:461
  59.0 3.5 %collective-permute-start.15 = (f32[2,4,16,128]{3,2,1,0:T(8,128)S(1)}, f32[2,4,16,128]{3,2,1,0:T(8,128)S(1)}, u32[]{:S(2)}, u32[]{:S(2)}) collective-permute-start(f32[2,4,16,128]{3,2,1,0:T(8,128)S(1)} %get-tuple-element.49), channel_id=1, source_target_pairs={{0,6},{1,7},{2,4},{3,5},{4,2},{5,3},{6,0},{7,1},{8,14},{9,15},{10,... | collective-permute-start | bytes 196616 | tf_op jit(solution)/shard_map/ppermute | solution.py:551
  62.5 5.4 %collective-permute-start.13 = (f32[2,4,16,128]{3,2,1,0:T(8,128)S(1)}, f32[2,4,16,128]{3,2,1,0:T(8,128)S(1)}, u32[]{:S(2)}, u32[]{:S(2)}) collective-permute-start(f32[2,4,16,128]{3,2,1,0:T(8,128)S(1)} %get-tuple-element.51), channel_id=1, source_target_pairs={{0,2},{1,3},{2,0},{3,1},{4,6},{5,7},{6,4},{7,5},{8,10},{9,11},{10,... | collective-permute-start | bytes 196616 | tf_op jit(solution)/shard_map/ppermute | solution.py:551
  67.9 2.5 %collective-permute-done.13.refs_1_ = f32[2,4,16,128]{3,2,1,0:T(8,128)S(1)} collective-permute-done((f32[2,4,16,128]{3,2,1,0:T(8,128)S(1)}, f32[2,4,16,128]{3,2,1,0:T(8,128)S(1)}, u32[]{:S(2)}, u32[]{:S(2)}) %collective-permute-start.13) | collective-permute-done | bytes 65568 | tf_op jit(solution)/shard_map/ppermute | solution.py:551
  70.3 3.6 %collective-permute-done.14.refs_2_ = f32[2,4,16,128]{3,2,1,0:T(8,128)S(1)} collective-permute-done((f32[2,4,16,128]{3,2,1,0:T(8,128)S(1)}, f32[2,4,16,128]{3,2,1,0:T(8,128)S(1)}, u32[]{:S(2)}, u32[]{:S(2)}) %collective-permute-start.14) | collective-permute-done | bytes 65568 | tf_op jit(solution)/shard_map/ppermute | solution.py:551
  73.9 1.0 %unpack.1 = f32[16,16,256]{2,1,0:T(8,128)} custom-call(f32[2,4,16,128]{3,2,1,0:T(8,128)S(1)} %get-tuple-element.50.refs_0_, f32[2,4,16,128]{3,2,1,0:T(8,128)S(1)} %collective-permute-done.13.refs_1_, f32[2,4,16,128]{3,2,1,0:T(8,128)S(1)} %collective-permute-done.14.refs_2_, f32[2,4,16,128]{3,2,1,0:T(8,128)S(1)} %collective-permute-done.15.refs_3_), custom_call_target="tpu_custom_call" | custom-call | tf_op jit(solution)/shard_map/unpack/pallas_call | solution.py:494
  (21 shorter events, 0.9 us)
Async XLA Ops:
  0.7 7.8 %collective-permute-start.1 = (f32[1,8,256]{2,1,0:T(8,128)S(1)}, f32[1,8,256]{2,1,0:T(8,128)S(1)}, u32[]{:S(2)}, u32[]{:S(2)}) collective-permute-start(f32[1,8,256]{2,1,0:T(8,128)S(1)} %get-tuple-element.47), channel_id=1, source_target_pairs={{8,0},{16,8},{24,16},{0,24},{9,1},{17,9},{25,17},{1,25},{10,2},{18... | collective-permute-start | bytes 24584 | tf_op jit(solution)/shard_map/ppermute | solution.py:570
  4.6 4.5 %collective-permute-start = (f32[1,8,256]{2,1,0:T(8,128)S(1)}, f32[1,8,256]{2,1,0:T(8,128)S(1)}, u32[]{:S(2)}, u32[]{:S(2)}) collective-permute-start(f32[1,8,256]{2,1,0:T(8,128)S(1)} %get-tuple-element.48), channel_id=1, source_target_pairs={{0,8},{8,16},{16,24},{24,0},{1,9},{9,17},{17,25},{25,1},{2,10},{10... | collective-permute-start | bytes 24584 | tf_op jit(solution)/shard_map/ppermute | solution.py:569
  4.6 1.2 %copy-start = (f32[128,8,256]{2,1,0:T(8,128)S(1)}, f32[128,8,256]{2,1,0:T(8,128)}, u32[]{:S(2)}) copy-start(f32[128,8,256]{2,1,0:T(8,128)} %param.7) | copy-start | bytes 3145732
  9.4 7.4 %collective-permute-start.3 = (f32[33,8,128]{2,1,0:T(8,128)S(1)}, f32[33,8,128]{2,1,0:T(8,128)S(1)}, u32[]{:S(2)}, u32[]{:S(2)}) collective-permute-start(f32[33,8,128]{2,1,0:T(8,128)S(1)} %get-tuple-element.28), channel_id=1, source_target_pairs={{0,2},{1,3},{2,0},{3,1},{4,6},{5,7},{6,4},{7,5},{8,10},{9,11},{10,... | collective-permute-start | bytes 405512 | tf_op jit(solution)/shard_map/ppermute | solution.py:551
  11.0 5.9 %collective-permute-start.4 = (f32[33,8,128]{2,1,0:T(8,128)S(1)}, f32[33,8,128]{2,1,0:T(8,128)S(1)}, u32[]{:S(2)}, u32[]{:S(2)}) collective-permute-start(f32[33,8,128]{2,1,0:T(8,128)S(1)} %get-tuple-element.29), channel_id=1, source_target_pairs={{0,3},{1,2},{2,1},{3,0},{4,7},{5,6},{6,5},{7,4},{8,11},{9,10},{10,... | collective-permute-start | bytes 405512 | tf_op jit(solution)/shard_map/ppermute | solution.py:551
  13.7 10.4 %collective-permute-start.2 = (f32[33,8,128]{2,1,0:T(8,128)S(1)}, f32[33,8,128]{2,1,0:T(8,128)S(1)}, u32[]{:S(2)}, u32[]{:S(2)}) collective-permute-start(f32[33,8,128]{2,1,0:T(8,128)S(1)} %get-tuple-element.27), channel_id=1, source_target_pairs={{0,1},{1,0},{2,3},{3,2},{4,5},{5,4},{6,7},{7,6},{8,9},{9,8},{10,11... | collective-permute-start | bytes 405512 | tf_op jit(solution)/shard_map/ppermute | solution.py:551
  14.2 18.9 %collective-permute-start.5 = (f32[33,8,128]{2,1,0:T(8,128)S(1)}, f32[33,8,128]{2,1,0:T(8,128)S(1)}, u32[]{:S(2)}, u32[]{:S(2)}) collective-permute-start(f32[33,8,128]{2,1,0:T(8,128)S(1)} %get-tuple-element.30), channel_id=1, source_target_pairs={{0,4},{1,5},{2,6},{3,7},{4,0},{5,1},{6,2},{7,3},{8,12},{9,13},{10,... | collective-permute-start | bytes 405512 | tf_op jit(solution)/shard_map/ppermute | solution.py:551
  16.8 17.3 %collective-permute-start.6 = (f32[33,8,128]{2,1,0:T(8,128)S(1)}, f32[33,8,128]{2,1,0:T(8,128)S(1)}, u32[]{:S(2)}, u32[]{:S(2)}) collective-permute-start(f32[33,8,128]{2,1,0:T(8,128)S(1)} %get-tuple-element.32), channel_id=1, source_target_pairs={{0,5},{1,4},{2,7},{3,6},{4,1},{5,0},{6,3},{7,2},{8,13},{9,12},{10,... | collective-permute-start | bytes 405512 | tf_op jit(solution)/shard_map/ppermute | solution.py:551
  16.9 17.2 %collective-permute-start.7 = (f32[33,8,128]{2,1,0:T(8,128)S(1)}, f32[33,8,128]{2,1,0:T(8,128)S(1)}, u32[]{:S(2)}, u32[]{:S(2)}) collective-permute-start(f32[33,8,128]{2,1,0:T(8,128)S(1)} %get-tuple-element.34), channel_id=1, source_target_pairs={{0,6},{1,7},{2,4},{3,5},{4,2},{5,3},{6,0},{7,1},{8,14},{9,15},{10,... | collective-permute-start | bytes 405512 | tf_op jit(solution)/shard_map/ppermute | solution.py:551
  20.1 14.1 %collective-permute-start.8 = (f32[33,8,128]{2,1,0:T(8,128)S(1)}, f32[33,8,128]{2,1,0:T(8,128)S(1)}, u32[]{:S(2)}, u32[]{:S(2)}) collective-permute-start(f32[33,8,128]{2,1,0:T(8,128)S(1)} %get-tuple-element.36), channel_id=1, source_target_pairs={{0,7},{1,6},{2,5},{3,4},{4,3},{5,2},{6,1},{7,0},{8,15},{9,14},{10,... | collective-permute-start | bytes 405512 | tf_op jit(solution)/shard_map/ppermute | solution.py:551
  22.2 0.7 copy-start.1
  22.9 0.7 copy-start.2
  37.8 6.0 %collective-permute-start.11 = (f32[18,16,128]{2,1,0:T(8,128)S(1)}, f32[18,16,128]{2,1,0:T(8,128)S(1)}, u32[]{:S(2)}, u32[]{:S(2)}) collective-permute-start(f32[18,16,128]{2,1,0:T(8,128)S(1)} %get-tuple-element.46), channel_id=1, source_target_pairs={{0,24},{8,0},{16,8},{24,16},{1,25},{9,1},{17,9},{25,17},{2,26},{10... | collective-permute-start | bytes 442376 | tf_op jit(solution)/shard_map/ppermute | solution.py:589
  40.2 9.5 %collective-permute-start.10 = (f32[18,16,128]{2,1,0:T(8,128)S(1)}, f32[18,16,128]{2,1,0:T(8,128)S(1)}, u32[]{:S(2)}, u32[]{:S(2)}) collective-permute-start(f32[18,16,128]{2,1,0:T(8,128)S(1)} %get-tuple-element.46), channel_id=1, source_target_pairs={{0,16},{8,24},{16,0},{24,8},{1,17},{9,25},{17,1},{25,9},{2,18},{10... | collective-permute-start | bytes 442376 | tf_op jit(solution)/shard_map/ppermute | solution.py:589
  40.7 9.0 %collective-permute-start.9 = (f32[18,16,128]{2,1,0:T(8,128)S(1)}, f32[18,16,128]{2,1,0:T(8,128)S(1)}, u32[]{:S(2)}, u32[]{:S(2)}) collective-permute-start(f32[18,16,128]{2,1,0:T(8,128)S(1)} %get-tuple-element.46), channel_id=1, source_target_pairs={{0,8},{8,16},{16,24},{24,0},{1,9},{9,17},{17,25},{25,1},{2,10},{10... | collective-permute-start | bytes 442376 | tf_op jit(solution)/shard_map/ppermute | solution.py:589
  54.1 4.8 %collective-permute-start.12 = (f32[4,4,16,128]{3,2,1,0:T(8,128)S(1)}, f32[4,4,16,128]{3,2,1,0:T(8,128)S(1)}, u32[]{:S(2)}, u32[]{:S(2)}) collective-permute-start(f32[4,4,16,128]{3,2,1,0:T(8,128)S(1)} %render.3), channel_id=1, source_target_pairs={{0,1},{1,0},{2,3},{3,2},{4,5},{5,4},{6,7},{7,6},{8,9},{9,8},{10,11... | collective-permute-start | bytes 393224 | tf_op jit(solution)/shard_map/ppermute | solution.py:551
  59.0 8.9 %collective-permute-start.15 = (f32[2,4,16,128]{3,2,1,0:T(8,128)S(1)}, f32[2,4,16,128]{3,2,1,0:T(8,128)S(1)}, u32[]{:S(2)}, u32[]{:S(2)}) collective-permute-start(f32[2,4,16,128]{3,2,1,0:T(8,128)S(1)} %get-tuple-element.49), channel_id=1, source_target_pairs={{0,6},{1,7},{2,4},{3,5},{4,2},{5,3},{6,0},{7,1},{8,14},{9,15},{10,... | collective-permute-start | bytes 196616 | tf_op jit(solution)/shard_map/ppermute | solution.py:551
  62.5 7.9 %collective-permute-start.13 = (f32[2,4,16,128]{3,2,1,0:T(8,128)S(1)}, f32[2,4,16,128]{3,2,1,0:T(8,128)S(1)}, u32[]{:S(2)}, u32[]{:S(2)}) collective-permute-start(f32[2,4,16,128]{3,2,1,0:T(8,128)S(1)} %get-tuple-element.51), channel_id=1, source_target_pairs={{0,2},{1,3},{2,0},{3,1},{4,6},{5,7},{6,4},{7,5},{8,10},{9,11},{10,... | collective-permute-start | bytes 196616 | tf_op jit(solution)/shard_map/ppermute | solution.py:551
  67.9 6.1 %collective-permute-start.14 = (f32[2,4,16,128]{3,2,1,0:T(8,128)S(1)}, f32[2,4,16,128]{3,2,1,0:T(8,128)S(1)}, u32[]{:S(2)}, u32[]{:S(2)}) collective-permute-start(f32[2,4,16,128]{3,2,1,0:T(8,128)S(1)} %get-tuple-element.52), channel_id=1, source_target_pairs={{0,4},{1,5},{2,6},{3,7},{4,0},{5,1},{6,2},{7,3},{8,12},{9,13},{10,... | collective-permute-start | bytes 196616 | tf_op jit(solution)/shard_map/ppermute | solution.py:551

commit v8 on v7

--- a/solution.py
+++ b/solution.py
@@ -177,16 +177,15 @@
     lax.fori_loop(0, steps, smooth, 0, unroll=2)
 
 
-def scan_quarters(groups, width, first_ref, second_ref, start_ref, total_ref, offset):
-    slots, colors = first_ref.shape[0], first_ref.shape[1]
+def scan_quarters(groups, width, sums_ref, start_ref, total_ref, offset):
+    slots, colors = sums_ref.shape[0], sums_ref.shape[1]
     group = group_ids((colors, LANES), width)
 
     def scan_groups(chunk, carry):
         packed = jnp.zeros((colors, LANES), jnp.float32)
         for k in range(groups):
             z = chunk * groups + k
-            first = first_ref[z]
-            both = first if second_ref is None else first + second_ref[z]
+            both = sums_ref[z]
             inclusive = both
             everything = both
             shift = 1
@@ -195,10 +194,7 @@
                 inclusive = inclusive + jnp.where(group >= shift, moved, 0.0)
                 everything = everything + pltpu.roll(everything, shift * width, 1)
                 shift *= 2
-            begin = inclusive - both
-            start_ref[0, z] = begin
-            if second_ref is not None:
-                start_ref[1, z] = begin + first
+            start_ref[z] = inclusive - both
             packed = jnp.where(group == k, everything, packed)
         total_ref[offset + chunk] = packed
         return carry
@@ -231,12 +227,8 @@
     return jnp.dot(table, jnp.concatenate(columns, axis=1), preferred_element_type=jnp.float32)
 
 
-def near_kernel(groups, width, bins, ratio, count, *refs):
-    pieces = refs[:count // 2]
-    (table_ref, lit_ref, unlit_ref, through_ref, start_ref, total_ref, raw, s_ref,
-     depth) = refs[count // 2:]
+def render_rows(bins, ratio, s_ref, table_ref, lit_ref, unlit_ref, through_ref, depth):
     steps, layers, colors, _ = lit_ref.shape
-    smooth_layers(groups, width, float(bins - 1), False, count, pieces, s_ref, raw)
     depth[...] = jnp.zeros(depth.shape, jnp.float32)
     table = table_ref[...]
     block = 8
@@ -244,10 +236,10 @@
     def advance(step, carry):
         through = jnp.ones((colors, LANES), jnp.float32)
         unlit = jnp.zeros((colors, LANES), jnp.float32)
-        for chunk in range(layers // block):
-            place = chunk * block
-            props = properties(s_ref[step, place:place + block, :], block, table, bins)
-            for r in range(block):
+        for place in range(0, layers, block):
+            size = min(block, layers - place)
+            props = properties(s_ref[step, place:place + block, :], size, table, bins)
+            for r in range(size):
                 part = props[:, r * LANES:(r + 1) * LANES]
                 sigma, color = part[:colors], part[colors:]
                 later = through * jnp.exp2(sigma)
@@ -261,7 +253,15 @@
         return carry
 
     lax.fori_loop(0, steps, advance, 0, unroll=4)
-    scan_quarters(groups, width, depth, None, start_ref, total_ref, 0)
+
+
+def near_kernel(groups, width, bins, ratio, count, *refs):
+    pieces = refs[:count // 2]
+    (table_ref, lit_ref, unlit_ref, through_ref, start_ref, total_ref, raw, s_ref,
+     depth) = refs[count // 2:]
+    smooth_layers(groups, width, float(bins - 1), False, count, pieces, s_ref, raw)
+    render_rows(bins, ratio, s_ref, table_ref, lit_ref, unlit_ref, through_ref, depth)
+    scan_quarters(groups, width, depth, start_ref, total_ref, 0)
 
 
 def render_near(pieces, table, colors, groups, width, bins, ratio, count):
@@ -274,7 +274,7 @@
             jax.ShapeDtypeStruct((steps, layers, colors, LANES), jnp.float32),
             plane,
             plane,
-            jax.ShapeDtypeStruct((1, layers, colors, LANES), jnp.float32),
+            jax.ShapeDtypeStruct((layers, colors, LANES), jnp.float32),
             jax.ShapeDtypeStruct((layers // groups, colors, LANES), jnp.float32),
         ),
         in_specs=[pl.BlockSpec(memory_space=pltpu.VMEM)] * (len(pieces) + 1),
@@ -296,42 +296,35 @@
     steps, depth = pieces[0].shape[-3] - 1, pieces[0].shape[-2]
     layers = depth * (count // 2)
     slots = s_ref.shape[1]
-    used = layers + 1
     smooth_layers(groups, width, float(bins - 1), True, count, pieces, s_ref, raw)
     edge = bin_edges(bins)
-    rows = steps // 2
 
     def count_layer(z, carry):
-        for half in range(2):
-            acc = jnp.zeros((bins, LANES), jnp.float32)
-            for step in range(rows):
-                row = jnp.broadcast_to(s_ref[half * rows + step, pl.ds(z, 1), :], (bins, LANES))
-                acc = acc + jnp.minimum(jnp.maximum(row, edge), edge + 1.0)
-            sums[half, z] = acc - edge * rows
+        acc = jnp.zeros((bins, LANES), jnp.float32)
+        for step in range(steps):
+            row = jnp.broadcast_to(s_ref[step, pl.ds(z, 1), :], (bins, LANES))
+            acc = acc + jnp.minimum(jnp.maximum(row, edge), edge + 1.0)
+        sums[z] = acc - edge * steps
         return carry
 
     lax.fori_loop(0, layers, count_layer, 0, unroll=2)
     count_layer(layers, 0)
-    for z in range(used, slots):
-        for half in range(2):
-            sums[half, z] = jnp.zeros((bins, LANES), jnp.float32)
+    for z in range(layers + 1, slots):
+        sums[z] = jnp.zeros((bins, LANES), jnp.float32)
     table = table_ref[...]
     at_once = 8
 
     def products(chunk, carry):
-        wide = [sums[half, chunk * at_once + k] for half in range(2) for k in range(at_once)]
+        wide = [sums[chunk * at_once + k] for k in range(at_once)]
         out = split_sum(table, jnp.concatenate(wide, axis=1))
-        for half in range(2):
-            for k in range(at_once):
-                place = (half * at_once + k) * LANES
-                products_ref[half, chunk * at_once + k] = out[:, place:place + LANES]
+        for k in range(at_once):
+            products_ref[chunk * at_once + k] = out[:, k * LANES:(k + 1) * LANES]
         return carry
 
     lax.fori_loop(0, slots // at_once, products, 0, unroll=True)
     ahead = near_ref.shape[0]
     total_ref[0:ahead] = near_ref[...]
-    scan_quarters(groups, width, products_ref.at[0], products_ref.at[1], start_ref, total_ref,
-                  ahead)
+    scan_quarters(groups, width, products_ref, start_ref, total_ref, ahead)
 
 
 def far_depths(pieces, near_total, table, groups, width, bins):
@@ -340,12 +333,12 @@
     layers = depth * (count // 2)
     slots = layers + max(groups, depth)
     colors = table.shape[0]
-    limit = 8 * MIB + slots * (LANES * 4 * 2) * (bins + 2 * colors)
+    limit = 8 * MIB + slots * (LANES * 4) * (bins + 2 * colors)
     return pl.pallas_call(
         functools.partial(depth_kernel, groups, width, bins, count),
         out_shape=(
             jax.ShapeDtypeStruct((steps, slots, LANES), jnp.float32),
-            jax.ShapeDtypeStruct((2, slots, colors, LANES), jnp.float32),
+            jax.ShapeDtypeStruct((slots, colors, LANES), jnp.float32),
             jax.ShapeDtypeStruct((near_total.shape[0] + slots // groups, colors, LANES),
                                  jnp.float32),
         ),
@@ -353,8 +346,8 @@
         out_specs=[pl.BlockSpec(memory_space=pltpu.VMEM)] * 3,
         scratch_shapes=[
             pltpu.VMEM((steps + 2, layers + 2 * depth, LANES), jnp.float32),
-            pltpu.VMEM((2, slots, bins, LANES), jnp.float32),
-            pltpu.VMEM((2, slots, colors, LANES), jnp.float32),
+            pltpu.VMEM((slots, bins, LANES), jnp.float32),
+            pltpu.VMEM((slots, colors, LANES), jnp.float32),
         ],
         compiler_params=pltpu.CompilerParams(vmem_limit_bytes=limit),
         cost_estimate=pl.CostEstimate(flops=0, bytes_accessed=0, transcendentals=0),
@@ -362,13 +355,28 @@
     )(*pieces, near_total, table)
 
 
-def render_kernel(groups, width, bins, ratio, turn, blocks, hops, s_ref, start_ref, table_ref,
-                  columns_ref, lit_ref, unlit_ref, near_through_ref, near_start_ref, *refs):
-    before_refs, out_ref, image, depth, light = refs[:hops], *refs[hops:]
-    rows, slots = image.shape[0], s_ref.shape[1]
-    colors = columns_ref.shape[1]
-    block = 8
-    layers = blocks * block
+def render_far(s, table, colors, bins, ratio, layers):
+    steps = s.shape[0]
+    plane = jax.ShapeDtypeStruct((steps, colors, LANES), jnp.float32)
+    return pl.pallas_call(
+        functools.partial(render_rows, bins, ratio),
+        out_shape=(jax.ShapeDtypeStruct((steps, layers, colors, LANES), jnp.float32), plane, plane),
+        in_specs=[pl.BlockSpec(memory_space=pltpu.VMEM)] * 2,
+        out_specs=[pl.BlockSpec(memory_space=pltpu.VMEM)] * 3,
+        scratch_shapes=[pltpu.VMEM((layers, colors, LANES), jnp.float32)],
+        compiler_params=pltpu.CompilerParams(vmem_limit_bytes=20 * MIB),
+        cost_estimate=pl.CostEstimate(
+            flops=10 ** 10, bytes_accessed=10 ** 7, transcendentals=10 ** 7),
+        name="render_far",
+    )(s, table)
+
+
+def join_kernel(groups, width, turn, blocks, columns_ref, *refs):
+    near_lit, near_unlit, near_through, near_start = refs[:4]
+    far_lit, far_unlit, far_through, far_start = refs[4:8]
+    before_refs, out_ref, image, near_light, far_light = refs[8:-4], *refs[-4:]
+    rows, colors, _ = image.shape
+    layers, far_layers = near_lit.shape[1], far_lit.shape[1]
     me = lax.axis_index("gz")
     lower = me < blocks
     half = (me + turn) % 2
@@ -376,66 +384,57 @@
     group = group_ids((colors, LANES), width)
     ahead = layers // groups
 
-    def before(chunk):
+    def begin(chunk, start_ref, offset, light):
         packed = jnp.zeros((colors, LANES), jnp.float32)
         for hop, ref in enumerate(before_refs, 1):
-            packed = packed + jnp.where(position >= hop, ref[chunk], 0.0)
-        values = []
+            packed = packed + jnp.where(position >= hop, ref[offset + chunk], 0.0)
         for k in range(groups):
             value = jnp.where(group == k, packed, 0.0)
             shift = 1
             while shift < groups:
                 value = value + pltpu.roll(value, shift * width, 1)
                 shift *= 2
-            values.append(value)
-        return values
+            z = chunk * groups + k
+            light[z] = jnp.exp2(start_ref[z] + value)
 
     def begin_near(chunk, carry):
-        for k, value in enumerate(before(chunk)):
-            z = chunk * groups + k
-            light[z] = jnp.exp2(near_start_ref[0, z] + value)
+        begin(chunk, near_start, 0, near_light)
         return carry
 
     def begin_far(chunk, carry):
-        for k, value in enumerate(before(ahead + chunk)):
-            z = chunk * groups + k
-            depth[z] = start_ref[half, z] + value
+        begin(chunk, far_start, ahead, far_light)
         return carry
 
     lax.fori_loop(0, ahead, begin_near, 0, unroll=4)
-    lax.fori_loop(0, slots // groups, begin_far, 0, unroll=4)
+    lax.fori_loop(0, far_start.shape[0] // groups, begin_far, 0, unroll=4)
     ambient = columns_ref[1]
-    table = table_ref[...]
-
-    def advance(step, carry):
-        row = half * rows + step
-        through = jnp.ones((colors, LANES), jnp.float32)
-        partial = jnp.zeros((colors, LANES), jnp.float32)
-        for chunk in range(blocks + 1):
-            place = chunk * block
-            size = block if chunk < blocks else 1
-            props = properties(s_ref[row, place:place + block, :], size, table, bins)
-            for r in range(size):
-                part = props[:, r * LANES:(r + 1) * LANES]
-                sigma, color = part[:colors], part[colors:]
-                later = through * jnp.exp2(sigma)
-                above = depth[place + r]
-                shade = color * (ambient + jnp.exp2(above))
-                partial = partial + (through - later) * shade
-                depth[place + r] = above + sigma * ratio
-                through = later
-        sums = [unlit_ref[row] * ambient] + [jnp.zeros((colors, LANES), jnp.float32)] * 3
-        for z in range(layers):
-            sums[z % 4] = sums[z % 4] + lit_ref[row, z] * light[z]
-        near_partial = (sums[0] + sums[1]) + (sums[2] + sums[3])
-        near_through = near_through_ref[row]
-        front = jnp.where(lower, near_partial, partial)
-        back = jnp.where(lower, partial, near_partial)
-        passed = jnp.where(lower, near_through, through)
-        image[step] = front + passed * back + through * near_through * columns_ref[2]
-        return carry
-
-    lax.fori_loop(0, rows, advance, 0, unroll=2)
+    backdrop = columns_ref[2]
+    at_once = 2
+
+    def light_rows(chunk, carry):
+        place = [chunk * at_once + k for k in range(at_once)]
+
+        def lit_sum(lit, unlit, light, count):
+            sums = [[unlit[half * rows + row] * ambient, jnp.zeros((colors, LANES), jnp.float32)]
+                    for row in place]
+            for z in range(count):
+                factor = light[z]
+                for k, row in enumerate(place):
+                    sums[k][z % 2] = sums[k][z % 2] + lit[half * rows + row, z] * factor
+            return [a + b for a, b in sums]
+
+        near = lit_sum(near_lit, near_unlit, near_light, layers)
+        far = lit_sum(far_lit, far_unlit, far_light, far_layers)
+        for k, row in enumerate(place):
+            through = far_through[half * rows + row]
+            passed = near_through[half * rows + row]
+            front = jnp.where(lower, near[k], far[k])
+            back = jnp.where(lower, far[k], near[k])
+            image[row] = (front + jnp.where(lower, passed, through) * back
+                          + through * passed * backdrop)
+        return carry
+
+    lax.fori_loop(0, rows // at_once, light_rows, 0, unroll=2)
     if len(out_ref.shape) == 3:
         out_ref[...] = image[...]
         return
@@ -449,28 +448,26 @@
             out_ref[slot, chunk] = image[chunk * groups + part]
 
 
-def render(s, start, table, columns, near, before, groups, width, bins, ratio, turn, blocks):
-    steps, slots, _ = s.shape
-    layers = near[0].shape[1]
-    colors = columns.shape[1]
+def join(columns, near, far, before, groups, width, turn, blocks):
+    steps, layers, colors, _ = near[0].shape
     share = steps // 2
     shape = (share, colors, LANES)
     if share % groups == 0:
         shape = (groups, share // groups, colors, LANES)
-    operands = [s, start, table, columns, *near, *before]
-    return pl.pallas_call(
-        functools.partial(render_kernel, groups, width, bins, ratio, turn, blocks, len(before)),
+    operands = [columns, *near, *far, *before]
+    return pl.pallas_call(
+        functools.partial(join_kernel, groups, width, turn, blocks),
         out_shape=jax.ShapeDtypeStruct(shape, jnp.float32),
         in_specs=[pl.BlockSpec(memory_space=pltpu.VMEM)] * len(operands),
         out_specs=pl.BlockSpec(memory_space=pltpu.VMEM),
         scratch_shapes=[
             pltpu.VMEM((share, colors, LANES), jnp.float32),
-            pltpu.VMEM((slots, colors, LANES), jnp.float32),
             pltpu.VMEM((layers, colors, LANES), jnp.float32),
+            pltpu.VMEM((far[3].shape[0], colors, LANES), jnp.float32),
         ],
-        compiler_params=pltpu.CompilerParams(vmem_limit_bytes=20 * MIB),
+        compiler_params=pltpu.CompilerParams(vmem_limit_bytes=24 * MIB),
         cost_estimate=pl.CostEstimate(flops=0, bytes_accessed=0, transcendentals=0),
-        name="render",
+        name="join",
     )(*operands)
 
 
@@ -577,6 +574,8 @@
             ahead = min(apart - count // 2 + 1, count // 2 - 1)
             give, _ = lax.optimization_barrier((give, pieces[ahead]))
         pieces[apart] = exchange(give, "gz", apart)
+    bin_rows, extinction_scale, ambient, backdrop, _ = lax.optimization_barrier(
+        (bin_rows, extinction_scale, ambient, backdrop, pieces[2]))
     columns = jnp.broadcast_to(
         jnp.stack([extinction_scale, ambient, backdrop])[:, :, None], (3, colors, LANES))
     sum_table, table = tables(bin_rows, tf_extinction, tf_color, columns, step_x, step_z)
@@ -589,8 +588,11 @@
     sums = [lax.ppermute(total, "gx", [(i, (i + hop) % size_x) for i in range(size_x)])
             for hop in range(1, size_x)]
 
+    layers = depth * blocks
+    far = [*render_far(s, table, colors, bins, ratio, layers + 1), start]
+
     def half_of(turn):
-        return render(s, start, table, columns, near, sums, groups, width, bins, ratio, turn, blocks)
+        return join(columns, near, far, sums, groups, width, turn, blocks)
 
     share = steps // 2
     if share % groups == 0:

time: 75.4 us -> 69.6 us (0.923)
  waiting for transfers between devices: 19.3 us -> 10.5 us
  Pallas kernels: 23.2 us -> 25.6 us
    ppermute x3, waiting for transfers between devices: 8.83 us -> 0.05 us  [local(): lax.ppermute(total, 'gx', [(i, (i + hop) % size_x) for i in range(size_x)])]
    ppermute x1, starting transfers between devices: 0.01 us -> 2.94 us  [local(): before = lax.ppermute(density[rows_x - 1:], 'gx', up)]
    ppermute x1, starting transfers between devices: 3.89 us -> 0.96 us  [local(): after = lax.ppermute(density[:1], 'gx', down)]
    pallas_call x2 -> x3, Pallas kernels: 8.96 us -> 11 us  [the longest x1 5.6 us: render_far(): pl.pallas_call(functools.partial(render_rows, bins, ratio), out_shape=(ja...]
    ppermute x3, starting transfers between devices: 3.02 us -> 4.94 us  [local(): lax.ppermute(total, 'gx', [(i, (i + hop) % size_x) for i in range(size_x)])]
    ppermute x11, starting transfers between devices: 17.9 us -> 16.6 us  [exchange(): return lax.ppermute(value, axis, pairs)]
  transfers between devices with their start and end apart: 16 -> 16, of which waited for: 8 -> 4; matrix products, arithmetic and copies ran while one was open for 5% -> 6% of each run, Pallas kernels for 19% -> 26%
where the time goes in v8:
time: 69.6 us; the launch traced here: 69.1 us
  Pallas kernels  25.6 us (37%)
  starting transfers between devices  25.5 us (37%)
  waiting for transfers between devices  10.5 us (15%)
  local copies, waits for them, and re-layouts  4.68 us (7%)
  other arithmetic  2.75 us (4%)
    ppermute x11, starting transfers between devices, exchange(): return lax.ppermute(value, axis, pairs)  16.6 us
    ppermute x11, waiting for transfers between devices, exchange(): return lax.ppermute(value, axis, pairs)  10.4 us
    pallas_call x1, Pallas kernels, render_near(): pl.pallas_call(functools.partial(near_kernel, groups, width, bins, ratio,...  6.29 us
    pallas_call x1, Pallas kernels, render_far(): pl.pallas_call(functools.partial(render_rows, bins, ratio), out_shape=(ja...  5.6 us
    pallas_call x2, Pallas kernels, join(): pl.pallas_call(functools.partial(join_kernel, groups, width, turn, blocks...  5.35 us
    ppermute x3, starting transfers between devices, local(): lax.ppermute(total, 'gx', [(i, (i + hop) % size_x) for i in range(size_x)])  4.94 us
    pallas_call x1, Pallas kernels, far_depths(): pl.pallas_call(functools.partial(depth_kernel, groups, width, bins, count...  4.04 us
    ppermute x1, starting transfers between devices, local(): before = lax.ppermute(density[rows_x - 1:], 'gx', up)  2.94 us
  transfers between devices with their start and end apart: 16, of which 4 were waited for; matrix products, arithmetic and copies ran while one was open for 6% of the time, Pallas kernels for 26%

profile of v8, /device:TPU:0, one launch (start us, length us, event | category | flops | bytes accessed | tf_op | source)
XLA Modules:
  0.0 69.1 jit_solution(16717529085419762761)
XLA Ops:
  0.0 0.7 %fusion.7 = (f32[1,8,256]{2,1,0:T(8,128)S(1)}, f32[1,8,256]{2,1,0:T(8,128)S(1)}) fusion(f32[128,8,256]{2,1,0:T(8,128)} %param.7), kind=kLoop, calls=%fused_computation.17 | loop fusion | bytes 32768 | tf_op jit(solution)/shard_map/slice | solution.py:567
  0.7 2.9 %collective-permute-start = (f32[1,8,256]{2,1,0:T(8,128)S(1)}, f32[1,8,256]{2,1,0:T(8,128)S(1)}, u32[]{:S(2)}, u32[]{:S(2)}) collective-permute-start(f32[1,8,256]{2,1,0:T(8,128)S(1)} %get-tuple-element.62), channel_id=1, source_target_pairs={{0,8},{8,16},{16,24},{24,0},{1,9},{9,17},{17,25},{25,1},{2,10},{10... | collective-permute-start | bytes 24584 | tf_op jit(solution)/shard_map/ppermute | solution.py:566
  3.7 1.0 %collective-permute-start.1 = (f32[1,8,256]{2,1,0:T(8,128)S(1)}, f32[1,8,256]{2,1,0:T(8,128)S(1)}, u32[]{:S(2)}, u32[]{:S(2)}) collective-permute-start(f32[1,8,256]{2,1,0:T(8,128)S(1)} %get-tuple-element.61), channel_id=1, source_target_pairs={{8,0},{16,8},{24,16},{0,24},{9,1},{17,9},{25,17},{1,25},{10,2},{18... | collective-permute-start | bytes 24584 | tf_op jit(solution)/shard_map/ppermute | solution.py:567
  4.6 1.2 %copy-done = f32[128,8,256]{2,1,0:T(8,128)S(1)} copy-done((f32[128,8,256]{2,1,0:T(8,128)S(1)}, f32[128,8,256]{2,1,0:T(8,128)}, u32[]{:S(2)}) %copy-start) | copy-done | bytes 1048600
  5.8 2.7 %pack.1.packed_ref = f32[8,32,8,128]{3,2,1,0:T(8,128)S(1)} custom-call(f32[4,32,8,256]{3,2,1,0:T(8,128)S(1)} %bitcast.20), custom_call_target="tpu_custom_call" | custom-call | tf_op jit(solution)/shard_map/pack/pallas_call | solution.py:71
  8.8 2.1 %collective-permute-start.2 = (f32[33,8,128]{2,1,0:T(8,128)S(1)}, f32[33,8,128]{2,1,0:T(8,128)S(1)}, u32[]{:S(2)}, u32[]{:S(2)}) collective-permute-start(f32[33,8,128]{2,1,0:T(8,128)S(1)} %get-tuple-element.33), channel_id=1, source_target_pairs={{0,2},{1,3},{2,0},{3,1},{4,6},{5,7},{6,4},{7,5},{8,10},{9,11},{10,... | collective-permute-start | bytes 405512 | tf_op jit(solution)/shard_map/ppermute | solution.py:548
  11.1 3.0 %collective-permute-start.5 = (f32[33,8,128]{2,1,0:T(8,128)S(1)}, f32[33,8,128]{2,1,0:T(8,128)S(1)}, u32[]{:S(2)}, u32[]{:S(2)}) collective-permute-start(f32[33,8,128]{2,1,0:T(8,128)S(1)} %get-tuple-element.46), channel_id=1, source_target_pairs={{0,4},{1,5},{2,6},{3,7},{4,0},{5,1},{6,2},{7,3},{8,12},{9,13},{10,... | collective-permute-start | bytes 405512 | tf_op jit(solution)/shard_map/ppermute | solution.py:548
  14.1 0.9 %collective-permute-done.2.refs_2_ = f32[33,8,128]{2,1,0:T(8,128)S(1)} collective-permute-done((f32[33,8,128]{2,1,0:T(8,128)S(1)}, f32[33,8,128]{2,1,0:T(8,128)S(1)}, u32[]{:S(2)}, u32[]{:S(2)}) %collective-permute-start.2) | collective-permute-done | bytes 135200 | tf_op jit(solution)/shard_map/ppermute | solution.py:548
  15.0 1.2 %slice.28 = s32[1]{0:T(128)} slice(s32[32]{0:T(128)} %param.8), slice={[31:32]} | slice | bytes 8 | tf_op jit(solution)/shard_map/jit(_roll_static)/slice | solution.py:532
  16.2 3.5 %collective-permute-done.4.refs_3_ = f32[33,8,128]{2,1,0:T(8,128)S(1)} collective-permute-done((f32[33,8,128]{2,1,0:T(8,128)S(1)}, f32[33,8,128]{2,1,0:T(8,128)S(1)}, u32[]{:S(2)}, u32[]{:S(2)}) %collective-permute-start.4) | collective-permute-done | bytes 135200 | tf_op jit(solution)/shard_map/ppermute | solution.py:548
  19.7 1.5 %collective-permute-start.7 = (f32[33,8,128]{2,1,0:T(8,128)S(1)}, f32[33,8,128]{2,1,0:T(8,128)S(1)}, u32[]{:S(2)}, u32[]{:S(2)}) collective-permute-start(f32[33,8,128]{2,1,0:T(8,128)S(1)} %get-tuple-element.50), channel_id=1, source_target_pairs={{0,6},{1,7},{2,4},{3,5},{4,2},{5,3},{6,0},{7,1},{8,14},{9,15},{10,... | collective-permute-start | bytes 405512 | tf_op jit(solution)/shard_map/ppermute | solution.py:548
  21.3 1.7 %collective-permute-start.8 = (f32[33,8,128]{2,1,0:T(8,128)S(1)}, f32[33,8,128]{2,1,0:T(8,128)S(1)}, u32[]{:S(2)}, u32[]{:S(2)}) collective-permute-start(f32[33,8,128]{2,1,0:T(8,128)S(1)} %get-tuple-element.52), channel_id=1, source_target_pairs={{0,7},{1,6},{2,5},{3,4},{4,3},{5,2},{6,1},{7,0},{8,15},{9,14},{10,... | collective-permute-start | bytes 405512 | tf_op jit(solution)/shard_map/ppermute | solution.py:548
  23.0 1.4 %add_bitcast_fusion = s32[1,32]{1,0:T(1,128)S(1)} fusion(s32[31]{0:T(128)} %bitcast.28, s32[1]{0:T(128)} %slice.28), kind=kLoop, calls=%fused_computation.16 | loop fusion | flops 32 | bytes 256 | tf_op jit(solution)/shard_map/stack | solution.py:532
  24.3 0.7 pad_add_fusion.bins_ref
  25.0 0.7 %pad_maximum_fusion.1 = f32[3,16]{1,0:T(4,128)S(1)} fusion(f32[1,16]{1,0:T(1,128)} %bitcast.25, f32[1,16]{1,0:T(1,128)} %bitcast.26, f32[1,16]{1,0:T(1,128)} %bitcast.27), kind=kLoop, calls=%fused_computation.14 | loop fusion | flops 96 | bytes 384 | tf_op jit(solution)/shard_map/stack | solution.py:580
  25.8 0.7 %copy-done.1 = f32[256,16]{0,1:T(8,128)S(1)} copy-done((f32[256,16]{0,1:T(8,128)S(1)}, f32[256,16]{0,1:T(8,128)}, u32[]{:S(2)}) %copy-start.1) | copy-done | bytes 16408
  26.5 0.7 %copy-done.2 = f32[256,16]{0,1:T(8,128)S(1)} copy-done((f32[256,16]{0,1:T(8,128)S(1)}, f32[256,16]{0,1:T(8,128)}, u32[]{:S(2)}) %copy-start.2) | copy-done | bytes 16408
  27.2 0.4 tables.1
  27.7 6.3 %render_near.1 = (f32[32,32,16,128]{3,2,1,0:T(8,128)S(1)}, f32[32,16,128]{2,1,0:T(8,128)S(1)}, f32[32,16,128]{2,1,0:T(8,128)S(1)}, f32[32,16,128]{2,1,0:T(8,128)S(1)}, f32[8,16,128]{2,1,0:T(8,128)S(1)}) custom-call(f32[33,8,128]{2,1,0:T(8,128)S(1)} %get-tuple-element.37.refs_0_, f32[33,8,128]{2,1,0:T(8,128)S(1)} %collective-permute-done.3.refs_1_, ...), custom_call_target="tpu_custom_call" | custom-call | tf_op jit(solution)/shard_map/render_near/pallas_call | solution.py:271
  34.0 4.0 %far_depths.1 = (f32[32,40,128]{2,1,0:T(8,128)S(1)}, f32[40,16,128]{2,1,0:T(8,128)S(1)}, f32[18,16,128]{2,1,0:T(8,128)S(1)}) custom-call(f32[33,8,128]{2,1,0:T(8,128)S(1)} %get-tuple-element.37.refs_0_, f32[33,8,128]{2,1,0:T(8,128)S(1)} %collective-permute-done.3.refs_1_, f32[33,8,128]{2,1,0:T(8,128)S(1)} %collective-permute-done.2.refs_2_, ...), custom_call_target="tpu_custom_call" | custom-call | tf_op jit(solution)/shard_map/far_depths/pallas_call | solution.py:337
  38.0 1.2 %collective-permute-start.9 = (f32[18,16,128]{2,1,0:T(8,128)S(1)}, f32[18,16,128]{2,1,0:T(8,128)S(1)}, u32[]{:S(2)}, u32[]{:S(2)}) collective-permute-start(f32[18,16,128]{2,1,0:T(8,128)S(1)} %get-tuple-element.60), channel_id=1, source_target_pairs={{0,8},{8,16},{16,24},{24,0},{1,9},{9,17},{17,25},{25,1},{2,10},{10... | collective-permute-start | bytes 442376 | tf_op jit(solution)/shard_map/ppermute | solution.py:588
  39.2 1.5 %collective-permute-start.10 = (f32[18,16,128]{2,1,0:T(8,128)S(1)}, f32[18,16,128]{2,1,0:T(8,128)S(1)}, u32[]{:S(2)}, u32[]{:S(2)}) collective-permute-start(f32[18,16,128]{2,1,0:T(8,128)S(1)} %get-tuple-element.60), channel_id=1, source_target_pairs={{0,16},{8,24},{16,0},{24,8},{1,17},{9,25},{17,1},{25,9},{2,18},{10... | collective-permute-start | bytes 442376 | tf_op jit(solution)/shard_map/ppermute | solution.py:588
  40.7 2.3 %collective-permute-start.11 = (f32[18,16,128]{2,1,0:T(8,128)S(1)}, f32[18,16,128]{2,1,0:T(8,128)S(1)}, u32[]{:S(2)}, u32[]{:S(2)}) collective-permute-start(f32[18,16,128]{2,1,0:T(8,128)S(1)} %get-tuple-element.60), channel_id=1, source_target_pairs={{0,24},{8,0},{16,8},{24,16},{1,25},{9,1},{17,9},{25,17},{2,26},{10... | collective-permute-start | bytes 442376 | tf_op jit(solution)/shard_map/ppermute | solution.py:588
  43.0 5.6 %render_far.1 = (f32[32,33,16,128]{3,2,1,0:T(8,128)S(1)}, f32[32,16,128]{2,1,0:T(8,128)S(1)}, f32[32,16,128]{2,1,0:T(8,128)S(1)}) custom-call(f32[32,40,128]{2,1,0:T(8,128)S(1)} %get-tuple-element.55.s_ref, bf16[32,96]{1,0:T(8,128)(2,1)S(1)} %get-tuple-element.41.refs_4_.table_ref), custom_call_target="tpu_custom_call" | custom-call | flops 10000000000 | bytes 10000000 | tf_op jit(solution)/shard_map/render_far/pallas_call | solution.py:361
  48.7 2.7 %join.3 = f32[4,4,16,128]{3,2,1,0:T(8,128)S(1)} custom-call(f32[3,16,128]{2,1,0:T(8,128)S(1)} %broadcast_in_dim.2.columns_ref, f32[32,32,16,128]{3,2,1,0:T(8,128)S(1)} %get-tuple-element.42.refs_0_, f32[32,16,128]{2,1,0:T(8,128)S(1)} %get-tuple-element.43.refs_1_, f32[32,16,128]{2,1,0:T(8,128)S(1)} %get-tuple-element.44.refs_2_, ...), custom_call_target="tpu_custom_call" | custom-call | tf_op jit(solution)/shard_map/join/pallas_call | solution.py:458
  51.4 2.7 %join.2 = f32[4,4,16,128]{3,2,1,0:T(8,128)S(1)} custom-call(f32[3,16,128]{2,1,0:T(8,128)S(1)} %broadcast_in_dim.2.columns_ref, f32[32,32,16,128]{3,2,1,0:T(8,128)S(1)} %get-tuple-element.42.refs_0_, f32[32,16,128]{2,1,0:T(8,128)S(1)} %get-tuple-element.43.refs_1_, f32[32,16,128]{2,1,0:T(8,128)S(1)} %get-tuple-element.44.refs_2_, ...), custom_call_target="tpu_custom_call" | custom-call | tf_op jit(solution)/shard_map/join/pallas_call | solution.py:458
  54.1 5.6 %collective-permute-start.13 = (f32[2,4,16,128]{3,2,1,0:T(8,128)S(1)}, f32[2,4,16,128]{3,2,1,0:T(8,128)S(1)}, u32[]{:S(2)}, u32[]{:S(2)}) collective-permute-start(f32[2,4,16,128]{3,2,1,0:T(8,128)S(1)} %get-tuple-element.65), channel_id=1, source_target_pairs={{0,2},{1,3},{2,0},{3,1},{4,6},{5,7},{6,4},{7,5},{8,10},{9,11},{10,... | collective-permute-start | bytes 196616 | tf_op jit(solution)/shard_map/ppermute | solution.py:548
  59.7 0.5 collective-permute-start.14
  60.3 1.9 %collective-permute-start.15 = (f32[2,4,16,128]{3,2,1,0:T(8,128)S(1)}, f32[2,4,16,128]{3,2,1,0:T(8,128)S(1)}, u32[]{:S(2)}, u32[]{:S(2)}) collective-permute-start(f32[2,4,16,128]{3,2,1,0:T(8,128)S(1)} %get-tuple-element.63), channel_id=1, source_target_pairs={{0,6},{1,7},{2,4},{3,5},{4,2},{5,3},{6,0},{7,1},{8,14},{9,15},{10,... | collective-permute-start | bytes 196616 | tf_op jit(solution)/shard_map/ppermute | solution.py:548
  62.2 0.3 collective-permute-done.13.refs_1_
  62.5 5.7 %collective-permute-done.14.refs_2_ = f32[2,4,16,128]{3,2,1,0:T(8,128)S(1)} collective-permute-done((f32[2,4,16,128]{3,2,1,0:T(8,128)S(1)}, f32[2,4,16,128]{3,2,1,0:T(8,128)S(1)}, u32[]{:S(2)}, u32[]{:S(2)}) %collective-permute-start.14) | collective-permute-done | bytes 65568 | tf_op jit(solution)/shard_map/ppermute | solution.py:548
  68.1 1.0 %unpack.1 = f32[16,16,256]{2,1,0:T(8,128)} custom-call(f32[2,4,16,128]{3,2,1,0:T(8,128)S(1)} %get-tuple-element.64.refs_0_, f32[2,4,16,128]{3,2,1,0:T(8,128)S(1)} %collective-permute-done.13.refs_1_, f32[2,4,16,128]{3,2,1,0:T(8,128)S(1)} %collective-permute-done.14.refs_2_, f32[2,4,16,128]{3,2,1,0:T(8,128)S(1)} %collective-permute-done.15.refs_3_), custom_call_target="tpu_custom_call" | custom-call | tf_op jit(solution)/shard_map/unpack/pallas_call | solution.py:491
  (22 shorter events, 0.7 us)
Async XLA Ops:
  0.7 7.8 %collective-permute-start = (f32[1,8,256]{2,1,0:T(8,128)S(1)}, f32[1,8,256]{2,1,0:T(8,128)S(1)}, u32[]{:S(2)}, u32[]{:S(2)}) collective-permute-start(f32[1,8,256]{2,1,0:T(8,128)S(1)} %get-tuple-element.62), channel_id=1, source_target_pairs={{0,8},{8,16},{16,24},{24,0},{1,9},{9,17},{17,25},{25,1},{2,10},{10... | collective-permute-start | bytes 24584 | tf_op jit(solution)/shard_map/ppermute | solution.py:566
  3.7 4.9 %collective-permute-start.1 = (f32[1,8,256]{2,1,0:T(8,128)S(1)}, f32[1,8,256]{2,1,0:T(8,128)S(1)}, u32[]{:S(2)}, u32[]{:S(2)}) collective-permute-start(f32[1,8,256]{2,1,0:T(8,128)S(1)} %get-tuple-element.61), channel_id=1, source_target_pairs={{8,0},{16,8},{24,16},{0,24},{9,1},{17,9},{25,17},{1,25},{10,2},{18... | collective-permute-start | bytes 24584 | tf_op jit(solution)/shard_map/ppermute | solution.py:567
  4.6 1.2 %copy-start = (f32[128,8,256]{2,1,0:T(8,128)S(1)}, f32[128,8,256]{2,1,0:T(8,128)}, u32[]{:S(2)}) copy-start(f32[128,8,256]{2,1,0:T(8,128)} %param.7) | copy-start | bytes 3145732
  8.8 6.2 %collective-permute-start.2 = (f32[33,8,128]{2,1,0:T(8,128)S(1)}, f32[33,8,128]{2,1,0:T(8,128)S(1)}, u32[]{:S(2)}, u32[]{:S(2)}) collective-permute-start(f32[33,8,128]{2,1,0:T(8,128)S(1)} %get-tuple-element.33), channel_id=1, source_target_pairs={{0,2},{1,3},{2,0},{3,1},{4,6},{5,7},{6,4},{7,5},{8,10},{9,11},{10,... | collective-permute-start | bytes 405512 | tf_op jit(solution)/shard_map/ppermute | solution.py:548
  10.9 8.8 %collective-permute-start.4 = (f32[33,8,128]{2,1,0:T(8,128)S(1)}, f32[33,8,128]{2,1,0:T(8,128)S(1)}, u32[]{:S(2)}, u32[]{:S(2)}) collective-permute-start(f32[33,8,128]{2,1,0:T(8,128)S(1)} %get-tuple-element.39), channel_id=1, source_target_pairs={{0,3},{1,2},{2,1},{3,0},{4,7},{5,6},{6,5},{7,4},{8,11},{9,10},{10,... | collective-permute-start | bytes 405512 | tf_op jit(solution)/shard_map/ppermute | solution.py:548
  10.9 16.7 %collective-permute-start.3 = (f32[33,8,128]{2,1,0:T(8,128)S(1)}, f32[33,8,128]{2,1,0:T(8,128)S(1)}, u32[]{:S(2)}, u32[]{:S(2)}) collective-permute-start(f32[33,8,128]{2,1,0:T(8,128)S(1)} %get-tuple-element.38), channel_id=1, source_target_pairs={{0,1},{1,0},{2,3},{3,2},{4,5},{5,4},{6,7},{7,6},{8,9},{9,8},{10,11... | collective-permute-start | bytes 405512 | tf_op jit(solution)/shard_map/ppermute | solution.py:548
  11.1 22.8 %collective-permute-start.5 = (f32[33,8,128]{2,1,0:T(8,128)S(1)}, f32[33,8,128]{2,1,0:T(8,128)S(1)}, u32[]{:S(2)}, u32[]{:S(2)}) collective-permute-start(f32[33,8,128]{2,1,0:T(8,128)S(1)} %get-tuple-element.46), channel_id=1, source_target_pairs={{0,4},{1,5},{2,6},{3,7},{4,0},{5,1},{6,2},{7,3},{8,12},{9,13},{10,... | collective-permute-start | bytes 405512 | tf_op jit(solution)/shard_map/ppermute | solution.py:548
  16.2 17.8 %collective-permute-start.6 = (f32[33,8,128]{2,1,0:T(8,128)S(1)}, f32[33,8,128]{2,1,0:T(8,128)S(1)}, u32[]{:S(2)}, u32[]{:S(2)}) collective-permute-start(f32[33,8,128]{2,1,0:T(8,128)S(1)} %get-tuple-element.48), channel_id=1, source_target_pairs={{0,5},{1,4},{2,7},{3,6},{4,1},{5,0},{6,3},{7,2},{8,13},{9,12},{10,... | collective-permute-start | bytes 405512 | tf_op jit(solution)/shard_map/ppermute | solution.py:548
  19.7 14.2 %collective-permute-start.7 = (f32[33,8,128]{2,1,0:T(8,128)S(1)}, f32[33,8,128]{2,1,0:T(8,128)S(1)}, u32[]{:S(2)}, u32[]{:S(2)}) collective-permute-start(f32[33,8,128]{2,1,0:T(8,128)S(1)} %get-tuple-element.50), channel_id=1, source_target_pairs={{0,6},{1,7},{2,4},{3,5},{4,2},{5,3},{6,0},{7,1},{8,14},{9,15},{10,... | collective-permute-start | bytes 405512 | tf_op jit(solution)/shard_map/ppermute | solution.py:548
  21.3 12.7 %collective-permute-start.8 = (f32[33,8,128]{2,1,0:T(8,128)S(1)}, f32[33,8,128]{2,1,0:T(8,128)S(1)}, u32[]{:S(2)}, u32[]{:S(2)}) collective-permute-start(f32[33,8,128]{2,1,0:T(8,128)S(1)} %get-tuple-element.52), channel_id=1, source_target_pairs={{0,7},{1,6},{2,5},{3,4},{4,3},{5,2},{6,1},{7,0},{8,15},{9,14},{10,... | collective-permute-start | bytes 405512 | tf_op jit(solution)/shard_map/ppermute | solution.py:548
  25.8 0.7 %copy-start.1 = (f32[256,16]{0,1:T(8,128)S(1)}, f32[256,16]{0,1:T(8,128)}, u32[]{:S(2)}) copy-start(f32[256,16]{0,1:T(8,128)} %param.9) | copy-start | bytes 49156
  26.5 0.7 %copy-start.2 = (f32[256,16]{0,1:T(8,128)S(1)}, f32[256,16]{0,1:T(8,128)}, u32[]{:S(2)}) copy-start(f32[256,16]{0,1:T(8,128)} %param.10) | copy-start | bytes 49156
  38.0 10.6 %collective-permute-start.9 = (f32[18,16,128]{2,1,0:T(8,128)S(1)}, f32[18,16,128]{2,1,0:T(8,128)S(1)}, u32[]{:S(2)}, u32[]{:S(2)}) collective-permute-start(f32[18,16,128]{2,1,0:T(8,128)S(1)} %get-tuple-element.60), channel_id=1, source_target_pairs={{0,8},{8,16},{16,24},{24,0},{1,9},{9,17},{17,25},{25,1},{2,10},{10... | collective-permute-start | bytes 442376 | tf_op jit(solution)/shard_map/ppermute | solution.py:588
  39.2 9.4 %collective-permute-start.10 = (f32[18,16,128]{2,1,0:T(8,128)S(1)}, f32[18,16,128]{2,1,0:T(8,128)S(1)}, u32[]{:S(2)}, u32[]{:S(2)}) collective-permute-start(f32[18,16,128]{2,1,0:T(8,128)S(1)} %get-tuple-element.60), channel_id=1, source_target_pairs={{0,16},{8,24},{16,0},{24,8},{1,17},{9,25},{17,1},{25,9},{2,18},{10... | collective-permute-start | bytes 442376 | tf_op jit(solution)/shard_map/ppermute | solution.py:588
  40.7 8.0 %collective-permute-start.11 = (f32[18,16,128]{2,1,0:T(8,128)S(1)}, f32[18,16,128]{2,1,0:T(8,128)S(1)}, u32[]{:S(2)}, u32[]{:S(2)}) collective-permute-start(f32[18,16,128]{2,1,0:T(8,128)S(1)} %get-tuple-element.60), channel_id=1, source_target_pairs={{0,24},{8,0},{16,8},{24,16},{1,25},{9,1},{17,9},{25,17},{2,26},{10... | collective-permute-start | bytes 442376 | tf_op jit(solution)/shard_map/ppermute | solution.py:588
  51.3 2.8 %collective-permute-start.12 = (f32[4,4,16,128]{3,2,1,0:T(8,128)S(1)}, f32[4,4,16,128]{3,2,1,0:T(8,128)S(1)}, u32[]{:S(2)}, u32[]{:S(2)}) collective-permute-start(f32[4,4,16,128]{3,2,1,0:T(8,128)S(1)} %join.3), channel_id=1, source_target_pairs={{0,1},{1,0},{2,3},{3,2},{4,5},{5,4},{6,7},{7,6},{8,9},{9,8},{10,11... | collective-permute-start | bytes 393224 | tf_op jit(solution)/shard_map/ppermute | solution.py:548
  54.1 8.3 %collective-permute-start.13 = (f32[2,4,16,128]{3,2,1,0:T(8,128)S(1)}, f32[2,4,16,128]{3,2,1,0:T(8,128)S(1)}, u32[]{:S(2)}, u32[]{:S(2)}) collective-permute-start(f32[2,4,16,128]{3,2,1,0:T(8,128)S(1)} %get-tuple-element.65), channel_id=1, source_target_pairs={{0,2},{1,3},{2,0},{3,1},{4,6},{5,7},{6,4},{7,5},{8,10},{9,11},{10,... | collective-permute-start | bytes 196616 | tf_op jit(solution)/shard_map/ppermute | solution.py:548
  59.7 8.4 %collective-permute-start.14 = (f32[2,4,16,128]{3,2,1,0:T(8,128)S(1)}, f32[2,4,16,128]{3,2,1,0:T(8,128)S(1)}, u32[]{:S(2)}, u32[]{:S(2)}) collective-permute-start(f32[2,4,16,128]{3,2,1,0:T(8,128)S(1)} %get-tuple-element.66), channel_id=1, source_target_pairs={{0,4},{1,5},{2,6},{3,7},{4,0},{5,1},{6,2},{7,3},{8,12},{9,13},{10,... | collective-permute-start | bytes 196616 | tf_op jit(solution)/shard_map/ppermute | solution.py:548
  60.3 7.9 %collective-permute-start.15 = (f32[2,4,16,128]{3,2,1,0:T(8,128)S(1)}, f32[2,4,16,128]{3,2,1,0:T(8,128)S(1)}, u32[]{:S(2)}, u32[]{:S(2)}) collective-permute-start(f32[2,4,16,128]{3,2,1,0:T(8,128)S(1)} %get-tuple-element.63), channel_id=1, source_target_pairs={{0,6},{1,7},{2,4},{3,5},{4,2},{5,3},{6,0},{7,1},{8,14},{9,15},{10,... | collective-permute-start | bytes 196616 | tf_op jit(solution)/shard_map/ppermute | solution.py:548

commit v9 on v8

--- a/solution.py
+++ b/solution.py
@@ -53,30 +53,32 @@
 
 def pack_kernel(groups, width, x_ref, out_ref):
     tile_count = x_ref.shape[3] // LANES
-    lane = lax.broadcasted_iota(jnp.int32, x_ref.shape[1:3] + (LANES,), 2)
-    wide = blur_rows(
-        [[x_ref[part, :, :, t * LANES:(t + 1) * LANES] for t in range(tile_count)]
-         for part in range(groups)], lane)
-    for t in range(tile_count):
-        swapped = swap_groups([wide[part][t] for part in range(groups)], groups, width)
-        for part in range(groups):
-            out_ref[t * groups + part] = swapped[part]
+    steps, depth = x_ref.shape[1], x_ref.shape[2]
+    size = 4
+    lane = lax.broadcasted_iota(jnp.int32, (size, depth, LANES), 2)
+    for first in range(0, steps, size):
+        place = pl.ds(first, size)
+        wide = blur_rows(
+            [[x_ref[group, place, :, t * LANES:(t + 1) * LANES] for t in range(tile_count)]
+             for group in range(groups)], lane)
+        for t in range(tile_count):
+            swapped = swap_groups([wide[group][t] for group in range(groups)], groups, width)
+            for group in range(groups):
+                out_ref[t * groups + group, place] = swapped[group]
 
 
 def pack(x, groups, width):
     steps = x.shape[0] // groups
     blocks = x.shape[2] // width
     depth, width_y = x.shape[1:]
-    size = 4
     return pl.pallas_call(
         functools.partial(pack_kernel, groups, width),
-        grid=(steps // size,),
         out_shape=jax.ShapeDtypeStruct((blocks, steps, depth, LANES), jnp.float32),
-        in_specs=[pl.BlockSpec((groups, size, depth, width_y), lambda i: (0, i, 0, 0))],
-        out_specs=pl.BlockSpec((blocks, size, depth, LANES), lambda i: (0, i, 0, 0)),
+        in_specs=[pl.BlockSpec(memory_space=pltpu.VMEM)],
+        out_specs=pl.BlockSpec(memory_space=pltpu.VMEM),
         compiler_params=pltpu.CompilerParams(vmem_limit_bytes=8 * MIB),
         name="pack",
-    )(x.reshape(groups, steps, x.shape[1], x.shape[2]))
+    )(x.reshape(groups, steps, depth, width_y))
 
 
 def address_kernel(groups, width, packed_ref, before_ref, after_ref, *refs):
@@ -297,14 +299,17 @@
     layers = depth * (count // 2)
     slots = s_ref.shape[1]
     smooth_layers(groups, width, float(bins - 1), True, count, pieces, s_ref, raw)
-    edge = bin_edges(bins)
+    edge = bin_edges(bins) + 1.0
+    first_bin = lax.broadcasted_iota(jnp.int32, (bins, LANES), 0) == 0
 
     def count_layer(z, carry):
-        acc = jnp.zeros((bins, LANES), jnp.float32)
+        acc = [jnp.zeros((bins, LANES), jnp.float32)] * 2
         for step in range(steps):
             row = jnp.broadcast_to(s_ref[step, pl.ds(z, 1), :], (bins, LANES))
-            acc = acc + jnp.minimum(jnp.maximum(row, edge), edge + 1.0)
-        sums[z] = acc - edge * steps
+            acc[step % 2] = acc[step % 2] + jnp.minimum(row, edge)
+        high = acc[0] + acc[1]
+        low = jnp.where(first_bin, -1.0 * steps, pltpu.roll(high, 1, 0))
+        sums[z] = high - low
         return carry
 
     lax.fori_loop(0, layers, count_layer, 0, unroll=2)
@@ -409,19 +414,18 @@
     lax.fori_loop(0, far_start.shape[0] // groups, begin_far, 0, unroll=4)
     ambient = columns_ref[1]
     backdrop = columns_ref[2]
-    at_once = 2
+    at_once = 4 if rows % 4 == 0 else 2
 
     def light_rows(chunk, carry):
         place = [chunk * at_once + k for k in range(at_once)]
 
         def lit_sum(lit, unlit, light, count):
-            sums = [[unlit[half * rows + row] * ambient, jnp.zeros((colors, LANES), jnp.float32)]
-                    for row in place]
+            sums = [unlit[half * rows + row] * ambient for row in place]
             for z in range(count):
                 factor = light[z]
                 for k, row in enumerate(place):
-                    sums[k][z % 2] = sums[k][z % 2] + lit[half * rows + row, z] * factor
-            return [a + b for a, b in sums]
+                    sums[k] = sums[k] + lit[half * rows + row, z] * factor
+            return sums
 
         near = lit_sum(near_lit, near_unlit, near_light, layers)
         far = lit_sum(far_lit, far_unlit, far_light, far_layers)

time: 69.6 us -> 67.6 us (0.971)
  Pallas kernels: 25.6 us -> 23.7 us
    pallas_call x1, Pallas kernels: 4.04 us -> 3.03 us  [far_depths(): pl.pallas_call(functools.partial(depth_kernel, groups, width, bins, count...]
  transfers between devices with their start and end apart: 16 -> 16, of which waited for: 4 -> 4; matrix products, arithmetic and copies ran while one was open for 6% -> 6% of each run, Pallas kernels for 26% -> 25%
where the time goes in v9:
time: 67.6 us; the launch traced here: 67.2 us
  starting transfers between devices  25.4 us (38%)
  Pallas kernels  23.7 us (35%)
  waiting for transfers between devices  10.5 us (16%)
  local copies, waits for them, and re-layouts  4.68 us (7%)
  other arithmetic  2.75 us (4%)
    ppermute x11, starting transfers between devices, exchange(): return lax.ppermute(value, axis, pairs)  16.6 us
    ppermute x11, waiting for transfers between devices, exchange(): return lax.ppermute(value, axis, pairs)  10.4 us
    pallas_call x1, Pallas kernels, render_near(): pl.pallas_call(functools.partial(near_kernel, groups, width, bins, ratio,...  6.29 us
    pallas_call x1, Pallas kernels, render_far(): pl.pallas_call(functools.partial(render_rows, bins, ratio), out_shape=(ja...  5.61 us
    ppermute x3, starting transfers between devices, local(): lax.ppermute(total, 'gx', [(i, (i + hop) % size_x) for i in range(size_x)])  4.94 us
    pallas_call x2, Pallas kernels, join(): pl.pallas_call(functools.partial(join_kernel, groups, width, turn, blocks...  4.69 us
    pallas_call x1, Pallas kernels, far_depths(): pl.pallas_call(functools.partial(depth_kernel, groups, width, bins, count...  3.03 us
    ppermute x1, starting transfers between devices, local(): before = lax.ppermute(density[rows_x - 1:], 'gx', up)  2.94 us
  transfers between devices with their start and end apart: 16, of which 4 were waited for; matrix products, arithmetic and copies ran while one was open for 6% of the time, Pallas kernels for 25%

profile of v9, /device:TPU:0, one launch (start us, length us, event | category | flops | bytes accessed | tf_op | source)
XLA Modules:
  0.0 67.2 jit_solution(11916900457163465032)
XLA Ops:
  0.0 0.7 %fusion.7 = (f32[1,8,256]{2,1,0:T(8,128)S(1)}, f32[1,8,256]{2,1,0:T(8,128)S(1)}) fusion(f32[128,8,256]{2,1,0:T(8,128)} %param.7), kind=kLoop, calls=%fused_computation.17 | loop fusion | bytes 32768 | tf_op jit(solution)/shard_map/slice | solution.py:571
  0.7 2.9 %collective-permute-start = (f32[1,8,256]{2,1,0:T(8,128)S(1)}, f32[1,8,256]{2,1,0:T(8,128)S(1)}, u32[]{:S(2)}, u32[]{:S(2)}) collective-permute-start(f32[1,8,256]{2,1,0:T(8,128)S(1)} %get-tuple-element.62), channel_id=1, source_target_pairs={{0,8},{8,16},{16,24},{24,0},{1,9},{9,17},{17,25},{25,1},{2,10},{10... | collective-permute-start | bytes 24584 | tf_op jit(solution)/shard_map/ppermute | solution.py:570
  3.7 1.0 %collective-permute-start.1 = (f32[1,8,256]{2,1,0:T(8,128)S(1)}, f32[1,8,256]{2,1,0:T(8,128)S(1)}, u32[]{:S(2)}, u32[]{:S(2)}) collective-permute-start(f32[1,8,256]{2,1,0:T(8,128)S(1)} %get-tuple-element.61), channel_id=1, source_target_pairs={{8,0},{16,8},{24,16},{0,24},{9,1},{17,9},{25,17},{1,25},{10,2},{18... | collective-permute-start | bytes 24584 | tf_op jit(solution)/shard_map/ppermute | solution.py:571
  4.6 1.2 %copy-done = f32[128,8,256]{2,1,0:T(8,128)S(1)} copy-done((f32[128,8,256]{2,1,0:T(8,128)S(1)}, f32[128,8,256]{2,1,0:T(8,128)}, u32[]{:S(2)}) %copy-start) | copy-done | bytes 1048600
  5.8 2.4 %pack.1.packed_ref = f32[8,32,8,128]{3,2,1,0:T(8,128)S(1)} custom-call(f32[4,32,8,256]{3,2,1,0:T(8,128)S(1)} %bitcast.20), custom_call_target="tpu_custom_call" | custom-call | tf_op jit(solution)/shard_map/pack/pallas_call | solution.py:74
  8.5 2.1 %collective-permute-start.2 = (f32[33,8,128]{2,1,0:T(8,128)S(1)}, f32[33,8,128]{2,1,0:T(8,128)S(1)}, u32[]{:S(2)}, u32[]{:S(2)}) collective-permute-start(f32[33,8,128]{2,1,0:T(8,128)S(1)} %get-tuple-element.33), channel_id=1, source_target_pairs={{0,2},{1,3},{2,0},{3,1},{4,6},{5,7},{6,4},{7,5},{8,10},{9,11},{10,... | collective-permute-start | bytes 405512 | tf_op jit(solution)/shard_map/ppermute | solution.py:552
  10.8 3.0 %collective-permute-start.5 = (f32[33,8,128]{2,1,0:T(8,128)S(1)}, f32[33,8,128]{2,1,0:T(8,128)S(1)}, u32[]{:S(2)}, u32[]{:S(2)}) collective-permute-start(f32[33,8,128]{2,1,0:T(8,128)S(1)} %get-tuple-element.46), channel_id=1, source_target_pairs={{0,4},{1,5},{2,6},{3,7},{4,0},{5,1},{6,2},{7,3},{8,12},{9,13},{10,... | collective-permute-start | bytes 405512 | tf_op jit(solution)/shard_map/ppermute | solution.py:552
  13.8 0.9 %collective-permute-done.2.refs_2_ = f32[33,8,128]{2,1,0:T(8,128)S(1)} collective-permute-done((f32[33,8,128]{2,1,0:T(8,128)S(1)}, f32[33,8,128]{2,1,0:T(8,128)S(1)}, u32[]{:S(2)}, u32[]{:S(2)}) %collective-permute-start.2) | collective-permute-done | bytes 135200 | tf_op jit(solution)/shard_map/ppermute | solution.py:552
  14.7 1.2 %slice.28 = s32[1]{0:T(128)} slice(s32[32]{0:T(128)} %param.8), slice={[31:32]} | slice | bytes 8 | tf_op jit(solution)/shard_map/jit(_roll_static)/slice | solution.py:536
  15.9 3.5 %collective-permute-done.4.refs_3_ = f32[33,8,128]{2,1,0:T(8,128)S(1)} collective-permute-done((f32[33,8,128]{2,1,0:T(8,128)S(1)}, f32[33,8,128]{2,1,0:T(8,128)S(1)}, u32[]{:S(2)}, u32[]{:S(2)}) %collective-permute-start.4) | collective-permute-done | bytes 135200 | tf_op jit(solution)/shard_map/ppermute | solution.py:552
  19.4 1.5 %collective-permute-start.7 = (f32[33,8,128]{2,1,0:T(8,128)S(1)}, f32[33,8,128]{2,1,0:T(8,128)S(1)}, u32[]{:S(2)}, u32[]{:S(2)}) collective-permute-start(f32[33,8,128]{2,1,0:T(8,128)S(1)} %get-tuple-element.50), channel_id=1, source_target_pairs={{0,6},{1,7},{2,4},{3,5},{4,2},{5,3},{6,0},{7,1},{8,14},{9,15},{10,... | collective-permute-start | bytes 405512 | tf_op jit(solution)/shard_map/ppermute | solution.py:552
  20.9 1.7 %collective-permute-start.8 = (f32[33,8,128]{2,1,0:T(8,128)S(1)}, f32[33,8,128]{2,1,0:T(8,128)S(1)}, u32[]{:S(2)}, u32[]{:S(2)}) collective-permute-start(f32[33,8,128]{2,1,0:T(8,128)S(1)} %get-tuple-element.52), channel_id=1, source_target_pairs={{0,7},{1,6},{2,5},{3,4},{4,3},{5,2},{6,1},{7,0},{8,15},{9,14},{10,... | collective-permute-start | bytes 405512 | tf_op jit(solution)/shard_map/ppermute | solution.py:552
  22.7 1.4 %add_bitcast_fusion = s32[1,32]{1,0:T(1,128)S(1)} fusion(s32[31]{0:T(128)} %bitcast.28, s32[1]{0:T(128)} %slice.28), kind=kLoop, calls=%fused_computation.16 | loop fusion | flops 32 | bytes 256 | tf_op jit(solution)/shard_map/stack | solution.py:536
  24.0 0.7 pad_add_fusion.bins_ref
  24.7 0.7 %pad_maximum_fusion.1 = f32[3,16]{1,0:T(4,128)S(1)} fusion(f32[1,16]{1,0:T(1,128)} %bitcast.25, f32[1,16]{1,0:T(1,128)} %bitcast.26, f32[1,16]{1,0:T(1,128)} %bitcast.27), kind=kLoop, calls=%fused_computation.14 | loop fusion | flops 96 | bytes 384 | tf_op jit(solution)/shard_map/stack | solution.py:584
  25.5 0.7 %copy-done.1 = f32[256,16]{0,1:T(8,128)S(1)} copy-done((f32[256,16]{0,1:T(8,128)S(1)}, f32[256,16]{0,1:T(8,128)}, u32[]{:S(2)}) %copy-start.1) | copy-done | bytes 16408
  26.2 0.7 %copy-done.2 = f32[256,16]{0,1:T(8,128)S(1)} copy-done((f32[256,16]{0,1:T(8,128)S(1)}, f32[256,16]{0,1:T(8,128)}, u32[]{:S(2)}) %copy-start.2) | copy-done | bytes 16408
  26.9 0.4 tables.1
  27.4 6.3 %render_near.1 = (f32[32,32,16,128]{3,2,1,0:T(8,128)S(1)}, f32[32,16,128]{2,1,0:T(8,128)S(1)}, f32[32,16,128]{2,1,0:T(8,128)S(1)}, f32[32,16,128]{2,1,0:T(8,128)S(1)}, f32[8,16,128]{2,1,0:T(8,128)S(1)}) custom-call(f32[33,8,128]{2,1,0:T(8,128)S(1)} %get-tuple-element.37.refs_0_, f32[33,8,128]{2,1,0:T(8,128)S(1)} %collective-permute-done.3.refs_1_, ...), custom_call_target="tpu_custom_call" | custom-call | tf_op jit(solution)/shard_map/render_near/pallas_call | solution.py:273
  33.7 3.0 %far_depths.1 = (f32[32,40,128]{2,1,0:T(8,128)S(1)}, f32[40,16,128]{2,1,0:T(8,128)S(1)}, f32[18,16,128]{2,1,0:T(8,128)S(1)}) custom-call(f32[33,8,128]{2,1,0:T(8,128)S(1)} %get-tuple-element.37.refs_0_, f32[33,8,128]{2,1,0:T(8,128)S(1)} %collective-permute-done.3.refs_1_, f32[33,8,128]{2,1,0:T(8,128)S(1)} %collective-permute-done.2.refs_2_, ...), custom_call_target="tpu_custom_call" | custom-call | tf_op jit(solution)/shard_map/far_depths/pallas_call | solution.py:342
  36.7 1.5 %collective-permute-start.9 = (f32[18,16,128]{2,1,0:T(8,128)S(1)}, f32[18,16,128]{2,1,0:T(8,128)S(1)}, u32[]{:S(2)}, u32[]{:S(2)}) collective-permute-start(f32[18,16,128]{2,1,0:T(8,128)S(1)} %get-tuple-element.60), channel_id=1, source_target_pairs={{0,8},{8,16},{16,24},{24,0},{1,9},{9,17},{17,25},{25,1},{2,10},{10... | collective-permute-start | bytes 442376 | tf_op jit(solution)/shard_map/ppermute | solution.py:592
  38.2 1.2 %collective-permute-start.10 = (f32[18,16,128]{2,1,0:T(8,128)S(1)}, f32[18,16,128]{2,1,0:T(8,128)S(1)}, u32[]{:S(2)}, u32[]{:S(2)}) collective-permute-start(f32[18,16,128]{2,1,0:T(8,128)S(1)} %get-tuple-element.60), channel_id=1, source_target_pairs={{0,16},{8,24},{16,0},{24,8},{1,17},{9,25},{17,1},{25,9},{2,18},{10... | collective-permute-start | bytes 442376 | tf_op jit(solution)/shard_map/ppermute | solution.py:592
  39.3 2.3 %collective-permute-start.11 = (f32[18,16,128]{2,1,0:T(8,128)S(1)}, f32[18,16,128]{2,1,0:T(8,128)S(1)}, u32[]{:S(2)}, u32[]{:S(2)}) collective-permute-start(f32[18,16,128]{2,1,0:T(8,128)S(1)} %get-tuple-element.60), channel_id=1, source_target_pairs={{0,24},{8,0},{16,8},{24,16},{1,25},{9,1},{17,9},{25,17},{2,26},{10... | collective-permute-start | bytes 442376 | tf_op jit(solution)/shard_map/ppermute | solution.py:592
  41.7 5.6 %render_far.1 = (f32[32,33,16,128]{3,2,1,0:T(8,128)S(1)}, f32[32,16,128]{2,1,0:T(8,128)S(1)}, f32[32,16,128]{2,1,0:T(8,128)S(1)}) custom-call(f32[32,40,128]{2,1,0:T(8,128)S(1)} %get-tuple-element.55.s_ref, bf16[32,96]{1,0:T(8,128)(2,1)S(1)} %get-tuple-element.41.refs_4_.table_ref), custom_call_target="tpu_custom_call" | custom-call | flops 10000000000 | bytes 10000000 | tf_op jit(solution)/shard_map/render_far/pallas_call | solution.py:366
  47.4 2.3 %join.3 = f32[4,4,16,128]{3,2,1,0:T(8,128)S(1)} custom-call(f32[3,16,128]{2,1,0:T(8,128)S(1)} %broadcast_in_dim.2.columns_ref, f32[32,32,16,128]{3,2,1,0:T(8,128)S(1)} %get-tuple-element.42.refs_0_, f32[32,16,128]{2,1,0:T(8,128)S(1)} %get-tuple-element.43.refs_1_, f32[32,16,128]{2,1,0:T(8,128)S(1)} %get-tuple-element.44.refs_2_, ...), custom_call_target="tpu_custom_call" | custom-call | tf_op jit(solution)/shard_map/join/pallas_call | solution.py:462
  49.8 2.4 %join.2 = f32[4,4,16,128]{3,2,1,0:T(8,128)S(1)} custom-call(f32[3,16,128]{2,1,0:T(8,128)S(1)} %broadcast_in_dim.2.columns_ref, f32[32,32,16,128]{3,2,1,0:T(8,128)S(1)} %get-tuple-element.42.refs_0_, f32[32,16,128]{2,1,0:T(8,128)S(1)} %get-tuple-element.43.refs_1_, f32[32,16,128]{2,1,0:T(8,128)S(1)} %get-tuple-element.44.refs_2_, ...), custom_call_target="tpu_custom_call" | custom-call | tf_op jit(solution)/shard_map/join/pallas_call | solution.py:462
  52.2 5.6 %collective-permute-start.13 = (f32[2,4,16,128]{3,2,1,0:T(8,128)S(1)}, f32[2,4,16,128]{3,2,1,0:T(8,128)S(1)}, u32[]{:S(2)}, u32[]{:S(2)}) collective-permute-start(f32[2,4,16,128]{3,2,1,0:T(8,128)S(1)} %get-tuple-element.65), channel_id=1, source_target_pairs={{0,2},{1,3},{2,0},{3,1},{4,6},{5,7},{6,4},{7,5},{8,10},{9,11},{10,... | collective-permute-start | bytes 196616 | tf_op jit(solution)/shard_map/ppermute | solution.py:552
  57.8 0.6 collective-permute-start.14
  58.3 1.9 %collective-permute-start.15 = (f32[2,4,16,128]{3,2,1,0:T(8,128)S(1)}, f32[2,4,16,128]{3,2,1,0:T(8,128)S(1)}, u32[]{:S(2)}, u32[]{:S(2)}) collective-permute-start(f32[2,4,16,128]{3,2,1,0:T(8,128)S(1)} %get-tuple-element.63), channel_id=1, source_target_pairs={{0,6},{1,7},{2,4},{3,5},{4,2},{5,3},{6,0},{7,1},{8,14},{9,15},{10,... | collective-permute-start | bytes 196616 | tf_op jit(solution)/shard_map/ppermute | solution.py:552
  60.2 0.3 collective-permute-done.13.refs_1_
  60.5 5.7 %collective-permute-done.14.refs_2_ = f32[2,4,16,128]{3,2,1,0:T(8,128)S(1)} collective-permute-done((f32[2,4,16,128]{3,2,1,0:T(8,128)S(1)}, f32[2,4,16,128]{3,2,1,0:T(8,128)S(1)}, u32[]{:S(2)}, u32[]{:S(2)}) %collective-permute-start.14) | collective-permute-done | bytes 65568 | tf_op jit(solution)/shard_map/ppermute | solution.py:552
  66.2 1.0 %unpack.1 = f32[16,16,256]{2,1,0:T(8,128)} custom-call(f32[2,4,16,128]{3,2,1,0:T(8,128)S(1)} %get-tuple-element.64.refs_0_, f32[2,4,16,128]{3,2,1,0:T(8,128)S(1)} %collective-permute-done.13.refs_1_, f32[2,4,16,128]{3,2,1,0:T(8,128)S(1)} %collective-permute-done.14.refs_2_, f32[2,4,16,128]{3,2,1,0:T(8,128)S(1)} %collective-permute-done.15.refs_3_), custom_call_target="tpu_custom_call" | custom-call | tf_op jit(solution)/shard_map/unpack/pallas_call | solution.py:495
  (22 shorter events, 0.7 us)
Async XLA Ops:
  0.7 7.5 %collective-permute-start = (f32[1,8,256]{2,1,0:T(8,128)S(1)}, f32[1,8,256]{2,1,0:T(8,128)S(1)}, u32[]{:S(2)}, u32[]{:S(2)}) collective-permute-start(f32[1,8,256]{2,1,0:T(8,128)S(1)} %get-tuple-element.62), channel_id=1, source_target_pairs={{0,8},{8,16},{16,24},{24,0},{1,9},{9,17},{17,25},{25,1},{2,10},{10... | collective-permute-start | bytes 24584 | tf_op jit(solution)/shard_map/ppermute | solution.py:570
  3.7 4.6 %collective-permute-start.1 = (f32[1,8,256]{2,1,0:T(8,128)S(1)}, f32[1,8,256]{2,1,0:T(8,128)S(1)}, u32[]{:S(2)}, u32[]{:S(2)}) collective-permute-start(f32[1,8,256]{2,1,0:T(8,128)S(1)} %get-tuple-element.61), channel_id=1, source_target_pairs={{8,0},{16,8},{24,16},{0,24},{9,1},{17,9},{25,17},{1,25},{10,2},{18... | collective-permute-start | bytes 24584 | tf_op jit(solution)/shard_map/ppermute | solution.py:571
  4.6 1.2 %copy-start = (f32[128,8,256]{2,1,0:T(8,128)S(1)}, f32[128,8,256]{2,1,0:T(8,128)}, u32[]{:S(2)}) copy-start(f32[128,8,256]{2,1,0:T(8,128)} %param.7) | copy-start | bytes 3145732
  8.5 6.2 %collective-permute-start.2 = (f32[33,8,128]{2,1,0:T(8,128)S(1)}, f32[33,8,128]{2,1,0:T(8,128)S(1)}, u32[]{:S(2)}, u32[]{:S(2)}) collective-permute-start(f32[33,8,128]{2,1,0:T(8,128)S(1)} %get-tuple-element.33), channel_id=1, source_target_pairs={{0,2},{1,3},{2,0},{3,1},{4,6},{5,7},{6,4},{7,5},{8,10},{9,11},{10,... | collective-permute-start | bytes 405512 | tf_op jit(solution)/shard_map/ppermute | solution.py:552
  10.6 8.8 %collective-permute-start.4 = (f32[33,8,128]{2,1,0:T(8,128)S(1)}, f32[33,8,128]{2,1,0:T(8,128)S(1)}, u32[]{:S(2)}, u32[]{:S(2)}) collective-permute-start(f32[33,8,128]{2,1,0:T(8,128)S(1)} %get-tuple-element.39), channel_id=1, source_target_pairs={{0,3},{1,2},{2,1},{3,0},{4,7},{5,6},{6,5},{7,4},{8,11},{9,10},{10,... | collective-permute-start | bytes 405512 | tf_op jit(solution)/shard_map/ppermute | solution.py:552
  10.6 16.7 %collective-permute-start.3 = (f32[33,8,128]{2,1,0:T(8,128)S(1)}, f32[33,8,128]{2,1,0:T(8,128)S(1)}, u32[]{:S(2)}, u32[]{:S(2)}) collective-permute-start(f32[33,8,128]{2,1,0:T(8,128)S(1)} %get-tuple-element.38), channel_id=1, source_target_pairs={{0,1},{1,0},{2,3},{3,2},{4,5},{5,4},{6,7},{7,6},{8,9},{9,8},{10,11... | collective-permute-start | bytes 405512 | tf_op jit(solution)/shard_map/ppermute | solution.py:552
  10.8 22.8 %collective-permute-start.5 = (f32[33,8,128]{2,1,0:T(8,128)S(1)}, f32[33,8,128]{2,1,0:T(8,128)S(1)}, u32[]{:S(2)}, u32[]{:S(2)}) collective-permute-start(f32[33,8,128]{2,1,0:T(8,128)S(1)} %get-tuple-element.46), channel_id=1, source_target_pairs={{0,4},{1,5},{2,6},{3,7},{4,0},{5,1},{6,2},{7,3},{8,12},{9,13},{10,... | collective-permute-start | bytes 405512 | tf_op jit(solution)/shard_map/ppermute | solution.py:552
  15.9 17.8 %collective-permute-start.6 = (f32[33,8,128]{2,1,0:T(8,128)S(1)}, f32[33,8,128]{2,1,0:T(8,128)S(1)}, u32[]{:S(2)}, u32[]{:S(2)}) collective-permute-start(f32[33,8,128]{2,1,0:T(8,128)S(1)} %get-tuple-element.48), channel_id=1, source_target_pairs={{0,5},{1,4},{2,7},{3,6},{4,1},{5,0},{6,3},{7,2},{8,13},{9,12},{10,... | collective-permute-start | bytes 405512 | tf_op jit(solution)/shard_map/ppermute | solution.py:552
  19.4 14.2 %collective-permute-start.7 = (f32[33,8,128]{2,1,0:T(8,128)S(1)}, f32[33,8,128]{2,1,0:T(8,128)S(1)}, u32[]{:S(2)}, u32[]{:S(2)}) collective-permute-start(f32[33,8,128]{2,1,0:T(8,128)S(1)} %get-tuple-element.50), channel_id=1, source_target_pairs={{0,6},{1,7},{2,4},{3,5},{4,2},{5,3},{6,0},{7,1},{8,14},{9,15},{10,... | collective-permute-start | bytes 405512 | tf_op jit(solution)/shard_map/ppermute | solution.py:552
  20.9 12.7 %collective-permute-start.8 = (f32[33,8,128]{2,1,0:T(8,128)S(1)}, f32[33,8,128]{2,1,0:T(8,128)S(1)}, u32[]{:S(2)}, u32[]{:S(2)}) collective-permute-start(f32[33,8,128]{2,1,0:T(8,128)S(1)} %get-tuple-element.52), channel_id=1, source_target_pairs={{0,7},{1,6},{2,5},{3,4},{4,3},{5,2},{6,1},{7,0},{8,15},{9,14},{10,... | collective-permute-start | bytes 405512 | tf_op jit(solution)/shard_map/ppermute | solution.py:552
  25.5 0.7 %copy-start.1 = (f32[256,16]{0,1:T(8,128)S(1)}, f32[256,16]{0,1:T(8,128)}, u32[]{:S(2)}) copy-start(f32[256,16]{0,1:T(8,128)} %param.9) | copy-start | bytes 49156
  26.2 0.7 %copy-start.2 = (f32[256,16]{0,1:T(8,128)S(1)}, f32[256,16]{0,1:T(8,128)}, u32[]{:S(2)}) copy-start(f32[256,16]{0,1:T(8,128)} %param.10) | copy-start | bytes 49156
  36.7 10.6 %collective-permute-start.9 = (f32[18,16,128]{2,1,0:T(8,128)S(1)}, f32[18,16,128]{2,1,0:T(8,128)S(1)}, u32[]{:S(2)}, u32[]{:S(2)}) collective-permute-start(f32[18,16,128]{2,1,0:T(8,128)S(1)} %get-tuple-element.60), channel_id=1, source_target_pairs={{0,8},{8,16},{16,24},{24,0},{1,9},{9,17},{17,25},{25,1},{2,10},{10... | collective-permute-start | bytes 442376 | tf_op jit(solution)/shard_map/ppermute | solution.py:592
  38.2 9.1 %collective-permute-start.10 = (f32[18,16,128]{2,1,0:T(8,128)S(1)}, f32[18,16,128]{2,1,0:T(8,128)S(1)}, u32[]{:S(2)}, u32[]{:S(2)}) collective-permute-start(f32[18,16,128]{2,1,0:T(8,128)S(1)} %get-tuple-element.60), channel_id=1, source_target_pairs={{0,16},{8,24},{16,0},{24,8},{1,17},{9,25},{17,1},{25,9},{2,18},{10... | collective-permute-start | bytes 442376 | tf_op jit(solution)/shard_map/ppermute | solution.py:592
  39.3 8.0 %collective-permute-start.11 = (f32[18,16,128]{2,1,0:T(8,128)S(1)}, f32[18,16,128]{2,1,0:T(8,128)S(1)}, u32[]{:S(2)}, u32[]{:S(2)}) collective-permute-start(f32[18,16,128]{2,1,0:T(8,128)S(1)} %get-tuple-element.60), channel_id=1, source_target_pairs={{0,24},{8,0},{16,8},{24,16},{1,25},{9,1},{17,9},{25,17},{2,26},{10... | collective-permute-start | bytes 442376 | tf_op jit(solution)/shard_map/ppermute | solution.py:592
  49.7 2.4 %collective-permute-start.12 = (f32[4,4,16,128]{3,2,1,0:T(8,128)S(1)}, f32[4,4,16,128]{3,2,1,0:T(8,128)S(1)}, u32[]{:S(2)}, u32[]{:S(2)}) collective-permute-start(f32[4,4,16,128]{3,2,1,0:T(8,128)S(1)} %join.3), channel_id=1, source_target_pairs={{0,1},{1,0},{2,3},{3,2},{4,5},{5,4},{6,7},{7,6},{8,9},{9,8},{10,11... | collective-permute-start | bytes 393224 | tf_op jit(solution)/shard_map/ppermute | solution.py:552
  52.2 8.3 %collective-permute-start.13 = (f32[2,4,16,128]{3,2,1,0:T(8,128)S(1)}, f32[2,4,16,128]{3,2,1,0:T(8,128)S(1)}, u32[]{:S(2)}, u32[]{:S(2)}) collective-permute-start(f32[2,4,16,128]{3,2,1,0:T(8,128)S(1)} %get-tuple-element.65), channel_id=1, source_target_pairs={{0,2},{1,3},{2,0},{3,1},{4,6},{5,7},{6,4},{7,5},{8,10},{9,11},{10,... | collective-permute-start | bytes 196616 | tf_op jit(solution)/shard_map/ppermute | solution.py:552
  57.8 8.4 %collective-permute-start.14 = (f32[2,4,16,128]{3,2,1,0:T(8,128)S(1)}, f32[2,4,16,128]{3,2,1,0:T(8,128)S(1)}, u32[]{:S(2)}, u32[]{:S(2)}) collective-permute-start(f32[2,4,16,128]{3,2,1,0:T(8,128)S(1)} %get-tuple-element.66), channel_id=1, source_target_pairs={{0,4},{1,5},{2,6},{3,7},{4,0},{5,1},{6,2},{7,3},{8,12},{9,13},{10,... | collective-permute-start | bytes 196616 | tf_op jit(solution)/shard_map/ppermute | solution.py:552
  58.3 7.8 %collective-permute-start.15 = (f32[2,4,16,128]{3,2,1,0:T(8,128)S(1)}, f32[2,4,16,128]{3,2,1,0:T(8,128)S(1)}, u32[]{:S(2)}, u32[]{:S(2)}) collective-permute-start(f32[2,4,16,128]{3,2,1,0:T(8,128)S(1)} %get-tuple-element.63), channel_id=1, source_target_pairs={{0,6},{1,7},{2,4},{3,5},{4,2},{5,3},{6,0},{7,1},{8,14},{9,15},{10,... | collective-permute-start | bytes 196616 | tf_op jit(solution)/shard_map/ppermute | solution.py:552

commit v10 on v9

--- a/solution.py
+++ b/solution.py
@@ -97,9 +97,9 @@
         swapped = swap_groups(tiles, groups, width)
         for part in range(groups):
             halo[t * groups + part] = swapped[part]
-    for apart in range(count):
-        out_refs[apart][0:steps] = packed_ref[me ^ apart]
-        out_refs[apart][steps] = halo[me ^ apart]
+    for apart, out_ref in enumerate(out_refs):
+        out_ref[0:steps] = packed_ref[me ^ apart]
+        out_ref[steps] = halo[me ^ apart]
 
 
 def address(packed, before, after, groups, width):
@@ -377,9 +377,12 @@
 
 
 def join_kernel(groups, width, turn, blocks, columns_ref, *refs):
-    near_lit, near_unlit, near_through, near_start = refs[:4]
-    far_lit, far_unlit, far_through, far_start = refs[4:8]
-    before_refs, out_ref, image, near_light, far_light = refs[8:-4], *refs[-4:]
+    near_lit, near_unlit, near_through, far_lit, far_unlit, far_through = refs[:6]
+    if turn:
+        near_start, far_start = refs[6:8]
+        before_refs, out_ref, near_light, far_light, image = refs[8:-4], *refs[-4:]
+    else:
+        near_light, far_light, out_ref, image = refs[6:]
     rows, colors, _ = image.shape
     layers, far_layers = near_lit.shape[1], far_lit.shape[1]
     me = lax.axis_index("gz")
@@ -410,8 +413,9 @@
         begin(chunk, far_start, ahead, far_light)
         return carry
 
-    lax.fori_loop(0, ahead, begin_near, 0, unroll=4)
-    lax.fori_loop(0, far_start.shape[0] // groups, begin_far, 0, unroll=4)
+    if turn:
+        lax.fori_loop(0, ahead, begin_near, 0, unroll=4)
+        lax.fori_loop(0, far_start.shape[0] // groups, begin_far, 0, unroll=4)
     ambient = columns_ref[1]
     backdrop = columns_ref[2]
     at_once = 4 if rows % 4 == 0 else 2
@@ -452,23 +456,22 @@
             out_ref[slot, chunk] = image[chunk * groups + part]
 
 
-def join(columns, near, far, before, groups, width, turn, blocks):
+def join(columns, near, far, light, groups, width, turn, blocks):
     steps, layers, colors, _ = near[0].shape
     share = steps // 2
     shape = (share, colors, LANES)
     if share % groups == 0:
         shape = (groups, share // groups, colors, LANES)
-    operands = [columns, *near, *far, *before]
+    shapes = [jax.ShapeDtypeStruct(shape, jnp.float32)]
+    if turn:
+        shapes += [jax.ShapeDtypeStruct(start.shape, jnp.float32) for start in light[:2]]
+    operands = [columns, *near, *far, *light]
     return pl.pallas_call(
         functools.partial(join_kernel, groups, width, turn, blocks),
-        out_shape=jax.ShapeDtypeStruct(shape, jnp.float32),
+        out_shape=shapes,
         in_specs=[pl.BlockSpec(memory_space=pltpu.VMEM)] * len(operands),
-        out_specs=pl.BlockSpec(memory_space=pltpu.VMEM),
-        scratch_shapes=[
-            pltpu.VMEM((share, colors, LANES), jnp.float32),
-            pltpu.VMEM((layers, colors, LANES), jnp.float32),
-            pltpu.VMEM((far[3].shape[0], colors, LANES), jnp.float32),
-        ],
+        out_specs=[pl.BlockSpec(memory_space=pltpu.VMEM)] * len(shapes),
+        scratch_shapes=[pltpu.VMEM((share, colors, LANES), jnp.float32)],
         compiler_params=pltpu.CompilerParams(vmem_limit_bytes=24 * MIB),
         cost_estimate=pl.CostEstimate(flops=0, bytes_accessed=0, transcendentals=0),
         name="join",
@@ -586,27 +589,27 @@
 
     blocks = count // 2
     ratio = step_x / step_z
-    *near, near_total = render_near(
+    *near, near_start, near_total = render_near(
         pieces[:blocks], table, colors, groups, width, bins, ratio, count)
     s, start, total = far_depths(pieces, near_total, sum_table, groups, width, bins)
     sums = [lax.ppermute(total, "gx", [(i, (i + hop) % size_x) for i in range(size_x)])
             for hop in range(1, size_x)]
 
     layers = depth * blocks
-    far = [*render_far(s, table, colors, bins, ratio, layers + 1), start]
-
-    def half_of(turn):
-        return join(columns, near, far, sums, groups, width, turn, blocks)
+    far = render_far(s, table, colors, bins, ratio, layers + 1)
+    other, *light = join(
+        columns, near, far, [near_start, start, *sums], groups, width, 1, blocks)
 
     share = steps // 2
     if share % groups == 0:
-        joined = exchange(half_of(1), "gz", 1)
-        both = jnp.stack([half_of(0), joined], axis=1)
+        joined = exchange(other, "gz", 1)
+        own, = join(columns, near, far, light, groups, width, 0, blocks)
+        both = jnp.stack([own, joined], axis=1)
         arrived = []
         for slot in range(count // 2):
             arrived.append(exchange(both[slot], "gz", 2 * slot) if slot else both[0])
         return unpack(arrived, groups, width)
-    halves = [half_of(0), half_of(1)]
+    halves = [*join(columns, near, far, light, groups, width, 0, blocks), other]
     even = me % 2 == 0
     image = jnp.stack([jnp.where(even, halves[0], halves[1]),
                        jnp.where(even, halves[1], halves[0])])

time: 67.6 us -> 66.1 us (0.978)
  starting transfers between devices: 25.4 us -> 22.2 us
  waiting for transfers between devices: 10.5 us -> 13.7 us
  Pallas kernels: 23.7 us -> 22.2 us
    ppermute x1, starting transfers between devices: 0.96 us -> 3.89 us  [local(): after = lax.ppermute(density[:1], 'gx', down)]
    ppermute x1, starting transfers between devices: 2.94 us -> 0.01 us  [local(): before = lax.ppermute(density[rows_x - 1:], 'gx', up)]
    ppermute x3, waiting for transfers between devices: 0.05 us -> 2.58 us  [local(): lax.ppermute(total, 'gx', [(i, (i + hop) % size_x) for i in range(size_x)])]
    ppermute x3, starting transfers between devices: 4.94 us -> 2.71 us  [local(): lax.ppermute(total, 'gx', [(i, (i + hop) % size_x) for i in range(size_x)])]
    pallas_call x2, Pallas kernels: 4.69 us -> 3.23 us  [join(): pl.pallas_call(functools.partial(join_kernel, groups, width, turn, blocks...]
    ppermute x11, starting transfers between devices: 16.6 us -> 15.6 us  [exchange(): return lax.ppermute(value, axis, pairs)]
    ppermute x1, waiting for transfers between devices: 0.01 us -> 0.92 us  [local(): before = lax.ppermute(density[rows_x - 1:], 'gx', up)]
  transfers between devices with their start and end apart: 16 -> 16, of which waited for: 4 -> 7; matrix products, arithmetic and copies ran while one was open for 6% -> 6% of each run, Pallas kernels for 25% -> 24%
where the time goes in v10:
time: 66.1 us; the launch traced here: 65.6 us
  starting transfers between devices  22.2 us (34%)
  Pallas kernels  22.2 us (34%)
  waiting for transfers between devices  13.7 us (21%)
  local copies, waits for them, and re-layouts  4.68 us (7%)
  other arithmetic  2.75 us (4%)
    ppermute x11, starting transfers between devices, exchange(): return lax.ppermute(value, axis, pairs)  15.6 us
    ppermute x11, waiting for transfers between devices, exchange(): return lax.ppermute(value, axis, pairs)  10.2 us
    pallas_call x1, Pallas kernels, render_near(): pl.pallas_call(functools.partial(near_kernel, groups, width, bins, ratio,...  6.29 us
    pallas_call x1, Pallas kernels, render_far(): pl.pallas_call(functools.partial(render_rows, bins, ratio), out_shape=(ja...  5.6 us
    ppermute x1, starting transfers between devices, local(): after = lax.ppermute(density[:1], 'gx', down)  3.89 us
    pallas_call x2, Pallas kernels, join(): pl.pallas_call(functools.partial(join_kernel, groups, width, turn, blocks...  3.23 us
    pallas_call x1, Pallas kernels, far_depths(): pl.pallas_call(functools.partial(depth_kernel, groups, width, bins, count...  3.03 us
    ppermute x3, starting transfers between devices, local(): lax.ppermute(total, 'gx', [(i, (i + hop) % size_x) for i in range(size_x)])  2.71 us
  transfers between devices with their start and end apart: 16, of which 7 were waited for; matrix products, arithmetic and copies ran while one was open for 6% of the time, Pallas kernels for 24%

profile of v10, /device:TPU:0, one launch (start us, length us, event | category | flops | bytes accessed | tf_op | source)
XLA Modules:
  0.0 65.6 jit_solution(17115064914663583957)
XLA Ops:
  0.0 0.7 %fusion.7 = (f32[1,8,256]{2,1,0:T(8,128)S(1)}, f32[1,8,256]{2,1,0:T(8,128)S(1)}) fusion(f32[128,8,256]{2,1,0:T(8,128)} %param.7), kind=kLoop, calls=%fused_computation.17 | loop fusion | bytes 32768 | tf_op jit(solution)/shard_map/slice | solution.py:574
  0.7 3.9 %collective-permute-start.1 = (f32[1,8,256]{2,1,0:T(8,128)S(1)}, f32[1,8,256]{2,1,0:T(8,128)S(1)}, u32[]{:S(2)}, u32[]{:S(2)}) collective-permute-start(f32[1,8,256]{2,1,0:T(8,128)S(1)} %get-tuple-element.67), channel_id=1, source_target_pairs={{8,0},{16,8},{24,16},{0,24},{9,1},{17,9},{25,17},{1,25},{10,2},{18... | collective-permute-start | bytes 24584 | tf_op jit(solution)/shard_map/ppermute | solution.py:574
  4.6 1.2 %copy-done = f32[128,8,256]{2,1,0:T(8,128)S(1)} copy-done((f32[128,8,256]{2,1,0:T(8,128)S(1)}, f32[128,8,256]{2,1,0:T(8,128)}, u32[]{:S(2)}) %copy-start) | copy-done | bytes 1048600
  5.8 2.4 %pack.1.packed_ref = f32[8,32,8,128]{3,2,1,0:T(8,128)S(1)} custom-call(f32[4,32,8,256]{3,2,1,0:T(8,128)S(1)} %bitcast.20), custom_call_target="tpu_custom_call" | custom-call | tf_op jit(solution)/shard_map/pack/pallas_call | solution.py:74
  8.2 0.9 %collective-permute-done.before_ref = f32[1,8,256]{2,1,0:T(8,128)S(1)} collective-permute-done((f32[1,8,256]{2,1,0:T(8,128)S(1)}, f32[1,8,256]{2,1,0:T(8,128)S(1)}, u32[]{:S(2)}, u32[]{:S(2)}) %collective-permute-start) | collective-permute-done | bytes 8224 | tf_op jit(solution)/shard_map/ppermute | solution.py:573
  9.4 1.6 %collective-permute-start.2 = (f32[33,8,128]{2,1,0:T(8,128)S(1)}, f32[33,8,128]{2,1,0:T(8,128)S(1)}, u32[]{:S(2)}, u32[]{:S(2)}) collective-permute-start(f32[33,8,128]{2,1,0:T(8,128)S(1)} %get-tuple-element.36), channel_id=1, source_target_pairs={{0,2},{1,3},{2,0},{3,1},{4,6},{5,7},{6,4},{7,5},{8,10},{9,11},{10,... | collective-permute-start | bytes 405512 | tf_op jit(solution)/shard_map/ppermute | solution.py:555
  11.0 0.6 collective-permute-start.3
  11.6 2.6 %collective-permute-start.5 = (f32[33,8,128]{2,1,0:T(8,128)S(1)}, f32[33,8,128]{2,1,0:T(8,128)S(1)}, u32[]{:S(2)}, u32[]{:S(2)}) collective-permute-start(f32[33,8,128]{2,1,0:T(8,128)S(1)} %get-tuple-element.48), channel_id=1, source_target_pairs={{0,4},{1,5},{2,6},{3,7},{4,0},{5,1},{6,2},{7,3},{8,12},{9,13},{10,... | collective-permute-start | bytes 405512 | tf_op jit(solution)/shard_map/ppermute | solution.py:555
  14.2 0.8 %collective-permute-done.2.refs_2_ = f32[33,8,128]{2,1,0:T(8,128)S(1)} collective-permute-done((f32[33,8,128]{2,1,0:T(8,128)S(1)}, f32[33,8,128]{2,1,0:T(8,128)S(1)}, u32[]{:S(2)}, u32[]{:S(2)}) %collective-permute-start.2) | collective-permute-done | bytes 135200 | tf_op jit(solution)/shard_map/ppermute | solution.py:555
  15.0 1.2 %slice.28 = s32[1]{0:T(128)} slice(s32[32]{0:T(128)} %param.8), slice={[31:32]} | slice | bytes 8 | tf_op jit(solution)/shard_map/jit(_roll_static)/slice | solution.py:539
  16.3 3.6 %collective-permute-done.4.refs_3_ = f32[33,8,128]{2,1,0:T(8,128)S(1)} collective-permute-done((f32[33,8,128]{2,1,0:T(8,128)S(1)}, f32[33,8,128]{2,1,0:T(8,128)S(1)}, u32[]{:S(2)}, u32[]{:S(2)}) %collective-permute-start.4) | collective-permute-done | bytes 135200 | tf_op jit(solution)/shard_map/ppermute | solution.py:555
  19.8 1.9 %collective-permute-start.7 = (f32[33,8,128]{2,1,0:T(8,128)S(1)}, f32[33,8,128]{2,1,0:T(8,128)S(1)}, u32[]{:S(2)}, u32[]{:S(2)}) collective-permute-start(f32[33,8,128]{2,1,0:T(8,128)S(1)} %get-tuple-element.52), channel_id=1, source_target_pairs={{0,6},{1,7},{2,4},{3,5},{4,2},{5,3},{6,0},{7,1},{8,14},{9,15},{10,... | collective-permute-start | bytes 405512 | tf_op jit(solution)/shard_map/ppermute | solution.py:555
  21.7 1.9 %collective-permute-start.8 = (f32[33,8,128]{2,1,0:T(8,128)S(1)}, f32[33,8,128]{2,1,0:T(8,128)S(1)}, u32[]{:S(2)}, u32[]{:S(2)}) collective-permute-start(f32[33,8,128]{2,1,0:T(8,128)S(1)} %get-tuple-element.54), channel_id=1, source_target_pairs={{0,7},{1,6},{2,5},{3,4},{4,3},{5,2},{6,1},{7,0},{8,15},{9,14},{10,... | collective-permute-start | bytes 405512 | tf_op jit(solution)/shard_map/ppermute | solution.py:555
  23.5 1.4 %add_bitcast_fusion = s32[1,32]{1,0:T(1,128)S(1)} fusion(s32[31]{0:T(128)} %bitcast.28, s32[1]{0:T(128)} %slice.28), kind=kLoop, calls=%fused_computation.16 | loop fusion | flops 32 | bytes 256 | tf_op jit(solution)/shard_map/stack | solution.py:539
  24.9 0.7 %pad_add_fusion.bins_ref = s32[2,32]{1,0:T(2,128)S(1)} fusion(s32[1,32]{1,0:T(1,128)S(1)} %add_bitcast_fusion, s32[1,32]{1,0:T(1,128)} %bitcast.29), kind=kLoop, calls=%fused_computation.15 | loop fusion | flops 64 | bytes 512 | tf_op jit(solution)/shard_map/stack | solution.py:539
  25.6 0.7 %pad_maximum_fusion.1 = f32[3,16]{1,0:T(4,128)S(1)} fusion(f32[1,16]{1,0:T(1,128)} %bitcast.25, f32[1,16]{1,0:T(1,128)} %bitcast.26, f32[1,16]{1,0:T(1,128)} %bitcast.27), kind=kLoop, calls=%fused_computation.14 | loop fusion | flops 96 | bytes 384 | tf_op jit(solution)/shard_map/stack | solution.py:587
  26.4 0.7 %copy-done.1 = f32[256,16]{0,1:T(8,128)S(1)} copy-done((f32[256,16]{0,1:T(8,128)S(1)}, f32[256,16]{0,1:T(8,128)}, u32[]{:S(2)}) %copy-start.1) | copy-done | bytes 16408
  27.1 0.7 %copy-done.2 = f32[256,16]{0,1:T(8,128)S(1)} copy-done((f32[256,16]{0,1:T(8,128)S(1)}, f32[256,16]{0,1:T(8,128)}, u32[]{:S(2)}) %copy-start.2) | copy-done | bytes 16408
  27.8 0.4 tables.1
  28.2 6.3 %render_near.1 = (f32[32,32,16,128]{3,2,1,0:T(8,128)S(1)}, f32[32,16,128]{2,1,0:T(8,128)S(1)}, f32[32,16,128]{2,1,0:T(8,128)S(1)}, f32[32,16,128]{2,1,0:T(8,128)S(1)}, f32[8,16,128]{2,1,0:T(8,128)S(1)}) custom-call(f32[33,8,128]{2,1,0:T(8,128)S(1)} %get-tuple-element.40.refs_0_, f32[33,8,128]{2,1,0:T(8,128)S(1)} %collective-permute-done.3.refs_1_, ...), custom_call_target="tpu_custom_call" | custom-call | tf_op jit(solution)/shard_map/render_near/pallas_call | solution.py:273
  34.6 3.0 %far_depths.1 = (f32[32,40,128]{2,1,0:T(8,128)S(1)}, f32[40,16,128]{2,1,0:T(8,128)S(1)}, f32[18,16,128]{2,1,0:T(8,128)S(1)}) custom-call(f32[33,8,128]{2,1,0:T(8,128)S(1)} %get-tuple-element.40.refs_0_, f32[33,8,128]{2,1,0:T(8,128)S(1)} %collective-permute-done.3.refs_1_, f32[33,8,128]{2,1,0:T(8,128)S(1)} %collective-permute-done.2.refs_2_, ...), custom_call_target="tpu_custom_call" | custom-call | tf_op jit(solution)/shard_map/far_depths/pallas_call | solution.py:342
  37.6 2.1 %collective-permute-start.11 = (f32[18,16,128]{2,1,0:T(8,128)S(1)}, f32[18,16,128]{2,1,0:T(8,128)S(1)}, u32[]{:S(2)}, u32[]{:S(2)}) collective-permute-start(f32[18,16,128]{2,1,0:T(8,128)S(1)} %get-tuple-element.63), channel_id=1, source_target_pairs={{0,24},{8,0},{16,8},{24,16},{1,25},{9,1},{17,9},{25,17},{2,26},{10... | collective-permute-start | bytes 442376 | tf_op jit(solution)/shard_map/ppermute | solution.py:595
  39.7 0.5 collective-permute-start.10
  40.3 5.6 %render_far.1 = (f32[32,33,16,128]{3,2,1,0:T(8,128)S(1)}, f32[32,16,128]{2,1,0:T(8,128)S(1)}, f32[32,16,128]{2,1,0:T(8,128)S(1)}) custom-call(f32[32,40,128]{2,1,0:T(8,128)S(1)} %get-tuple-element.57.s_ref, bf16[32,96]{1,0:T(8,128)(2,1)S(1)} %get-tuple-element.44.refs_4_.table_ref), custom_call_target="tpu_custom_call" | custom-call | flops 10000000000 | bytes 10000000 | tf_op jit(solution)/shard_map/render_far/pallas_call | solution.py:366
  45.9 2.6 %collective-permute-done.10.refs_9_ = f32[18,16,128]{2,1,0:T(8,128)S(1)} collective-permute-done((f32[18,16,128]{2,1,0:T(8,128)S(1)}, f32[18,16,128]{2,1,0:T(8,128)S(1)}, u32[]{:S(2)}, u32[]{:S(2)}) %collective-permute-start.10) | collective-permute-done | bytes 147488 | tf_op jit(solution)/shard_map/ppermute | solution.py:595
  48.5 2.1 %join.2 = (f32[4,4,16,128]{3,2,1,0:T(8,128)S(1)}, f32[32,16,128]{2,1,0:T(8,128)S(1)}, f32[40,16,128]{2,1,0:T(8,128)S(1)}) custom-call(f32[3,16,128]{2,1,0:T(8,128)S(1)} %broadcast_in_dim.2.columns_ref, f32[32,32,16,128]{3,2,1,0:T(8,128)S(1)} %get-tuple-element.45.refs_0_, f32[32,16,128]{2,1,0:T(8,128)S(1)} %get-tuple-element.46.refs_1_, ...), custom_call_target="tpu_custom_call" | custom-call | tf_op jit(solution)/shard_map/join/pallas_call | solution.py:469
  50.7 1.1 %join.3 = f32[4,4,16,128]{3,2,1,0:T(8,128)S(1)} custom-call(f32[3,16,128]{2,1,0:T(8,128)S(1)} %broadcast_in_dim.2.columns_ref, f32[32,32,16,128]{3,2,1,0:T(8,128)S(1)} %get-tuple-element.45.refs_0_, f32[32,16,128]{2,1,0:T(8,128)S(1)} %get-tuple-element.46.refs_1_, f32[32,16,128]{2,1,0:T(8,128)S(1)} %get-tuple-element.47.refs_2_, ...), custom_call_target="tpu_custom_call" | custom-call | tf_op jit(solution)/shard_map/join/pallas_call | solution.py:469
  52.1 1.9 %collective-permute-start.15 = (f32[2,4,16,128]{3,2,1,0:T(8,128)S(1)}, f32[2,4,16,128]{3,2,1,0:T(8,128)S(1)}, u32[]{:S(2)}, u32[]{:S(2)}) collective-permute-start(f32[2,4,16,128]{3,2,1,0:T(8,128)S(1)} %get-tuple-element.69), channel_id=1, source_target_pairs={{0,6},{1,7},{2,4},{3,5},{4,2},{5,3},{6,0},{7,1},{8,14},{9,15},{10,... | collective-permute-start | bytes 196616 | tf_op jit(solution)/shard_map/ppermute | solution.py:555
  54.0 4.7 %collective-permute-start.13 = (f32[2,4,16,128]{3,2,1,0:T(8,128)S(1)}, f32[2,4,16,128]{3,2,1,0:T(8,128)S(1)}, u32[]{:S(2)}, u32[]{:S(2)}) collective-permute-start(f32[2,4,16,128]{3,2,1,0:T(8,128)S(1)} %get-tuple-element.71), channel_id=1, source_target_pairs={{0,2},{1,3},{2,0},{3,1},{4,6},{5,7},{6,4},{7,5},{8,10},{9,11},{10,... | collective-permute-start | bytes 196616 | tf_op jit(solution)/shard_map/ppermute | solution.py:555
  59.1 1.9 %collective-permute-done.13.refs_1_ = f32[2,4,16,128]{3,2,1,0:T(8,128)S(1)} collective-permute-done((f32[2,4,16,128]{3,2,1,0:T(8,128)S(1)}, f32[2,4,16,128]{3,2,1,0:T(8,128)S(1)}, u32[]{:S(2)}, u32[]{:S(2)}) %collective-permute-start.13) | collective-permute-done | bytes 65568 | tf_op jit(solution)/shard_map/ppermute | solution.py:555
  61.0 3.6 %collective-permute-done.14.refs_2_ = f32[2,4,16,128]{3,2,1,0:T(8,128)S(1)} collective-permute-done((f32[2,4,16,128]{3,2,1,0:T(8,128)S(1)}, f32[2,4,16,128]{3,2,1,0:T(8,128)S(1)}, u32[]{:S(2)}, u32[]{:S(2)}) %collective-permute-start.14) | collective-permute-done | bytes 65568 | tf_op jit(solution)/shard_map/ppermute | solution.py:555
  64.6 1.0 %unpack.1 = f32[16,16,256]{2,1,0:T(8,128)} custom-call(f32[2,4,16,128]{3,2,1,0:T(8,128)S(1)} %get-tuple-element.70.refs_0_, f32[2,4,16,128]{3,2,1,0:T(8,128)S(1)} %collective-permute-done.13.refs_1_, f32[2,4,16,128]{3,2,1,0:T(8,128)S(1)} %collective-permute-done.14.refs_2_, f32[2,4,16,128]{3,2,1,0:T(8,128)S(1)} %collective-permute-done.15.refs_3_), custom_call_target="tpu_custom_call" | custom-call | tf_op jit(solution)/shard_map/unpack/pallas_call | solution.py:498
  (22 shorter events, 1.1 us)
Async XLA Ops:
  0.7 7.5 %collective-permute-start.1 = (f32[1,8,256]{2,1,0:T(8,128)S(1)}, f32[1,8,256]{2,1,0:T(8,128)S(1)}, u32[]{:S(2)}, u32[]{:S(2)}) collective-permute-start(f32[1,8,256]{2,1,0:T(8,128)S(1)} %get-tuple-element.67), channel_id=1, source_target_pairs={{8,0},{16,8},{24,16},{0,24},{9,1},{17,9},{25,17},{1,25},{10,2},{18... | collective-permute-start | bytes 24584 | tf_op jit(solution)/shard_map/ppermute | solution.py:574
  4.6 4.5 %collective-permute-start = (f32[1,8,256]{2,1,0:T(8,128)S(1)}, f32[1,8,256]{2,1,0:T(8,128)S(1)}, u32[]{:S(2)}, u32[]{:S(2)}) collective-permute-start(f32[1,8,256]{2,1,0:T(8,128)S(1)} %get-tuple-element.68), channel_id=1, source_target_pairs={{0,8},{8,16},{16,24},{24,0},{1,9},{9,17},{17,25},{25,1},{2,10},{10... | collective-permute-start | bytes 24584 | tf_op jit(solution)/shard_map/ppermute | solution.py:573
  4.6 1.2 %copy-start = (f32[128,8,256]{2,1,0:T(8,128)S(1)}, f32[128,8,256]{2,1,0:T(8,128)}, u32[]{:S(2)}) copy-start(f32[128,8,256]{2,1,0:T(8,128)} %param.7) | copy-start | bytes 3145732
  9.4 5.6 %collective-permute-start.2 = (f32[33,8,128]{2,1,0:T(8,128)S(1)}, f32[33,8,128]{2,1,0:T(8,128)S(1)}, u32[]{:S(2)}, u32[]{:S(2)}) collective-permute-start(f32[33,8,128]{2,1,0:T(8,128)S(1)} %get-tuple-element.36), channel_id=1, source_target_pairs={{0,2},{1,3},{2,0},{3,1},{4,6},{5,7},{6,4},{7,5},{8,10},{9,11},{10,... | collective-permute-start | bytes 405512 | tf_op jit(solution)/shard_map/ppermute | solution.py:555
  11.0 8.8 %collective-permute-start.4 = (f32[33,8,128]{2,1,0:T(8,128)S(1)}, f32[33,8,128]{2,1,0:T(8,128)S(1)}, u32[]{:S(2)}, u32[]{:S(2)}) collective-permute-start(f32[33,8,128]{2,1,0:T(8,128)S(1)} %get-tuple-element.42), channel_id=1, source_target_pairs={{0,3},{1,2},{2,1},{3,0},{4,7},{5,6},{6,5},{7,4},{8,11},{9,10},{10,... | collective-permute-start | bytes 405512 | tf_op jit(solution)/shard_map/ppermute | solution.py:555
  11.0 17.2 %collective-permute-start.3 = (f32[33,8,128]{2,1,0:T(8,128)S(1)}, f32[33,8,128]{2,1,0:T(8,128)S(1)}, u32[]{:S(2)}, u32[]{:S(2)}) collective-permute-start(f32[33,8,128]{2,1,0:T(8,128)S(1)} %get-tuple-element.41), channel_id=1, source_target_pairs={{0,1},{1,0},{2,3},{3,2},{4,5},{5,4},{6,7},{7,6},{8,9},{9,8},{10,11... | collective-permute-start | bytes 405512 | tf_op jit(solution)/shard_map/ppermute | solution.py:555
  11.6 22.9 %collective-permute-start.5 = (f32[33,8,128]{2,1,0:T(8,128)S(1)}, f32[33,8,128]{2,1,0:T(8,128)S(1)}, u32[]{:S(2)}, u32[]{:S(2)}) collective-permute-start(f32[33,8,128]{2,1,0:T(8,128)S(1)} %get-tuple-element.48), channel_id=1, source_target_pairs={{0,4},{1,5},{2,6},{3,7},{4,0},{5,1},{6,2},{7,3},{8,12},{9,13},{10,... | collective-permute-start | bytes 405512 | tf_op jit(solution)/shard_map/ppermute | solution.py:555
  16.2 18.3 %collective-permute-start.6 = (f32[33,8,128]{2,1,0:T(8,128)S(1)}, f32[33,8,128]{2,1,0:T(8,128)S(1)}, u32[]{:S(2)}, u32[]{:S(2)}) collective-permute-start(f32[33,8,128]{2,1,0:T(8,128)S(1)} %get-tuple-element.50), channel_id=1, source_target_pairs={{0,5},{1,4},{2,7},{3,6},{4,1},{5,0},{6,3},{7,2},{8,13},{9,12},{10,... | collective-permute-start | bytes 405512 | tf_op jit(solution)/shard_map/ppermute | solution.py:555
  19.8 14.7 %collective-permute-start.7 = (f32[33,8,128]{2,1,0:T(8,128)S(1)}, f32[33,8,128]{2,1,0:T(8,128)S(1)}, u32[]{:S(2)}, u32[]{:S(2)}) collective-permute-start(f32[33,8,128]{2,1,0:T(8,128)S(1)} %get-tuple-element.52), channel_id=1, source_target_pairs={{0,6},{1,7},{2,4},{3,5},{4,2},{5,3},{6,0},{7,1},{8,14},{9,15},{10,... | collective-permute-start | bytes 405512 | tf_op jit(solution)/shard_map/ppermute | solution.py:555
  21.7 12.9 %collective-permute-start.8 = (f32[33,8,128]{2,1,0:T(8,128)S(1)}, f32[33,8,128]{2,1,0:T(8,128)S(1)}, u32[]{:S(2)}, u32[]{:S(2)}) collective-permute-start(f32[33,8,128]{2,1,0:T(8,128)S(1)} %get-tuple-element.54), channel_id=1, source_target_pairs={{0,7},{1,6},{2,5},{3,4},{4,3},{5,2},{6,1},{7,0},{8,15},{9,14},{10,... | collective-permute-start | bytes 405512 | tf_op jit(solution)/shard_map/ppermute | solution.py:555
  26.4 0.7 %copy-start.1 = (f32[256,16]{0,1:T(8,128)S(1)}, f32[256,16]{0,1:T(8,128)}, u32[]{:S(2)}) copy-start(f32[256,16]{0,1:T(8,128)} %param.9) | copy-start | bytes 49156
  27.1 0.7 %copy-start.2 = (f32[256,16]{0,1:T(8,128)S(1)}, f32[256,16]{0,1:T(8,128)}, u32[]{:S(2)}) copy-start(f32[256,16]{0,1:T(8,128)} %param.10) | copy-start | bytes 49156
  37.6 8.3 %collective-permute-start.11 = (f32[18,16,128]{2,1,0:T(8,128)S(1)}, f32[18,16,128]{2,1,0:T(8,128)S(1)}, u32[]{:S(2)}, u32[]{:S(2)}) collective-permute-start(f32[18,16,128]{2,1,0:T(8,128)S(1)} %get-tuple-element.63), channel_id=1, source_target_pairs={{0,24},{8,0},{16,8},{24,16},{1,25},{9,1},{17,9},{25,17},{2,26},{10... | collective-permute-start | bytes 442376 | tf_op jit(solution)/shard_map/ppermute | solution.py:595
  39.7 8.8 %collective-permute-start.10 = (f32[18,16,128]{2,1,0:T(8,128)S(1)}, f32[18,16,128]{2,1,0:T(8,128)S(1)}, u32[]{:S(2)}, u32[]{:S(2)}) collective-permute-start(f32[18,16,128]{2,1,0:T(8,128)S(1)} %get-tuple-element.63), channel_id=1, source_target_pairs={{0,16},{8,24},{16,0},{24,8},{1,17},{9,25},{17,1},{25,9},{2,18},{10... | collective-permute-start | bytes 442376 | tf_op jit(solution)/shard_map/ppermute | solution.py:595
  40.2 8.3 %collective-permute-start.9 = (f32[18,16,128]{2,1,0:T(8,128)S(1)}, f32[18,16,128]{2,1,0:T(8,128)S(1)}, u32[]{:S(2)}, u32[]{:S(2)}) collective-permute-start(f32[18,16,128]{2,1,0:T(8,128)S(1)} %get-tuple-element.63), channel_id=1, source_target_pairs={{0,8},{8,16},{16,24},{24,0},{1,9},{9,17},{17,25},{25,1},{2,10},{10... | collective-permute-start | bytes 442376 | tf_op jit(solution)/shard_map/ppermute | solution.py:595
  50.6 1.4 %collective-permute-start.12 = (f32[4,4,16,128]{3,2,1,0:T(8,128)S(1)}, f32[4,4,16,128]{3,2,1,0:T(8,128)S(1)}, u32[]{:S(2)}, u32[]{:S(2)}) collective-permute-start(f32[4,4,16,128]{3,2,1,0:T(8,128)S(1)} %get-tuple-element.66), channel_id=1, source_target_pairs={{0,1},{1,0},{2,3},{3,2},{4,5},{5,4},{6,7},{7,6},{8,9},{9,8},{10,11... | collective-permute-start | bytes 393224 | tf_op jit(solution)/shard_map/ppermute | solution.py:555
  52.1 7.0 %collective-permute-start.15 = (f32[2,4,16,128]{3,2,1,0:T(8,128)S(1)}, f32[2,4,16,128]{3,2,1,0:T(8,128)S(1)}, u32[]{:S(2)}, u32[]{:S(2)}) collective-permute-start(f32[2,4,16,128]{3,2,1,0:T(8,128)S(1)} %get-tuple-element.69), channel_id=1, source_target_pairs={{0,6},{1,7},{2,4},{3,5},{4,2},{5,3},{6,0},{7,1},{8,14},{9,15},{10,... | collective-permute-start | bytes 196616 | tf_op jit(solution)/shard_map/ppermute | solution.py:555
  54.0 6.9 %collective-permute-start.13 = (f32[2,4,16,128]{3,2,1,0:T(8,128)S(1)}, f32[2,4,16,128]{3,2,1,0:T(8,128)S(1)}, u32[]{:S(2)}, u32[]{:S(2)}) collective-permute-start(f32[2,4,16,128]{3,2,1,0:T(8,128)S(1)} %get-tuple-element.71), channel_id=1, source_target_pairs={{0,2},{1,3},{2,0},{3,1},{4,6},{5,7},{6,4},{7,5},{8,10},{9,11},{10,... | collective-permute-start | bytes 196616 | tf_op jit(solution)/shard_map/ppermute | solution.py:555
  58.7 5.9 %collective-permute-start.14 = (f32[2,4,16,128]{3,2,1,0:T(8,128)S(1)}, f32[2,4,16,128]{3,2,1,0:T(8,128)S(1)}, u32[]{:S(2)}, u32[]{:S(2)}) collective-permute-start(f32[2,4,16,128]{3,2,1,0:T(8,128)S(1)} %get-tuple-element.72), channel_id=1, source_target_pairs={{0,4},{1,5},{2,6},{3,7},{4,0},{5,1},{6,2},{7,3},{8,12},{9,13},{10,... | collective-permute-start | bytes 196616 | tf_op jit(solution)/shard_map/ppermute | solution.py:555

commit v11 on v10

--- a/solution.py
+++ b/solution.py
@@ -28,8 +28,13 @@
                 continue
             a, b = tiles[first], tiles[first | bit]
             axis = a.ndim - 1
-            tiles[first] = jnp.where(upper, pltpu.roll(b, shift, axis), a)
-            tiles[first | bit] = jnp.where(upper, b, pltpu.roll(a, LANES - shift, axis))
+            if 2 * shift == LANES:
+                moved = pltpu.roll(jnp.where(upper, a, b), shift, axis)
+                tiles[first] = jnp.where(upper, moved, a)
+                tiles[first | bit] = jnp.where(upper, b, moved)
+            else:
+                tiles[first] = jnp.where(upper, pltpu.roll(b, shift, axis), a)
+                tiles[first | bit] = jnp.where(upper, b, pltpu.roll(a, LANES - shift, axis))
         bit *= 2
     return tiles
 
@@ -51,18 +56,26 @@
     return out
 
 
-def pack_kernel(groups, width, x_ref, out_ref):
+def pack_kernel(groups, width, x_ref, out_ref, blurred):
     tile_count = x_ref.shape[3] // LANES
-    steps, depth = x_ref.shape[1], x_ref.shape[2]
+    steps, depth, width_y = x_ref.shape[1:]
+    row = lax.broadcasted_iota(jnp.int32, (width_y, width_y), 0)
+    column = lax.broadcasted_iota(jnp.int32, (width_y, width_y), 1)
+    weights = jnp.maximum(2 - jnp.abs(row - column), 0).astype(jnp.float32).astype(jnp.bfloat16)
+    for group in range(groups):
+        x = x_ref[group].reshape(steps * depth, width_y)
+        coarse = x.astype(jnp.bfloat16)
+        fine = (x - coarse.astype(jnp.float32)).astype(jnp.bfloat16)
+        blurred[group] = (jnp.dot(coarse, weights, preferred_element_type=jnp.float32)
+                          + jnp.dot(fine, weights, preferred_element_type=jnp.float32)
+                          ).reshape(steps, depth, width_y)
     size = 4
-    lane = lax.broadcasted_iota(jnp.int32, (size, depth, LANES), 2)
     for first in range(0, steps, size):
         place = pl.ds(first, size)
-        wide = blur_rows(
-            [[x_ref[group, place, :, t * LANES:(t + 1) * LANES] for t in range(tile_count)]
-             for group in range(groups)], lane)
         for t in range(tile_count):
-            swapped = swap_groups([wide[group][t] for group in range(groups)], groups, width)
+            swapped = swap_groups(
+                [blurred[group, place, :, t * LANES:(t + 1) * LANES] for group in range(groups)],
+                groups, width)
             for group in range(groups):
                 out_ref[t * groups + group, place] = swapped[group]
 
@@ -76,6 +89,7 @@
         out_shape=jax.ShapeDtypeStruct((blocks, steps, depth, LANES), jnp.float32),
         in_specs=[pl.BlockSpec(memory_space=pltpu.VMEM)],
         out_specs=pl.BlockSpec(memory_space=pltpu.VMEM),
+        scratch_shapes=[pltpu.VMEM((groups, steps, depth, width_y), jnp.float32)],
         compiler_params=pltpu.CompilerParams(vmem_limit_bytes=8 * MIB),
         name="pack",
     )(x.reshape(groups, steps, depth, width_y))
@@ -396,12 +410,11 @@
         packed = jnp.zeros((colors, LANES), jnp.float32)
         for hop, ref in enumerate(before_refs, 1):
             packed = packed + jnp.where(position >= hop, ref[offset + chunk], 0.0)
+        moved = [packed] + [pltpu.roll(packed, k * width, 1) for k in range(1, groups)]
         for k in range(groups):
-            value = jnp.where(group == k, packed, 0.0)
-            shift = 1
-            while shift < groups:
-                value = value + pltpu.roll(value, shift * width, 1)
-                shift *= 2
+            value = moved[-k % groups]
+            for place in range(1, groups):
+                value = jnp.where(group == place, moved[(place - k) % groups], value)
             z = chunk * groups + k
             light[z] = jnp.exp2(start_ref[z] + value)
 

time: 66.1 us -> 63.9 us (0.967)
  Pallas kernels: 22.2 us -> 20 us
    ppermute x1, waiting for transfers between devices: 0.92 us -> 2.56 us  [local(): before = lax.ppermute(density[rows_x - 1:], 'gx', up)]
    pallas_call x1, Pallas kernels: 2.39 us -> 0.75 us  [pack(): pl.pallas_call(functools.partial(pack_kernel, groups, width), out_shape=j...]
    ppermute x3, waiting for transfers between devices: 2.58 us -> 1.07 us  [local(): lax.ppermute(total, 'gx', [(i, (i + hop) % size_x) for i in range(size_x)])]
  transfers between devices with their start and end apart: 16 -> 16, of which waited for: 7 -> 7; matrix products, arithmetic and copies ran while one was open for 6% -> 6% of each run, Pallas kernels for 24% -> 22%
where the time goes in v11:
time: 63.9 us; the launch traced here: 63.4 us
  starting transfers between devices  22.1 us (35%)
  Pallas kernels  20 us (31%)
  waiting for transfers between devices  13.8 us (22%)
  local copies, waits for them, and re-layouts  4.68 us (7%)
  other arithmetic  2.75 us (4%)
    ppermute x11, starting transfers between devices, exchange(): return lax.ppermute(value, axis, pairs)  15.6 us
    ppermute x11, waiting for transfers between devices, exchange(): return lax.ppermute(value, axis, pairs)  10.2 us
    pallas_call x1, Pallas kernels, render_near(): pl.pallas_call(functools.partial(near_kernel, groups, width, bins, ratio,...  6.28 us
    pallas_call x1, Pallas kernels, render_far(): pl.pallas_call(functools.partial(render_rows, bins, ratio), out_shape=(ja...  5.61 us
    ppermute x1, starting transfers between devices, local(): after = lax.ppermute(density[:1], 'gx', down)  3.89 us
    pallas_call x1, Pallas kernels, far_depths(): pl.pallas_call(functools.partial(depth_kernel, groups, width, bins, count...  3.03 us
    pallas_call x2, Pallas kernels, join(): pl.pallas_call(functools.partial(join_kernel, groups, width, turn, blocks...  2.77 us
    unnamed x6, local copies, waits for them, and re-layouts  2.66 us
  transfers between devices with their start and end apart: 16, of which 7 were waited for; matrix products, arithmetic and copies ran while one was open for 6% of the time, Pallas kernels for 22%

profile of v11, /device:TPU:0, one launch (start us, length us, event | category | flops | bytes accessed | tf_op | source)
XLA Modules:
  0.0 63.4 jit_solution(1014007569237216819)
XLA Ops:
  0.0 0.7 %fusion.7 = (f32[1,8,256]{2,1,0:T(8,128)S(1)}, f32[1,8,256]{2,1,0:T(8,128)S(1)}) fusion(f32[128,8,256]{2,1,0:T(8,128)} %param.7), kind=kLoop, calls=%fused_computation.17 | loop fusion | bytes 32768 | tf_op jit(solution)/shard_map/slice | solution.py:587
  0.7 3.9 %collective-permute-start.1 = (f32[1,8,256]{2,1,0:T(8,128)S(1)}, f32[1,8,256]{2,1,0:T(8,128)S(1)}, u32[]{:S(2)}, u32[]{:S(2)}) collective-permute-start(f32[1,8,256]{2,1,0:T(8,128)S(1)} %get-tuple-element.67), channel_id=1, source_target_pairs={{8,0},{16,8},{24,16},{0,24},{9,1},{17,9},{25,17},{1,25},{10,2},{18... | collective-permute-start | bytes 24584 | tf_op jit(solution)/shard_map/ppermute | solution.py:587
  4.6 1.2 %copy-done = f32[128,8,256]{2,1,0:T(8,128)S(1)} copy-done((f32[128,8,256]{2,1,0:T(8,128)S(1)}, f32[128,8,256]{2,1,0:T(8,128)}, u32[]{:S(2)}) %copy-start) | copy-done | bytes 1048600
  5.8 0.7 %pack.1.packed_ref = f32[8,32,8,128]{3,2,1,0:T(8,128)S(1)} custom-call(f32[4,32,8,256]{3,2,1,0:T(8,128)S(1)} %bitcast.20), custom_call_target="tpu_custom_call" | custom-call | tf_op jit(solution)/shard_map/pack/pallas_call | solution.py:87
  6.6 2.6 %collective-permute-done.before_ref = f32[1,8,256]{2,1,0:T(8,128)S(1)} collective-permute-done((f32[1,8,256]{2,1,0:T(8,128)S(1)}, f32[1,8,256]{2,1,0:T(8,128)S(1)}, u32[]{:S(2)}, u32[]{:S(2)}) %collective-permute-start) | collective-permute-done | bytes 8224 | tf_op jit(solution)/shard_map/ppermute | solution.py:586
  9.4 1.6 %collective-permute-start.2 = (f32[33,8,128]{2,1,0:T(8,128)S(1)}, f32[33,8,128]{2,1,0:T(8,128)S(1)}, u32[]{:S(2)}, u32[]{:S(2)}) collective-permute-start(f32[33,8,128]{2,1,0:T(8,128)S(1)} %get-tuple-element.36), channel_id=1, source_target_pairs={{0,2},{1,3},{2,0},{3,1},{4,6},{5,7},{6,4},{7,5},{8,10},{9,11},{10,... | collective-permute-start | bytes 405512 | tf_op jit(solution)/shard_map/ppermute | solution.py:568
  11.0 0.6 collective-permute-start.3
  11.6 2.6 %collective-permute-start.5 = (f32[33,8,128]{2,1,0:T(8,128)S(1)}, f32[33,8,128]{2,1,0:T(8,128)S(1)}, u32[]{:S(2)}, u32[]{:S(2)}) collective-permute-start(f32[33,8,128]{2,1,0:T(8,128)S(1)} %get-tuple-element.48), channel_id=1, source_target_pairs={{0,4},{1,5},{2,6},{3,7},{4,0},{5,1},{6,2},{7,3},{8,12},{9,13},{10,... | collective-permute-start | bytes 405512 | tf_op jit(solution)/shard_map/ppermute | solution.py:568
  14.2 0.8 %collective-permute-done.2.refs_2_ = f32[33,8,128]{2,1,0:T(8,128)S(1)} collective-permute-done((f32[33,8,128]{2,1,0:T(8,128)S(1)}, f32[33,8,128]{2,1,0:T(8,128)S(1)}, u32[]{:S(2)}, u32[]{:S(2)}) %collective-permute-start.2) | collective-permute-done | bytes 135200 | tf_op jit(solution)/shard_map/ppermute | solution.py:568
  15.0 1.2 %slice.28 = s32[1]{0:T(128)} slice(s32[32]{0:T(128)} %param.8), slice={[31:32]} | slice | bytes 8 | tf_op jit(solution)/shard_map/jit(_roll_static)/slice | solution.py:552
  16.2 3.6 %collective-permute-done.4.refs_3_ = f32[33,8,128]{2,1,0:T(8,128)S(1)} collective-permute-done((f32[33,8,128]{2,1,0:T(8,128)S(1)}, f32[33,8,128]{2,1,0:T(8,128)S(1)}, u32[]{:S(2)}, u32[]{:S(2)}) %collective-permute-start.4) | collective-permute-done | bytes 135200 | tf_op jit(solution)/shard_map/ppermute | solution.py:568
  19.8 1.9 %collective-permute-start.7 = (f32[33,8,128]{2,1,0:T(8,128)S(1)}, f32[33,8,128]{2,1,0:T(8,128)S(1)}, u32[]{:S(2)}, u32[]{:S(2)}) collective-permute-start(f32[33,8,128]{2,1,0:T(8,128)S(1)} %get-tuple-element.52), channel_id=1, source_target_pairs={{0,6},{1,7},{2,4},{3,5},{4,2},{5,3},{6,0},{7,1},{8,14},{9,15},{10,... | collective-permute-start | bytes 405512 | tf_op jit(solution)/shard_map/ppermute | solution.py:568
  21.7 1.9 %collective-permute-start.8 = (f32[33,8,128]{2,1,0:T(8,128)S(1)}, f32[33,8,128]{2,1,0:T(8,128)S(1)}, u32[]{:S(2)}, u32[]{:S(2)}) collective-permute-start(f32[33,8,128]{2,1,0:T(8,128)S(1)} %get-tuple-element.54), channel_id=1, source_target_pairs={{0,7},{1,6},{2,5},{3,4},{4,3},{5,2},{6,1},{7,0},{8,15},{9,14},{10,... | collective-permute-start | bytes 405512 | tf_op jit(solution)/shard_map/ppermute | solution.py:568
  23.5 1.4 %add_bitcast_fusion = s32[1,32]{1,0:T(1,128)S(1)} fusion(s32[31]{0:T(128)} %bitcast.28, s32[1]{0:T(128)} %slice.28), kind=kLoop, calls=%fused_computation.16 | loop fusion | flops 32 | bytes 256 | tf_op jit(solution)/shard_map/stack | solution.py:552
  24.9 0.7 %pad_add_fusion.bins_ref = s32[2,32]{1,0:T(2,128)S(1)} fusion(s32[1,32]{1,0:T(1,128)S(1)} %add_bitcast_fusion, s32[1,32]{1,0:T(1,128)} %bitcast.29), kind=kLoop, calls=%fused_computation.15 | loop fusion | flops 64 | bytes 512 | tf_op jit(solution)/shard_map/stack | solution.py:552
  25.6 0.7 %pad_maximum_fusion.1 = f32[3,16]{1,0:T(4,128)S(1)} fusion(f32[1,16]{1,0:T(1,128)} %bitcast.25, f32[1,16]{1,0:T(1,128)} %bitcast.26, f32[1,16]{1,0:T(1,128)} %bitcast.27), kind=kLoop, calls=%fused_computation.14 | loop fusion | flops 96 | bytes 384 | tf_op jit(solution)/shard_map/stack | solution.py:600
  26.4 0.7 %copy-done.1 = f32[256,16]{0,1:T(8,128)S(1)} copy-done((f32[256,16]{0,1:T(8,128)S(1)}, f32[256,16]{0,1:T(8,128)}, u32[]{:S(2)}) %copy-start.1) | copy-done | bytes 16408
  27.1 0.7 %copy-done.2 = f32[256,16]{0,1:T(8,128)S(1)} copy-done((f32[256,16]{0,1:T(8,128)S(1)}, f32[256,16]{0,1:T(8,128)}, u32[]{:S(2)}) %copy-start.2) | copy-done | bytes 16408
  27.8 0.4 tables.1
  28.2 6.3 %render_near.1 = (f32[32,32,16,128]{3,2,1,0:T(8,128)S(1)}, f32[32,16,128]{2,1,0:T(8,128)S(1)}, f32[32,16,128]{2,1,0:T(8,128)S(1)}, f32[32,16,128]{2,1,0:T(8,128)S(1)}, f32[8,16,128]{2,1,0:T(8,128)S(1)}) custom-call(f32[33,8,128]{2,1,0:T(8,128)S(1)} %get-tuple-element.40.refs_0_, f32[33,8,128]{2,1,0:T(8,128)S(1)} %collective-permute-done.3.refs_1_, ...), custom_call_target="tpu_custom_call" | custom-call | tf_op jit(solution)/shard_map/render_near/pallas_call | solution.py:287
  34.6 3.0 %far_depths.1 = (f32[32,40,128]{2,1,0:T(8,128)S(1)}, f32[40,16,128]{2,1,0:T(8,128)S(1)}, f32[18,16,128]{2,1,0:T(8,128)S(1)}) custom-call(f32[33,8,128]{2,1,0:T(8,128)S(1)} %get-tuple-element.40.refs_0_, f32[33,8,128]{2,1,0:T(8,128)S(1)} %collective-permute-done.3.refs_1_, f32[33,8,128]{2,1,0:T(8,128)S(1)} %collective-permute-done.2.refs_2_, ...), custom_call_target="tpu_custom_call" | custom-call | tf_op jit(solution)/shard_map/far_depths/pallas_call | solution.py:356
  38.0 0.5 collective-permute-start.10
  38.5 1.6 %collective-permute-start.9 = (f32[18,16,128]{2,1,0:T(8,128)S(1)}, f32[18,16,128]{2,1,0:T(8,128)S(1)}, u32[]{:S(2)}, u32[]{:S(2)}) collective-permute-start(f32[18,16,128]{2,1,0:T(8,128)S(1)} %get-tuple-element.63), channel_id=1, source_target_pairs={{0,8},{8,16},{16,24},{24,0},{1,9},{9,17},{17,25},{25,1},{2,10},{10... | collective-permute-start | bytes 442376 | tf_op jit(solution)/shard_map/ppermute | solution.py:608
  40.2 5.6 %render_far.1 = (f32[32,33,16,128]{3,2,1,0:T(8,128)S(1)}, f32[32,16,128]{2,1,0:T(8,128)S(1)}, f32[32,16,128]{2,1,0:T(8,128)S(1)}) custom-call(f32[32,40,128]{2,1,0:T(8,128)S(1)} %get-tuple-element.57.s_ref, bf16[32,96]{1,0:T(8,128)(2,1)S(1)} %get-tuple-element.44.refs_4_.table_ref), custom_call_target="tpu_custom_call" | custom-call | flops 10000000000 | bytes 10000000 | tf_op jit(solution)/shard_map/render_far/pallas_call | solution.py:380
  45.8 1.1 %collective-permute-done.10.refs_9_ = f32[18,16,128]{2,1,0:T(8,128)S(1)} collective-permute-done((f32[18,16,128]{2,1,0:T(8,128)S(1)}, f32[18,16,128]{2,1,0:T(8,128)S(1)}, u32[]{:S(2)}, u32[]{:S(2)}) %collective-permute-start.10) | collective-permute-done | bytes 147488 | tf_op jit(solution)/shard_map/ppermute | solution.py:608
  46.9 1.7 %join.2 = (f32[4,4,16,128]{3,2,1,0:T(8,128)S(1)}, f32[32,16,128]{2,1,0:T(8,128)S(1)}, f32[40,16,128]{2,1,0:T(8,128)S(1)}) custom-call(f32[3,16,128]{2,1,0:T(8,128)S(1)} %broadcast_in_dim.2.columns_ref, f32[32,32,16,128]{3,2,1,0:T(8,128)S(1)} %get-tuple-element.45.refs_0_, f32[32,16,128]{2,1,0:T(8,128)S(1)} %get-tuple-element.46.refs_1_, ...), custom_call_target="tpu_custom_call" | custom-call | tf_op jit(solution)/shard_map/join/pallas_call | solution.py:482
  48.6 1.1 %join.3 = f32[4,4,16,128]{3,2,1,0:T(8,128)S(1)} custom-call(f32[3,16,128]{2,1,0:T(8,128)S(1)} %broadcast_in_dim.2.columns_ref, f32[32,32,16,128]{3,2,1,0:T(8,128)S(1)} %get-tuple-element.45.refs_0_, f32[32,16,128]{2,1,0:T(8,128)S(1)} %get-tuple-element.46.refs_1_, f32[32,16,128]{2,1,0:T(8,128)S(1)} %get-tuple-element.47.refs_2_, ...), custom_call_target="tpu_custom_call" | custom-call | tf_op jit(solution)/shard_map/join/pallas_call | solution.py:482
  50.0 2.0 %collective-permute-start.15 = (f32[2,4,16,128]{3,2,1,0:T(8,128)S(1)}, f32[2,4,16,128]{3,2,1,0:T(8,128)S(1)}, u32[]{:S(2)}, u32[]{:S(2)}) collective-permute-start(f32[2,4,16,128]{3,2,1,0:T(8,128)S(1)} %get-tuple-element.69), channel_id=1, source_target_pairs={{0,6},{1,7},{2,4},{3,5},{4,2},{5,3},{6,0},{7,1},{8,14},{9,15},{10,... | collective-permute-start | bytes 196616 | tf_op jit(solution)/shard_map/ppermute | solution.py:568
  52.0 4.7 %collective-permute-start.13 = (f32[2,4,16,128]{3,2,1,0:T(8,128)S(1)}, f32[2,4,16,128]{3,2,1,0:T(8,128)S(1)}, u32[]{:S(2)}, u32[]{:S(2)}) collective-permute-start(f32[2,4,16,128]{3,2,1,0:T(8,128)S(1)} %get-tuple-element.71), channel_id=1, source_target_pairs={{0,2},{1,3},{2,0},{3,1},{4,6},{5,7},{6,4},{7,5},{8,10},{9,11},{10,... | collective-permute-start | bytes 196616 | tf_op jit(solution)/shard_map/ppermute | solution.py:568
  57.0 1.9 %collective-permute-done.13.refs_1_ = f32[2,4,16,128]{3,2,1,0:T(8,128)S(1)} collective-permute-done((f32[2,4,16,128]{3,2,1,0:T(8,128)S(1)}, f32[2,4,16,128]{3,2,1,0:T(8,128)S(1)}, u32[]{:S(2)}, u32[]{:S(2)}) %collective-permute-start.13) | collective-permute-done | bytes 65568 | tf_op jit(solution)/shard_map/ppermute | solution.py:568
  58.9 3.6 %collective-permute-done.14.refs_2_ = f32[2,4,16,128]{3,2,1,0:T(8,128)S(1)} collective-permute-done((f32[2,4,16,128]{3,2,1,0:T(8,128)S(1)}, f32[2,4,16,128]{3,2,1,0:T(8,128)S(1)}, u32[]{:S(2)}, u32[]{:S(2)}) %collective-permute-start.14) | collective-permute-done | bytes 65568 | tf_op jit(solution)/shard_map/ppermute | solution.py:568
  62.5 0.9 %unpack.1 = f32[16,16,256]{2,1,0:T(8,128)} custom-call(f32[2,4,16,128]{3,2,1,0:T(8,128)S(1)} %get-tuple-element.70.refs_0_, f32[2,4,16,128]{3,2,1,0:T(8,128)S(1)} %collective-permute-done.13.refs_1_, f32[2,4,16,128]{3,2,1,0:T(8,128)S(1)} %collective-permute-done.14.refs_2_, f32[2,4,16,128]{3,2,1,0:T(8,128)S(1)} %collective-permute-done.15.refs_3_), custom_call_target="tpu_custom_call" | custom-call | tf_op jit(solution)/shard_map/unpack/pallas_call | solution.py:511
  (22 shorter events, 1.4 us)
Async XLA Ops:
  0.7 5.9 %collective-permute-start.1 = (f32[1,8,256]{2,1,0:T(8,128)S(1)}, f32[1,8,256]{2,1,0:T(8,128)S(1)}, u32[]{:S(2)}, u32[]{:S(2)}) collective-permute-start(f32[1,8,256]{2,1,0:T(8,128)S(1)} %get-tuple-element.67), channel_id=1, source_target_pairs={{8,0},{16,8},{24,16},{0,24},{9,1},{17,9},{25,17},{1,25},{10,2},{18... | collective-permute-start | bytes 24584 | tf_op jit(solution)/shard_map/ppermute | solution.py:587
  4.6 4.5 %collective-permute-start = (f32[1,8,256]{2,1,0:T(8,128)S(1)}, f32[1,8,256]{2,1,0:T(8,128)S(1)}, u32[]{:S(2)}, u32[]{:S(2)}) collective-permute-start(f32[1,8,256]{2,1,0:T(8,128)S(1)} %get-tuple-element.68), channel_id=1, source_target_pairs={{0,8},{8,16},{16,24},{24,0},{1,9},{9,17},{17,25},{25,1},{2,10},{10... | collective-permute-start | bytes 24584 | tf_op jit(solution)/shard_map/ppermute | solution.py:586
  4.6 1.2 %copy-start = (f32[128,8,256]{2,1,0:T(8,128)S(1)}, f32[128,8,256]{2,1,0:T(8,128)}, u32[]{:S(2)}) copy-start(f32[128,8,256]{2,1,0:T(8,128)} %param.7) | copy-start | bytes 3145732
  9.4 5.6 %collective-permute-start.2 = (f32[33,8,128]{2,1,0:T(8,128)S(1)}, f32[33,8,128]{2,1,0:T(8,128)S(1)}, u32[]{:S(2)}, u32[]{:S(2)}) collective-permute-start(f32[33,8,128]{2,1,0:T(8,128)S(1)} %get-tuple-element.36), channel_id=1, source_target_pairs={{0,2},{1,3},{2,0},{3,1},{4,6},{5,7},{6,4},{7,5},{8,10},{9,11},{10,... | collective-permute-start | bytes 405512 | tf_op jit(solution)/shard_map/ppermute | solution.py:568
  11.0 8.8 %collective-permute-start.4 = (f32[33,8,128]{2,1,0:T(8,128)S(1)}, f32[33,8,128]{2,1,0:T(8,128)S(1)}, u32[]{:S(2)}, u32[]{:S(2)}) collective-permute-start(f32[33,8,128]{2,1,0:T(8,128)S(1)} %get-tuple-element.42), channel_id=1, source_target_pairs={{0,3},{1,2},{2,1},{3,0},{4,7},{5,6},{6,5},{7,4},{8,11},{9,10},{10,... | collective-permute-start | bytes 405512 | tf_op jit(solution)/shard_map/ppermute | solution.py:568
  11.0 17.2 %collective-permute-start.3 = (f32[33,8,128]{2,1,0:T(8,128)S(1)}, f32[33,8,128]{2,1,0:T(8,128)S(1)}, u32[]{:S(2)}, u32[]{:S(2)}) collective-permute-start(f32[33,8,128]{2,1,0:T(8,128)S(1)} %get-tuple-element.41), channel_id=1, source_target_pairs={{0,1},{1,0},{2,3},{3,2},{4,5},{5,4},{6,7},{7,6},{8,9},{9,8},{10,11... | collective-permute-start | bytes 405512 | tf_op jit(solution)/shard_map/ppermute | solution.py:568
  11.6 22.9 %collective-permute-start.5 = (f32[33,8,128]{2,1,0:T(8,128)S(1)}, f32[33,8,128]{2,1,0:T(8,128)S(1)}, u32[]{:S(2)}, u32[]{:S(2)}) collective-permute-start(f32[33,8,128]{2,1,0:T(8,128)S(1)} %get-tuple-element.48), channel_id=1, source_target_pairs={{0,4},{1,5},{2,6},{3,7},{4,0},{5,1},{6,2},{7,3},{8,12},{9,13},{10,... | collective-permute-start | bytes 405512 | tf_op jit(solution)/shard_map/ppermute | solution.py:568
  16.2 18.3 %collective-permute-start.6 = (f32[33,8,128]{2,1,0:T(8,128)S(1)}, f32[33,8,128]{2,1,0:T(8,128)S(1)}, u32[]{:S(2)}, u32[]{:S(2)}) collective-permute-start(f32[33,8,128]{2,1,0:T(8,128)S(1)} %get-tuple-element.50), channel_id=1, source_target_pairs={{0,5},{1,4},{2,7},{3,6},{4,1},{5,0},{6,3},{7,2},{8,13},{9,12},{10,... | collective-permute-start | bytes 405512 | tf_op jit(solution)/shard_map/ppermute | solution.py:568
  19.8 14.7 %collective-permute-start.7 = (f32[33,8,128]{2,1,0:T(8,128)S(1)}, f32[33,8,128]{2,1,0:T(8,128)S(1)}, u32[]{:S(2)}, u32[]{:S(2)}) collective-permute-start(f32[33,8,128]{2,1,0:T(8,128)S(1)} %get-tuple-element.52), channel_id=1, source_target_pairs={{0,6},{1,7},{2,4},{3,5},{4,2},{5,3},{6,0},{7,1},{8,14},{9,15},{10,... | collective-permute-start | bytes 405512 | tf_op jit(solution)/shard_map/ppermute | solution.py:568
  21.7 12.9 %collective-permute-start.8 = (f32[33,8,128]{2,1,0:T(8,128)S(1)}, f32[33,8,128]{2,1,0:T(8,128)S(1)}, u32[]{:S(2)}, u32[]{:S(2)}) collective-permute-start(f32[33,8,128]{2,1,0:T(8,128)S(1)} %get-tuple-element.54), channel_id=1, source_target_pairs={{0,7},{1,6},{2,5},{3,4},{4,3},{5,2},{6,1},{7,0},{8,15},{9,14},{10,... | collective-permute-start | bytes 405512 | tf_op jit(solution)/shard_map/ppermute | solution.py:568
  26.3 0.7 %copy-start.1 = (f32[256,16]{0,1:T(8,128)S(1)}, f32[256,16]{0,1:T(8,128)}, u32[]{:S(2)}) copy-start(f32[256,16]{0,1:T(8,128)} %param.9) | copy-start | bytes 49156
  27.1 0.7 %copy-start.2 = (f32[256,16]{0,1:T(8,128)S(1)}, f32[256,16]{0,1:T(8,128)}, u32[]{:S(2)}) copy-start(f32[256,16]{0,1:T(8,128)} %param.10) | copy-start | bytes 49156
  37.6 8.2 %collective-permute-start.11 = (f32[18,16,128]{2,1,0:T(8,128)S(1)}, f32[18,16,128]{2,1,0:T(8,128)S(1)}, u32[]{:S(2)}, u32[]{:S(2)}) collective-permute-start(f32[18,16,128]{2,1,0:T(8,128)S(1)} %get-tuple-element.63), channel_id=1, source_target_pairs={{0,24},{8,0},{16,8},{24,16},{1,25},{9,1},{17,9},{25,17},{2,26},{10... | collective-permute-start | bytes 442376 | tf_op jit(solution)/shard_map/ppermute | solution.py:608
  38.0 8.8 %collective-permute-start.10 = (f32[18,16,128]{2,1,0:T(8,128)S(1)}, f32[18,16,128]{2,1,0:T(8,128)S(1)}, u32[]{:S(2)}, u32[]{:S(2)}) collective-permute-start(f32[18,16,128]{2,1,0:T(8,128)S(1)} %get-tuple-element.63), channel_id=1, source_target_pairs={{0,16},{8,24},{16,0},{24,8},{1,17},{9,25},{17,1},{25,9},{2,18},{10... | collective-permute-start | bytes 442376 | tf_op jit(solution)/shard_map/ppermute | solution.py:608
  38.5 8.3 %collective-permute-start.9 = (f32[18,16,128]{2,1,0:T(8,128)S(1)}, f32[18,16,128]{2,1,0:T(8,128)S(1)}, u32[]{:S(2)}, u32[]{:S(2)}) collective-permute-start(f32[18,16,128]{2,1,0:T(8,128)S(1)} %get-tuple-element.63), channel_id=1, source_target_pairs={{0,8},{8,16},{16,24},{24,0},{1,9},{9,17},{17,25},{25,1},{2,10},{10... | collective-permute-start | bytes 442376 | tf_op jit(solution)/shard_map/ppermute | solution.py:608
  48.6 1.4 %collective-permute-start.12 = (f32[4,4,16,128]{3,2,1,0:T(8,128)S(1)}, f32[4,4,16,128]{3,2,1,0:T(8,128)S(1)}, u32[]{:S(2)}, u32[]{:S(2)}) collective-permute-start(f32[4,4,16,128]{3,2,1,0:T(8,128)S(1)} %get-tuple-element.66), channel_id=1, source_target_pairs={{0,1},{1,0},{2,3},{3,2},{4,5},{5,4},{6,7},{7,6},{8,9},{9,8},{10,11... | collective-permute-start | bytes 393224 | tf_op jit(solution)/shard_map/ppermute | solution.py:568
  50.0 7.0 %collective-permute-start.15 = (f32[2,4,16,128]{3,2,1,0:T(8,128)S(1)}, f32[2,4,16,128]{3,2,1,0:T(8,128)S(1)}, u32[]{:S(2)}, u32[]{:S(2)}) collective-permute-start(f32[2,4,16,128]{3,2,1,0:T(8,128)S(1)} %get-tuple-element.69), channel_id=1, source_target_pairs={{0,6},{1,7},{2,4},{3,5},{4,2},{5,3},{6,0},{7,1},{8,14},{9,15},{10,... | collective-permute-start | bytes 196616 | tf_op jit(solution)/shard_map/ppermute | solution.py:568
  52.0 6.9 %collective-permute-start.13 = (f32[2,4,16,128]{3,2,1,0:T(8,128)S(1)}, f32[2,4,16,128]{3,2,1,0:T(8,128)S(1)}, u32[]{:S(2)}, u32[]{:S(2)}) collective-permute-start(f32[2,4,16,128]{3,2,1,0:T(8,128)S(1)} %get-tuple-element.71), channel_id=1, source_target_pairs={{0,2},{1,3},{2,0},{3,1},{4,6},{5,7},{6,4},{7,5},{8,10},{9,11},{10,... | collective-permute-start | bytes 196616 | tf_op jit(solution)/shard_map/ppermute | solution.py:568
  56.6 5.9 %collective-permute-start.14 = (f32[2,4,16,128]{3,2,1,0:T(8,128)S(1)}, f32[2,4,16,128]{3,2,1,0:T(8,128)S(1)}, u32[]{:S(2)}, u32[]{:S(2)}) collective-permute-start(f32[2,4,16,128]{3,2,1,0:T(8,128)S(1)} %get-tuple-element.72), channel_id=1, source_target_pairs={{0,4},{1,5},{2,6},{3,7},{4,0},{5,1},{6,2},{7,3},{8,12},{9,13},{10,... | collective-permute-start | bytes 196616 | tf_op jit(solution)/shard_map/ppermute | solution.py:568

commit v12 on v11

--- a/solution.py
+++ b/solution.py
@@ -190,7 +190,7 @@
             s_ref[step] = jnp.where(empty, -1.0, total[depth:depth + layers])
         return carry
 
-    lax.fori_loop(0, steps, smooth, 0, unroll=2)
+    lax.fori_loop(0, steps, smooth, 0, unroll=4)
 
 
 def scan_quarters(groups, width, sums_ref, start_ref, total_ref, offset):
@@ -202,15 +202,13 @@
         for k in range(groups):
             z = chunk * groups + k
             both = sums_ref[z]
-            inclusive = both
+            moved = [pltpu.roll(both, k * width, 1) for k in range(1, groups)]
+            begin = jnp.zeros((colors, LANES), jnp.float32)
             everything = both
-            shift = 1
-            while shift < groups:
-                moved = pltpu.roll(inclusive, shift * width, 1)
-                inclusive = inclusive + jnp.where(group >= shift, moved, 0.0)
-                everything = everything + pltpu.roll(everything, shift * width, 1)
-                shift *= 2
-            start_ref[z] = inclusive - both
+            for place, value in enumerate(moved, 1):
+                begin = begin + jnp.where(group >= place, value, 0.0)
+                everything = everything + value
+            start_ref[z] = begin
             packed = jnp.where(group == k, everything, packed)
         total_ref[offset + chunk] = packed
         return carry
@@ -326,7 +324,7 @@
         sums[z] = high - low
         return carry
 
-    lax.fori_loop(0, layers, count_layer, 0, unroll=2)
+    lax.fori_loop(0, layers, count_layer, 0, unroll=4)
     count_layer(layers, 0)
     for z in range(layers + 1, slots):
         sums[z] = jnp.zeros((bins, LANES), jnp.float32)
@@ -519,14 +517,29 @@
     )(*arrived)
 
 
-def table_kernel(step_x, step_z, bins_ref, extinction_ref, color_ref, columns_ref, sum_ref,
-                 split_ref):
-    rows, bins = extinction_ref.shape[1], bins_ref.shape[1]
+def table_kernel(step_x, step_z, bins_ref, scale_ref, ambient_ref, backdrop_ref, extinction_ref,
+                 color_ref, sum_ref, split_ref, columns_ref):
+    rows, bins = extinction_ref.shape[1], bins_ref.shape[0]
     colors = extinction_ref.shape[0]
     row = lax.broadcasted_iota(jnp.int32, (rows, bins), 0)
-    bin_id = lax.broadcasted_iota(jnp.int32, (rows, bins), 1)
-    here = (row == bins_ref[0:1, :]).astype(jnp.float32)
-    below = ((row == bins_ref[1:2, :]) & (bin_id > 0)).astype(jnp.float32)
+    lane = lax.broadcasted_iota(jnp.int32, (8, bins), 1)
+    this = jnp.full((8, bins), -1, jnp.int32)
+    last = jnp.full((8, bins), -1, jnp.int32)
+    for k in range(bins):
+        this = jnp.where(lane == k, bins_ref[k], this)
+        if k:
+            last = jnp.where(lane == k, bins_ref[k - 1], last)
+    here = (row == this[0:1, :]).astype(jnp.float32)
+    below = (row == last[0:1, :]).astype(jnp.float32)
+    place = lax.broadcasted_iota(jnp.int32, (colors, LANES), 0)
+    columns = []
+    for ref in (scale_ref, ambient_ref, backdrop_ref):
+        column = jnp.zeros((colors, LANES), jnp.float32)
+        for k in range(colors):
+            column = jnp.where(place == k, ref[k], column)
+        columns.append(column)
+    for k, column in enumerate(columns):
+        columns_ref[k] = column
 
     def rise(ref):
         now = jnp.dot(ref[...], here, precision=lax.Precision.HIGHEST,
@@ -540,27 +553,28 @@
         fine = (value - coarse.astype(jnp.float32)).astype(jnp.bfloat16)
         return jnp.concatenate([coarse, fine, coarse], axis=1)
 
-    sigma = rise(extinction_ref) * columns_ref[0, :, 0:bins]
+    sigma = rise(extinction_ref) * columns[0][:, 0:bins]
     sum_ref[...] = split(sigma * (-step_x * LOG2E))
     split_ref[0:colors] = split(sigma * (-step_z * LOG2E))
     split_ref[colors:2 * colors] = split(rise(color_ref))
 
 
-def tables(bin_rows, tf_extinction, tf_color, columns, step_x, step_z):
+def tables(bin_rows, scale, ambient, backdrop, tf_extinction, tf_color, step_x, step_z):
     bins = bin_rows.shape[0]
     colors = tf_color.shape[1]
-    shifted = jnp.stack([bin_rows, jnp.roll(bin_rows, 1)])
     return pl.pallas_call(
         functools.partial(table_kernel, step_x, step_z),
         out_shape=(
             jax.ShapeDtypeStruct((colors, 3 * bins), jnp.bfloat16),
             jax.ShapeDtypeStruct((2 * colors, 3 * bins), jnp.bfloat16),
+            jax.ShapeDtypeStruct((3, colors, LANES), jnp.float32),
         ),
-        in_specs=[pl.BlockSpec(memory_space=pltpu.VMEM)] * 4,
-        out_specs=[pl.BlockSpec(memory_space=pltpu.VMEM)] * 2,
+        in_specs=[pl.BlockSpec(memory_space=pltpu.SMEM)] * 4
+        + [pl.BlockSpec(memory_space=pltpu.VMEM)] * 2,
+        out_specs=[pl.BlockSpec(memory_space=pltpu.VMEM)] * 3,
         compiler_params=pltpu.CompilerParams(vmem_limit_bytes=4 * MIB),
         name="tables",
-    )(shifted, tf_extinction.T, tf_color.T, columns)
+    )(bin_rows, scale, ambient, backdrop, tf_extinction.T, tf_color.T)
 
 
 def exchange(value, axis, apart):
@@ -591,14 +605,13 @@
     for apart in range(1, count):
         give = pieces[apart]
         if apart > count // 2:
-            ahead = min(apart - count // 2 + 1, count // 2 - 1)
+            ahead = max(apart - count // 2 - 1, 1)
             give, _ = lax.optimization_barrier((give, pieces[ahead]))
         pieces[apart] = exchange(give, "gz", apart)
     bin_rows, extinction_scale, ambient, backdrop, _ = lax.optimization_barrier(
         (bin_rows, extinction_scale, ambient, backdrop, pieces[2]))
-    columns = jnp.broadcast_to(
-        jnp.stack([extinction_scale, ambient, backdrop])[:, :, None], (3, colors, LANES))
-    sum_table, table = tables(bin_rows, tf_extinction, tf_color, columns, step_x, step_z)
+    sum_table, table, columns = tables(
+        bin_rows, extinction_scale, ambient, backdrop, tf_extinction, tf_color, step_x, step_z)
 
     blocks = count // 2
     ratio = step_x / step_z

time: 63.9 us -> 63.5 us (level)
  other arithmetic: 2.75 us -> 0.02 us
  local copies, waits for them, and re-layouts: 4.68 us -> 5.99 us
  waiting for transfers between devices: 13.8 us -> 14.5 us
    another operation x3 -> x0, other arithmetic: 2.73 us -> none  [the longest x2 2.04 us: tables(): shifted = jnp.stack([bin_rows, jnp.roll(bin_rows, 1)])]
    unnamed x6 -> x14, local copies, waits for them, and re-layouts: 2.66 us -> 5.28 us
    slice x1 -> x0, local copies, waits for them, and re-layouts: 1.24 us -> none  [tables(): shifted = jnp.stack([bin_rows, jnp.roll(bin_rows, 1)])]
    ppermute x11, waiting for transfers between devices: 10.2 us -> 10.9 us  [exchange(): return lax.ppermute(value, axis, pairs)]
  transfers between devices with their start and end apart: 16 -> 16, of which waited for: 7 -> 8; matrix products, arithmetic and copies ran while one was open for 6% -> 0% of each run, Pallas kernels for 22% -> 23%
where the time goes in v12:
time: 63.5 us; the launch traced here: 63.1 us
  starting transfers between devices  22.3 us (35%)
  Pallas kernels  20.2 us (32%)
  waiting for transfers between devices  14.5 us (23%)
  local copies, waits for them, and re-layouts  5.99 us (9%)
    ppermute x11, starting transfers between devices, exchange(): return lax.ppermute(value, axis, pairs)  15.9 us
    ppermute x11, waiting for transfers between devices, exchange(): return lax.ppermute(value, axis, pairs)  10.9 us
    pallas_call x1, Pallas kernels, render_near(): pl.pallas_call(functools.partial(near_kernel, groups, width, bins, ratio,...  6.14 us
    pallas_call x1, Pallas kernels, render_far(): pl.pallas_call(functools.partial(render_rows, bins, ratio), out_shape=(ja...  5.61 us
    unnamed x14, local copies, waits for them, and re-layouts  5.28 us
    ppermute x1, starting transfers between devices, local(): after = lax.ppermute(density[:1], 'gx', down)  3.89 us
    pallas_call x2, Pallas kernels, join(): pl.pallas_call(functools.partial(join_kernel, groups, width, turn, blocks...  2.77 us
    pallas_call x1, Pallas kernels, far_depths(): pl.pallas_call(functools.partial(depth_kernel, groups, width, bins, count...  2.72 us
  transfers between devices with their start and end apart: 16, of which 8 were waited for; matrix products, arithmetic and copies ran while one was open for 0% of the time, Pallas kernels for 23%

profile of v12, /device:TPU:0, one launch (start us, length us, event | category | flops | bytes accessed | tf_op | source)
XLA Modules:
  0.0 63.1 jit_solution(14549321753202079233)
XLA Ops:
  0.0 0.7 %fusion.7 = (f32[1,8,256]{2,1,0:T(8,128)S(1)}, f32[1,8,256]{2,1,0:T(8,128)S(1)}) fusion(f32[128,8,256]{2,1,0:T(8,128)} %param.7), kind=kLoop, calls=%fused_computation.14 | loop fusion | bytes 32768 | tf_op jit(solution)/shard_map/slice | solution.py:601
  0.7 3.9 %collective-permute-start.1 = (f32[1,8,256]{2,1,0:T(8,128)S(1)}, f32[1,8,256]{2,1,0:T(8,128)S(1)}, u32[]{:S(2)}, u32[]{:S(2)}) collective-permute-start(f32[1,8,256]{2,1,0:T(8,128)S(1)} %get-tuple-element.69), channel_id=1, source_target_pairs={{8,0},{16,8},{24,16},{0,24},{9,1},{17,9},{25,17},{1,25},{10,2},{18... | collective-permute-start | bytes 24584 | tf_op jit(solution)/shard_map/ppermute | solution.py:601
  4.6 1.2 %copy-done = f32[128,8,256]{2,1,0:T(8,128)S(1)} copy-done((f32[128,8,256]{2,1,0:T(8,128)S(1)}, f32[128,8,256]{2,1,0:T(8,128)}, u32[]{:S(2)}) %copy-start) | copy-done | bytes 1048600
  5.8 0.7 %pack.1.packed_ref = f32[8,32,8,128]{3,2,1,0:T(8,128)S(1)} custom-call(f32[4,32,8,256]{3,2,1,0:T(8,128)S(1)} %bitcast.13), custom_call_target="tpu_custom_call" | custom-call | tf_op jit(solution)/shard_map/pack/pallas_call | solution.py:87
  6.6 2.6 %collective-permute-done.before_ref = f32[1,8,256]{2,1,0:T(8,128)S(1)} collective-permute-done((f32[1,8,256]{2,1,0:T(8,128)S(1)}, f32[1,8,256]{2,1,0:T(8,128)S(1)}, u32[]{:S(2)}, u32[]{:S(2)}) %collective-permute-start) | collective-permute-done | bytes 8224 | tf_op jit(solution)/shard_map/ppermute | solution.py:600
  9.4 1.6 %collective-permute-start.2 = (f32[33,8,128]{2,1,0:T(8,128)S(1)}, f32[33,8,128]{2,1,0:T(8,128)S(1)}, u32[]{:S(2)}, u32[]{:S(2)}) collective-permute-start(f32[33,8,128]{2,1,0:T(8,128)S(1)} %get-tuple-element.37), channel_id=1, source_target_pairs={{0,2},{1,3},{2,0},{3,1},{4,6},{5,7},{6,4},{7,5},{8,10},{9,11},{10,... | collective-permute-start | bytes 405512 | tf_op jit(solution)/shard_map/ppermute | solution.py:582
  11.6 2.6 %collective-permute-start.5 = (f32[33,8,128]{2,1,0:T(8,128)S(1)}, f32[33,8,128]{2,1,0:T(8,128)S(1)}, u32[]{:S(2)}, u32[]{:S(2)}) collective-permute-start(f32[33,8,128]{2,1,0:T(8,128)S(1)} %get-tuple-element.50), channel_id=1, source_target_pairs={{0,4},{1,5},{2,6},{3,7},{4,0},{5,1},{6,2},{7,3},{8,12},{9,13},{10,... | collective-permute-start | bytes 405512 | tf_op jit(solution)/shard_map/ppermute | solution.py:582
  14.2 0.8 %collective-permute-done.2.refs_2_ = f32[33,8,128]{2,1,0:T(8,128)S(1)} collective-permute-done((f32[33,8,128]{2,1,0:T(8,128)S(1)}, f32[33,8,128]{2,1,0:T(8,128)S(1)}, u32[]{:S(2)}, u32[]{:S(2)}) %collective-permute-start.2) | collective-permute-done | bytes 135200 | tf_op jit(solution)/shard_map/ppermute | solution.py:582
  15.0 3.7 %collective-permute-start.6 = (f32[33,8,128]{2,1,0:T(8,128)S(1)}, f32[33,8,128]{2,1,0:T(8,128)S(1)}, u32[]{:S(2)}, u32[]{:S(2)}) collective-permute-start(f32[33,8,128]{2,1,0:T(8,128)S(1)} %get-tuple-element.52), channel_id=1, source_target_pairs={{0,5},{1,4},{2,7},{3,6},{4,1},{5,0},{6,3},{7,2},{8,13},{9,12},{10,... | collective-permute-start | bytes 405512 | tf_op jit(solution)/shard_map/ppermute | solution.py:582
  18.7 2.4 %collective-permute-start.7 = (f32[33,8,128]{2,1,0:T(8,128)S(1)}, f32[33,8,128]{2,1,0:T(8,128)S(1)}, u32[]{:S(2)}, u32[]{:S(2)}) collective-permute-start(f32[33,8,128]{2,1,0:T(8,128)S(1)} %get-tuple-element.54), channel_id=1, source_target_pairs={{0,6},{1,7},{2,4},{3,5},{4,2},{5,3},{6,0},{7,1},{8,14},{9,15},{10,... | collective-permute-start | bytes 405512 | tf_op jit(solution)/shard_map/ppermute | solution.py:582
  21.0 0.7 %copy-done.1 = f32[256,16]{0,1:T(8,128)S(1)} copy-done((f32[256,16]{0,1:T(8,128)S(1)}, f32[256,16]{0,1:T(8,128)}, u32[]{:S(2)}) %copy-start.1) | copy-done | bytes 16408
  21.8 0.7 %copy-done.2 = f32[256,16]{0,1:T(8,128)S(1)} copy-done((f32[256,16]{0,1:T(8,128)S(1)}, f32[256,16]{0,1:T(8,128)}, u32[]{:S(2)}) %copy-start.2) | copy-done | bytes 16408
  22.5 0.7 %copy-done.3 = s32[32]{0:T(128)S(1)} copy-done((s32[32]{0:T(128)S(1)}, s32[32]{0:T(128)}, u32[]{:S(2)}) %copy-start.3) | copy-done | bytes 152
  23.1 0.7 %copy-done.4 = f32[16]{0:T(128)S(1)} copy-done((f32[16]{0:T(128)S(1)}, f32[16]{0:T(128)}, u32[]{:S(2)}) %copy-start.4) | copy-done | bytes 88
  23.8 0.7 %copy-done.5 = f32[16]{0:T(128)S(1)} copy-done((f32[16]{0:T(128)S(1)}, f32[16]{0:T(128)}, u32[]{:S(2)}) %copy-start.5) | copy-done | bytes 88
  24.4 0.7 %copy-done.6 = f32[16]{0:T(128)S(1)} copy-done((f32[16]{0:T(128)S(1)}, f32[16]{0:T(128)}, u32[]{:S(2)}) %copy-start.6) | copy-done | bytes 88
  25.1 1.0 %tables.1 = (bf16[16,96]{1,0:T(8,128)(2,1)S(1)}, bf16[32,96]{1,0:T(8,128)(2,1)S(1)}, f32[3,16,128]{2,1,0:T(8,128)S(1)}) custom-call(s32[32]{0:T(128)S(1)} %copy-done.3, f32[16]{0:T(128)S(1)} %copy-done.4, f32[16]{0:T(128)S(1)} %copy-done.5, f32[16]{0:T(128)S(1)} %copy-done.6, f32[16,256]{1,0:T(8,128)S(1)} %bitcast.15, f32[16,256]{1,0:T(8,128)S(1)} %bitcast.16), custom_call_target="tpu_custom_call" | custom-call | tf_op jit(solution)/shard_map/tables/pallas_call | solution.py:565
  26.1 6.1 %render_near.1 = (f32[32,32,16,128]{3,2,1,0:T(8,128)S(1)}, f32[32,16,128]{2,1,0:T(8,128)S(1)}, f32[32,16,128]{2,1,0:T(8,128)S(1)}, f32[32,16,128]{2,1,0:T(8,128)S(1)}, f32[8,16,128]{2,1,0:T(8,128)S(1)}) custom-call(f32[33,8,128]{2,1,0:T(8,128)S(1)} %get-tuple-element.43.refs_0_, f32[33,8,128]{2,1,0:T(8,128)S(1)} %collective-permute-done.3.refs_1_, ...), custom_call_target="tpu_custom_call" | custom-call | tf_op jit(solution)/shard_map/render_near/pallas_call | solution.py:285
  32.3 4.5 %collective-permute-done.6.refs_5_ = f32[33,8,128]{2,1,0:T(8,128)S(1)} collective-permute-done((f32[33,8,128]{2,1,0:T(8,128)S(1)}, f32[33,8,128]{2,1,0:T(8,128)S(1)}, u32[]{:S(2)}, u32[]{:S(2)}) %collective-permute-start.6) | collective-permute-done | bytes 135200 | tf_op jit(solution)/shard_map/ppermute | solution.py:582
  36.8 2.7 %far_depths.1 = (f32[32,40,128]{2,1,0:T(8,128)S(1)}, f32[40,16,128]{2,1,0:T(8,128)S(1)}, f32[18,16,128]{2,1,0:T(8,128)S(1)}) custom-call(f32[33,8,128]{2,1,0:T(8,128)S(1)} %get-tuple-element.43.refs_0_, f32[33,8,128]{2,1,0:T(8,128)S(1)} %collective-permute-done.3.refs_1_, f32[33,8,128]{2,1,0:T(8,128)S(1)} %collective-permute-done.2.refs_2_, ...), custom_call_target="tpu_custom_call" | custom-call | tf_op jit(solution)/shard_map/far_depths/pallas_call | solution.py:354
  40.4 1.6 %collective-permute-start.9 = (f32[18,16,128]{2,1,0:T(8,128)S(1)}, f32[18,16,128]{2,1,0:T(8,128)S(1)}, u32[]{:S(2)}, u32[]{:S(2)}) collective-permute-start(f32[18,16,128]{2,1,0:T(8,128)S(1)} %get-tuple-element.65), channel_id=1, source_target_pairs={{0,8},{8,16},{16,24},{24,0},{1,9},{9,17},{17,25},{25,1},{2,10},{10... | collective-permute-start | bytes 442376 | tf_op jit(solution)/shard_map/ppermute | solution.py:621
  42.1 5.6 %render_far.1 = (f32[32,33,16,128]{3,2,1,0:T(8,128)S(1)}, f32[32,16,128]{2,1,0:T(8,128)S(1)}, f32[32,16,128]{2,1,0:T(8,128)S(1)}) custom-call(f32[32,40,128]{2,1,0:T(8,128)S(1)} %get-tuple-element.59.s_ref, bf16[32,96]{1,0:T(8,128)(2,1)S(1)} %get-tuple-element.46.refs_4_.table_ref), custom_call_target="tpu_custom_call" | custom-call | flops 10000000000 | bytes 10000000 | tf_op jit(solution)/shard_map/render_far/pallas_call | solution.py:378
  47.7 1.0 %collective-permute-done.10.refs_9_ = f32[18,16,128]{2,1,0:T(8,128)S(1)} collective-permute-done((f32[18,16,128]{2,1,0:T(8,128)S(1)}, f32[18,16,128]{2,1,0:T(8,128)S(1)}, u32[]{:S(2)}, u32[]{:S(2)}) %collective-permute-start.10) | collective-permute-done | bytes 147488 | tf_op jit(solution)/shard_map/ppermute | solution.py:621
  48.7 1.7 %join.2 = (f32[4,4,16,128]{3,2,1,0:T(8,128)S(1)}, f32[32,16,128]{2,1,0:T(8,128)S(1)}, f32[40,16,128]{2,1,0:T(8,128)S(1)}) custom-call(f32[3,16,128]{2,1,0:T(8,128)S(1)} %get-tuple-element.42.columns_ref, f32[32,32,16,128]{3,2,1,0:T(8,128)S(1)} %get-tuple-element.47.refs_0_, f32[32,16,128]{2,1,0:T(8,128)S(1)} %get-tuple-element.48.refs_1_, ...), custom_call_target="tpu_custom_call" | custom-call | tf_op jit(solution)/shard_map/join/pallas_call | solution.py:480
  50.4 1.1 %join.3 = f32[4,4,16,128]{3,2,1,0:T(8,128)S(1)} custom-call(f32[3,16,128]{2,1,0:T(8,128)S(1)} %get-tuple-element.42.columns_ref, f32[32,32,16,128]{3,2,1,0:T(8,128)S(1)} %get-tuple-element.47.refs_0_, f32[32,16,128]{2,1,0:T(8,128)S(1)} %get-tuple-element.48.refs_1_, f32[32,16,128]{2,1,0:T(8,128)S(1)} %get-tuple-element.49.refs_2_, ...), custom_call_target="tpu_custom_call" | custom-call | tf_op jit(solution)/shard_map/join/pallas_call | solution.py:480
  51.8 2.6 %collective-permute-start.15 = (f32[2,4,16,128]{3,2,1,0:T(8,128)S(1)}, f32[2,4,16,128]{3,2,1,0:T(8,128)S(1)}, u32[]{:S(2)}, u32[]{:S(2)}) collective-permute-start(f32[2,4,16,128]{3,2,1,0:T(8,128)S(1)} %get-tuple-element.71), channel_id=1, source_target_pairs={{0,6},{1,7},{2,4},{3,5},{4,2},{5,3},{6,0},{7,1},{8,14},{9,15},{10,... | collective-permute-start | bytes 196616 | tf_op jit(solution)/shard_map/ppermute | solution.py:582
  54.4 1.6 %collective-permute-start.13 = (f32[2,4,16,128]{3,2,1,0:T(8,128)S(1)}, f32[2,4,16,128]{3,2,1,0:T(8,128)S(1)}, u32[]{:S(2)}, u32[]{:S(2)}) collective-permute-start(f32[2,4,16,128]{3,2,1,0:T(8,128)S(1)} %get-tuple-element.73), channel_id=1, source_target_pairs={{0,2},{1,3},{2,0},{3,1},{4,6},{5,7},{6,4},{7,5},{8,10},{9,11},{10,... | collective-permute-start | bytes 196616 | tf_op jit(solution)/shard_map/ppermute | solution.py:582
  56.0 0.8 %collective-permute-start.14 = (f32[2,4,16,128]{3,2,1,0:T(8,128)S(1)}, f32[2,4,16,128]{3,2,1,0:T(8,128)S(1)}, u32[]{:S(2)}, u32[]{:S(2)}) collective-permute-start(f32[2,4,16,128]{3,2,1,0:T(8,128)S(1)} %get-tuple-element.74), channel_id=1, source_target_pairs={{0,4},{1,5},{2,6},{3,7},{4,0},{5,1},{6,2},{7,3},{8,12},{9,13},{10,... | collective-permute-start | bytes 196616 | tf_op jit(solution)/shard_map/ppermute | solution.py:582
  56.8 1.3 %collective-permute-done.15.refs_3_ = f32[2,4,16,128]{3,2,1,0:T(8,128)S(1)} collective-permute-done((f32[2,4,16,128]{3,2,1,0:T(8,128)S(1)}, f32[2,4,16,128]{3,2,1,0:T(8,128)S(1)}, u32[]{:S(2)}, u32[]{:S(2)}) %collective-permute-start.15) | collective-permute-done | bytes 65568 | tf_op jit(solution)/shard_map/ppermute | solution.py:582
  58.0 1.5 %collective-permute-done.13.refs_1_ = f32[2,4,16,128]{3,2,1,0:T(8,128)S(1)} collective-permute-done((f32[2,4,16,128]{3,2,1,0:T(8,128)S(1)}, f32[2,4,16,128]{3,2,1,0:T(8,128)S(1)}, u32[]{:S(2)}, u32[]{:S(2)}) %collective-permute-start.13) | collective-permute-done | bytes 65568 | tf_op jit(solution)/shard_map/ppermute | solution.py:582
  59.5 2.7 %collective-permute-done.14.refs_2_ = f32[2,4,16,128]{3,2,1,0:T(8,128)S(1)} collective-permute-done((f32[2,4,16,128]{3,2,1,0:T(8,128)S(1)}, f32[2,4,16,128]{3,2,1,0:T(8,128)S(1)}, u32[]{:S(2)}, u32[]{:S(2)}) %collective-permute-start.14) | collective-permute-done | bytes 65568 | tf_op jit(solution)/shard_map/ppermute | solution.py:582
  62.2 0.9 %unpack.1 = f32[16,16,256]{2,1,0:T(8,128)} custom-call(f32[2,4,16,128]{3,2,1,0:T(8,128)S(1)} %get-tuple-element.72.refs_0_, f32[2,4,16,128]{3,2,1,0:T(8,128)S(1)} %collective-permute-done.13.refs_1_, f32[2,4,16,128]{3,2,1,0:T(8,128)S(1)} %collective-permute-done.14.refs_2_, f32[2,4,16,128]{3,2,1,0:T(8,128)S(1)} %collective-permute-done.15.refs_3_), custom_call_target="tpu_custom_call" | custom-call | tf_op jit(solution)/shard_map/unpack/pallas_call | solution.py:509
  (25 shorter events, 2.1 us)
Async XLA Ops:
  0.7 5.9 %collective-permute-start.1 = (f32[1,8,256]{2,1,0:T(8,128)S(1)}, f32[1,8,256]{2,1,0:T(8,128)S(1)}, u32[]{:S(2)}, u32[]{:S(2)}) collective-permute-start(f32[1,8,256]{2,1,0:T(8,128)S(1)} %get-tuple-element.69), channel_id=1, source_target_pairs={{8,0},{16,8},{24,16},{0,24},{9,1},{17,9},{25,17},{1,25},{10,2},{18... | collective-permute-start | bytes 24584 | tf_op jit(solution)/shard_map/ppermute | solution.py:601
  4.6 4.5 %collective-permute-start = (f32[1,8,256]{2,1,0:T(8,128)S(1)}, f32[1,8,256]{2,1,0:T(8,128)S(1)}, u32[]{:S(2)}, u32[]{:S(2)}) collective-permute-start(f32[1,8,256]{2,1,0:T(8,128)S(1)} %get-tuple-element.70), channel_id=1, source_target_pairs={{0,8},{8,16},{16,24},{24,0},{1,9},{9,17},{17,25},{25,1},{2,10},{10... | collective-permute-start | bytes 24584 | tf_op jit(solution)/shard_map/ppermute | solution.py:600
  4.6 1.2 %copy-start = (f32[128,8,256]{2,1,0:T(8,128)S(1)}, f32[128,8,256]{2,1,0:T(8,128)}, u32[]{:S(2)}) copy-start(f32[128,8,256]{2,1,0:T(8,128)} %param.7) | copy-start | bytes 3145732
  9.4 5.6 %collective-permute-start.2 = (f32[33,8,128]{2,1,0:T(8,128)S(1)}, f32[33,8,128]{2,1,0:T(8,128)S(1)}, u32[]{:S(2)}, u32[]{:S(2)}) collective-permute-start(f32[33,8,128]{2,1,0:T(8,128)S(1)} %get-tuple-element.37), channel_id=1, source_target_pairs={{0,2},{1,3},{2,0},{3,1},{4,6},{5,7},{6,4},{7,5},{8,10},{9,11},{10,... | collective-permute-start | bytes 405512 | tf_op jit(solution)/shard_map/ppermute | solution.py:582
  11.0 4.0 %collective-permute-start.3 = (f32[33,8,128]{2,1,0:T(8,128)S(1)}, f32[33,8,128]{2,1,0:T(8,128)S(1)}, u32[]{:S(2)}, u32[]{:S(2)}) collective-permute-start(f32[33,8,128]{2,1,0:T(8,128)S(1)} %get-tuple-element.44), channel_id=1, source_target_pairs={{0,1},{1,0},{2,3},{3,2},{4,5},{5,4},{6,7},{7,6},{8,9},{9,8},{10,11... | collective-permute-start | bytes 405512 | tf_op jit(solution)/shard_map/ppermute | solution.py:582
  11.0 15.1 %collective-permute-start.4 = (f32[33,8,128]{2,1,0:T(8,128)S(1)}, f32[33,8,128]{2,1,0:T(8,128)S(1)}, u32[]{:S(2)}, u32[]{:S(2)}) collective-permute-start(f32[33,8,128]{2,1,0:T(8,128)S(1)} %get-tuple-element.45), channel_id=1, source_target_pairs={{0,3},{1,2},{2,1},{3,0},{4,7},{5,6},{6,5},{7,4},{8,11},{9,10},{10,... | collective-permute-start | bytes 405512 | tf_op jit(solution)/shard_map/ppermute | solution.py:582
  11.6 20.6 %collective-permute-start.5 = (f32[33,8,128]{2,1,0:T(8,128)S(1)}, f32[33,8,128]{2,1,0:T(8,128)S(1)}, u32[]{:S(2)}, u32[]{:S(2)}) collective-permute-start(f32[33,8,128]{2,1,0:T(8,128)S(1)} %get-tuple-element.50), channel_id=1, source_target_pairs={{0,4},{1,5},{2,6},{3,7},{4,0},{5,1},{6,2},{7,3},{8,12},{9,13},{10,... | collective-permute-start | bytes 405512 | tf_op jit(solution)/shard_map/ppermute | solution.py:582
  15.0 17.2 %collective-permute-start.8 = (f32[33,8,128]{2,1,0:T(8,128)S(1)}, f32[33,8,128]{2,1,0:T(8,128)S(1)}, u32[]{:S(2)}, u32[]{:S(2)}) collective-permute-start(f32[33,8,128]{2,1,0:T(8,128)S(1)} %get-tuple-element.56), channel_id=1, source_target_pairs={{0,7},{1,6},{2,5},{3,4},{4,3},{5,2},{6,1},{7,0},{8,15},{9,14},{10,... | collective-permute-start | bytes 405512 | tf_op jit(solution)/shard_map/ppermute | solution.py:582
  15.0 21.8 %collective-permute-start.6 = (f32[33,8,128]{2,1,0:T(8,128)S(1)}, f32[33,8,128]{2,1,0:T(8,128)S(1)}, u32[]{:S(2)}, u32[]{:S(2)}) collective-permute-start(f32[33,8,128]{2,1,0:T(8,128)S(1)} %get-tuple-element.52), channel_id=1, source_target_pairs={{0,5},{1,4},{2,7},{3,6},{4,1},{5,0},{6,3},{7,2},{8,13},{9,12},{10,... | collective-permute-start | bytes 405512 | tf_op jit(solution)/shard_map/ppermute | solution.py:582
  18.7 18.1 %collective-permute-start.7 = (f32[33,8,128]{2,1,0:T(8,128)S(1)}, f32[33,8,128]{2,1,0:T(8,128)S(1)}, u32[]{:S(2)}, u32[]{:S(2)}) collective-permute-start(f32[33,8,128]{2,1,0:T(8,128)S(1)} %get-tuple-element.54), channel_id=1, source_target_pairs={{0,6},{1,7},{2,4},{3,5},{4,2},{5,3},{6,0},{7,1},{8,14},{9,15},{10,... | collective-permute-start | bytes 405512 | tf_op jit(solution)/shard_map/ppermute | solution.py:582
  21.0 0.7 %copy-start.1 = (f32[256,16]{0,1:T(8,128)S(1)}, f32[256,16]{0,1:T(8,128)}, u32[]{:S(2)}) copy-start(f32[256,16]{0,1:T(8,128)} %param.9) | copy-start | bytes 49156
  21.8 0.7 %copy-start.2 = (f32[256,16]{0,1:T(8,128)S(1)}, f32[256,16]{0,1:T(8,128)}, u32[]{:S(2)}) copy-start(f32[256,16]{0,1:T(8,128)} %param.10) | copy-start | bytes 49156
  22.5 0.7 %copy-start.3 = (s32[32]{0:T(128)S(1)}, s32[32]{0:T(128)}, u32[]{:S(2)}) copy-start(s32[32]{0:T(128)} %bins_ref) | copy-start | bytes 388
  23.1 0.7 %copy-start.4 = (f32[16]{0:T(128)S(1)}, f32[16]{0:T(128)}, u32[]{:S(2)}) copy-start(f32[16]{0:T(128)} %scale_ref) | copy-start | bytes 196
  23.8 0.7 %copy-start.5 = (f32[16]{0:T(128)S(1)}, f32[16]{0:T(128)}, u32[]{:S(2)}) copy-start(f32[16]{0:T(128)} %ambient_ref) | copy-start | bytes 196
  24.4 0.7 %copy-start.6 = (f32[16]{0:T(128)S(1)}, f32[16]{0:T(128)}, u32[]{:S(2)}) copy-start(f32[16]{0:T(128)} %backdrop_ref) | copy-start | bytes 196
  39.5 8.2 %collective-permute-start.11 = (f32[18,16,128]{2,1,0:T(8,128)S(1)}, f32[18,16,128]{2,1,0:T(8,128)S(1)}, u32[]{:S(2)}, u32[]{:S(2)}) collective-permute-start(f32[18,16,128]{2,1,0:T(8,128)S(1)} %get-tuple-element.65), channel_id=1, source_target_pairs={{0,24},{8,0},{16,8},{24,16},{1,25},{9,1},{17,9},{25,17},{2,26},{10... | collective-permute-start | bytes 442376 | tf_op jit(solution)/shard_map/ppermute | solution.py:621
  39.9 8.7 %collective-permute-start.10 = (f32[18,16,128]{2,1,0:T(8,128)S(1)}, f32[18,16,128]{2,1,0:T(8,128)S(1)}, u32[]{:S(2)}, u32[]{:S(2)}) collective-permute-start(f32[18,16,128]{2,1,0:T(8,128)S(1)} %get-tuple-element.65), channel_id=1, source_target_pairs={{0,16},{8,24},{16,0},{24,8},{1,17},{9,25},{17,1},{25,9},{2,18},{10... | collective-permute-start | bytes 442376 | tf_op jit(solution)/shard_map/ppermute | solution.py:621
  40.4 8.2 %collective-permute-start.9 = (f32[18,16,128]{2,1,0:T(8,128)S(1)}, f32[18,16,128]{2,1,0:T(8,128)S(1)}, u32[]{:S(2)}, u32[]{:S(2)}) collective-permute-start(f32[18,16,128]{2,1,0:T(8,128)S(1)} %get-tuple-element.65), channel_id=1, source_target_pairs={{0,8},{8,16},{16,24},{24,0},{1,9},{9,17},{17,25},{25,1},{2,10},{10... | collective-permute-start | bytes 442376 | tf_op jit(solution)/shard_map/ppermute | solution.py:621
  50.4 1.4 %collective-permute-start.12 = (f32[4,4,16,128]{3,2,1,0:T(8,128)S(1)}, f32[4,4,16,128]{3,2,1,0:T(8,128)S(1)}, u32[]{:S(2)}, u32[]{:S(2)}) collective-permute-start(f32[4,4,16,128]{3,2,1,0:T(8,128)S(1)} %get-tuple-element.68), channel_id=1, source_target_pairs={{0,1},{1,0},{2,3},{3,2},{4,5},{5,4},{6,7},{7,6},{8,9},{9,8},{10,11... | collective-permute-start | bytes 393224 | tf_op jit(solution)/shard_map/ppermute | solution.py:582
  51.8 6.2 %collective-permute-start.15 = (f32[2,4,16,128]{3,2,1,0:T(8,128)S(1)}, f32[2,4,16,128]{3,2,1,0:T(8,128)S(1)}, u32[]{:S(2)}, u32[]{:S(2)}) collective-permute-start(f32[2,4,16,128]{3,2,1,0:T(8,128)S(1)} %get-tuple-element.71), channel_id=1, source_target_pairs={{0,6},{1,7},{2,4},{3,5},{4,2},{5,3},{6,0},{7,1},{8,14},{9,15},{10,... | collective-permute-start | bytes 196616 | tf_op jit(solution)/shard_map/ppermute | solution.py:582
  54.4 5.1 %collective-permute-start.13 = (f32[2,4,16,128]{3,2,1,0:T(8,128)S(1)}, f32[2,4,16,128]{3,2,1,0:T(8,128)S(1)}, u32[]{:S(2)}, u32[]{:S(2)}) collective-permute-start(f32[2,4,16,128]{3,2,1,0:T(8,128)S(1)} %get-tuple-element.73), channel_id=1, source_target_pairs={{0,2},{1,3},{2,0},{3,1},{4,6},{5,7},{6,4},{7,5},{8,10},{9,11},{10,... | collective-permute-start | bytes 196616 | tf_op jit(solution)/shard_map/ppermute | solution.py:582
  56.0 6.2 %collective-permute-start.14 = (f32[2,4,16,128]{3,2,1,0:T(8,128)S(1)}, f32[2,4,16,128]{3,2,1,0:T(8,128)S(1)}, u32[]{:S(2)}, u32[]{:S(2)}) collective-permute-start(f32[2,4,16,128]{3,2,1,0:T(8,128)S(1)} %get-tuple-element.74), channel_id=1, source_target_pairs={{0,4},{1,5},{2,6},{3,7},{4,0},{5,1},{6,2},{7,3},{8,12},{9,13},{10,... | collective-permute-start | bytes 196616 | tf_op jit(solution)/shard_map/ppermute | solution.py:582

commit v13 on v12

--- a/solution.py
+++ b/solution.py
@@ -194,7 +194,7 @@
 
 
 def scan_quarters(groups, width, sums_ref, start_ref, total_ref, offset):
-    slots, colors = sums_ref.shape[0], sums_ref.shape[1]
+    colors = sums_ref.shape[1]
     group = group_ids((colors, LANES), width)
 
     def scan_groups(chunk, carry):
@@ -213,7 +213,7 @@
         total_ref[offset + chunk] = packed
         return carry
 
-    lax.fori_loop(0, slots // groups, scan_groups, 0, unroll=4)
+    lax.fori_loop(0, total_ref.shape[0] - offset, scan_groups, 0, unroll=4)
 
 
 def bin_edges(bins):
@@ -356,7 +356,7 @@
         out_shape=(
             jax.ShapeDtypeStruct((steps, slots, LANES), jnp.float32),
             jax.ShapeDtypeStruct((slots, colors, LANES), jnp.float32),
-            jax.ShapeDtypeStruct((near_total.shape[0] + slots // groups, colors, LANES),
+            jax.ShapeDtypeStruct((near_total.shape[0] + layers // groups + 1, colors, LANES),
                                  jnp.float32),
         ),
         in_specs=[pl.BlockSpec(memory_space=pltpu.VMEM)] * (count + 2),
@@ -426,7 +426,7 @@
 
     if turn:
         lax.fori_loop(0, ahead, begin_near, 0, unroll=4)
-        lax.fori_loop(0, far_start.shape[0] // groups, begin_far, 0, unroll=4)
+        lax.fori_loop(0, before_refs[0].shape[0] - ahead, begin_far, 0, unroll=4)
     ambient = columns_ref[1]
     backdrop = columns_ref[2]
     at_once = 4 if rows % 4 == 0 else 2

time: 63.5 us -> 63.2 us (level)
  no operation moved by 1% of the time
where the time goes in v13:
time: 63.2 us; the launch traced here: 62.7 us
  starting transfers between devices  22.4 us (35%)
  Pallas kernels  20.2 us (32%)
  waiting for transfers between devices  14.1 us (22%)
  local copies, waits for them, and re-layouts  5.99 us (9%)
    ppermute x11, starting transfers between devices, exchange(): return lax.ppermute(value, axis, pairs)  15.9 us
    ppermute x11, waiting for transfers between devices, exchange(): return lax.ppermute(value, axis, pairs)  10.9 us
    pallas_call x1, Pallas kernels, render_near(): pl.pallas_call(functools.partial(near_kernel, groups, width, bins, ratio,...  6.14 us
    pallas_call x1, Pallas kernels, render_far(): pl.pallas_call(functools.partial(render_rows, bins, ratio), out_shape=(ja...  5.61 us
    unnamed x14, local copies, waits for them, and re-layouts  5.28 us
    ppermute x1, starting transfers between devices, local(): after = lax.ppermute(density[:1], 'gx', down)  3.89 us
    pallas_call x2, Pallas kernels, join(): pl.pallas_call(functools.partial(join_kernel, groups, width, turn, blocks...  2.89 us
    pallas_call x1, Pallas kernels, far_depths(): pl.pallas_call(functools.partial(depth_kernel, groups, width, bins, count...  2.62 us
  transfers between devices with their start and end apart: 16, of which 8 were waited for; matrix products, arithmetic and copies ran while one was open for 0% of the time, Pallas kernels for 23%

profile of v13, /device:TPU:0, one launch (start us, length us, event | category | flops | bytes accessed | tf_op | source)
XLA Modules:
  0.0 62.7 jit_solution(9900933543952623308)
XLA Ops:
  0.0 0.7 %fusion.7 = (f32[1,8,256]{2,1,0:T(8,128)S(1)}, f32[1,8,256]{2,1,0:T(8,128)S(1)}) fusion(f32[128,8,256]{2,1,0:T(8,128)} %param.7), kind=kLoop, calls=%fused_computation.14 | loop fusion | bytes 32768 | tf_op jit(solution)/shard_map/slice | solution.py:601
  0.7 3.9 %collective-permute-start.1 = (f32[1,8,256]{2,1,0:T(8,128)S(1)}, f32[1,8,256]{2,1,0:T(8,128)S(1)}, u32[]{:S(2)}, u32[]{:S(2)}) collective-permute-start(f32[1,8,256]{2,1,0:T(8,128)S(1)} %get-tuple-element.69), channel_id=1, source_target_pairs={{8,0},{16,8},{24,16},{0,24},{9,1},{17,9},{25,17},{1,25},{10,2},{18... | collective-permute-start | bytes 24584 | tf_op jit(solution)/shard_map/ppermute | solution.py:601
  4.6 1.2 %copy-done = f32[128,8,256]{2,1,0:T(8,128)S(1)} copy-done((f32[128,8,256]{2,1,0:T(8,128)S(1)}, f32[128,8,256]{2,1,0:T(8,128)}, u32[]{:S(2)}) %copy-start) | copy-done | bytes 1048600
  5.8 0.7 %pack.1.packed_ref = f32[8,32,8,128]{3,2,1,0:T(8,128)S(1)} custom-call(f32[4,32,8,256]{3,2,1,0:T(8,128)S(1)} %bitcast.13), custom_call_target="tpu_custom_call" | custom-call | tf_op jit(solution)/shard_map/pack/pallas_call | solution.py:87
  6.6 2.6 %collective-permute-done.before_ref = f32[1,8,256]{2,1,0:T(8,128)S(1)} collective-permute-done((f32[1,8,256]{2,1,0:T(8,128)S(1)}, f32[1,8,256]{2,1,0:T(8,128)S(1)}, u32[]{:S(2)}, u32[]{:S(2)}) %collective-permute-start) | collective-permute-done | bytes 8224 | tf_op jit(solution)/shard_map/ppermute | solution.py:600
  9.4 1.6 %collective-permute-start.2 = (f32[33,8,128]{2,1,0:T(8,128)S(1)}, f32[33,8,128]{2,1,0:T(8,128)S(1)}, u32[]{:S(2)}, u32[]{:S(2)}) collective-permute-start(f32[33,8,128]{2,1,0:T(8,128)S(1)} %get-tuple-element.37), channel_id=1, source_target_pairs={{0,2},{1,3},{2,0},{3,1},{4,6},{5,7},{6,4},{7,5},{8,10},{9,11},{10,... | collective-permute-start | bytes 405512 | tf_op jit(solution)/shard_map/ppermute | solution.py:582
  11.6 2.6 %collective-permute-start.5 = (f32[33,8,128]{2,1,0:T(8,128)S(1)}, f32[33,8,128]{2,1,0:T(8,128)S(1)}, u32[]{:S(2)}, u32[]{:S(2)}) collective-permute-start(f32[33,8,128]{2,1,0:T(8,128)S(1)} %get-tuple-element.50), channel_id=1, source_target_pairs={{0,4},{1,5},{2,6},{3,7},{4,0},{5,1},{6,2},{7,3},{8,12},{9,13},{10,... | collective-permute-start | bytes 405512 | tf_op jit(solution)/shard_map/ppermute | solution.py:582
  14.2 0.8 %collective-permute-done.2.refs_2_ = f32[33,8,128]{2,1,0:T(8,128)S(1)} collective-permute-done((f32[33,8,128]{2,1,0:T(8,128)S(1)}, f32[33,8,128]{2,1,0:T(8,128)S(1)}, u32[]{:S(2)}, u32[]{:S(2)}) %collective-permute-start.2) | collective-permute-done | bytes 135200 | tf_op jit(solution)/shard_map/ppermute | solution.py:582
  15.0 3.7 %collective-permute-start.6 = (f32[33,8,128]{2,1,0:T(8,128)S(1)}, f32[33,8,128]{2,1,0:T(8,128)S(1)}, u32[]{:S(2)}, u32[]{:S(2)}) collective-permute-start(f32[33,8,128]{2,1,0:T(8,128)S(1)} %get-tuple-element.52), channel_id=1, source_target_pairs={{0,5},{1,4},{2,7},{3,6},{4,1},{5,0},{6,3},{7,2},{8,13},{9,12},{10,... | collective-permute-start | bytes 405512 | tf_op jit(solution)/shard_map/ppermute | solution.py:582
  18.7 2.4 %collective-permute-start.7 = (f32[33,8,128]{2,1,0:T(8,128)S(1)}, f32[33,8,128]{2,1,0:T(8,128)S(1)}, u32[]{:S(2)}, u32[]{:S(2)}) collective-permute-start(f32[33,8,128]{2,1,0:T(8,128)S(1)} %get-tuple-element.54), channel_id=1, source_target_pairs={{0,6},{1,7},{2,4},{3,5},{4,2},{5,3},{6,0},{7,1},{8,14},{9,15},{10,... | collective-permute-start | bytes 405512 | tf_op jit(solution)/shard_map/ppermute | solution.py:582
  21.0 0.7 %copy-done.1 = f32[256,16]{0,1:T(8,128)S(1)} copy-done((f32[256,16]{0,1:T(8,128)S(1)}, f32[256,16]{0,1:T(8,128)}, u32[]{:S(2)}) %copy-start.1) | copy-done | bytes 16408
  21.8 0.7 %copy-done.2 = f32[256,16]{0,1:T(8,128)S(1)} copy-done((f32[256,16]{0,1:T(8,128)S(1)}, f32[256,16]{0,1:T(8,128)}, u32[]{:S(2)}) %copy-start.2) | copy-done | bytes 16408
  22.5 0.7 %copy-done.3 = s32[32]{0:T(128)S(1)} copy-done((s32[32]{0:T(128)S(1)}, s32[32]{0:T(128)}, u32[]{:S(2)}) %copy-start.3) | copy-done | bytes 152
  23.1 0.7 %copy-done.4 = f32[16]{0:T(128)S(1)} copy-done((f32[16]{0:T(128)S(1)}, f32[16]{0:T(128)}, u32[]{:S(2)}) %copy-start.4) | copy-done | bytes 88
  23.8 0.7 %copy-done.5 = f32[16]{0:T(128)S(1)} copy-done((f32[16]{0:T(128)S(1)}, f32[16]{0:T(128)}, u32[]{:S(2)}) %copy-start.5) | copy-done | bytes 88
  24.4 0.7 %copy-done.6 = f32[16]{0:T(128)S(1)} copy-done((f32[16]{0:T(128)S(1)}, f32[16]{0:T(128)}, u32[]{:S(2)}) %copy-start.6) | copy-done | bytes 88
  25.1 1.0 %tables.1 = (bf16[16,96]{1,0:T(8,128)(2,1)S(1)}, bf16[32,96]{1,0:T(8,128)(2,1)S(1)}, f32[3,16,128]{2,1,0:T(8,128)S(1)}) custom-call(s32[32]{0:T(128)S(1)} %copy-done.3, f32[16]{0:T(128)S(1)} %copy-done.4, f32[16]{0:T(128)S(1)} %copy-done.5, f32[16]{0:T(128)S(1)} %copy-done.6, f32[16,256]{1,0:T(8,128)S(1)} %bitcast.15, f32[16,256]{1,0:T(8,128)S(1)} %bitcast.16), custom_call_target="tpu_custom_call" | custom-call | tf_op jit(solution)/shard_map/tables/pallas_call | solution.py:565
  26.1 6.1 %render_near.1 = (f32[32,32,16,128]{3,2,1,0:T(8,128)S(1)}, f32[32,16,128]{2,1,0:T(8,128)S(1)}, f32[32,16,128]{2,1,0:T(8,128)S(1)}, f32[32,16,128]{2,1,0:T(8,128)S(1)}, f32[8,16,128]{2,1,0:T(8,128)S(1)}) custom-call(f32[33,8,128]{2,1,0:T(8,128)S(1)} %get-tuple-element.43.refs_0_, f32[33,8,128]{2,1,0:T(8,128)S(1)} %collective-permute-done.3.refs_1_, ...), custom_call_target="tpu_custom_call" | custom-call | tf_op jit(solution)/shard_map/render_near/pallas_call | solution.py:285
  32.3 4.5 %collective-permute-done.6.refs_5_ = f32[33,8,128]{2,1,0:T(8,128)S(1)} collective-permute-done((f32[33,8,128]{2,1,0:T(8,128)S(1)}, f32[33,8,128]{2,1,0:T(8,128)S(1)}, u32[]{:S(2)}, u32[]{:S(2)}) %collective-permute-start.6) | collective-permute-done | bytes 135200 | tf_op jit(solution)/shard_map/ppermute | solution.py:582
  36.8 2.6 %far_depths.1 = (f32[32,40,128]{2,1,0:T(8,128)S(1)}, f32[40,16,128]{2,1,0:T(8,128)S(1)}, f32[17,16,128]{2,1,0:T(8,128)S(1)}) custom-call(f32[33,8,128]{2,1,0:T(8,128)S(1)} %get-tuple-element.43.refs_0_, f32[33,8,128]{2,1,0:T(8,128)S(1)} %collective-permute-done.3.refs_1_, f32[33,8,128]{2,1,0:T(8,128)S(1)} %collective-permute-done.2.refs_2_, ...), custom_call_target="tpu_custom_call" | custom-call | tf_op jit(solution)/shard_map/far_depths/pallas_call | solution.py:354
  40.3 1.6 %collective-permute-start.9 = (f32[17,16,128]{2,1,0:T(8,128)S(1)}, f32[17,16,128]{2,1,0:T(8,128)S(1)}, u32[]{:S(2)}, u32[]{:S(2)}) collective-permute-start(f32[17,16,128]{2,1,0:T(8,128)S(1)} %get-tuple-element.65), channel_id=1, source_target_pairs={{0,8},{8,16},{16,24},{24,0},{1,9},{9,17},{17,25},{25,1},{2,10},{10... | collective-permute-start | bytes 417800 | tf_op jit(solution)/shard_map/ppermute | solution.py:621
  42.0 5.6 %render_far.1 = (f32[32,33,16,128]{3,2,1,0:T(8,128)S(1)}, f32[32,16,128]{2,1,0:T(8,128)S(1)}, f32[32,16,128]{2,1,0:T(8,128)S(1)}) custom-call(f32[32,40,128]{2,1,0:T(8,128)S(1)} %get-tuple-element.59.s_ref, bf16[32,96]{1,0:T(8,128)(2,1)S(1)} %get-tuple-element.46.refs_4_.table_ref), custom_call_target="tpu_custom_call" | custom-call | flops 10000000000 | bytes 10000000 | tf_op jit(solution)/shard_map/render_far/pallas_call | solution.py:378
  47.6 0.6 collective-permute-done.10.refs_9_
  48.2 1.7 %join.2 = (f32[4,4,16,128]{3,2,1,0:T(8,128)S(1)}, f32[32,16,128]{2,1,0:T(8,128)S(1)}, f32[40,16,128]{2,1,0:T(8,128)S(1)}) custom-call(f32[3,16,128]{2,1,0:T(8,128)S(1)} %get-tuple-element.42.columns_ref, f32[32,32,16,128]{3,2,1,0:T(8,128)S(1)} %get-tuple-element.47.refs_0_, f32[32,16,128]{2,1,0:T(8,128)S(1)} %get-tuple-element.48.refs_1_, ...), custom_call_target="tpu_custom_call" | custom-call | tf_op jit(solution)/shard_map/join/pallas_call | solution.py:480
  50.0 1.2 %join.3 = f32[4,4,16,128]{3,2,1,0:T(8,128)S(1)} custom-call(f32[3,16,128]{2,1,0:T(8,128)S(1)} %get-tuple-element.42.columns_ref, f32[32,32,16,128]{3,2,1,0:T(8,128)S(1)} %get-tuple-element.47.refs_0_, f32[32,16,128]{2,1,0:T(8,128)S(1)} %get-tuple-element.48.refs_1_, f32[32,16,128]{2,1,0:T(8,128)S(1)} %get-tuple-element.49.refs_2_, ...), custom_call_target="tpu_custom_call" | custom-call | tf_op jit(solution)/shard_map/join/pallas_call | solution.py:480
  51.4 2.7 %collective-permute-start.15 = (f32[2,4,16,128]{3,2,1,0:T(8,128)S(1)}, f32[2,4,16,128]{3,2,1,0:T(8,128)S(1)}, u32[]{:S(2)}, u32[]{:S(2)}) collective-permute-start(f32[2,4,16,128]{3,2,1,0:T(8,128)S(1)} %get-tuple-element.71), channel_id=1, source_target_pairs={{0,6},{1,7},{2,4},{3,5},{4,2},{5,3},{6,0},{7,1},{8,14},{9,15},{10,... | collective-permute-start | bytes 196616 | tf_op jit(solution)/shard_map/ppermute | solution.py:582
  54.0 1.6 %collective-permute-start.13 = (f32[2,4,16,128]{3,2,1,0:T(8,128)S(1)}, f32[2,4,16,128]{3,2,1,0:T(8,128)S(1)}, u32[]{:S(2)}, u32[]{:S(2)}) collective-permute-start(f32[2,4,16,128]{3,2,1,0:T(8,128)S(1)} %get-tuple-element.73), channel_id=1, source_target_pairs={{0,2},{1,3},{2,0},{3,1},{4,6},{5,7},{6,4},{7,5},{8,10},{9,11},{10,... | collective-permute-start | bytes 196616 | tf_op jit(solution)/shard_map/ppermute | solution.py:582
  55.6 0.8 %collective-permute-start.14 = (f32[2,4,16,128]{3,2,1,0:T(8,128)S(1)}, f32[2,4,16,128]{3,2,1,0:T(8,128)S(1)}, u32[]{:S(2)}, u32[]{:S(2)}) collective-permute-start(f32[2,4,16,128]{3,2,1,0:T(8,128)S(1)} %get-tuple-element.74), channel_id=1, source_target_pairs={{0,4},{1,5},{2,6},{3,7},{4,0},{5,1},{6,2},{7,3},{8,12},{9,13},{10,... | collective-permute-start | bytes 196616 | tf_op jit(solution)/shard_map/ppermute | solution.py:582
  56.4 1.3 %collective-permute-done.15.refs_3_ = f32[2,4,16,128]{3,2,1,0:T(8,128)S(1)} collective-permute-done((f32[2,4,16,128]{3,2,1,0:T(8,128)S(1)}, f32[2,4,16,128]{3,2,1,0:T(8,128)S(1)}, u32[]{:S(2)}, u32[]{:S(2)}) %collective-permute-start.15) | collective-permute-done | bytes 65568 | tf_op jit(solution)/shard_map/ppermute | solution.py:582
  57.7 1.4 %collective-permute-done.13.refs_1_ = f32[2,4,16,128]{3,2,1,0:T(8,128)S(1)} collective-permute-done((f32[2,4,16,128]{3,2,1,0:T(8,128)S(1)}, f32[2,4,16,128]{3,2,1,0:T(8,128)S(1)}, u32[]{:S(2)}, u32[]{:S(2)}) %collective-permute-start.13) | collective-permute-done | bytes 65568 | tf_op jit(solution)/shard_map/ppermute | solution.py:582
  59.1 2.7 %collective-permute-done.14.refs_2_ = f32[2,4,16,128]{3,2,1,0:T(8,128)S(1)} collective-permute-done((f32[2,4,16,128]{3,2,1,0:T(8,128)S(1)}, f32[2,4,16,128]{3,2,1,0:T(8,128)S(1)}, u32[]{:S(2)}, u32[]{:S(2)}) %collective-permute-start.14) | collective-permute-done | bytes 65568 | tf_op jit(solution)/shard_map/ppermute | solution.py:582
  61.8 0.9 %unpack.1 = f32[16,16,256]{2,1,0:T(8,128)} custom-call(f32[2,4,16,128]{3,2,1,0:T(8,128)S(1)} %get-tuple-element.72.refs_0_, f32[2,4,16,128]{3,2,1,0:T(8,128)S(1)} %collective-permute-done.13.refs_1_, f32[2,4,16,128]{3,2,1,0:T(8,128)S(1)} %collective-permute-done.14.refs_2_, f32[2,4,16,128]{3,2,1,0:T(8,128)S(1)} %collective-permute-done.15.refs_3_), custom_call_target="tpu_custom_call" | custom-call | tf_op jit(solution)/shard_map/unpack/pallas_call | solution.py:509
  (25 shorter events, 2.0 us)
Async XLA Ops:
  0.7 5.9 %collective-permute-start.1 = (f32[1,8,256]{2,1,0:T(8,128)S(1)}, f32[1,8,256]{2,1,0:T(8,128)S(1)}, u32[]{:S(2)}, u32[]{:S(2)}) collective-permute-start(f32[1,8,256]{2,1,0:T(8,128)S(1)} %get-tuple-element.69), channel_id=1, source_target_pairs={{8,0},{16,8},{24,16},{0,24},{9,1},{17,9},{25,17},{1,25},{10,2},{18... | collective-permute-start | bytes 24584 | tf_op jit(solution)/shard_map/ppermute | solution.py:601
  4.6 4.5 %collective-permute-start = (f32[1,8,256]{2,1,0:T(8,128)S(1)}, f32[1,8,256]{2,1,0:T(8,128)S(1)}, u32[]{:S(2)}, u32[]{:S(2)}) collective-permute-start(f32[1,8,256]{2,1,0:T(8,128)S(1)} %get-tuple-element.70), channel_id=1, source_target_pairs={{0,8},{8,16},{16,24},{24,0},{1,9},{9,17},{17,25},{25,1},{2,10},{10... | collective-permute-start | bytes 24584 | tf_op jit(solution)/shard_map/ppermute | solution.py:600
  4.6 1.2 %copy-start = (f32[128,8,256]{2,1,0:T(8,128)S(1)}, f32[128,8,256]{2,1,0:T(8,128)}, u32[]{:S(2)}) copy-start(f32[128,8,256]{2,1,0:T(8,128)} %param.7) | copy-start | bytes 3145732
  9.4 5.6 %collective-permute-start.2 = (f32[33,8,128]{2,1,0:T(8,128)S(1)}, f32[33,8,128]{2,1,0:T(8,128)S(1)}, u32[]{:S(2)}, u32[]{:S(2)}) collective-permute-start(f32[33,8,128]{2,1,0:T(8,128)S(1)} %get-tuple-element.37), channel_id=1, source_target_pairs={{0,2},{1,3},{2,0},{3,1},{4,6},{5,7},{6,4},{7,5},{8,10},{9,11},{10,... | collective-permute-start | bytes 405512 | tf_op jit(solution)/shard_map/ppermute | solution.py:582
  11.0 4.0 %collective-permute-start.3 = (f32[33,8,128]{2,1,0:T(8,128)S(1)}, f32[33,8,128]{2,1,0:T(8,128)S(1)}, u32[]{:S(2)}, u32[]{:S(2)}) collective-permute-start(f32[33,8,128]{2,1,0:T(8,128)S(1)} %get-tuple-element.44), channel_id=1, source_target_pairs={{0,1},{1,0},{2,3},{3,2},{4,5},{5,4},{6,7},{7,6},{8,9},{9,8},{10,11... | collective-permute-start | bytes 405512 | tf_op jit(solution)/shard_map/ppermute | solution.py:582
  11.0 15.1 %collective-permute-start.4 = (f32[33,8,128]{2,1,0:T(8,128)S(1)}, f32[33,8,128]{2,1,0:T(8,128)S(1)}, u32[]{:S(2)}, u32[]{:S(2)}) collective-permute-start(f32[33,8,128]{2,1,0:T(8,128)S(1)} %get-tuple-element.45), channel_id=1, source_target_pairs={{0,3},{1,2},{2,1},{3,0},{4,7},{5,6},{6,5},{7,4},{8,11},{9,10},{10,... | collective-permute-start | bytes 405512 | tf_op jit(solution)/shard_map/ppermute | solution.py:582
  11.6 20.6 %collective-permute-start.5 = (f32[33,8,128]{2,1,0:T(8,128)S(1)}, f32[33,8,128]{2,1,0:T(8,128)S(1)}, u32[]{:S(2)}, u32[]{:S(2)}) collective-permute-start(f32[33,8,128]{2,1,0:T(8,128)S(1)} %get-tuple-element.50), channel_id=1, source_target_pairs={{0,4},{1,5},{2,6},{3,7},{4,0},{5,1},{6,2},{7,3},{8,12},{9,13},{10,... | collective-permute-start | bytes 405512 | tf_op jit(solution)/shard_map/ppermute | solution.py:582
  15.0 17.2 %collective-permute-start.8 = (f32[33,8,128]{2,1,0:T(8,128)S(1)}, f32[33,8,128]{2,1,0:T(8,128)S(1)}, u32[]{:S(2)}, u32[]{:S(2)}) collective-permute-start(f32[33,8,128]{2,1,0:T(8,128)S(1)} %get-tuple-element.56), channel_id=1, source_target_pairs={{0,7},{1,6},{2,5},{3,4},{4,3},{5,2},{6,1},{7,0},{8,15},{9,14},{10,... | collective-permute-start | bytes 405512 | tf_op jit(solution)/shard_map/ppermute | solution.py:582
  15.0 21.8 %collective-permute-start.6 = (f32[33,8,128]{2,1,0:T(8,128)S(1)}, f32[33,8,128]{2,1,0:T(8,128)S(1)}, u32[]{:S(2)}, u32[]{:S(2)}) collective-permute-start(f32[33,8,128]{2,1,0:T(8,128)S(1)} %get-tuple-element.52), channel_id=1, source_target_pairs={{0,5},{1,4},{2,7},{3,6},{4,1},{5,0},{6,3},{7,2},{8,13},{9,12},{10,... | collective-permute-start | bytes 405512 | tf_op jit(solution)/shard_map/ppermute | solution.py:582
  18.7 18.1 %collective-permute-start.7 = (f32[33,8,128]{2,1,0:T(8,128)S(1)}, f32[33,8,128]{2,1,0:T(8,128)S(1)}, u32[]{:S(2)}, u32[]{:S(2)}) collective-permute-start(f32[33,8,128]{2,1,0:T(8,128)S(1)} %get-tuple-element.54), channel_id=1, source_target_pairs={{0,6},{1,7},{2,4},{3,5},{4,2},{5,3},{6,0},{7,1},{8,14},{9,15},{10,... | collective-permute-start | bytes 405512 | tf_op jit(solution)/shard_map/ppermute | solution.py:582
  21.0 0.7 %copy-start.1 = (f32[256,16]{0,1:T(8,128)S(1)}, f32[256,16]{0,1:T(8,128)}, u32[]{:S(2)}) copy-start(f32[256,16]{0,1:T(8,128)} %param.9) | copy-start | bytes 49156
  21.8 0.7 %copy-start.2 = (f32[256,16]{0,1:T(8,128)S(1)}, f32[256,16]{0,1:T(8,128)}, u32[]{:S(2)}) copy-start(f32[256,16]{0,1:T(8,128)} %param.10) | copy-start | bytes 49156
  22.5 0.7 %copy-start.3 = (s32[32]{0:T(128)S(1)}, s32[32]{0:T(128)}, u32[]{:S(2)}) copy-start(s32[32]{0:T(128)} %bins_ref) | copy-start | bytes 388
  23.1 0.7 %copy-start.4 = (f32[16]{0:T(128)S(1)}, f32[16]{0:T(128)}, u32[]{:S(2)}) copy-start(f32[16]{0:T(128)} %scale_ref) | copy-start | bytes 196
  23.8 0.7 %copy-start.5 = (f32[16]{0:T(128)S(1)}, f32[16]{0:T(128)}, u32[]{:S(2)}) copy-start(f32[16]{0:T(128)} %ambient_ref) | copy-start | bytes 196
  24.4 0.7 %copy-start.6 = (f32[16]{0:T(128)S(1)}, f32[16]{0:T(128)}, u32[]{:S(2)}) copy-start(f32[16]{0:T(128)} %backdrop_ref) | copy-start | bytes 196
  39.4 8.2 %collective-permute-start.11 = (f32[17,16,128]{2,1,0:T(8,128)S(1)}, f32[17,16,128]{2,1,0:T(8,128)S(1)}, u32[]{:S(2)}, u32[]{:S(2)}) collective-permute-start(f32[17,16,128]{2,1,0:T(8,128)S(1)} %get-tuple-element.65), channel_id=1, source_target_pairs={{0,24},{8,0},{16,8},{24,16},{1,25},{9,1},{17,9},{25,17},{2,26},{10... | collective-permute-start | bytes 417800 | tf_op jit(solution)/shard_map/ppermute | solution.py:621
  39.8 8.4 %collective-permute-start.10 = (f32[17,16,128]{2,1,0:T(8,128)S(1)}, f32[17,16,128]{2,1,0:T(8,128)S(1)}, u32[]{:S(2)}, u32[]{:S(2)}) collective-permute-start(f32[17,16,128]{2,1,0:T(8,128)S(1)} %get-tuple-element.65), channel_id=1, source_target_pairs={{0,16},{8,24},{16,0},{24,8},{1,17},{9,25},{17,1},{25,9},{2,18},{10... | collective-permute-start | bytes 417800 | tf_op jit(solution)/shard_map/ppermute | solution.py:621
  40.3 7.9 %collective-permute-start.9 = (f32[17,16,128]{2,1,0:T(8,128)S(1)}, f32[17,16,128]{2,1,0:T(8,128)S(1)}, u32[]{:S(2)}, u32[]{:S(2)}) collective-permute-start(f32[17,16,128]{2,1,0:T(8,128)S(1)} %get-tuple-element.65), channel_id=1, source_target_pairs={{0,8},{8,16},{16,24},{24,0},{1,9},{9,17},{17,25},{25,1},{2,10},{10... | collective-permute-start | bytes 417800 | tf_op jit(solution)/shard_map/ppermute | solution.py:621
  49.9 1.4 %collective-permute-start.12 = (f32[4,4,16,128]{3,2,1,0:T(8,128)S(1)}, f32[4,4,16,128]{3,2,1,0:T(8,128)S(1)}, u32[]{:S(2)}, u32[]{:S(2)}) collective-permute-start(f32[4,4,16,128]{3,2,1,0:T(8,128)S(1)} %get-tuple-element.68), channel_id=1, source_target_pairs={{0,1},{1,0},{2,3},{3,2},{4,5},{5,4},{6,7},{7,6},{8,9},{9,8},{10,11... | collective-permute-start | bytes 393224 | tf_op jit(solution)/shard_map/ppermute | solution.py:582
  51.4 6.3 %collective-permute-start.15 = (f32[2,4,16,128]{3,2,1,0:T(8,128)S(1)}, f32[2,4,16,128]{3,2,1,0:T(8,128)S(1)}, u32[]{:S(2)}, u32[]{:S(2)}) collective-permute-start(f32[2,4,16,128]{3,2,1,0:T(8,128)S(1)} %get-tuple-element.71), channel_id=1, source_target_pairs={{0,6},{1,7},{2,4},{3,5},{4,2},{5,3},{6,0},{7,1},{8,14},{9,15},{10,... | collective-permute-start | bytes 196616 | tf_op jit(solution)/shard_map/ppermute | solution.py:582
  54.0 5.1 %collective-permute-start.13 = (f32[2,4,16,128]{3,2,1,0:T(8,128)S(1)}, f32[2,4,16,128]{3,2,1,0:T(8,128)S(1)}, u32[]{:S(2)}, u32[]{:S(2)}) collective-permute-start(f32[2,4,16,128]{3,2,1,0:T(8,128)S(1)} %get-tuple-element.73), channel_id=1, source_target_pairs={{0,2},{1,3},{2,0},{3,1},{4,6},{5,7},{6,4},{7,5},{8,10},{9,11},{10,... | collective-permute-start | bytes 196616 | tf_op jit(solution)/shard_map/ppermute | solution.py:582
  55.6 6.2 %collective-permute-start.14 = (f32[2,4,16,128]{3,2,1,0:T(8,128)S(1)}, f32[2,4,16,128]{3,2,1,0:T(8,128)S(1)}, u32[]{:S(2)}, u32[]{:S(2)}) collective-permute-start(f32[2,4,16,128]{3,2,1,0:T(8,128)S(1)} %get-tuple-element.74), channel_id=1, source_target_pairs={{0,4},{1,5},{2,6},{3,7},{4,0},{5,1},{6,2},{7,3},{8,12},{9,13},{10,... | collective-permute-start | bytes 196616 | tf_op jit(solution)/shard_map/ppermute | solution.py:582

commit v14 on v13

--- a/solution.py
+++ b/solution.py
@@ -190,7 +190,7 @@
             s_ref[step] = jnp.where(empty, -1.0, total[depth:depth + layers])
         return carry
 
-    lax.fori_loop(0, steps, smooth, 0, unroll=4)
+    lax.fori_loop(0, steps, smooth, 0, unroll=8)
 
 
 def scan_quarters(groups, width, sums_ref, start_ref, total_ref, offset):
@@ -266,7 +266,7 @@
         unlit_ref[step], through_ref[step] = unlit, through
         return carry
 
-    lax.fori_loop(0, steps, advance, 0, unroll=4)
+    lax.fori_loop(0, steps, advance, 0, unroll=8)
 
 
 def near_kernel(groups, width, bins, ratio, count, *refs):
@@ -306,7 +306,7 @@
 
 def depth_kernel(groups, width, bins, count, *refs):
     pieces = refs[:count]
-    near_ref, table_ref, s_ref, start_ref, total_ref, raw, sums, products_ref = refs[count:]
+    _, table_ref, s_ref, start_ref, total_ref, raw, sums, products_ref = refs[count:]
     steps, depth = pieces[0].shape[-3] - 1, pieces[0].shape[-2]
     layers = depth * (count // 2)
     slots = s_ref.shape[1]
@@ -339,9 +339,7 @@
         return carry
 
     lax.fori_loop(0, slots // at_once, products, 0, unroll=True)
-    ahead = near_ref.shape[0]
-    total_ref[0:ahead] = near_ref[...]
-    scan_quarters(groups, width, products_ref, start_ref, total_ref, ahead)
+    scan_quarters(groups, width, products_ref, start_ref, total_ref, 0)
 
 
 def far_depths(pieces, near_total, table, groups, width, bins):
@@ -356,8 +354,7 @@
         out_shape=(
             jax.ShapeDtypeStruct((steps, slots, LANES), jnp.float32),
             jax.ShapeDtypeStruct((slots, colors, LANES), jnp.float32),
-            jax.ShapeDtypeStruct((near_total.shape[0] + layers // groups + 1, colors, LANES),
-                                 jnp.float32),
+            jax.ShapeDtypeStruct((layers // groups + 1, colors, LANES), jnp.float32),
         ),
         in_specs=[pl.BlockSpec(memory_space=pltpu.VMEM)] * (count + 2),
         out_specs=[pl.BlockSpec(memory_space=pltpu.VMEM)] * 3,
@@ -393,6 +390,7 @@
     if turn:
         near_start, far_start = refs[6:8]
         before_refs, out_ref, near_light, far_light, image = refs[8:-4], *refs[-4:]
+        hops = len(before_refs) // 2
     else:
         near_light, far_light, out_ref, image = refs[6:]
     rows, colors, _ = image.shape
@@ -404,10 +402,10 @@
     group = group_ids((colors, LANES), width)
     ahead = layers // groups
 
-    def begin(chunk, start_ref, offset, light):
+    def begin(chunk, start_ref, refs, light):
         packed = jnp.zeros((colors, LANES), jnp.float32)
-        for hop, ref in enumerate(before_refs, 1):
-            packed = packed + jnp.where(position >= hop, ref[offset + chunk], 0.0)
+        for hop, ref in enumerate(refs, 1):
+            packed = packed + jnp.where(position >= hop, ref[chunk], 0.0)
         moved = [packed] + [pltpu.roll(packed, k * width, 1) for k in range(1, groups)]
         for k in range(groups):
             value = moved[-k % groups]
@@ -417,16 +415,16 @@
             light[z] = jnp.exp2(start_ref[z] + value)
 
     def begin_near(chunk, carry):
-        begin(chunk, near_start, 0, near_light)
+        begin(chunk, near_start, before_refs[:hops], near_light)
         return carry
 
     def begin_far(chunk, carry):
-        begin(chunk, far_start, ahead, far_light)
+        begin(chunk, far_start, before_refs[hops:], far_light)
         return carry
 
     if turn:
         lax.fori_loop(0, ahead, begin_near, 0, unroll=4)
-        lax.fori_loop(0, before_refs[0].shape[0] - ahead, begin_far, 0, unroll=4)
+        lax.fori_loop(0, before_refs[hops].shape[0], begin_far, 0, unroll=3)
     ambient = columns_ref[1]
     backdrop = columns_ref[2]
     at_once = 4 if rows % 4 == 0 else 2
@@ -617,10 +615,9 @@
     ratio = step_x / step_z
     *near, near_start, near_total = render_near(
         pieces[:blocks], table, colors, groups, width, bins, ratio, count)
-    s, start, total = far_depths(pieces, near_total, sum_table, groups, width, bins)
+    s, start, far_total = far_depths(pieces, near_total, sum_table, groups, width, bins)
     sums = [lax.ppermute(total, "gx", [(i, (i + hop) % size_x) for i in range(size_x)])
-            for hop in range(1, size_x)]
-
+            for total in (near_total, far_total) for hop in range(1, size_x)]
     layers = depth * blocks
     far = render_far(s, table, colors, bins, ratio, layers + 1)
     other, *light = join(

time: 63.2 us -> 62.6 us (level)
  waiting for transfers between devices: 14.1 us -> 11.5 us
  starting transfers between devices: 22.4 us -> 24.9 us
  Pallas kernels: 20.2 us -> 19.5 us
    ppermute x3 -> x6, starting transfers between devices: 2.58 us -> 5.17 us  [local(): lax.ppermute(total, 'gx', [(i, (i + hop) % size_x) for i in range(size_x)])]
    ppermute x11, waiting for transfers between devices: 10.9 us -> 8.94 us  [exchange(): return lax.ppermute(value, axis, pairs)]
  transfers between devices with their start and end apart: 16 -> 19, of which waited for: 8 -> 7; matrix products, arithmetic and copies ran while one was open for 0% -> 0% of each run, Pallas kernels for 23% -> 27%
where the time goes in v14:
time: 62.6 us; the launch traced here: 62.1 us
  starting transfers between devices  24.9 us (40%)
  Pallas kernels  19.5 us (31%)
  waiting for transfers between devices  11.5 us (18%)
  local copies, waits for them, and re-layouts  5.99 us (10%)
    ppermute x11, starting transfers between devices, exchange(): return lax.ppermute(value, axis, pairs)  15.9 us
    ppermute x11, waiting for transfers between devices, exchange(): return lax.ppermute(value, axis, pairs)  8.94 us
    pallas_call x1, Pallas kernels, render_near(): pl.pallas_call(functools.partial(near_kernel, groups, width, bins, ratio,...  5.82 us
    pallas_call x1, Pallas kernels, render_far(): pl.pallas_call(functools.partial(render_rows, bins, ratio), out_shape=(ja...  5.3 us
    unnamed x14, local copies, waits for them, and re-layouts  5.28 us
    ppermute x6, starting transfers between devices, local(): lax.ppermute(total, 'gx', [(i, (i + hop) % size_x) for i in range(size_x)])  5.17 us
    ppermute x1, starting transfers between devices, local(): after = lax.ppermute(density[:1], 'gx', down)  3.89 us
    pallas_call x2, Pallas kernels, join(): pl.pallas_call(functools.partial(join_kernel, groups, width, turn, blocks...  2.92 us
  transfers between devices with their start and end apart: 19, of which 7 were waited for; matrix products, arithmetic and copies ran while one was open for 0% of the time, Pallas kernels for 27%

profile of v14, /device:TPU:0, one launch (start us, length us, event | category | flops | bytes accessed | tf_op | source)
XLA Modules:
  0.0 62.1 jit_solution(9410755162758512102)
XLA Ops:
  0.0 0.7 %fusion.7 = (f32[1,8,256]{2,1,0:T(8,128)S(1)}, f32[1,8,256]{2,1,0:T(8,128)S(1)}) fusion(f32[128,8,256]{2,1,0:T(8,128)} %param.7), kind=kLoop, calls=%fused_computation.14 | loop fusion | bytes 32768 | tf_op jit(solution)/shard_map/slice | solution.py:599
  0.7 3.9 %collective-permute-start.1 = (f32[1,8,256]{2,1,0:T(8,128)S(1)}, f32[1,8,256]{2,1,0:T(8,128)S(1)}, u32[]{:S(2)}, u32[]{:S(2)}) collective-permute-start(f32[1,8,256]{2,1,0:T(8,128)S(1)} %get-tuple-element.69), channel_id=1, source_target_pairs={{8,0},{16,8},{24,16},{0,24},{9,1},{17,9},{25,17},{1,25},{10,2},{18... | collective-permute-start | bytes 24584 | tf_op jit(solution)/shard_map/ppermute | solution.py:599
  4.6 1.2 %copy-done = f32[128,8,256]{2,1,0:T(8,128)S(1)} copy-done((f32[128,8,256]{2,1,0:T(8,128)S(1)}, f32[128,8,256]{2,1,0:T(8,128)}, u32[]{:S(2)}) %copy-start) | copy-done | bytes 1048600
  5.8 0.7 %pack.1.packed_ref = f32[8,32,8,128]{3,2,1,0:T(8,128)S(1)} custom-call(f32[4,32,8,256]{3,2,1,0:T(8,128)S(1)} %bitcast.13), custom_call_target="tpu_custom_call" | custom-call | tf_op jit(solution)/shard_map/pack/pallas_call | solution.py:87
  6.6 2.6 %collective-permute-done.before_ref = f32[1,8,256]{2,1,0:T(8,128)S(1)} collective-permute-done((f32[1,8,256]{2,1,0:T(8,128)S(1)}, f32[1,8,256]{2,1,0:T(8,128)S(1)}, u32[]{:S(2)}, u32[]{:S(2)}) %collective-permute-start) | collective-permute-done | bytes 8224 | tf_op jit(solution)/shard_map/ppermute | solution.py:598
  9.4 1.6 %collective-permute-start.2 = (f32[33,8,128]{2,1,0:T(8,128)S(1)}, f32[33,8,128]{2,1,0:T(8,128)S(1)}, u32[]{:S(2)}, u32[]{:S(2)}) collective-permute-start(f32[33,8,128]{2,1,0:T(8,128)S(1)} %get-tuple-element.37), channel_id=1, source_target_pairs={{0,2},{1,3},{2,0},{3,1},{4,6},{5,7},{6,4},{7,5},{8,10},{9,11},{10,... | collective-permute-start | bytes 405512 | tf_op jit(solution)/shard_map/ppermute | solution.py:580
  11.0 0.6 collective-permute-start.4
  11.6 2.6 %collective-permute-start.5 = (f32[33,8,128]{2,1,0:T(8,128)S(1)}, f32[33,8,128]{2,1,0:T(8,128)S(1)}, u32[]{:S(2)}, u32[]{:S(2)}) collective-permute-start(f32[33,8,128]{2,1,0:T(8,128)S(1)} %get-tuple-element.50), channel_id=1, source_target_pairs={{0,4},{1,5},{2,6},{3,7},{4,0},{5,1},{6,2},{7,3},{8,12},{9,13},{10,... | collective-permute-start | bytes 405512 | tf_op jit(solution)/shard_map/ppermute | solution.py:580
  14.2 0.8 %collective-permute-done.2.refs_2_ = f32[33,8,128]{2,1,0:T(8,128)S(1)} collective-permute-done((f32[33,8,128]{2,1,0:T(8,128)S(1)}, f32[33,8,128]{2,1,0:T(8,128)S(1)}, u32[]{:S(2)}, u32[]{:S(2)}) %collective-permute-start.2) | collective-permute-done | bytes 135200 | tf_op jit(solution)/shard_map/ppermute | solution.py:580
  15.0 3.7 %collective-permute-start.6 = (f32[33,8,128]{2,1,0:T(8,128)S(1)}, f32[33,8,128]{2,1,0:T(8,128)S(1)}, u32[]{:S(2)}, u32[]{:S(2)}) collective-permute-start(f32[33,8,128]{2,1,0:T(8,128)S(1)} %get-tuple-element.52), channel_id=1, source_target_pairs={{0,5},{1,4},{2,7},{3,6},{4,1},{5,0},{6,3},{7,2},{8,13},{9,12},{10,... | collective-permute-start | bytes 405512 | tf_op jit(solution)/shard_map/ppermute | solution.py:580
  18.7 2.4 %collective-permute-start.7 = (f32[33,8,128]{2,1,0:T(8,128)S(1)}, f32[33,8,128]{2,1,0:T(8,128)S(1)}, u32[]{:S(2)}, u32[]{:S(2)}) collective-permute-start(f32[33,8,128]{2,1,0:T(8,128)S(1)} %get-tuple-element.54), channel_id=1, source_target_pairs={{0,6},{1,7},{2,4},{3,5},{4,2},{5,3},{6,0},{7,1},{8,14},{9,15},{10,... | collective-permute-start | bytes 405512 | tf_op jit(solution)/shard_map/ppermute | solution.py:580
  21.0 0.7 %copy-done.1 = f32[256,16]{0,1:T(8,128)S(1)} copy-done((f32[256,16]{0,1:T(8,128)S(1)}, f32[256,16]{0,1:T(8,128)}, u32[]{:S(2)}) %copy-start.1) | copy-done | bytes 16408
  21.8 0.7 %copy-done.2 = f32[256,16]{0,1:T(8,128)S(1)} copy-done((f32[256,16]{0,1:T(8,128)S(1)}, f32[256,16]{0,1:T(8,128)}, u32[]{:S(2)}) %copy-start.2) | copy-done | bytes 16408
  22.5 0.7 %copy-done.3 = s32[32]{0:T(128)S(1)} copy-done((s32[32]{0:T(128)S(1)}, s32[32]{0:T(128)}, u32[]{:S(2)}) %copy-start.3) | copy-done | bytes 152
  23.1 0.7 %copy-done.4 = f32[16]{0:T(128)S(1)} copy-done((f32[16]{0:T(128)S(1)}, f32[16]{0:T(128)}, u32[]{:S(2)}) %copy-start.4) | copy-done | bytes 88
  23.8 0.7 %copy-done.5 = f32[16]{0:T(128)S(1)} copy-done((f32[16]{0:T(128)S(1)}, f32[16]{0:T(128)}, u32[]{:S(2)}) %copy-start.5) | copy-done | bytes 88
  24.4 0.7 %copy-done.6 = f32[16]{0:T(128)S(1)} copy-done((f32[16]{0:T(128)S(1)}, f32[16]{0:T(128)}, u32[]{:S(2)}) %copy-start.6) | copy-done | bytes 88
  25.1 1.0 %tables.1 = (bf16[16,96]{1,0:T(8,128)(2,1)S(1)}, bf16[32,96]{1,0:T(8,128)(2,1)S(1)}, f32[3,16,128]{2,1,0:T(8,128)S(1)}) custom-call(s32[32]{0:T(128)S(1)} %copy-done.3, f32[16]{0:T(128)S(1)} %copy-done.4, f32[16]{0:T(128)S(1)} %copy-done.5, f32[16]{0:T(128)S(1)} %copy-done.6, f32[16,256]{1,0:T(8,128)S(1)} %bitcast.15, f32[16,256]{1,0:T(8,128)S(1)} %bitcast.16), custom_call_target="tpu_custom_call" | custom-call | tf_op jit(solution)/shard_map/tables/pallas_call | solution.py:563
  26.1 5.8 %render_near.1 = (f32[32,32,16,128]{3,2,1,0:T(8,128)S(1)}, f32[32,16,128]{2,1,0:T(8,128)S(1)}, f32[32,16,128]{2,1,0:T(8,128)S(1)}, f32[32,16,128]{2,1,0:T(8,128)S(1)}, f32[8,16,128]{2,1,0:T(8,128)S(1)}) custom-call(f32[33,8,128]{2,1,0:T(8,128)S(1)} %get-tuple-element.43.refs_0_, f32[33,8,128]{2,1,0:T(8,128)S(1)} %collective-permute-done.3.refs_1_, ...), custom_call_target="tpu_custom_call" | custom-call | tf_op jit(solution)/shard_map/render_near/pallas_call | solution.py:285
  32.9 1.6 %collective-permute-start.9 = (f32[8,16,128]{2,1,0:T(8,128)S(1)}, f32[8,16,128]{2,1,0:T(8,128)S(1)}, u32[]{:S(2)}, u32[]{:S(2)}) collective-permute-start(f32[8,16,128]{2,1,0:T(8,128)S(1)} %get-tuple-element.57.refs_8_), channel_id=1, source_target_pairs={{0,8},{8,16},{16,24},{24,0},{1,9},{9,17},{17,25},{25,1},{2,10},{10... | collective-permute-start | bytes 196616 | tf_op jit(solution)/shard_map/ppermute | solution.py:619
  34.5 2.3 %collective-permute-done.6.refs_5_ = f32[33,8,128]{2,1,0:T(8,128)S(1)} collective-permute-done((f32[33,8,128]{2,1,0:T(8,128)S(1)}, f32[33,8,128]{2,1,0:T(8,128)S(1)}, u32[]{:S(2)}, u32[]{:S(2)}) %collective-permute-start.6) | collective-permute-done | bytes 135200 | tf_op jit(solution)/shard_map/ppermute | solution.py:580
  36.8 2.6 %far_depths.1 = (f32[32,40,128]{2,1,0:T(8,128)S(1)}, f32[40,16,128]{2,1,0:T(8,128)S(1)}, f32[9,16,128]{2,1,0:T(8,128)S(1)}) custom-call(f32[33,8,128]{2,1,0:T(8,128)S(1)} %get-tuple-element.43.refs_0_, f32[33,8,128]{2,1,0:T(8,128)S(1)} %collective-permute-done.3.refs_1_, f32[33,8,128]{2,1,0:T(8,128)S(1)} %collective-permute-done.2.refs_2_, ...), custom_call_target="tpu_custom_call" | custom-call | tf_op jit(solution)/shard_map/far_depths/pallas_call | solution.py:352
  40.3 1.6 %collective-permute-start.12 = (f32[9,16,128]{2,1,0:T(8,128)S(1)}, f32[9,16,128]{2,1,0:T(8,128)S(1)}, u32[]{:S(2)}, u32[]{:S(2)}) collective-permute-start(f32[9,16,128]{2,1,0:T(8,128)S(1)} %get-tuple-element.65), channel_id=1, source_target_pairs={{0,8},{8,16},{16,24},{24,0},{1,9},{9,17},{17,25},{25,1},{2,10},{10... | collective-permute-start | bytes 221192 | tf_op jit(solution)/shard_map/ppermute | solution.py:619
  42.0 5.3 %render_far.1 = (f32[32,33,16,128]{3,2,1,0:T(8,128)S(1)}, f32[32,16,128]{2,1,0:T(8,128)S(1)}, f32[32,16,128]{2,1,0:T(8,128)S(1)}) custom-call(f32[32,40,128]{2,1,0:T(8,128)S(1)} %get-tuple-element.59.s_ref, bf16[32,96]{1,0:T(8,128)(2,1)S(1)} %get-tuple-element.46.refs_4_.table_ref), custom_call_target="tpu_custom_call" | custom-call | flops 10000000000 | bytes 10000000 | tf_op jit(solution)/shard_map/render_far/pallas_call | solution.py:375
  47.3 1.7 %join.2 = (f32[4,4,16,128]{3,2,1,0:T(8,128)S(1)}, f32[32,16,128]{2,1,0:T(8,128)S(1)}, f32[40,16,128]{2,1,0:T(8,128)S(1)}) custom-call(f32[3,16,128]{2,1,0:T(8,128)S(1)} %get-tuple-element.42.columns_ref, f32[32,32,16,128]{3,2,1,0:T(8,128)S(1)} %get-tuple-element.47.refs_0_, f32[32,16,128]{2,1,0:T(8,128)S(1)} %get-tuple-element.48.refs_1_, ...), custom_call_target="tpu_custom_call" | custom-call | tf_op jit(solution)/shard_map/join/pallas_call | solution.py:478
  49.1 1.2 %join.3 = f32[4,4,16,128]{3,2,1,0:T(8,128)S(1)} custom-call(f32[3,16,128]{2,1,0:T(8,128)S(1)} %get-tuple-element.42.columns_ref, f32[32,32,16,128]{3,2,1,0:T(8,128)S(1)} %get-tuple-element.47.refs_0_, f32[32,16,128]{2,1,0:T(8,128)S(1)} %get-tuple-element.48.refs_1_, f32[32,16,128]{2,1,0:T(8,128)S(1)} %get-tuple-element.49.refs_2_, ...), custom_call_target="tpu_custom_call" | custom-call | tf_op jit(solution)/shard_map/join/pallas_call | solution.py:478
  50.5 1.8 %collective-permute-start.18 = (f32[2,4,16,128]{3,2,1,0:T(8,128)S(1)}, f32[2,4,16,128]{3,2,1,0:T(8,128)S(1)}, u32[]{:S(2)}, u32[]{:S(2)}) collective-permute-start(f32[2,4,16,128]{3,2,1,0:T(8,128)S(1)} %get-tuple-element.71), channel_id=1, source_target_pairs={{0,6},{1,7},{2,4},{3,5},{4,2},{5,3},{6,0},{7,1},{8,14},{9,15},{10,... | collective-permute-start | bytes 196616 | tf_op jit(solution)/shard_map/ppermute | solution.py:580
  52.3 3.0 %collective-permute-start.16 = (f32[2,4,16,128]{3,2,1,0:T(8,128)S(1)}, f32[2,4,16,128]{3,2,1,0:T(8,128)S(1)}, u32[]{:S(2)}, u32[]{:S(2)}) collective-permute-start(f32[2,4,16,128]{3,2,1,0:T(8,128)S(1)} %get-tuple-element.73), channel_id=1, source_target_pairs={{0,2},{1,3},{2,0},{3,1},{4,6},{5,7},{6,4},{7,5},{8,10},{9,11},{10,... | collective-permute-start | bytes 196616 | tf_op jit(solution)/shard_map/ppermute | solution.py:580
  55.5 1.3 %collective-permute-done.18.refs_3_ = f32[2,4,16,128]{3,2,1,0:T(8,128)S(1)} collective-permute-done((f32[2,4,16,128]{3,2,1,0:T(8,128)S(1)}, f32[2,4,16,128]{3,2,1,0:T(8,128)S(1)}, u32[]{:S(2)}, u32[]{:S(2)}) %collective-permute-start.18) | collective-permute-done | bytes 65568 | tf_op jit(solution)/shard_map/ppermute | solution.py:580
  56.8 1.4 %collective-permute-done.16.refs_1_ = f32[2,4,16,128]{3,2,1,0:T(8,128)S(1)} collective-permute-done((f32[2,4,16,128]{3,2,1,0:T(8,128)S(1)}, f32[2,4,16,128]{3,2,1,0:T(8,128)S(1)}, u32[]{:S(2)}, u32[]{:S(2)}) %collective-permute-start.16) | collective-permute-done | bytes 65568 | tf_op jit(solution)/shard_map/ppermute | solution.py:580
  58.1 3.1 %collective-permute-done.17.refs_2_ = f32[2,4,16,128]{3,2,1,0:T(8,128)S(1)} collective-permute-done((f32[2,4,16,128]{3,2,1,0:T(8,128)S(1)}, f32[2,4,16,128]{3,2,1,0:T(8,128)S(1)}, u32[]{:S(2)}, u32[]{:S(2)}) %collective-permute-start.17) | collective-permute-done | bytes 65568 | tf_op jit(solution)/shard_map/ppermute | solution.py:580
  61.2 0.9 %unpack.1 = f32[16,16,256]{2,1,0:T(8,128)} custom-call(f32[2,4,16,128]{3,2,1,0:T(8,128)S(1)} %get-tuple-element.72.refs_0_, f32[2,4,16,128]{3,2,1,0:T(8,128)S(1)} %collective-permute-done.16.refs_1_, f32[2,4,16,128]{3,2,1,0:T(8,128)S(1)} %collective-permute-done.17.refs_2_, f32[2,4,16,128]{3,2,1,0:T(8,128)S(1)} %collective-permute-done.18.refs_3_), custom_call_target="tpu_custom_call" | custom-call | tf_op jit(solution)/shard_map/unpack/pallas_call | solution.py:507
  (31 shorter events, 2.6 us)
Async XLA Ops:
  0.7 5.9 %collective-permute-start.1 = (f32[1,8,256]{2,1,0:T(8,128)S(1)}, f32[1,8,256]{2,1,0:T(8,128)S(1)}, u32[]{:S(2)}, u32[]{:S(2)}) collective-permute-start(f32[1,8,256]{2,1,0:T(8,128)S(1)} %get-tuple-element.69), channel_id=1, source_target_pairs={{8,0},{16,8},{24,16},{0,24},{9,1},{17,9},{25,17},{1,25},{10,2},{18... | collective-permute-start | bytes 24584 | tf_op jit(solution)/shard_map/ppermute | solution.py:599
  4.6 4.5 %collective-permute-start = (f32[1,8,256]{2,1,0:T(8,128)S(1)}, f32[1,8,256]{2,1,0:T(8,128)S(1)}, u32[]{:S(2)}, u32[]{:S(2)}) collective-permute-start(f32[1,8,256]{2,1,0:T(8,128)S(1)} %get-tuple-element.70), channel_id=1, source_target_pairs={{0,8},{8,16},{16,24},{24,0},{1,9},{9,17},{17,25},{25,1},{2,10},{10... | collective-permute-start | bytes 24584 | tf_op jit(solution)/shard_map/ppermute | solution.py:598
  4.6 1.2 %copy-start = (f32[128,8,256]{2,1,0:T(8,128)S(1)}, f32[128,8,256]{2,1,0:T(8,128)}, u32[]{:S(2)}) copy-start(f32[128,8,256]{2,1,0:T(8,128)} %param.7) | copy-start | bytes 3145732
  9.4 5.6 %collective-permute-start.2 = (f32[33,8,128]{2,1,0:T(8,128)S(1)}, f32[33,8,128]{2,1,0:T(8,128)S(1)}, u32[]{:S(2)}, u32[]{:S(2)}) collective-permute-start(f32[33,8,128]{2,1,0:T(8,128)S(1)} %get-tuple-element.37), channel_id=1, source_target_pairs={{0,2},{1,3},{2,0},{3,1},{4,6},{5,7},{6,4},{7,5},{8,10},{9,11},{10,... | collective-permute-start | bytes 405512 | tf_op jit(solution)/shard_map/ppermute | solution.py:580
  11.0 4.0 %collective-permute-start.3 = (f32[33,8,128]{2,1,0:T(8,128)S(1)}, f32[33,8,128]{2,1,0:T(8,128)S(1)}, u32[]{:S(2)}, u32[]{:S(2)}) collective-permute-start(f32[33,8,128]{2,1,0:T(8,128)S(1)} %get-tuple-element.44), channel_id=1, source_target_pairs={{0,1},{1,0},{2,3},{3,2},{4,5},{5,4},{6,7},{7,6},{8,9},{9,8},{10,11... | collective-permute-start | bytes 405512 | tf_op jit(solution)/shard_map/ppermute | solution.py:580
  11.0 15.1 %collective-permute-start.4 = (f32[33,8,128]{2,1,0:T(8,128)S(1)}, f32[33,8,128]{2,1,0:T(8,128)S(1)}, u32[]{:S(2)}, u32[]{:S(2)}) collective-permute-start(f32[33,8,128]{2,1,0:T(8,128)S(1)} %get-tuple-element.45), channel_id=1, source_target_pairs={{0,3},{1,2},{2,1},{3,0},{4,7},{5,6},{6,5},{7,4},{8,11},{9,10},{10,... | collective-permute-start | bytes 405512 | tf_op jit(solution)/shard_map/ppermute | solution.py:580
  11.6 20.8 %collective-permute-start.5 = (f32[33,8,128]{2,1,0:T(8,128)S(1)}, f32[33,8,128]{2,1,0:T(8,128)S(1)}, u32[]{:S(2)}, u32[]{:S(2)}) collective-permute-start(f32[33,8,128]{2,1,0:T(8,128)S(1)} %get-tuple-element.50), channel_id=1, source_target_pairs={{0,4},{1,5},{2,6},{3,7},{4,0},{5,1},{6,2},{7,3},{8,12},{9,13},{10,... | collective-permute-start | bytes 405512 | tf_op jit(solution)/shard_map/ppermute | solution.py:580
  15.0 17.9 %collective-permute-start.8 = (f32[33,8,128]{2,1,0:T(8,128)S(1)}, f32[33,8,128]{2,1,0:T(8,128)S(1)}, u32[]{:S(2)}, u32[]{:S(2)}) collective-permute-start(f32[33,8,128]{2,1,0:T(8,128)S(1)} %get-tuple-element.56), channel_id=1, source_target_pairs={{0,7},{1,6},{2,5},{3,4},{4,3},{5,2},{6,1},{7,0},{8,15},{9,14},{10,... | collective-permute-start | bytes 405512 | tf_op jit(solution)/shard_map/ppermute | solution.py:580
  15.0 21.8 %collective-permute-start.6 = (f32[33,8,128]{2,1,0:T(8,128)S(1)}, f32[33,8,128]{2,1,0:T(8,128)S(1)}, u32[]{:S(2)}, u32[]{:S(2)}) collective-permute-start(f32[33,8,128]{2,1,0:T(8,128)S(1)} %get-tuple-element.52), channel_id=1, source_target_pairs={{0,5},{1,4},{2,7},{3,6},{4,1},{5,0},{6,3},{7,2},{8,13},{9,12},{10,... | collective-permute-start | bytes 405512 | tf_op jit(solution)/shard_map/ppermute | solution.py:580
  18.7 18.1 %collective-permute-start.7 = (f32[33,8,128]{2,1,0:T(8,128)S(1)}, f32[33,8,128]{2,1,0:T(8,128)S(1)}, u32[]{:S(2)}, u32[]{:S(2)}) collective-permute-start(f32[33,8,128]{2,1,0:T(8,128)S(1)} %get-tuple-element.54), channel_id=1, source_target_pairs={{0,6},{1,7},{2,4},{3,5},{4,2},{5,3},{6,0},{7,1},{8,14},{9,15},{10,... | collective-permute-start | bytes 405512 | tf_op jit(solution)/shard_map/ppermute | solution.py:580
  21.0 0.7 %copy-start.1 = (f32[256,16]{0,1:T(8,128)S(1)}, f32[256,16]{0,1:T(8,128)}, u32[]{:S(2)}) copy-start(f32[256,16]{0,1:T(8,128)} %param.9) | copy-start | bytes 49156
  21.8 0.7 %copy-start.2 = (f32[256,16]{0,1:T(8,128)S(1)}, f32[256,16]{0,1:T(8,128)}, u32[]{:S(2)}) copy-start(f32[256,16]{0,1:T(8,128)} %param.10) | copy-start | bytes 49156
  22.5 0.7 %copy-start.3 = (s32[32]{0:T(128)S(1)}, s32[32]{0:T(128)}, u32[]{:S(2)}) copy-start(s32[32]{0:T(128)} %bins_ref) | copy-start | bytes 388
  23.1 0.7 %copy-start.4 = (f32[16]{0:T(128)S(1)}, f32[16]{0:T(128)}, u32[]{:S(2)}) copy-start(f32[16]{0:T(128)} %scale_ref) | copy-start | bytes 196
  23.8 0.7 %copy-start.5 = (f32[16]{0:T(128)S(1)}, f32[16]{0:T(128)}, u32[]{:S(2)}) copy-start(f32[16]{0:T(128)} %ambient_ref) | copy-start | bytes 196
  24.4 0.7 %copy-start.6 = (f32[16]{0:T(128)S(1)}, f32[16]{0:T(128)}, u32[]{:S(2)}) copy-start(f32[16]{0:T(128)} %backdrop_ref) | copy-start | bytes 196
  31.9 8.4 %collective-permute-start.11 = (f32[8,16,128]{2,1,0:T(8,128)S(1)}, f32[8,16,128]{2,1,0:T(8,128)S(1)}, u32[]{:S(2)}, u32[]{:S(2)}) collective-permute-start(f32[8,16,128]{2,1,0:T(8,128)S(1)} %get-tuple-element.57.refs_8_), channel_id=1, source_target_pairs={{0,24},{8,0},{16,8},{24,16},{1,25},{9,1},{17,9},{25,17},{2,26},{10... | collective-permute-start | bytes 196616 | tf_op jit(solution)/shard_map/ppermute | solution.py:619
  32.4 14.9 %collective-permute-start.10 = (f32[8,16,128]{2,1,0:T(8,128)S(1)}, f32[8,16,128]{2,1,0:T(8,128)S(1)}, u32[]{:S(2)}, u32[]{:S(2)}) collective-permute-start(f32[8,16,128]{2,1,0:T(8,128)S(1)} %get-tuple-element.57.refs_8_), channel_id=1, source_target_pairs={{0,16},{8,24},{16,0},{24,8},{1,17},{9,25},{17,1},{25,9},{2,18},{10... | collective-permute-start | bytes 196616 | tf_op jit(solution)/shard_map/ppermute | solution.py:619
  32.9 14.4 %collective-permute-start.9 = (f32[8,16,128]{2,1,0:T(8,128)S(1)}, f32[8,16,128]{2,1,0:T(8,128)S(1)}, u32[]{:S(2)}, u32[]{:S(2)}) collective-permute-start(f32[8,16,128]{2,1,0:T(8,128)S(1)} %get-tuple-element.57.refs_8_), channel_id=1, source_target_pairs={{0,8},{8,16},{16,24},{24,0},{1,9},{9,17},{17,25},{25,1},{2,10},{10... | collective-permute-start | bytes 196616 | tf_op jit(solution)/shard_map/ppermute | solution.py:619
  39.4 7.9 %collective-permute-start.14 = (f32[9,16,128]{2,1,0:T(8,128)S(1)}, f32[9,16,128]{2,1,0:T(8,128)S(1)}, u32[]{:S(2)}, u32[]{:S(2)}) collective-permute-start(f32[9,16,128]{2,1,0:T(8,128)S(1)} %get-tuple-element.65), channel_id=1, source_target_pairs={{0,24},{8,0},{16,8},{24,16},{1,25},{9,1},{17,9},{25,17},{2,26},{10... | collective-permute-start | bytes 221192 | tf_op jit(solution)/shard_map/ppermute | solution.py:619
  39.8 7.5 %collective-permute-start.13 = (f32[9,16,128]{2,1,0:T(8,128)S(1)}, f32[9,16,128]{2,1,0:T(8,128)S(1)}, u32[]{:S(2)}, u32[]{:S(2)}) collective-permute-start(f32[9,16,128]{2,1,0:T(8,128)S(1)} %get-tuple-element.65), channel_id=1, source_target_pairs={{0,16},{8,24},{16,0},{24,8},{1,17},{9,25},{17,1},{25,9},{2,18},{10... | collective-permute-start | bytes 221192 | tf_op jit(solution)/shard_map/ppermute | solution.py:619
  40.3 7.0 %collective-permute-start.12 = (f32[9,16,128]{2,1,0:T(8,128)S(1)}, f32[9,16,128]{2,1,0:T(8,128)S(1)}, u32[]{:S(2)}, u32[]{:S(2)}) collective-permute-start(f32[9,16,128]{2,1,0:T(8,128)S(1)} %get-tuple-element.65), channel_id=1, source_target_pairs={{0,8},{8,16},{16,24},{24,0},{1,9},{9,17},{17,25},{25,1},{2,10},{10... | collective-permute-start | bytes 221192 | tf_op jit(solution)/shard_map/ppermute | solution.py:619
  49.1 1.4 %collective-permute-start.15 = (f32[4,4,16,128]{3,2,1,0:T(8,128)S(1)}, f32[4,4,16,128]{3,2,1,0:T(8,128)S(1)}, u32[]{:S(2)}, u32[]{:S(2)}) collective-permute-start(f32[4,4,16,128]{3,2,1,0:T(8,128)S(1)} %get-tuple-element.68), channel_id=1, source_target_pairs={{0,1},{1,0},{2,3},{3,2},{4,5},{5,4},{6,7},{7,6},{8,9},{9,8},{10,11... | collective-permute-start | bytes 393224 | tf_op jit(solution)/shard_map/ppermute | solution.py:580
  50.5 6.3 %collective-permute-start.18 = (f32[2,4,16,128]{3,2,1,0:T(8,128)S(1)}, f32[2,4,16,128]{3,2,1,0:T(8,128)S(1)}, u32[]{:S(2)}, u32[]{:S(2)}) collective-permute-start(f32[2,4,16,128]{3,2,1,0:T(8,128)S(1)} %get-tuple-element.71), channel_id=1, source_target_pairs={{0,6},{1,7},{2,4},{3,5},{4,2},{5,3},{6,0},{7,1},{8,14},{9,15},{10,... | collective-permute-start | bytes 196616 | tf_op jit(solution)/shard_map/ppermute | solution.py:580
  52.3 5.8 %collective-permute-start.16 = (f32[2,4,16,128]{3,2,1,0:T(8,128)S(1)}, f32[2,4,16,128]{3,2,1,0:T(8,128)S(1)}, u32[]{:S(2)}, u32[]{:S(2)}) collective-permute-start(f32[2,4,16,128]{3,2,1,0:T(8,128)S(1)} %get-tuple-element.73), channel_id=1, source_target_pairs={{0,2},{1,3},{2,0},{3,1},{4,6},{5,7},{6,4},{7,5},{8,10},{9,11},{10,... | collective-permute-start | bytes 196616 | tf_op jit(solution)/shard_map/ppermute | solution.py:580
  55.3 5.9 %collective-permute-start.17 = (f32[2,4,16,128]{3,2,1,0:T(8,128)S(1)}, f32[2,4,16,128]{3,2,1,0:T(8,128)S(1)}, u32[]{:S(2)}, u32[]{:S(2)}) collective-permute-start(f32[2,4,16,128]{3,2,1,0:T(8,128)S(1)} %get-tuple-element.74), channel_id=1, source_target_pairs={{0,4},{1,5},{2,6},{3,7},{4,0},{5,1},{6,2},{7,3},{8,12},{9,13},{10,... | collective-permute-start | bytes 196616 | tf_op jit(solution)/shard_map/ppermute | solution.py:580
